TPU v7x, 32 devices: a whole 2x2x4 slice. The times are simulated.
32 devices in a mesh: sec: 2 (over core), tile: 16 (over z, y, x).
Axes of the slice: x: 2, y: 2, z: 4, core: 2. Of those that a mesh axis runs over, the one named last changes fastest.
Arguments:
- velocity: float32 [3, 64, 128, 128], P(None, 'tile', 'sec'), may hold values from -6 to 6
- stresses: float32 [6, 64, 128, 128], P(None, 'tile', 'sec'), may hold values from -6 to 6
- buoyancy: float32 [64, 128, 128], P('tile', 'sec'), may hold values from 0.5 to 1.5
- lame_first: float32 [64, 128, 128], P('tile', 'sec'), may hold values from 0.5 to 1.5
- shear_mod: float32 [64, 128, 128], P('tile', 'sec'), may hold values from 0.3 to 1
- ocean_state: float32 [3, 1024, 512], P(None, 'tile', 'sec'), may hold values from -6 to 6
- depth_map: float32 [1024, 512], P('tile', 'sec'), may hold values from 0.5 to 2
- wet_mask: int32 [1024, 512], P('tile', 'sec'), may hold values 0 or 1
- intersection_src: int32 [1024], P('tile'), may hold values from 0 to 15, as said below
- intersection_share: float32 [1024], P('tile'), may hold values from 0.3 to 1
Outputs:
- velocity_out: float32 [3, 64, 128, 128], P(None, 'tile', 'sec')
- stress_out: float32 [6, 64, 128, 128], P(None, 'tile', 'sec')
- ocean_out: float32 [3, 1024, 512], P(None, 'tile', 'sec')
Inputs may be any that keep to these rules, and one draw needn't show every extreme that they name: intersection_src[r] differs from r // 64 by at most 2.
All inputs are finite; a program needn't handle non-finite values. No bound on the sum of `wet_mask` on one device may be relied on, other than what follows from the above.
Results may differ from a plain program's by a relative error of at most 0.000096.
Values sent between devices are 32-bit elements; how exact they have to be, the bound alone decides.
No kernel may reach another device: no remote copies, remote signals or barrier semaphores. Data moves between devices by JAX's collectives and lax.ppermute only.
A program may use at most 64 MiB of HBM per device.

v0:
```python
import jax
import jax.numpy as jnp
from jax import lax
from jax.sharding import PartitionSpec as P

STEPS = 2
OSTEPS = 2
REACH = 2


NEAR_COEF = 9.0 / 8.0
FAR_COEF = -1.0 / 24.0
TIME_STEP = 0.15
OCEAN_STEP = 0.3


def extended(cells, sides, width):
    for axis, dim in sides:
        count = lax.axis_size(axis)
        ends = count - 1
        head = lax.slice_in_dim(cells, 0, width, axis=dim)
        tail = lax.slice_in_dim(cells, cells.shape[dim] - width, cells.shape[dim], axis=dim)
        cells = jnp.concatenate(
            [
                lax.ppermute(tail, axis, [(i, (i + 1) % count) for i in range(ends)]),
                cells,
                lax.ppermute(head, axis, [((i + 1) % count, i) for i in range(ends)]),
            ],
            axis=dim,
        )
    return cells


def from_behind(value, axis, steps):
    count = lax.axis_size(axis)
    leading, last = (max(0, -steps), min(count, count - steps))
    return lax.ppermute(value, axis, [(source, source + steps) for source in range(leading, last)])


def offset_slice(field, shift, dimension):
    window = []
    for current in range(3):
        displaced = shift if current == dimension else 0
        window.append(slice(2 + displaced, field.shape[current] - 2 + displaced))
    return field[tuple(window)]


def forward_diff(field, dimension):
    return NEAR_COEF * (
        offset_slice(field, 1, dimension) - offset_slice(field, 0, dimension)
    ) + FAR_COEF * (offset_slice(field, 2, dimension) - offset_slice(field, -1, dimension))


def backward_diff(field, dimension):
    return NEAR_COEF * (
        offset_slice(field, 0, dimension) - offset_slice(field, -1, dimension)
    ) + FAR_COEF * (offset_slice(field, 1, dimension) - offset_slice(field, -2, dimension))


def update_velocity(velocity, stress_pad, buoyancy):
    accel_x = (
        forward_diff(stress_pad[0], 0)
        + backward_diff(stress_pad[3], 1)
        + backward_diff(stress_pad[4], 2)
    )
    accel_y = (
        backward_diff(stress_pad[3], 0)
        + forward_diff(stress_pad[1], 1)
        + backward_diff(stress_pad[5], 2)
    )
    accel_z = (
        backward_diff(stress_pad[4], 0)
        + backward_diff(stress_pad[5], 1)
        + forward_diff(stress_pad[2], 2)
    )
    return velocity + TIME_STEP * buoyancy * jnp.stack([accel_x, accel_y, accel_z])


def update_stress(stresses, velocity_pad, lame_first, shear_mod):
    strain_x = backward_diff(velocity_pad[0], 0)
    strain_y = backward_diff(velocity_pad[1], 1)
    strain_z = backward_diff(velocity_pad[2], 2)
    volume = strain_x + strain_y + strain_z
    normal_x = stresses[0] + TIME_STEP * (lame_first * volume + 2.0 * shear_mod * strain_x)
    normal_y = stresses[1] + TIME_STEP * (lame_first * volume + 2.0 * shear_mod * strain_y)
    normal_z = stresses[2] + TIME_STEP * (lame_first * volume + 2.0 * shear_mod * strain_z)
    shear_xy = stresses[3] + TIME_STEP * shear_mod * (
        forward_diff(velocity_pad[0], 1) + forward_diff(velocity_pad[1], 0)
    )
    shear_xz = stresses[4] + TIME_STEP * shear_mod * (
        forward_diff(velocity_pad[0], 2) + forward_diff(velocity_pad[2], 0)
    )
    shear_yz = stresses[5] + TIME_STEP * shear_mod * (
        forward_diff(velocity_pad[1], 2) + forward_diff(velocity_pad[2], 1)
    )
    return jnp.stack([normal_x, normal_y, normal_z, shear_xy, shear_xz, shear_yz])


def depth_pad(stacked):
    return jnp.pad(stacked, ((0, 0), (0, 0), (0, 0), (2, 2)))


def shards(
    velocity,
    stresses,
    buoyancy,
    lame_first,
    shear_mod,
    ocean_state,
    depth_map,
    wet_mask,
    intersection_src,
    intersection_share,
):
    for step_index in range(STEPS):
        stress_pad = depth_pad(extended(stresses, (("tile", 1), ("sec", 2)), 2))
        velocity = update_velocity(velocity, stress_pad, buoyancy)
        velocity_pad = depth_pad(extended(velocity, (("tile", 1), ("sec", 2)), 2))
        stresses = update_stress(stresses, velocity_pad, lame_first, shear_mod)
    patch = velocity[2, :, :, 0].reshape(-1)
    candidates = []
    for offset in range(-REACH, REACH + 1):
        if offset == 0:
            candidates.append(patch)
        else:
            candidates.append(from_behind(patch, "tile", -offset))
    candidates = jnp.stack(candidates)
    relative = intersection_src - lax.axis_index("tile") + REACH
    selector = (relative[:, None] == jnp.arange(2 * REACH + 1, dtype=jnp.int32)[None, :]).astype(
        jnp.float32
    )
    uplift = jnp.dot(
        selector, candidates, precision=lax.Precision.HIGHEST, preferred_element_type=jnp.float32
    )
    wet_float = wet_mask.astype(jnp.float32)
    source = intersection_share[:, None] * wet_float * uplift
    for step_index in range(OSTEPS):
        surface = ocean_state[0]
        padded = extended(surface, (("tile", 0), ("sec", 1)), 1)
        grad_x = (padded[2:, 1:-1] - padded[:-2, 1:-1]) * 0.5
        grad_y = (padded[1:-1, 2:] - padded[1:-1, :-2]) * 0.5
        flow_x = wet_float * (ocean_state[1] - OCEAN_STEP * grad_x)
        flow_y = wet_float * (ocean_state[2] - OCEAN_STEP * grad_y)
        flux_pad = extended(
            jnp.stack([depth_map * flow_x, depth_map * flow_y]), (("tile", 1), ("sec", 2)), 1
        )
        spread = (flux_pad[0, 2:, 1:-1] - flux_pad[0, :-2, 1:-1]) * 0.5 + (
            flux_pad[1, 1:-1, 2:] - flux_pad[1, 1:-1, :-2]
        ) * 0.5
        surface = surface - OCEAN_STEP * spread + OCEAN_STEP * source
        ocean_state = jnp.stack([surface, flow_x, flow_y])
    return (velocity, stresses, ocean_state)


def solution(mesh):
    return jax.shard_map(
        shards,
        mesh=mesh,
        in_specs=(
            P(None, "tile", "sec", None),
            P(None, "tile", "sec", None),
            P("tile", "sec", None),
            P("tile", "sec", None),
            P("tile", "sec", None),
            P(None, "tile", "sec"),
            P("tile", "sec"),
            P("tile", "sec"),
            P("tile"),
            P("tile"),
        ),
        out_specs=(
            P(None, "tile", "sec", None),
            P(None, "tile", "sec", None),
            P(None, "tile", "sec"),
        ),
        check_vma=False,
    )
```

profile of v0, /device:TPU:21, one launch (start us, length us, event | category | flops | bytes accessed | tf_op | source)
XLA Modules:
  0.0 160.3 jit_solution(13695257177950902978)
XLA Ops:
  1.9 3.3 %collective-permute-start = (f32[6,2,64,128]{3,2,1,0:T(8,128)S(1)}, f32[6,2,64,128]{3,2,1,0:T(8,128)S(1)}, u32[]{:S(2)}, u32[]{:S(2)}) collective-permute-start(f32[6,2,64,128]{3,2,1,0:T(8,128)S(1)} %get-tuple-element.53), channel_id=1, source_target_pairs={{0,1},{1,2},{2,3},{3,4},{4,5},{5,6},{6,7},{7,8},{8,9},{9,10},{10,1... | collective-permute-start | bytes 1179656 | tf_op jit(solution)/shard_map/ppermute | solution.py:25
  5.2 3.1 %collective-permute-start.1 = (f32[6,2,64,128]{3,2,1,0:T(8,128)S(1)}, f32[6,2,64,128]{3,2,1,0:T(8,128)S(1)}, u32[]{:S(2)}, u32[]{:S(2)}) collective-permute-start(f32[6,2,64,128]{3,2,1,0:T(8,128)S(1)} %get-tuple-element.52), channel_id=1, source_target_pairs={{1,0},{2,1},{3,2},{4,3},{5,4},{6,5},{7,6},{8,7},{9,8},{10,9},{11,1... | collective-permute-start | bytes 1179656 | tf_op jit(solution)/shard_map/ppermute | solution.py:27
  9.0 2.2 %collective-permute-start.16 = (f32[1,256]{1,0:T(1,128)S(1)}, f32[1,256]{1,0:T(1,128)S(1)}, u32[]{:S(2)}, u32[]{:S(2)}) collective-permute-start(f32[1,256]{1,0:T(1,128)S(1)} %get-tuple-element.60), channel_id=1, source_target_pairs={{1,0},{2,1},{3,2},{4,3},{5,4},{6,5},{7,6},{8,7},{9,8},{10,9},{11,1... | collective-permute-start | bytes 3080 | tf_op jit(solution)/shard_map/ppermute | solution.py:27
  11.1 3.1 %collective-permute-start.17 = (f32[1,256]{1,0:T(1,128)S(1)}, f32[1,256]{1,0:T(1,128)S(1)}, u32[]{:S(2)}, u32[]{:S(2)}) collective-permute-start(f32[1,256]{1,0:T(1,128)S(1)} %get-tuple-element.59), channel_id=1, source_target_pairs={{0,1},{1,2},{2,3},{3,4},{4,5},{5,6},{6,7},{7,8},{8,9},{9,10},{10,1... | collective-permute-start | bytes 3080 | tf_op jit(solution)/shard_map/ppermute | solution.py:25
  14.9 9.3 %collective-permute-done.1 = f32[6,2,64,128]{3,2,1,0:T(8,128)S(1)} collective-permute-done((f32[6,2,64,128]{3,2,1,0:T(8,128)S(1)}, f32[6,2,64,128]{3,2,1,0:T(8,128)S(1)}, u32[]{:S(2)}, u32[]{:S(2)}) %collective-permute-start.1) | collective-permute-done | bytes 393248 | tf_op jit(solution)/shard_map/ppermute | solution.py:27
  25.6 3.0 %collective-permute-start.3 = (f32[6,8,2,128]{3,2,1,0:T(2,128)S(1)}, f32[6,8,2,128]{3,2,1,0:T(2,128)S(1)}, u32[]{:S(2)}, u32[]{:S(2)}) collective-permute-start(f32[6,8,2,128]{3,2,1,0:T(2,128)S(1)} %get-tuple-element.45), channel_id=1, source_target_pairs={{16,0},{17,1},{18,2},{19,3},{20,4},{21,5},{22,6},{23,7},{24,8},{25... | collective-permute-start | bytes 147464 | tf_op jit(solution)/shard_map/ppermute | solution.py:27
  32.6 1.9 %collective-permute-start.4 = (f32[3,2,64,128]{3,2,1,0:T(8,128)S(1)}, f32[3,2,64,128]{3,2,1,0:T(8,128)S(1)}, u32[]{:S(2)}, u32[]{:S(2)}) collective-permute-start(f32[3,2,64,128]{3,2,1,0:T(8,128)S(1)} %get-tuple-element.57), channel_id=1, source_target_pairs={{0,1},{1,2},{2,3},{3,4},{4,5},{5,6},{6,7},{7,8},{8,9},{9,10},{10,1... | collective-permute-start | bytes 589832 | tf_op jit(solution)/shard_map/ppermute | solution.py:25
  34.6 4.3 %collective-permute-start.5 = (f32[3,2,64,128]{3,2,1,0:T(8,128)S(1)}, f32[3,2,64,128]{3,2,1,0:T(8,128)S(1)}, u32[]{:S(2)}, u32[]{:S(2)}) collective-permute-start(f32[3,2,64,128]{3,2,1,0:T(8,128)S(1)} %get-tuple-element.58), channel_id=1, source_target_pairs={{1,0},{2,1},{3,2},{4,3},{5,4},{6,5},{7,6},{8,7},{9,8},{10,9},{11,1... | collective-permute-start | bytes 589832 | tf_op jit(solution)/shard_map/ppermute | solution.py:27
  38.9 2.6 %collective-permute-done.4 = f32[3,2,64,128]{3,2,1,0:T(8,128)S(1)} collective-permute-done((f32[3,2,64,128]{3,2,1,0:T(8,128)S(1)}, f32[3,2,64,128]{3,2,1,0:T(8,128)S(1)}, u32[]{:S(2)}, u32[]{:S(2)}) %collective-permute-start.4) | collective-permute-done | bytes 196640 | tf_op jit(solution)/shard_map/ppermute | solution.py:25
  41.6 4.3 %collective-permute-done.5 = f32[3,2,64,128]{3,2,1,0:T(8,128)S(1)} collective-permute-done((f32[3,2,64,128]{3,2,1,0:T(8,128)S(1)}, f32[3,2,64,128]{3,2,1,0:T(8,128)S(1)}, u32[]{:S(2)}, u32[]{:S(2)}) %collective-permute-start.5) | collective-permute-done | bytes 196640 | tf_op jit(solution)/shard_map/ppermute | solution.py:27
  47.2 3.0 %collective-permute-start.7 = (f32[3,8,2,128]{3,2,1,0:T(2,128)S(1)}, f32[3,8,2,128]{3,2,1,0:T(2,128)S(1)}, u32[]{:S(2)}, u32[]{:S(2)}) collective-permute-start(f32[3,8,2,128]{3,2,1,0:T(2,128)S(1)} %get-tuple-element.51), channel_id=1, source_target_pairs={{16,0},{17,1},{18,2},{19,3},{20,4},{21,5},{22,6},{23,7},{24,8},{25... | collective-permute-start | bytes 73736 | tf_op jit(solution)/shard_map/ppermute | solution.py:27
  56.9 2.3 %collective-permute-start.8 = (f32[6,2,64,128]{3,2,1,0:T(8,128)S(1)}, f32[6,2,64,128]{3,2,1,0:T(8,128)S(1)}, u32[]{:S(2)}, u32[]{:S(2)}) collective-permute-start(f32[6,2,64,128]{3,2,1,0:T(8,128)S(1)} %get-tuple-element.48), channel_id=1, source_target_pairs={{0,1},{1,2},{2,3},{3,4},{4,5},{5,6},{6,7},{7,8},{8,9},{9,10},{10,1... | collective-permute-start | bytes 1179656 | tf_op jit(solution)/shard_map/ppermute | solution.py:25
  59.2 3.8 %collective-permute-start.9 = (f32[6,2,64,128]{3,2,1,0:T(8,128)S(1)}, f32[6,2,64,128]{3,2,1,0:T(8,128)S(1)}, u32[]{:S(2)}, u32[]{:S(2)}) collective-permute-start(f32[6,2,64,128]{3,2,1,0:T(8,128)S(1)} %get-tuple-element.49), channel_id=1, source_target_pairs={{1,0},{2,1},{3,2},{4,3},{5,4},{6,5},{7,6},{8,7},{9,8},{10,9},{11,1... | collective-permute-start | bytes 1179656 | tf_op jit(solution)/shard_map/ppermute | solution.py:27
  66.4 3.4 %collective-permute-start.21 = (f32[2,1,256]{2,1,0:T(1,128)S(1)}, f32[2,1,256]{2,1,0:T(1,128)S(1)}, u32[]{:S(2)}, u32[]{:S(2)}) collective-permute-start(f32[2,1,256]{2,1,0:T(1,128)S(1)} %get-tuple-element.67), channel_id=1, source_target_pairs={{0,1},{1,2},{2,3},{3,4},{4,5},{5,6},{6,7},{7,8},{8,9},{9,10},{10,1... | collective-permute-start | bytes 6152 | tf_op jit(solution)/shard_map/ppermute | solution.py:25
  69.8 9.3 %collective-permute-done.9 = f32[6,2,64,128]{3,2,1,0:T(8,128)S(1)} collective-permute-done((f32[6,2,64,128]{3,2,1,0:T(8,128)S(1)}, f32[6,2,64,128]{3,2,1,0:T(8,128)S(1)}, u32[]{:S(2)}, u32[]{:S(2)}) %collective-permute-start.9) | collective-permute-done | bytes 393248 | tf_op jit(solution)/shard_map/ppermute | solution.py:27
  80.5 3.0 %collective-permute-start.11 = (f32[6,8,2,128]{3,2,1,0:T(2,128)S(1)}, f32[6,8,2,128]{3,2,1,0:T(2,128)S(1)}, u32[]{:S(2)}, u32[]{:S(2)}) collective-permute-start(f32[6,8,2,128]{3,2,1,0:T(2,128)S(1)} %get-tuple-element.43), channel_id=1, source_target_pairs={{16,0},{17,1},{18,2},{19,3},{20,4},{21,5},{22,6},{23,7},{24,8},{25... | collective-permute-start | bytes 147464 | tf_op jit(solution)/shard_map/ppermute | solution.py:27
  84.4 2.2 %select_maximum_fusion = f32[6,8,68,132]{3,2,1,0:T(8,128)S(1)} fusion(f32[6,8,2,128]{3,2,1,0:T(2,128)S(1)} %collective-permute-done.11, f32[6,8,2,128]{3,2,1,0:T(2,128)S(1)} %collective-permute-done.10, f32[6,2,64,128]{3,2,1,0:T(8,128)S(1)} %collective-permute-done.9, f32[6,4,64,128]{3,2,1,0:T(8,128)S(1)} %get-tuple-element.13, ...), kind=kLoop, calls=%fused_computation.2 | loop fusion | flops 5170176 | bytes 3394560 | tf_op jit(solution)/shard_map/concatenate | solution.py:23
  88.6 2.7 %collective-permute-start.24 = (f32[256]{0:T(256)S(1)}, f32[256]{0:T(256)S(1)}, u32[]{:S(2)}, u32[]{:S(2)}) collective-permute-start(f32[256]{0:T(256)S(1)} %reshape_squeeze.3), channel_id=1, source_target_pairs={{0,2},{1,3},{2,4},{3,5},{4,6},{5,7},{6,8},{7,9},{8,10},{9,11},{10,... | collective-permute-start | bytes 3080 | tf_op jit(solution)/shard_map/ppermute | solution.py:37
  91.2 1.9 %collective-permute-start.25 = (f32[256]{0:T(256)S(1)}, f32[256]{0:T(256)S(1)}, u32[]{:S(2)}, u32[]{:S(2)}) collective-permute-start(f32[256]{0:T(256)S(1)} %reshape_squeeze.3), channel_id=1, source_target_pairs={{0,1},{1,2},{2,3},{3,4},{4,5},{5,6},{6,7},{7,8},{8,9},{9,10},{10,1... | collective-permute-start | bytes 3080 | tf_op jit(solution)/shard_map/ppermute | solution.py:37
  93.2 4.3 %collective-permute-start.26 = (f32[256]{0:T(256)S(1)}, f32[256]{0:T(256)S(1)}, u32[]{:S(2)}, u32[]{:S(2)}) collective-permute-start(f32[256]{0:T(256)S(1)} %reshape_squeeze.3), channel_id=1, source_target_pairs={{1,0},{2,1},{3,2},{4,3},{5,4},{6,5},{7,6},{8,7},{9,8},{10,9},{11,1... | collective-permute-start | bytes 3080 | tf_op jit(solution)/shard_map/ppermute | solution.py:37
  97.4 3.5 %collective-permute-start.27 = (f32[256]{0:T(256)S(1)}, f32[256]{0:T(256)S(1)}, u32[]{:S(2)}, u32[]{:S(2)}) collective-permute-start(f32[256]{0:T(256)S(1)} %reshape_squeeze.3), channel_id=1, source_target_pairs={{2,0},{3,1},{4,2},{5,3},{6,4},{7,5},{8,6},{9,7},{10,8},{11,9},{12,... | collective-permute-start | bytes 3080 | tf_op jit(solution)/shard_map/ppermute | solution.py:37
  101.1 3.4 %collective-permute-start.22 = (f32[2,66,1]{2,1,0:T(8,128)S(1)}, f32[2,66,1]{2,1,0:T(8,128)S(1)}, u32[]{:S(2)}, u32[]{:S(2)}) collective-permute-start(f32[2,66,1]{2,1,0:T(8,128)S(1)} %get-tuple-element.63), channel_id=1, source_target_pairs={{16,0},{17,1},{18,2},{19,3},{20,4},{21,5},{22,6},{23,7},{24,8},{25... | collective-permute-start | bytes 1592 | tf_op jit(solution)/shard_map/ppermute | solution.py:27
  110.6 3.4 %collective-permute-start.29 = (f32[1,256]{1,0:T(1,128)S(1)}, f32[1,256]{1,0:T(1,128)S(1)}, u32[]{:S(2)}, u32[]{:S(2)}) collective-permute-start(f32[1,256]{1,0:T(1,128)S(1)} %get-tuple-element.73), channel_id=1, source_target_pairs={{0,1},{1,2},{2,3},{3,4},{4,5},{5,6},{6,7},{7,8},{8,9},{9,10},{10,1... | collective-permute-start | bytes 3080 | tf_op jit(solution)/shard_map/ppermute | solution.py:25
  115.9 3.2 %collective-permute-start.30 = (f32[66,1]{1,0:T(8,128)S(1)}, f32[66,1]{1,0:T(8,128)S(1)}, u32[]{:S(2)}, u32[]{:S(2)}) collective-permute-start(f32[66,1]{1,0:T(8,128)S(1)} %get-tuple-element.69), channel_id=1, source_target_pairs={{16,0},{17,1},{18,2},{19,3},{20,4},{21,5},{22,6},{23,7},{24,8},{25... | collective-permute-start | bytes 800 | tf_op jit(solution)/shard_map/ppermute | solution.py:27
  122.4 2.2 %collective-permute-start.32 = (f32[2,1,256]{2,1,0:T(1,128)S(1)}, f32[2,1,256]{2,1,0:T(1,128)S(1)}, u32[]{:S(2)}, u32[]{:S(2)}) collective-permute-start(f32[2,1,256]{2,1,0:T(1,128)S(1)} %get-tuple-element.66), channel_id=1, source_target_pairs={{1,0},{2,1},{3,2},{4,3},{5,4},{6,5},{7,6},{8,7},{9,8},{10,9},{11,1... | collective-permute-start | bytes 6152 | tf_op jit(solution)/shard_map/ppermute | solution.py:27
  124.6 3.1 %collective-permute-start.33 = (f32[2,1,256]{2,1,0:T(1,128)S(1)}, f32[2,1,256]{2,1,0:T(1,128)S(1)}, u32[]{:S(2)}, u32[]{:S(2)}) collective-permute-start(f32[2,1,256]{2,1,0:T(1,128)S(1)} %get-tuple-element.65), channel_id=1, source_target_pairs={{0,1},{1,2},{2,3},{3,4},{4,5},{5,6},{6,7},{7,8},{8,9},{9,10},{10,1... | collective-permute-start | bytes 6152 | tf_op jit(solution)/shard_map/ppermute | solution.py:25
  127.7 2.1 %collective-permute-done.33 = f32[2,1,256]{2,1,0:T(1,128)S(1)} collective-permute-done((f32[2,1,256]{2,1,0:T(1,128)S(1)}, f32[2,1,256]{2,1,0:T(1,128)S(1)}, u32[]{:S(2)}, u32[]{:S(2)}) %collective-permute-start.33) | collective-permute-done | bytes 2080 | tf_op jit(solution)/shard_map/ppermute | solution.py:25
  129.9 3.6 %collective-permute-start.34 = (f32[2,66,1]{2,1,0:T(8,128)S(1)}, f32[2,66,1]{2,1,0:T(8,128)S(1)}, u32[]{:S(2)}, u32[]{:S(2)}) collective-permute-start(f32[2,66,1]{2,1,0:T(8,128)S(1)} %get-tuple-element.61), channel_id=1, source_target_pairs={{16,0},{17,1},{18,2},{19,3},{20,4},{21,5},{22,6},{23,7},{24,8},{25... | collective-permute-start | bytes 1592 | tf_op jit(solution)/shard_map/ppermute | solution.py:27
  134.9 2.8 %collective-permute-start.12 = (f32[3,2,64,128]{3,2,1,0:T(8,128)S(1)}, f32[3,2,64,128]{3,2,1,0:T(8,128)S(1)}, u32[]{:S(2)}, u32[]{:S(2)}) collective-permute-start(f32[3,2,64,128]{3,2,1,0:T(8,128)S(1)} %get-tuple-element.55), channel_id=1, source_target_pairs={{0,1},{1,2},{2,3},{3,4},{4,5},{5,6},{6,7},{7,8},{8,9},{9,10},{10,1... | collective-permute-start | bytes 589832 | tf_op jit(solution)/shard_map/ppermute | solution.py:25
  137.7 3.5 %collective-permute-start.13 = (f32[3,2,64,128]{3,2,1,0:T(8,128)S(1)}, f32[3,2,64,128]{3,2,1,0:T(8,128)S(1)}, u32[]{:S(2)}, u32[]{:S(2)}) collective-permute-start(f32[3,2,64,128]{3,2,1,0:T(8,128)S(1)} %get-tuple-element.56), channel_id=1, source_target_pairs={{1,0},{2,1},{3,2},{4,3},{5,4},{6,5},{7,6},{8,7},{9,8},{10,9},{11,1... | collective-permute-start | bytes 589832 | tf_op jit(solution)/shard_map/ppermute | solution.py:27
  142.9 8.0 %collective-permute-done.13 = f32[3,2,64,128]{3,2,1,0:T(8,128)S(1)} collective-permute-done((f32[3,2,64,128]{3,2,1,0:T(8,128)S(1)}, f32[3,2,64,128]{3,2,1,0:T(8,128)S(1)}, u32[]{:S(2)}, u32[]{:S(2)}) %collective-permute-start.13) | collective-permute-done | bytes 196640 | tf_op jit(solution)/shard_map/ppermute | solution.py:27
  152.3 3.0 %collective-permute-start.15 = (f32[3,8,2,128]{3,2,1,0:T(2,128)S(1)}, f32[3,8,2,128]{3,2,1,0:T(2,128)S(1)}, u32[]{:S(2)}, u32[]{:S(2)}) collective-permute-start(f32[3,8,2,128]{3,2,1,0:T(2,128)S(1)} %get-tuple-element.47), channel_id=1, source_target_pairs={{16,0},{17,1},{18,2},{19,3},{20,4},{21,5},{22,6},{23,7},{24,8},{25... | collective-permute-start | bytes 73736 | tf_op jit(solution)/shard_map/ppermute | solution.py:27
  (140 shorter events, 43.8 us)
Async XLA Ops:
  1.9 12.9 %collective-permute-start = (f32[6,2,64,128]{3,2,1,0:T(8,128)S(1)}, f32[6,2,64,128]{3,2,1,0:T(8,128)S(1)}, u32[]{:S(2)}, u32[]{:S(2)}) collective-permute-start(f32[6,2,64,128]{3,2,1,0:T(8,128)S(1)} %get-tuple-element.53), channel_id=1, source_target_pairs={{0,1},{1,2},{2,3},{3,4},{4,5},{5,6},{6,7},{7,8},{8,9},{9,10},{10,1... | collective-permute-start | bytes 1179656 | tf_op jit(solution)/shard_map/ppermute | solution.py:25
  5.2 19.1 %collective-permute-start.1 = (f32[6,2,64,128]{3,2,1,0:T(8,128)S(1)}, f32[6,2,64,128]{3,2,1,0:T(8,128)S(1)}, u32[]{:S(2)}, u32[]{:S(2)}) collective-permute-start(f32[6,2,64,128]{3,2,1,0:T(8,128)S(1)} %get-tuple-element.52), channel_id=1, source_target_pairs={{1,0},{2,1},{3,2},{4,3},{5,4},{6,5},{7,6},{8,7},{9,8},{10,9},{11,1... | collective-permute-start | bytes 1179656 | tf_op jit(solution)/shard_map/ppermute | solution.py:27
  9.0 29.9 %collective-permute-start.16 = (f32[1,256]{1,0:T(1,128)S(1)}, f32[1,256]{1,0:T(1,128)S(1)}, u32[]{:S(2)}, u32[]{:S(2)}) collective-permute-start(f32[1,256]{1,0:T(1,128)S(1)} %get-tuple-element.60), channel_id=1, source_target_pairs={{1,0},{2,1},{3,2},{4,3},{5,4},{6,5},{7,6},{8,7},{9,8},{10,9},{11,1... | collective-permute-start | bytes 3080 | tf_op jit(solution)/shard_map/ppermute | solution.py:27
  11.1 27.8 %collective-permute-start.17 = (f32[1,256]{1,0:T(1,128)S(1)}, f32[1,256]{1,0:T(1,128)S(1)}, u32[]{:S(2)}, u32[]{:S(2)}) collective-permute-start(f32[1,256]{1,0:T(1,128)S(1)} %get-tuple-element.59), channel_id=1, source_target_pairs={{0,1},{1,2},{2,3},{3,4},{4,5},{5,6},{6,7},{7,8},{8,9},{9,10},{10,1... | collective-permute-start | bytes 3080 | tf_op jit(solution)/shard_map/ppermute | solution.py:25
  24.3 4.4 %collective-permute-start.2 = (f32[6,8,2,128]{3,2,1,0:T(2,128)S(1)}, f32[6,8,2,128]{3,2,1,0:T(2,128)S(1)}, u32[]{:S(2)}, u32[]{:S(2)}) collective-permute-start(f32[6,8,2,128]{3,2,1,0:T(2,128)S(1)} %get-tuple-element.44), channel_id=1, source_target_pairs={{0,16},{1,17},{2,18},{3,19},{4,20},{5,21},{6,22},{7,23},{8,24},{9,... | collective-permute-start | bytes 147464 | tf_op jit(solution)/shard_map/ppermute | solution.py:25
  25.6 3.9 %collective-permute-start.3 = (f32[6,8,2,128]{3,2,1,0:T(2,128)S(1)}, f32[6,8,2,128]{3,2,1,0:T(2,128)S(1)}, u32[]{:S(2)}, u32[]{:S(2)}) collective-permute-start(f32[6,8,2,128]{3,2,1,0:T(2,128)S(1)} %get-tuple-element.45), channel_id=1, source_target_pairs={{16,0},{17,1},{18,2},{19,3},{20,4},{21,5},{22,6},{23,7},{24,8},{25... | collective-permute-start | bytes 147464 | tf_op jit(solution)/shard_map/ppermute | solution.py:27
  32.6 8.9 %collective-permute-start.4 = (f32[3,2,64,128]{3,2,1,0:T(8,128)S(1)}, f32[3,2,64,128]{3,2,1,0:T(8,128)S(1)}, u32[]{:S(2)}, u32[]{:S(2)}) collective-permute-start(f32[3,2,64,128]{3,2,1,0:T(8,128)S(1)} %get-tuple-element.57), channel_id=1, source_target_pairs={{0,1},{1,2},{2,3},{3,4},{4,5},{5,6},{6,7},{7,8},{8,9},{9,10},{10,1... | collective-permute-start | bytes 589832 | tf_op jit(solution)/shard_map/ppermute | solution.py:25
  34.6 11.3 %collective-permute-start.5 = (f32[3,2,64,128]{3,2,1,0:T(8,128)S(1)}, f32[3,2,64,128]{3,2,1,0:T(8,128)S(1)}, u32[]{:S(2)}, u32[]{:S(2)}) collective-permute-start(f32[3,2,64,128]{3,2,1,0:T(8,128)S(1)} %get-tuple-element.58), channel_id=1, source_target_pairs={{1,0},{2,1},{3,2},{4,3},{5,4},{6,5},{7,6},{8,7},{9,8},{10,9},{11,1... | collective-permute-start | bytes 589832 | tf_op jit(solution)/shard_map/ppermute | solution.py:27
  45.9 7.0 %collective-permute-start.6 = (f32[3,8,2,128]{3,2,1,0:T(2,128)S(1)}, f32[3,8,2,128]{3,2,1,0:T(2,128)S(1)}, u32[]{:S(2)}, u32[]{:S(2)}) collective-permute-start(f32[3,8,2,128]{3,2,1,0:T(2,128)S(1)} %get-tuple-element.50), channel_id=1, source_target_pairs={{0,16},{1,17},{2,18},{3,19},{4,20},{5,21},{6,22},{7,23},{8,24},{9,... | collective-permute-start | bytes 73736 | tf_op jit(solution)/shard_map/ppermute | solution.py:25
  47.2 5.7 %collective-permute-start.7 = (f32[3,8,2,128]{3,2,1,0:T(2,128)S(1)}, f32[3,8,2,128]{3,2,1,0:T(2,128)S(1)}, u32[]{:S(2)}, u32[]{:S(2)}) collective-permute-start(f32[3,8,2,128]{3,2,1,0:T(2,128)S(1)} %get-tuple-element.51), channel_id=1, source_target_pairs={{16,0},{17,1},{18,2},{19,3},{20,4},{21,5},{22,6},{23,7},{24,8},{25... | collective-permute-start | bytes 73736 | tf_op jit(solution)/shard_map/ppermute | solution.py:27
  50.4 13.3 %collective-permute-start.18 = (f32[66,1]{1,0:T(8,128)S(1)}, f32[66,1]{1,0:T(8,128)S(1)}, u32[]{:S(2)}, u32[]{:S(2)}) collective-permute-start(f32[66,1]{1,0:T(8,128)S(1)} %get-tuple-element.71), channel_id=1, source_target_pairs={{16,0},{17,1},{18,2},{19,3},{20,4},{21,5},{22,6},{23,7},{24,8},{25... | collective-permute-start | bytes 800 | tf_op jit(solution)/shard_map/ppermute | solution.py:27
  51.6 12.0 %collective-permute-start.19 = (f32[66,1]{1,0:T(8,128)S(1)}, f32[66,1]{1,0:T(8,128)S(1)}, u32[]{:S(2)}, u32[]{:S(2)}) collective-permute-start(f32[66,1]{1,0:T(8,128)S(1)} %get-tuple-element.72), channel_id=1, source_target_pairs={{0,16},{1,17},{2,18},{3,19},{4,20},{5,21},{6,22},{7,23},{8,24},{9,... | collective-permute-start | bytes 800 | tf_op jit(solution)/shard_map/ppermute | solution.py:25
  56.9 12.9 %collective-permute-start.8 = (f32[6,2,64,128]{3,2,1,0:T(8,128)S(1)}, f32[6,2,64,128]{3,2,1,0:T(8,128)S(1)}, u32[]{:S(2)}, u32[]{:S(2)}) collective-permute-start(f32[6,2,64,128]{3,2,1,0:T(8,128)S(1)} %get-tuple-element.48), channel_id=1, source_target_pairs={{0,1},{1,2},{2,3},{3,4},{4,5},{5,6},{6,7},{7,8},{8,9},{9,10},{10,1... | collective-permute-start | bytes 1179656 | tf_op jit(solution)/shard_map/ppermute | solution.py:25
  59.2 19.9 %collective-permute-start.9 = (f32[6,2,64,128]{3,2,1,0:T(8,128)S(1)}, f32[6,2,64,128]{3,2,1,0:T(8,128)S(1)}, u32[]{:S(2)}, u32[]{:S(2)}) collective-permute-start(f32[6,2,64,128]{3,2,1,0:T(8,128)S(1)} %get-tuple-element.49), channel_id=1, source_target_pairs={{1,0},{2,1},{3,2},{4,3},{5,4},{6,5},{7,6},{8,7},{9,8},{10,9},{11,1... | collective-permute-start | bytes 1179656 | tf_op jit(solution)/shard_map/ppermute | solution.py:27
  64.5 19.0 %collective-permute-start.20 = (f32[2,1,256]{2,1,0:T(1,128)S(1)}, f32[2,1,256]{2,1,0:T(1,128)S(1)}, u32[]{:S(2)}, u32[]{:S(2)}) collective-permute-start(f32[2,1,256]{2,1,0:T(1,128)S(1)} %get-tuple-element.68), channel_id=1, source_target_pairs={{1,0},{2,1},{3,2},{4,3},{5,4},{6,5},{7,6},{8,7},{9,8},{10,9},{11,1... | collective-permute-start | bytes 6152 | tf_op jit(solution)/shard_map/ppermute | solution.py:27
  66.4 17.1 %collective-permute-start.21 = (f32[2,1,256]{2,1,0:T(1,128)S(1)}, f32[2,1,256]{2,1,0:T(1,128)S(1)}, u32[]{:S(2)}, u32[]{:S(2)}) collective-permute-start(f32[2,1,256]{2,1,0:T(1,128)S(1)} %get-tuple-element.67), channel_id=1, source_target_pairs={{0,1},{1,2},{2,3},{3,4},{4,5},{5,6},{6,7},{7,8},{8,9},{9,10},{10,1... | collective-permute-start | bytes 6152 | tf_op jit(solution)/shard_map/ppermute | solution.py:25
  79.2 4.4 %collective-permute-start.10 = (f32[6,8,2,128]{3,2,1,0:T(2,128)S(1)}, f32[6,8,2,128]{3,2,1,0:T(2,128)S(1)}, u32[]{:S(2)}, u32[]{:S(2)}) collective-permute-start(f32[6,8,2,128]{3,2,1,0:T(2,128)S(1)} %get-tuple-element.42), channel_id=1, source_target_pairs={{0,16},{1,17},{2,18},{3,19},{4,20},{5,21},{6,22},{7,23},{8,24},{9,... | collective-permute-start | bytes 147464 | tf_op jit(solution)/shard_map/ppermute | solution.py:25
  88.6 15.9 %collective-permute-start.24 = (f32[256]{0:T(256)S(1)}, f32[256]{0:T(256)S(1)}, u32[]{:S(2)}, u32[]{:S(2)}) collective-permute-start(f32[256]{0:T(256)S(1)} %reshape_squeeze.3), channel_id=1, source_target_pairs={{0,2},{1,3},{2,4},{3,5},{4,6},{5,7},{6,8},{7,9},{8,10},{9,11},{10,... | collective-permute-start | bytes 3080 | tf_op jit(solution)/shard_map/ppermute | solution.py:37
  91.2 14.6 %collective-permute-start.25 = (f32[256]{0:T(256)S(1)}, f32[256]{0:T(256)S(1)}, u32[]{:S(2)}, u32[]{:S(2)}) collective-permute-start(f32[256]{0:T(256)S(1)} %reshape_squeeze.3), channel_id=1, source_target_pairs={{0,1},{1,2},{2,3},{3,4},{4,5},{5,6},{6,7},{7,8},{8,9},{9,10},{10,1... | collective-permute-start | bytes 3080 | tf_op jit(solution)/shard_map/ppermute | solution.py:37
  93.2 12.7 %collective-permute-start.26 = (f32[256]{0:T(256)S(1)}, f32[256]{0:T(256)S(1)}, u32[]{:S(2)}, u32[]{:S(2)}) collective-permute-start(f32[256]{0:T(256)S(1)} %reshape_squeeze.3), channel_id=1, source_target_pairs={{1,0},{2,1},{3,2},{4,3},{5,4},{6,5},{7,6},{8,7},{9,8},{10,9},{11,1... | collective-permute-start | bytes 3080 | tf_op jit(solution)/shard_map/ppermute | solution.py:37
  97.4 8.4 %collective-permute-start.27 = (f32[256]{0:T(256)S(1)}, f32[256]{0:T(256)S(1)}, u32[]{:S(2)}, u32[]{:S(2)}) collective-permute-start(f32[256]{0:T(256)S(1)} %reshape_squeeze.3), channel_id=1, source_target_pairs={{2,0},{3,1},{4,2},{5,3},{6,4},{7,5},{8,6},{9,7},{10,8},{11,9},{12,... | collective-permute-start | bytes 3080 | tf_op jit(solution)/shard_map/ppermute | solution.py:37
  101.1 4.8 %collective-permute-start.22 = (f32[2,66,1]{2,1,0:T(8,128)S(1)}, f32[2,66,1]{2,1,0:T(8,128)S(1)}, u32[]{:S(2)}, u32[]{:S(2)}) collective-permute-start(f32[2,66,1]{2,1,0:T(8,128)S(1)} %get-tuple-element.63), channel_id=1, source_target_pairs={{16,0},{17,1},{18,2},{19,3},{20,4},{21,5},{22,6},{23,7},{24,8},{25... | collective-permute-start | bytes 1592 | tf_op jit(solution)/shard_map/ppermute | solution.py:27
  108.7 5.3 %collective-permute-start.28 = (f32[1,256]{1,0:T(1,128)S(1)}, f32[1,256]{1,0:T(1,128)S(1)}, u32[]{:S(2)}, u32[]{:S(2)}) collective-permute-start(f32[1,256]{1,0:T(1,128)S(1)} %get-tuple-element.74), channel_id=1, source_target_pairs={{1,0},{2,1},{3,2},{4,3},{5,4},{6,5},{7,6},{8,7},{9,8},{10,9},{11,1... | collective-permute-start | bytes 3080 | tf_op jit(solution)/shard_map/ppermute | solution.py:27
  110.6 5.2 %collective-permute-start.29 = (f32[1,256]{1,0:T(1,128)S(1)}, f32[1,256]{1,0:T(1,128)S(1)}, u32[]{:S(2)}, u32[]{:S(2)}) collective-permute-start(f32[1,256]{1,0:T(1,128)S(1)} %get-tuple-element.73), channel_id=1, source_target_pairs={{0,1},{1,2},{2,3},{3,4},{4,5},{5,6},{6,7},{7,8},{8,9},{9,10},{10,1... | collective-permute-start | bytes 3080 | tf_op jit(solution)/shard_map/ppermute | solution.py:25
  115.9 5.4 %collective-permute-start.30 = (f32[66,1]{1,0:T(8,128)S(1)}, f32[66,1]{1,0:T(8,128)S(1)}, u32[]{:S(2)}, u32[]{:S(2)}) collective-permute-start(f32[66,1]{1,0:T(8,128)S(1)} %get-tuple-element.69), channel_id=1, source_target_pairs={{16,0},{17,1},{18,2},{19,3},{20,4},{21,5},{22,6},{23,7},{24,8},{25... | collective-permute-start | bytes 800 | tf_op jit(solution)/shard_map/ppermute | solution.py:27
  122.4 5.3 %collective-permute-start.32 = (f32[2,1,256]{2,1,0:T(1,128)S(1)}, f32[2,1,256]{2,1,0:T(1,128)S(1)}, u32[]{:S(2)}, u32[]{:S(2)}) collective-permute-start(f32[2,1,256]{2,1,0:T(1,128)S(1)} %get-tuple-element.66), channel_id=1, source_target_pairs={{1,0},{2,1},{3,2},{4,3},{5,4},{6,5},{7,6},{8,7},{9,8},{10,9},{11,1... | collective-permute-start | bytes 6152 | tf_op jit(solution)/shard_map/ppermute | solution.py:27
  124.6 5.2 %collective-permute-start.33 = (f32[2,1,256]{2,1,0:T(1,128)S(1)}, f32[2,1,256]{2,1,0:T(1,128)S(1)}, u32[]{:S(2)}, u32[]{:S(2)}) collective-permute-start(f32[2,1,256]{2,1,0:T(1,128)S(1)} %get-tuple-element.65), channel_id=1, source_target_pairs={{0,1},{1,2},{2,3},{3,4},{4,5},{5,6},{6,7},{7,8},{8,9},{9,10},{10,1... | collective-permute-start | bytes 6152 | tf_op jit(solution)/shard_map/ppermute | solution.py:25
  129.9 11.3 %collective-permute-start.34 = (f32[2,66,1]{2,1,0:T(8,128)S(1)}, f32[2,66,1]{2,1,0:T(8,128)S(1)}, u32[]{:S(2)}, u32[]{:S(2)}) collective-permute-start(f32[2,66,1]{2,1,0:T(8,128)S(1)} %get-tuple-element.61), channel_id=1, source_target_pairs={{16,0},{17,1},{18,2},{19,3},{20,4},{21,5},{22,6},{23,7},{24,8},{25... | collective-permute-start | bytes 1592 | tf_op jit(solution)/shard_map/ppermute | solution.py:27
  133.5 7.7 %collective-permute-start.35 = (f32[2,66,1]{2,1,0:T(8,128)S(1)}, f32[2,66,1]{2,1,0:T(8,128)S(1)}, u32[]{:S(2)}, u32[]{:S(2)}) collective-permute-start(f32[2,66,1]{2,1,0:T(8,128)S(1)} %get-tuple-element.62), channel_id=1, source_target_pairs={{0,16},{1,17},{2,18},{3,19},{4,20},{5,21},{6,22},{7,23},{8,24},{9,... | collective-permute-start | bytes 1592 | tf_op jit(solution)/shard_map/ppermute | solution.py:25
  134.9 8.1 %collective-permute-start.12 = (f32[3,2,64,128]{3,2,1,0:T(8,128)S(1)}, f32[3,2,64,128]{3,2,1,0:T(8,128)S(1)}, u32[]{:S(2)}, u32[]{:S(2)}) collective-permute-start(f32[3,2,64,128]{3,2,1,0:T(8,128)S(1)} %get-tuple-element.55), channel_id=1, source_target_pairs={{0,1},{1,2},{2,3},{3,4},{4,5},{5,6},{6,7},{7,8},{8,9},{9,10},{10,1... | collective-permute-start | bytes 589832 | tf_op jit(solution)/shard_map/ppermute | solution.py:25
  137.7 13.2 %collective-permute-start.13 = (f32[3,2,64,128]{3,2,1,0:T(8,128)S(1)}, f32[3,2,64,128]{3,2,1,0:T(8,128)S(1)}, u32[]{:S(2)}, u32[]{:S(2)}) collective-permute-start(f32[3,2,64,128]{3,2,1,0:T(8,128)S(1)} %get-tuple-element.56), channel_id=1, source_target_pairs={{1,0},{2,1},{3,2},{4,3},{5,4},{6,5},{7,6},{8,7},{9,8},{10,9},{11,1... | collective-permute-start | bytes 589832 | tf_op jit(solution)/shard_map/ppermute | solution.py:27
  151.0 5.0 %collective-permute-start.14 = (f32[3,8,2,128]{3,2,1,0:T(2,128)S(1)}, f32[3,8,2,128]{3,2,1,0:T(2,128)S(1)}, u32[]{:S(2)}, u32[]{:S(2)}) collective-permute-start(f32[3,8,2,128]{3,2,1,0:T(2,128)S(1)} %get-tuple-element.46), channel_id=1, source_target_pairs={{0,16},{1,17},{2,18},{3,19},{4,20},{5,21},{6,22},{7,23},{8,24},{9,... | collective-permute-start | bytes 73736 | tf_op jit(solution)/shard_map/ppermute | solution.py:25
  (22 other events, 241.7 us)
where the time goes:
time: 161 us; the launch traced here: 160 us
  starting transfers between devices  92.4 us (57%)
  waiting for transfers between devices  44.1 us (27%)
  other arithmetic  14.7 us (9%)
  local copies, waits for them, and re-layouts  6.34 us (4%)
    ppermute x16, starting transfers between devices, extended(): lax.ppermute(head, axis, [((i + 1) % count, i) for i in range(ends)])  46.4 us
    ppermute x16, starting transfers between devices, extended(): lax.ppermute(tail, axis, [(i, (i + 1) % count) for i in range(ends)])  33.6 us
    ppermute x16, waiting for transfers between devices, extended(): lax.ppermute(head, axis, [((i + 1) % count, i) for i in range(ends)])  32.8 us
    ppermute x4, starting transfers between devices, from_behind(): lax.ppermute(value, axis, [(source, source + steps) for source in range(l...  12.4 us
    ppermute x16, waiting for transfers between devices, extended(): lax.ppermute(tail, axis, [(i, (i + 1) % count) for i in range(ends)])  11.3 us
    concatenate x8, other arithmetic, extended(): jnp.concatenate([lax.ppermute(tail, axis, [(i, (i + 1) % count) for i in...  4.76 us
  transfers between devices with their start and end apart: 36, of which 14 were waited for; matrix products, arithmetic and copies ran while one was open for 6% of the time, Pallas kernels for 0%

commit v1 on v0

v1 whole, which is shorter than its diff:
```python
import functools

import jax
import jax.numpy as jnp
from jax import lax
from jax.experimental import pallas as pl
from jax.experimental.pallas import tpu as pltpu
from jax.sharding import PartitionSpec as P

STEPS = 2
REACH = 2
NEAR = 9.0 / 8.0
FAR = 1.0 / 24.0
DT = 0.15
ODT = 0.3
F32 = jnp.float32
EDGE = 5
SIDE = 8
WINDOW = 8


def depth_weights(width):
    lane = lax.broadcasted_iota(jnp.int32, (1, width), 1)

    def weight(value, first, last):
        return jnp.where((lane >= first) & (lane < last), value, 0.0).astype(F32)

    forward = (weight(NEAR, 0, width - 1), weight(-FAR, 0, width - 2), weight(FAR, 1, width))
    backward = (weight(-NEAR, 1, width), weight(-FAR, 0, width - 1), weight(FAR, 2, width))
    return forward, backward


def forward_z(f, weights):
    near, far, behind = weights
    n = f.shape[-1]
    return (
        pltpu.roll(f, n - 1, 1) * near
        - NEAR * f
        + pltpu.roll(f, n - 2, 1) * far
        + pltpu.roll(f, 1, 1) * behind
    )


def backward_z(f, weights):
    near, far, behind = weights
    n = f.shape[-1]
    return (
        NEAR * f
        + pltpu.roll(f, 1, 1) * near
        + pltpu.roll(f, n - 1, 1) * far
        + pltpu.roll(f, 2, 1) * behind
    )


def forward(at, i):
    return NEAR * (at(i + 1) - at(i)) - FAR * (at(i + 2) - at(i - 1))


def backward(at, i):
    return NEAR * (at(i) - at(i - 1)) - FAR * (at(i + 1) - at(i - 2))


def sides(odd, from_b, from_a, rows):
    def low(k):
        part = slice(k * rows, (k + 1) * rows)
        return jnp.where(odd, from_a[part, :], from_b[part, :])

    def high(k):
        part = slice(k * rows, (k + 1) * rows)
        return jnp.where(odd, from_b[part, :], from_a[part, :])

    return low, high


def along(own, count, low, low_from, high, high_from):
    def at(x):
        if x < 0:
            return low(low_from[x])
        if x >= count:
            return high(high_from[x])
        return own(x)

    return at


def fill_rows(rows_ref, comps, own, side_ref, sec, cx, cy):
    low_on = (sec == 1).astype(F32)
    high_on = (sec == 0).astype(F32)
    for k, comp in enumerate(comps):
        for x in range(cx):
            rows_ref[k, x, SIDE : SIDE + cy, :] = own(comp, x)
            got = side_ref[(k * cx + x) * SIDE : (k * cx + x + 1) * SIDE, :]
            rows_ref[k, x, 0:SIDE, :] = got * low_on
            rows_ref[k, x, SIDE + cy : SIDE + cy + SIDE, :] = got * high_on


def rows_at(rows_ref, k, x, cy):
    return lambda shift: rows_ref[k, x, SIDE + shift : SIDE + shift + cy, :]


def send_sides(odd, up, down, pay_b, pay_a, rows, get):
    for k, (u, d) in enumerate(zip(up, down)):
        part = slice(k * rows, (k + 1) * rows)
        upper, lower = get(*u), get(*d)
        pay_b[part, :] = jnp.where(odd, upper, lower)
        pay_a[part, :] = jnp.where(odd, lower, upper)


def send_rows(sec, comps, pay_s, get_rows, cx, cy):
    for k, comp in enumerate(comps):
        for x in range(cx):
            part = slice((k * cx + x) * SIDE, (k * cx + x + 1) * SIDE)
            pay_s[part, :] = jnp.where(
                sec == 0, get_rows(comp, x, cy - SIDE), get_rows(comp, x, 0)
            )


STRESS_ROWS = (1, 3, 5)
VELOCITY_ROWS = (0, 1, 2)


def stress_up(cx):
    return [(0, cx - 1), (3, cx - 2), (3, cx - 1), (4, cx - 2), (4, cx - 1)]


def stress_down(cx):
    return [(0, 0), (0, 1), (3, 0), (4, 0), (4, 0)]


def velocity_up(cx):
    return [(0, cx - 2), (0, cx - 1), (1, cx - 1), (2, cx - 1), (2, cx - 1)]


def velocity_down(cx):
    return [(0, 0), (1, 0), (1, 1), (2, 0), (2, 1)]


def step_velocity(info, s, v, b, from_b, from_a, from_s, v_out, pay_b, pay_a, pay_s, rows_ref):
    odd, sec = info[0] == 1, info[1]
    _, cx, cy, nz = s.shape
    fw, bw = depth_weights(nz)
    low, high = sides(odd, from_b, from_a, cy)
    fill_rows(rows_ref, STRESS_ROWS, lambda c, x: s[c, x], from_s, sec, cx, cy)
    xx = along(lambda x: s[0, x], cx, low, {-1: 0}, high, {cx: 0, cx + 1: 1})
    xy = along(lambda x: s[3, x], cx, low, {-2: 1, -1: 2}, high, {cx: 2})
    xz = along(lambda x: s[4, x], cx, low, {-2: 3, -1: 4}, high, {cx: 3})
    for x in range(cx):
        scale = DT * b[x]
        yy = rows_at(rows_ref, 0, x, cy)
        xy_rows = rows_at(rows_ref, 1, x, cy)
        yz = rows_at(rows_ref, 2, x, cy)
        v_out[0, x] = v[0, x] + scale * (
            forward(xx, x) + backward(xy_rows, 0) + backward_z(s[4, x], bw)
        )
        v_out[1, x] = v[1, x] + scale * (
            backward(xy, x) + forward(yy, 0) + backward_z(s[5, x], bw)
        )
        v_out[2, x] = v[2, x] + scale * (
            backward(xz, x) + backward(yz, 0) + forward_z(s[2, x], fw)
        )
    send_sides(odd, velocity_up(cx), velocity_down(cx), pay_b, pay_a, cy, lambda c, x: v_out[c, x])
    send_rows(sec, VELOCITY_ROWS, pay_s, lambda c, x, y: v_out[c, x, y : y + SIDE, :], cx, cy)


def last_velocity(
    info, s, v, b, from_b, from_a, from_s, ocean, marks, v_out, pay_b, pay_a, pay_s, patch, rows_ref
):
    step_velocity(info, s, v, b, from_b, from_a, from_s, v_out, pay_b, pay_a, pay_s, rows_ref)
    odd = info[0] == 1
    _, cx, cy, nz = s.shape
    first = (lax.broadcasted_iota(jnp.int32, (8, nz), 1) == 0).astype(F32)
    floor = jnp.concatenate([v_out[2, x] for x in range(cx)], axis=0)
    line = lax.dot_general(
        first,
        floor,
        (((1,), (1,)), ((), ())),
        precision=lax.Precision.HIGHEST,
        preferred_element_type=F32,
    )
    patch[...] = line[0:1, :]
    fields, rows, columns = ocean.shape
    base = EDGE * cy
    tiles = columns // 128
    for f in range(fields + 1):
        for k in range(tiles if f < fields else 1):
            part = slice(base, base + SIDE)
            if f < fields:
                upper = ocean[f, rows - SIDE : rows, k * 128 : (k + 1) * 128]
                lower = ocean[f, 0:SIDE, k * 128 : (k + 1) * 128]
            else:
                upper, lower = marks[rows - SIDE : rows, :], marks[0:SIDE, :]
            pay_b[part, :] = jnp.where(odd, upper, lower)
            pay_a[part, :] = jnp.where(odd, lower, upper)
            base += SIDE


def update_stress(info, v, s, lam, mu, from_b, from_a, from_s, s_out, rows_ref):
    odd, sec = info[0] == 1, info[1]
    _, cx, cy, nz = s.shape
    fw, bw = depth_weights(nz)
    low, high = sides(odd, from_b, from_a, cy)
    fill_rows(rows_ref, VELOCITY_ROWS, lambda c, x: v[c, x], from_s, sec, cx, cy)
    vx = along(lambda x: v[0, x], cx, low, {-2: 0, -1: 1}, high, {cx: 0})
    vy = along(lambda x: v[1, x], cx, low, {-1: 2}, high, {cx: 1, cx + 1: 2})
    vz = along(lambda x: v[2, x], cx, low, {-1: 3}, high, {cx: 3, cx + 1: 4})
    for x in range(cx):
        shear = DT * mu[x]
        double = 2.0 * shear
        vx_rows, vy_rows, vz_rows = (rows_at(rows_ref, k, x, cy) for k in range(3))
        exx = backward(vx, x)
        eyy = backward(vy_rows, 0)
        ezz = backward_z(v[2, x], bw)
        volume = (DT * lam[x]) * (exx + eyy + ezz)
        s_out[0, x] = s[0, x] + (volume + double * exx)
        s_out[1, x] = s[1, x] + (volume + double * eyy)
        s_out[2, x] = s[2, x] + (volume + double * ezz)
        s_out[3, x] = s[3, x] + shear * (forward(vx_rows, 0) + forward(vy, x))
        s_out[4, x] = s[4, x] + shear * (forward_z(v[0, x], fw) + forward(vz, x))
        s_out[5, x] = s[5, x] + shear * (forward_z(v[1, x], fw) + forward(vz_rows, 0))


def step_stress(
    info, v, s, lam, mu, from_b, from_a, from_s, s_out, pay_b, pay_a, pay_s, rows_ref
):
    odd, sec = info[0] == 1, info[1]
    _, cx, cy, nz = s.shape
    update_stress(info, v, s, lam, mu, from_b, from_a, from_s, s_out, rows_ref)
    send_sides(odd, stress_up(cx), stress_down(cx), pay_b, pay_a, cy, lambda c, x: s_out[c, x])
    send_rows(sec, STRESS_ROWS, pay_s, lambda c, x, y: s_out[c, x, y : y + SIDE, :], cx, cy)


def last_stress(
    info,
    v,
    s,
    lam,
    mu,
    from_b,
    from_a,
    from_s,
    ocean,
    marks,
    patches,
    s_out,
    ocean_out,
    rows_ref,
    ocean_ref,
    marks_ref,
):
    odd, sec, tile, count, base = info[0] == 1, info[1], info[2], info[3], info[4]
    _, cx, cy, nz = s.shape
    update_stress(info, v, s, lam, mu, from_b, from_a, from_s, s_out, rows_ref)

    fields, rows, columns = ocean.shape
    own = ocean_out.shape[2]
    at = EDGE * cy
    top, bottom = slice(0, SIDE), slice(SIDE + rows, SIDE + rows + SIDE)
    for f in range(fields):
        ocean_ref[f, SIDE : SIDE + rows, :] = ocean[f]
        for k in range(columns // 128):
            lanes = slice(k * 128, (k + 1) * 128)
            b, a = from_b[at : at + SIDE, :], from_a[at : at + SIDE, :]
            ocean_ref[f, top, lanes] = jnp.where(odd, a, b)
            ocean_ref[f, bottom, lanes] = jnp.where(odd, b, a)
            at += SIDE
    b, a = from_b[at : at + SIDE, :], from_a[at : at + SIDE, :]
    marks_ref[SIDE : SIDE + rows, :] = marks[...]
    marks_ref[top, :] = jnp.where(odd, a, b)
    marks_ref[bottom, :] = jnp.where(odd, b, a)

    total = rows + 2 * SIDE
    lane = lax.broadcasted_iota(jnp.int32, (1, columns), 1)
    ahead = jnp.where((lane == own - 1) & (sec == 1), 0.0, 0.5).astype(F32)
    behind = jnp.where((lane == 0) & (sec == 0), 0.0, 0.5).astype(F32)
    line = lax.broadcasted_iota(jnp.int32, (total, 1), 0)
    inside = ((line >= SIDE) | (tile > 0)) & ((line < SIDE + rows) | (tile < count - 1))
    inside = inside.astype(F32)

    def across(f):
        return pltpu.roll(f, columns - 1, 1) * ahead - pltpu.roll(f, 1, 1) * behind

    def down(f):
        return 0.5 * (pltpu.roll(f, total - 1, 0) - pltpu.roll(f, 1, 0))

    eta, u, v_sea = ocean_ref[0], ocean_ref[1], ocean_ref[2]
    depth, wet = ocean_ref[3], ocean_ref[4]
    owner = marks_ref[:, 0:1] - base.astype(F32)
    share = marks_ref[:, 1:2]
    uplift = jnp.zeros((total, columns), F32)
    for k in range(patches.shape[0]):
        uplift = jnp.where(owner == float(k), patches[k : k + 1, :], uplift)
    lift = ODT * (share * wet * uplift)
    for _ in range(2):
        u = wet * (u - ODT * down(eta))
        v_sea = wet * (v_sea - ODT * across(eta))
        eta = inside * (eta - ODT * (down(depth * u) + across(depth * v_sea)) + lift)
    part = slice(SIDE, SIDE + rows)
    ocean_out[0] = eta[part, :own]
    ocean_out[1] = u[part, :own]
    ocean_out[2] = v_sea[part, :own]


def call(body, name, outs, scratch, operands, flops):
    shapes = [jax.ShapeDtypeStruct(o, F32) for o in outs]
    smem = pl.BlockSpec(memory_space=pltpu.SMEM)
    vmem = pl.BlockSpec(memory_space=pltpu.VMEM)
    moved = sum(o.size for o in operands) * 4 + sum(o.size for o in shapes) * 4
    return pl.pallas_call(
        body,
        name=name,
        out_shape=shapes,
        in_specs=[smem] + [vmem] * (len(operands) - 1),
        out_specs=[vmem] * len(outs),
        scratch_shapes=[pltpu.VMEM(shape, F32) for shape in scratch],
        compiler_params=pltpu.CompilerParams(vmem_limit_bytes=32 * 1024 * 1024),
        cost_estimate=pl.CostEstimate(flops=flops, bytes_accessed=moved, transcendentals=0),
    )(*operands)


def exchange(pay_b, pay_a, count):
    def swap(pay, first):
        pairs = []
        for i in range(first, count - 1, 2):
            pairs += [(i, i + 1), (i + 1, i)]
        return lax.ppermute(pay, "tile", pairs)

    return swap(pay_b, 1), swap(pay_a, 0)


def across(pay):
    return lax.ppermute(pay, "sec", [(0, 1), (1, 0)])


def shards(
    velocity,
    stresses,
    buoyancy,
    lame_first,
    shear_mod,
    ocean_state,
    depth_map,
    wet_mask,
    intersection_src,
    intersection_share,
):
    count = lax.axis_size("tile")
    tile, sec = lax.axis_index("tile"), lax.axis_index("sec")
    odd = lax.rem(tile, 2)
    _, cx, cy, nz = stresses.shape
    _, rows, columns = ocean_state.shape
    base = jnp.clip(tile - REACH - 1, 0, max(count - WINDOW, 0))
    info = jnp.stack([odd, sec, tile, jnp.int32(count), base]).astype(jnp.int32)

    up = jnp.concatenate([stresses[c, x] for c, x in stress_up(cx)])
    down = jnp.concatenate([stresses[c, x] for c, x in stress_down(cx)])
    pay_b, pay_a = jnp.where(odd == 1, up, down), jnp.where(odd == 1, down, up)
    from_b, from_a = exchange(pay_b, pay_a, count)

    edge = jnp.stack([stresses[c] for c in STRESS_ROWS])
    edge = jnp.where(sec == 0, edge[:, :, cy - SIDE :, :], edge[:, :, :SIDE, :])
    fields = jnp.concatenate([ocean_state, depth_map[None], wet_mask.astype(F32)[None]])
    near = jnp.where(sec == 0, fields[:, :, columns - 128 :], fields[:, :, :128])
    got = across(jnp.concatenate([edge.reshape(-1, nz), near.reshape(-1, 128)]))
    from_s = got[: 3 * cx * SIDE]
    ocean = jnp.concatenate([fields, got[3 * cx * SIDE :].reshape(-1, rows, 128)], axis=2)
    lane = lax.broadcasted_iota(jnp.int32, (rows, 128), 1)
    marks = jnp.where(
        lane == 0,
        intersection_src.astype(F32)[:, None],
        jnp.where(lane == 1, intersection_share[:, None], 0.0),
    )

    cells = cx * cy * nz
    side = (EDGE * cy, nz)
    strip = (3 * cx * SIDE, nz)
    halo_rows = (3, cx, cy + 2 * SIDE, nz)
    tiles = (ocean.shape[0] * ocean.shape[2] // 128 + 1) * SIDE
    long_side = (EDGE * cy + tiles, nz)
    velocity, pay_b, pay_a, pay_s = call(
        step_velocity,
        "velocity_step",
        [velocity.shape, side, side, strip],
        [halo_rows],
        [info, stresses, velocity, buoyancy, from_b, from_a, from_s],
        60 * cells,
    )
    from_b, from_a = exchange(pay_b, pay_a, count)
    from_s = across(pay_s)
    stresses, pay_b, pay_a, pay_s = call(
        step_stress,
        "stress_step",
        [stresses.shape, side, side, strip],
        [halo_rows],
        [info, velocity, stresses, lame_first, shear_mod, from_b, from_a, from_s],
        70 * cells,
    )
    from_b, from_a = exchange(pay_b, pay_a, count)
    from_s = across(pay_s)
    velocity, pay_b, pay_a, pay_s, patch = call(
        last_velocity,
        "velocity_last",
        [velocity.shape, long_side, long_side, strip, (1, cx * cy)],
        [halo_rows],
        [info, stresses, velocity, buoyancy, from_b, from_a, from_s, ocean, marks],
        60 * cells,
    )
    from_b, from_a = exchange(pay_b, pay_a, count)
    from_s = across(pay_s)
    spread = jnp.broadcast_to(patch.reshape(1, -1, 128), (2 * count, cx * cy // 128, 128))
    patches = lax.all_to_all(spread, ("sec", "tile"), 0, 0).reshape(2, count, cx * cy)
    window = min(WINDOW, count)
    mine = lax.dynamic_slice(patches, (sec, base, 0), (1, window, cx * cy))[0]
    theirs = lax.dynamic_slice(
        patches, (1 - sec, base, sec * (cx * cy - 128)), (1, window, 128)
    )[0]
    patches = jnp.concatenate([mine, theirs], axis=1)
    stresses, ocean_state = call(
        last_stress,
        "stress_last",
        [stresses.shape, ocean_state.shape],
        [
            halo_rows,
            (ocean.shape[0], rows + 2 * SIDE, ocean.shape[2]),
            (rows + 2 * SIDE, 128),
        ],
        [info, velocity, stresses, lame_first, shear_mod, from_b, from_a, from_s, ocean, marks]
        + [patches],
        80 * cells,
    )
    return velocity, stresses, ocean_state


def solution(mesh):
    cube = P("tile", "sec", None)
    return jax.shard_map(
        shards,
        mesh=mesh,
        in_specs=(
            P(None, "tile", "sec", None),
            P(None, "tile", "sec", None),
            cube,
            cube,
            cube,
            P(None, "tile", "sec"),
            P("tile", "sec"),
            P("tile", "sec"),
            P("tile"),
            P("tile"),
        ),
        out_specs=(
            P(None, "tile", "sec", None),
            P(None, "tile", "sec", None),
            P(None, "tile", "sec"),
        ),
        check_vma=False,
    )
```

time: 161 us -> 67.5 us (0.42)
  the two profiles are of different devices: /device:TPU:21 before, /device:TPU:0 now
where the time goes in v1:
time: 67.5 us; the launch traced here: 67.1 us
  starting transfers between devices  28.5 us (42%)
  waiting for transfers between devices  25.6 us (38%)
  Pallas kernels  6.27 us (9%)
  local copies, waits for them, and re-layouts  4.85 us (7%)
  other arithmetic  1.07 us (2%)
  between operations  0.9 us (1%)
    ppermute x8, waiting for transfers between devices, swap(): return lax.ppermute(pay, 'tile', pairs)  22 us
    ppermute x8, starting transfers between devices, swap(): return lax.ppermute(pay, 'tile', pairs)  21.8 us
    pallas_call x4, Pallas kernels, call(): pl.pallas_call(body, name=name, out_shape=shapes, in_specs=[smem] + [vmem...  6.27 us
    all_to_all x1, starting transfers between devices, shards(): lax.all_to_all(spread, ('sec', 'tile'), 0, 0).reshape(2, count, cx * cy)  5.79 us
    unnamed x24, local copies, waits for them, and re-layouts  2.89 us
    all_to_all x1, waiting for transfers between devices, shards(): lax.all_to_all(spread, ('sec', 'tile'), 0, 0).reshape(2, count, cx * cy)  1.78 us
    ppermute x4, waiting for transfers between devices, across(): return lax.ppermute(pay, 'sec', [(0, 1), (1, 0)])  1.75 us
  transfers between devices with their start and end apart: 13, of which 7 were waited for; matrix products, arithmetic and copies ran while one was open for 1% of the time, Pallas kernels for 0%

profile of v1, /device:TPU:0, one launch (start us, length us, event | category | flops | bytes accessed | tf_op | source)
XLA Modules:
  0.0 67.1 jit_solution(13962518096580668772)
XLA Ops:
  0.6 0.8 %convert_bitcast_fusion = f32[1,64,256]{2,1,0:T(8,128)S(1)} fusion(s32[64,256]{1,0:T(8,128)} %param.17), kind=kLoop, calls=%fused_computation.6 | loop fusion | flops 16384 | bytes 131072 | tf_op jit(solution)/shard_map/broadcast_in_dim | solution.py:361
  1.5 1.1 %fusion.1 = (f32[1,4,64,128]{3,2,1,0:T(8,128)S(1)}, f32[1,4,64,128]{3,2,1,0:T(8,128)S(1)}, f32[1,4,64,128]{3,2,1,0:T(8,128)S(1)}) fusion(f32[6,4,64,128]{3,2,1,0:T(8,128)} %s.3), kind=kLoop, calls=%fused_computation.26 | loop fusion | bytes 786432 | tf_op jit(solution)/shard_map/slice | solution.py:359
  2.7 0.5 collective-permute-start.2
  3.3 0.5 copy-done
  3.9 3.0 %collective-permute-start.1 = (f32[320,128]{1,0:T(8,128)S(1)}, f32[320,128]{1,0:T(8,128)S(1)}, u32[]{:S(2)}, u32[]{:S(2)}) collective-permute-start(f32[320,128]{1,0:T(8,128)S(1)} %get-tuple-element.46), channel_id=1, source_target_pairs={{0,1},{1,0},{2,3},{3,2},{4,5},{5,4},{6,7},{7,6},{8,9},{9,8},{10,11... | collective-permute-start | bytes 491528 | tf_op jit(solution)/shard_map/ppermute | solution.py:325
  6.9 0.7 collective-permute-start
  7.6 0.1 stack.22.info
  7.7 3.4 %collective-permute-done.1.from_a = f32[320,128]{1,0:T(8,128)S(1)} collective-permute-done((f32[320,128]{1,0:T(8,128)S(1)}, f32[320,128]{1,0:T(8,128)S(1)}, u32[]{:S(2)}, u32[]{:S(2)}) %collective-permute-start.1) | collective-permute-done | bytes 163872 | tf_op jit(solution)/shard_map/ppermute | solution.py:325
  11.1 1.0 %velocity_step.1 = (f32[3,4,64,128]{3,2,1,0:T(8,128)S(1)}, f32[320,128]{1,0:T(8,128)S(1)}, f32[320,128]{1,0:T(8,128)S(1)}, f32[96,128]{1,0:T(8,128)S(1)}) custom-call(s32[5]{0:T(128)S(1)} %stack.22.info, f32[6,4,64,128]{3,2,1,0:T(8,128)S(1)} %copy-done, f32[3,4,64,128]{3,2,1,0:T(8,128)S(1)} %copy-done.4, f32[4,64,128]{2,1,0:T(8,128)S(1)} %copy-done.1, ...), custom_call_target="tpu_custom_call" | custom-call | flops 1966080 | bytes 2457620 | tf_op jit(solution)/shard_map/velocity_step/pallas_call | solution.py:308
  12.1 0.7 collective-permute-start.3
  12.8 8.5 %collective-permute-start.4 = (f32[320,128]{1,0:T(8,128)S(1)}, f32[320,128]{1,0:T(8,128)S(1)}, u32[]{:S(2)}, u32[]{:S(2)}) collective-permute-start(f32[320,128]{1,0:T(8,128)S(1)} %get-tuple-element.20), channel_id=1, source_target_pairs={{0,1},{1,0},{2,3},{3,2},{4,5},{5,4},{6,7},{7,6},{8,9},{9,8},{10,11... | collective-permute-start | bytes 491528 | tf_op jit(solution)/shard_map/ppermute | solution.py:325
  21.3 0.6 copy-done.9
  22.0 0.6 collective-permute-done.5.from_s
  22.5 4.9 %collective-permute-done.4.from_a = f32[320,128]{1,0:T(8,128)S(1)} collective-permute-done((f32[320,128]{1,0:T(8,128)S(1)}, f32[320,128]{1,0:T(8,128)S(1)}, u32[]{:S(2)}, u32[]{:S(2)}) %collective-permute-start.4) | collective-permute-done | bytes 163872 | tf_op jit(solution)/shard_map/ppermute | solution.py:325
  27.5 1.1 %stress_step.1 = (f32[6,4,64,128]{3,2,1,0:T(8,128)S(1)}, f32[320,128]{1,0:T(8,128)S(1)}, f32[320,128]{1,0:T(8,128)S(1)}, f32[96,128]{1,0:T(8,128)S(1)}) custom-call(s32[5]{0:T(128)S(1)} %stack.22.info, f32[3,4,64,128]{3,2,1,0:T(8,128)S(1)} %get-tuple-element.18.v, f32[6,4,64,128]{3,2,1,0:T(8,128)S(1)} %copy-done, f32[4,64,128]{2,1,0:T(8,128)S(1)} %copy-done.2, ...), custom_call_target="tpu_custom_call" | custom-call | flops 2293760 | bytes 2981908 | tf_op jit(solution)/shard_map/stress_step/pallas_call | solution.py:308
  28.5 0.7 collective-permute-start.6
  29.2 3.1 %collective-permute-start.7 = (f32[320,128]{1,0:T(8,128)S(1)}, f32[320,128]{1,0:T(8,128)S(1)}, u32[]{:S(2)}, u32[]{:S(2)}) collective-permute-start(f32[320,128]{1,0:T(8,128)S(1)} %get-tuple-element.24), channel_id=1, source_target_pairs={{0,1},{1,0},{2,3},{3,2},{4,5},{5,4},{6,7},{7,6},{8,9},{9,8},{10,11... | collective-permute-start | bytes 491528 | tf_op jit(solution)/shard_map/ppermute | solution.py:325
  32.4 0.7 copy-done.8
  33.0 0.1 select_select_fusion.marks
  33.2 1.2 %collective-permute-done.8.from_s = f32[96,128]{1,0:T(8,128)S(1)} collective-permute-done((f32[96,128]{1,0:T(8,128)S(1)}, f32[96,128]{1,0:T(8,128)S(1)}, u32[]{:S(2)}, u32[]{:S(2)}) %collective-permute-start.8) | collective-permute-done | bytes 49184 | tf_op jit(solution)/shard_map/ppermute | solution.py:331
  34.4 4.9 %collective-permute-done.7.from_a = f32[320,128]{1,0:T(8,128)S(1)} collective-permute-done((f32[320,128]{1,0:T(8,128)S(1)}, f32[320,128]{1,0:T(8,128)S(1)}, u32[]{:S(2)}, u32[]{:S(2)}) %collective-permute-start.7) | collective-permute-done | bytes 163872 | tf_op jit(solution)/shard_map/ppermute | solution.py:325
  39.3 1.8 %velocity_last.1 = (f32[3,4,64,128]{3,2,1,0:T(8,128)}, f32[448,128]{1,0:T(8,128)S(1)}, f32[448,128]{1,0:T(8,128)S(1)}, f32[96,128]{1,0:T(8,128)S(1)}, f32[1,256]{1,0:T(1,128)S(1)}) custom-call(s32[5]{0:T(128)S(1)} %stack.22.info, f32[6,4,64,128]{3,2,1,0:T(8,128)S(1)} %get-tuple-element.22.s, f32[3,4,64,128]{3,2,1,0:T(8,128)S(1)} %get-tuple-element.18.v, ...), custom_call_target="tpu_custom_call" | custom-call | flops 1966080 | bytes 3114004 | tf_op jit(solution)/shard_map/velocity_last/pallas_call | solution.py:308
  41.1 0.6 broadcast_in_dim.41
  41.8 5.8 %all-to-all-start = ((f32[32,2,128]{2,1,0:T(2,128)}), f32[32,2,128]{2,1,0:T(2,128)S(1)}, u32[]{:S(2)}, u32[]{:S(2)}) async-start(f32[32,2,128]{2,1,0:T(2,128)} %broadcast_in_dim.41), calls=%async_computation | async-start | bytes 65536 | tf_op jit(solution)/shard_map/all_to_all | solution.py:410
  47.5 0.3 collective-permute-start.11
  47.9 0.7 collective-permute-start.9
  48.5 4.4 %collective-permute-start.10 = (f32[448,128]{1,0:T(8,128)S(1)}, f32[448,128]{1,0:T(8,128)S(1)}, u32[]{:S(2)}, u32[]{:S(2)}) collective-permute-start(f32[448,128]{1,0:T(8,128)S(1)} %get-tuple-element.28), channel_id=1, source_target_pairs={{0,1},{1,0},{2,3},{3,2},{4,5},{5,4},{6,7},{7,6},{8,9},{9,8},{10,11... | collective-permute-start | bytes 688136 | tf_op jit(solution)/shard_map/ppermute | solution.py:325
  53.0 1.8 %all-to-all-done = f32[32,2,128]{2,1,0:T(2,128)S(1)} async-done(((f32[32,2,128]{2,1,0:T(2,128)}), f32[32,2,128]{2,1,0:T(2,128)S(1)}, u32[]{:S(2)}, u32[]{:S(2)}) %all-to-all-start) | async-done | bytes 32800 | tf_op jit(solution)/shard_map/all_to_all | solution.py:410
  54.8 0.1 dynamic-slice_bitcast_fusion.1
  54.9 8.8 %collective-permute-done.10.from_a = f32[448,128]{1,0:T(8,128)S(1)} collective-permute-done((f32[448,128]{1,0:T(8,128)S(1)}, f32[448,128]{1,0:T(8,128)S(1)}, u32[]{:S(2)}, u32[]{:S(2)}) %collective-permute-start.10) | collective-permute-done | bytes 229408 | tf_op jit(solution)/shard_map/ppermute | solution.py:325
  63.7 1.0 %copy-done.5 = f32[3,4,64,128]{3,2,1,0:T(8,128)S(1)} copy-done((f32[3,4,64,128]{3,2,1,0:T(8,128)S(1)}, f32[3,4,64,128]{3,2,1,0:T(8,128)}, u32[]{:S(2)}) %copy-start.5) | copy-done | bytes 393240
  64.7 2.4 %stress_last.1 = (f32[6,4,64,128]{3,2,1,0:T(8,128)}, f32[3,64,256]{2,1,0:T(8,128)}) custom-call(s32[5]{0:T(128)S(1)} %stack.22.info, f32[3,4,64,128]{3,2,1,0:T(8,128)S(1)} %copy-done.5, f32[6,4,64,128]{3,2,1,0:T(8,128)S(1)} %get-tuple-element.22.s, f32[4,64,128]{2,1,0:T(8,128)S(1)} %copy-done.2, f32[4,64,128]{2,1,0:T(8,128)S(1)} %copy-done.3, ...), custom_call_target="tpu_custom_call" | custom-call | flops 2621440 | bytes 3469332 | tf_op jit(solution)/shard_map/stress_last/pallas_call | solution.py:308
  (42 shorter events, 0.4 us)
Async XLA Ops:
  1.5 1.1 %copy-start.6 = (f32[3,64,256]{2,1,0:T(8,128)S(1)}, f32[3,64,256]{2,1,0:T(8,128)}, u32[]{:S(2)}) copy-start(f32[3,64,256]{2,1,0:T(8,128)} %param.15) | copy-start | bytes 589828
  1.5 1.1 %copy-start.7 = (f32[64,256]{1,0:T(8,128)S(1)}, f32[64,256]{1,0:T(8,128)}, u32[]{:S(2)}) copy-start(f32[64,256]{1,0:T(8,128)} %param.16) | copy-start | bytes 196612
  2.7 1.1 %copy-start = (f32[6,4,64,128]{3,2,1,0:T(8,128)S(1)}, f32[6,4,64,128]{3,2,1,0:T(8,128)}, u32[]{:S(2)}) copy-start(f32[6,4,64,128]{3,2,1,0:T(8,128)} %s.3) | copy-start | bytes 2359300
  2.7 4.9 %collective-permute-start.2 = (f32[416,128]{1,0:T(8,128)S(1)}, f32[416,128]{1,0:T(8,128)S(1)}, u32[]{:S(2)}, u32[]{:S(2)}) collective-permute-start(f32[416,128]{1,0:T(8,128)S(1)} %pad_maximum_fusion.2), channel_id=1, source_target_pairs={{0,16},{16,0},{1,17},{17,1},{2,18},{18,2},{3,19},{19,3},{4,20},{20... | collective-permute-start | bytes 638984 | tf_op jit(solution)/shard_map/ppermute | solution.py:331
  3.9 7.3 %copy-start.4 = (f32[3,4,64,128]{3,2,1,0:T(8,128)S(1)}, f32[3,4,64,128]{3,2,1,0:T(8,128)}, u32[]{:S(2)}) copy-start(f32[3,4,64,128]{3,2,1,0:T(8,128)} %v.1) | copy-start | bytes 1179652
  3.9 7.3 %copy-start.1 = (f32[4,64,128]{2,1,0:T(8,128)S(1)}, f32[4,64,128]{2,1,0:T(8,128)}, u32[]{:S(2)}) copy-start(f32[4,64,128]{2,1,0:T(8,128)} %b.3) | copy-start | bytes 393220
  3.9 7.2 %collective-permute-start.1 = (f32[320,128]{1,0:T(8,128)S(1)}, f32[320,128]{1,0:T(8,128)S(1)}, u32[]{:S(2)}, u32[]{:S(2)}) collective-permute-start(f32[320,128]{1,0:T(8,128)S(1)} %get-tuple-element.46), channel_id=1, source_target_pairs={{0,1},{1,0},{2,3},{3,2},{4,5},{5,4},{6,7},{7,6},{8,9},{9,8},{10,11... | collective-permute-start | bytes 491528 | tf_op jit(solution)/shard_map/ppermute | solution.py:325
  6.9 4.2 %collective-permute-start = (f32[320,128]{1,0:T(8,128)S(1)}, f32[320,128]{1,0:T(8,128)S(1)}, u32[]{:S(2)}, u32[]{:S(2)}) collective-permute-start(f32[320,128]{1,0:T(8,128)S(1)} %get-tuple-element.47), channel_id=1, source_target_pairs={{1,2},{2,1},{3,4},{4,3},{5,6},{6,5},{7,8},{8,7},{9,10},{10,9},{11,... | collective-permute-start | bytes 491528 | tf_op jit(solution)/shard_map/ppermute | solution.py:325
  7.7 19.8 %copy-start.2 = (f32[4,64,128]{2,1,0:T(8,128)S(1)}, f32[4,64,128]{2,1,0:T(8,128)}, u32[]{:S(2)}) copy-start(f32[4,64,128]{2,1,0:T(8,128)} %lam.3) | copy-start | bytes 393220
  7.7 19.8 %copy-start.3 = (f32[4,64,128]{2,1,0:T(8,128)S(1)}, f32[4,64,128]{2,1,0:T(8,128)}, u32[]{:S(2)}) copy-start(f32[4,64,128]{2,1,0:T(8,128)} %mu.3) | copy-start | bytes 393220
  12.1 10.4 %collective-permute-start.3 = (f32[320,128]{1,0:T(8,128)S(1)}, f32[320,128]{1,0:T(8,128)S(1)}, u32[]{:S(2)}, u32[]{:S(2)}) collective-permute-start(f32[320,128]{1,0:T(8,128)S(1)} %get-tuple-element.19), channel_id=1, source_target_pairs={{1,2},{2,1},{3,4},{4,3},{5,6},{6,5},{7,8},{8,7},{9,10},{10,9},{11,... | collective-permute-start | bytes 491528 | tf_op jit(solution)/shard_map/ppermute | solution.py:325
  12.8 14.7 %collective-permute-start.4 = (f32[320,128]{1,0:T(8,128)S(1)}, f32[320,128]{1,0:T(8,128)S(1)}, u32[]{:S(2)}, u32[]{:S(2)}) collective-permute-start(f32[320,128]{1,0:T(8,128)S(1)} %get-tuple-element.20), channel_id=1, source_target_pairs={{0,1},{1,0},{2,3},{3,2},{4,5},{5,4},{6,7},{7,6},{8,9},{9,8},{10,11... | collective-permute-start | bytes 491528 | tf_op jit(solution)/shard_map/ppermute | solution.py:325
  21.3 0.7 copy-start.9
  21.3 1.2 %collective-permute-start.5 = (f32[96,128]{1,0:T(8,128)S(1)}, f32[96,128]{1,0:T(8,128)S(1)}, u32[]{:S(2)}, u32[]{:S(2)}) collective-permute-start(f32[96,128]{1,0:T(8,128)S(1)} %get-tuple-element.21), channel_id=1, source_target_pairs={{0,16},{16,0},{1,17},{17,1},{2,18},{18,2},{3,19},{19,3},{4,20},{20... | collective-permute-start | bytes 147464 | tf_op jit(solution)/shard_map/ppermute | solution.py:331
  28.5 5.9 %collective-permute-start.6 = (f32[320,128]{1,0:T(8,128)S(1)}, f32[320,128]{1,0:T(8,128)S(1)}, u32[]{:S(2)}, u32[]{:S(2)}) collective-permute-start(f32[320,128]{1,0:T(8,128)S(1)} %get-tuple-element.23), channel_id=1, source_target_pairs={{1,2},{2,1},{3,4},{4,3},{5,6},{6,5},{7,8},{8,7},{9,10},{10,9},{11,... | collective-permute-start | bytes 491528 | tf_op jit(solution)/shard_map/ppermute | solution.py:325
  29.2 10.1 %collective-permute-start.7 = (f32[320,128]{1,0:T(8,128)S(1)}, f32[320,128]{1,0:T(8,128)S(1)}, u32[]{:S(2)}, u32[]{:S(2)}) collective-permute-start(f32[320,128]{1,0:T(8,128)S(1)} %get-tuple-element.24), channel_id=1, source_target_pairs={{0,1},{1,0},{2,3},{3,2},{4,5},{5,4},{6,7},{7,6},{8,9},{9,8},{10,11... | collective-permute-start | bytes 491528 | tf_op jit(solution)/shard_map/ppermute | solution.py:325
  32.4 0.7 copy-start.8
  33.1 1.3 %collective-permute-start.8 = (f32[96,128]{1,0:T(8,128)S(1)}, f32[96,128]{1,0:T(8,128)S(1)}, u32[]{:S(2)}, u32[]{:S(2)}) collective-permute-start(f32[96,128]{1,0:T(8,128)S(1)} %get-tuple-element.25), channel_id=1, source_target_pairs={{0,16},{16,0},{1,17},{17,1},{2,18},{18,2},{3,19},{19,3},{4,20},{20... | collective-permute-start | bytes 147464 | tf_op jit(solution)/shard_map/ppermute | solution.py:331
  41.8 13.0 %all-to-all-start = ((f32[32,2,128]{2,1,0:T(2,128)}), f32[32,2,128]{2,1,0:T(2,128)S(1)}, u32[]{:S(2)}, u32[]{:S(2)}) async-start(f32[32,2,128]{2,1,0:T(2,128)} %broadcast_in_dim.41), calls=%async_computation | async-start | bytes 65536 | tf_op jit(solution)/shard_map/all_to_all | solution.py:410
  47.5 7.3 %collective-permute-start.11 = (f32[96,128]{1,0:T(8,128)S(1)}, f32[96,128]{1,0:T(8,128)S(1)}, u32[]{:S(2)}, u32[]{:S(2)}) collective-permute-start(f32[96,128]{1,0:T(8,128)S(1)} %get-tuple-element.29), channel_id=1, source_target_pairs={{0,16},{16,0},{1,17},{17,1},{2,18},{18,2},{3,19},{19,3},{4,20},{20... | collective-permute-start | bytes 147464 | tf_op jit(solution)/shard_map/ppermute | solution.py:331
  47.9 7.0 %collective-permute-start.9 = (f32[448,128]{1,0:T(8,128)S(1)}, f32[448,128]{1,0:T(8,128)S(1)}, u32[]{:S(2)}, u32[]{:S(2)}) collective-permute-start(f32[448,128]{1,0:T(8,128)S(1)} %get-tuple-element.27), channel_id=1, source_target_pairs={{1,2},{2,1},{3,4},{4,3},{5,6},{6,5},{7,8},{8,7},{9,10},{10,9},{11,... | collective-permute-start | bytes 688136 | tf_op jit(solution)/shard_map/ppermute | solution.py:325
  48.5 15.1 %collective-permute-start.10 = (f32[448,128]{1,0:T(8,128)S(1)}, f32[448,128]{1,0:T(8,128)S(1)}, u32[]{:S(2)}, u32[]{:S(2)}) collective-permute-start(f32[448,128]{1,0:T(8,128)S(1)} %get-tuple-element.28), channel_id=1, source_target_pairs={{0,1},{1,0},{2,3},{3,2},{4,5},{5,4},{6,7},{7,6},{8,9},{9,8},{10,11... | collective-permute-start | bytes 688136 | tf_op jit(solution)/shard_map/ppermute | solution.py:325
  63.7 1.0 %copy-start.5 = (f32[3,4,64,128]{3,2,1,0:T(8,128)S(1)}, f32[3,4,64,128]{3,2,1,0:T(8,128)}, u32[]{:S(2)}) copy-start(f32[3,4,64,128]{3,2,1,0:T(8,128)} %get-tuple-element.15.v) | copy-start | bytes 1179652

commit v2 on v1

--- a/solution.py
+++ b/solution.py
@@ -17,6 +17,8 @@
 EDGE = 5
 SIDE = 8
 WINDOW = 8
+DEEP = (4, 3, 3, 3, 3)
+PACK = sum(DEEP)
 
 
 def depth_weights(width):
@@ -58,6 +60,11 @@
 
 def backward(at, i):
     return NEAR * (at(i) - at(i - 1)) - FAR * (at(i + 1) - at(i - 2))
+
+
+def place():
+    tile, sec = lax.axis_index("tile"), lax.axis_index("sec")
+    return lax.rem(tile, 2) == 1, sec, tile
 
 
 def sides(odd, from_b, from_a, rows):
@@ -135,8 +142,27 @@
     return [(0, 0), (1, 0), (1, 1), (2, 0), (2, 1)]
 
 
-def step_velocity(info, s, v, b, from_b, from_a, from_s, v_out, pay_b, pay_a, pay_s, rows_ref):
-    odd, sec = info[0] == 1, info[1]
+def first_sides(s, pay_b, pay_a, pay_s, sems):
+    odd, sec, _ = place()
+    _, cx, cy, _ = s.shape
+    copies = []
+    for k, (u, d) in enumerate(zip(stress_up(cx), stress_down(cx))):
+        part = pl.ds(k * cy, cy)
+        for pay, (p, q) in ((pay_b, (u, d)), (pay_a, (d, u))):
+            source = s.at[jnp.where(odd, p[0], q[0]), jnp.where(odd, p[1], q[1])]
+            copies.append(pltpu.make_async_copy(source, pay.at[part], sems.at[len(copies)]))
+    begin = pl.multiple_of(jnp.where(sec == 0, cy - SIDE, 0), SIDE)
+    for k, comp in enumerate(STRESS_ROWS):
+        source = s.at[comp, :, pl.ds(begin, SIDE), :]
+        copies.append(pltpu.make_async_copy(source, pay_s.at[k], sems.at[len(copies)]))
+    for copy in copies:
+        copy.start()
+    for copy in copies:
+        copy.wait()
+
+
+def step_velocity(s, v, b, from_b, from_a, from_s, v_out, pay_b, pay_a, pay_s, rows_ref):
+    odd, sec, _ = place()
     _, cx, cy, nz = s.shape
     fw, bw = depth_weights(nz)
     low, high = sides(odd, from_b, from_a, cy)
@@ -163,10 +189,10 @@
 
 
 def last_velocity(
-    info, s, v, b, from_b, from_a, from_s, ocean, marks, v_out, pay_b, pay_a, pay_s, patch, rows_ref
+    s, v, b, from_b, from_a, from_s, ocean, marks, v_out, pay_b, pay_a, pay_s, patch, rows_ref
 ):
-    step_velocity(info, s, v, b, from_b, from_a, from_s, v_out, pay_b, pay_a, pay_s, rows_ref)
-    odd = info[0] == 1
+    step_velocity(s, v, b, from_b, from_a, from_s, v_out, pay_b, pay_a, pay_s, rows_ref)
+    odd, _, _ = place()
     _, cx, cy, nz = s.shape
     first = (lax.broadcasted_iota(jnp.int32, (8, nz), 1) == 0).astype(F32)
     floor = jnp.concatenate([v_out[2, x] for x in range(cx)], axis=0)
@@ -177,25 +203,30 @@
         precision=lax.Precision.HIGHEST,
         preferred_element_type=F32,
     )
-    patch[...] = line[0:1, :]
+    pieces = cx * cy // 128
+    turn = lax.rem(lax.broadcasted_iota(jnp.int32, (8, 128), 0), pieces)
+    tiled = line[:, 0:128]
+    for k in range(1, pieces):
+        tiled = jnp.where(turn == k, line[:, k * 128 : (k + 1) * 128], tiled)
+    for k in range(0, patch.shape[0], 8):
+        patch[k : k + 8, :] = tiled
     fields, rows, columns = ocean.shape
     base = EDGE * cy
-    tiles = columns // 128
-    for f in range(fields + 1):
-        for k in range(tiles if f < fields else 1):
-            part = slice(base, base + SIDE)
-            if f < fields:
-                upper = ocean[f, rows - SIDE : rows, k * 128 : (k + 1) * 128]
-                lower = ocean[f, 0:SIDE, k * 128 : (k + 1) * 128]
-            else:
-                upper, lower = marks[rows - SIDE : rows, :], marks[0:SIDE, :]
-            pay_b[part, :] = jnp.where(odd, upper, lower)
-            pay_a[part, :] = jnp.where(odd, lower, upper)
-            base += SIDE
-
-
-def update_stress(info, v, s, lam, mu, from_b, from_a, from_s, s_out, rows_ref):
-    odd, sec = info[0] == 1, info[1]
+    for k in range(columns // 128):
+        lanes = slice(k * 128, (k + 1) * 128)
+        for f in range(fields):
+            n = DEEP[f]
+            upper, lower = ocean[f, rows - n : rows, lanes], ocean[f, 0:n, lanes]
+            pay_b[base : base + n, :] = jnp.where(odd, upper, lower)
+            pay_a[base : base + n, :] = jnp.where(odd, lower, upper)
+            base += n
+    upper, lower = marks[rows - SIDE : rows, :], marks[0:SIDE, :]
+    pay_b[base : base + SIDE, :] = jnp.where(odd, upper, lower)
+    pay_a[base : base + SIDE, :] = jnp.where(odd, lower, upper)
+
+
+def update_stress(v, s, lam, mu, from_b, from_a, from_s, s_out, rows_ref, each=None):
+    odd, sec, _ = place()
     _, cx, cy, nz = s.shape
     fw, bw = depth_weights(nz)
     low, high = sides(odd, from_b, from_a, cy)
@@ -217,52 +248,52 @@
         s_out[3, x] = s[3, x] + shear * (forward(vx_rows, 0) + forward(vy, x))
         s_out[4, x] = s[4, x] + shear * (forward_z(v[0, x], fw) + forward(vz, x))
         s_out[5, x] = s[5, x] + shear * (forward_z(v[1, x], fw) + forward(vz_rows, 0))
-
-
-def step_stress(
-    info, v, s, lam, mu, from_b, from_a, from_s, s_out, pay_b, pay_a, pay_s, rows_ref
-):
-    odd, sec = info[0] == 1, info[1]
+        if each is not None:
+            each(x)
+
+
+def step_stress(v, s, lam, mu, from_b, from_a, from_s, s_out, pay_b, pay_a, pay_s, rows_ref):
+    odd, sec, _ = place()
     _, cx, cy, nz = s.shape
-    update_stress(info, v, s, lam, mu, from_b, from_a, from_s, s_out, rows_ref)
+    update_stress(v, s, lam, mu, from_b, from_a, from_s, s_out, rows_ref)
     send_sides(odd, stress_up(cx), stress_down(cx), pay_b, pay_a, cy, lambda c, x: s_out[c, x])
     send_rows(sec, STRESS_ROWS, pay_s, lambda c, x, y: s_out[c, x, y : y + SIDE, :], cx, cy)
 
 
-def last_stress(
-    info,
-    v,
-    s,
-    lam,
-    mu,
-    from_b,
-    from_a,
-    from_s,
-    ocean,
-    marks,
-    patches,
-    s_out,
-    ocean_out,
-    rows_ref,
-    ocean_ref,
-    marks_ref,
-):
-    odd, sec, tile, count, base = info[0] == 1, info[1], info[2], info[3], info[4]
-    _, cx, cy, nz = s.shape
-    update_stress(info, v, s, lam, mu, from_b, from_a, from_s, s_out, rows_ref)
-
+def last_stress(v, s, lam, mu, from_b, from_a, from_s, v_out, s_out, rows_ref, made, sems):
+    cx = s.shape[1]
+    copies = [pltpu.make_async_copy(v, v_out, sems.at[cx])]
+    copies[0].start()
+
+    def each(x):
+        copy = pltpu.make_async_copy(made.at[:, x], s_out.at[:, x], sems.at[x])
+        copy.start()
+        copies.append(copy)
+
+    update_stress(v, s, lam, mu, from_b, from_a, from_s, made, rows_ref, each)
+    for copy in copies:
+        copy.wait()
+
+
+def ocean_steps(start, from_b, from_a, ocean, marks, patches, ocean_out, ocean_ref, marks_ref):
+    odd, sec, tile = place()
+    count = lax.axis_size("tile")
     fields, rows, columns = ocean.shape
     own = ocean_out.shape[2]
-    at = EDGE * cy
     top, bottom = slice(0, SIDE), slice(SIDE + rows, SIDE + rows + SIDE)
+    at = start
     for f in range(fields):
         ocean_ref[f, SIDE : SIDE + rows, :] = ocean[f]
-        for k in range(columns // 128):
-            lanes = slice(k * 128, (k + 1) * 128)
-            b, a = from_b[at : at + SIDE, :], from_a[at : at + SIDE, :]
-            ocean_ref[f, top, lanes] = jnp.where(odd, a, b)
-            ocean_ref[f, bottom, lanes] = jnp.where(odd, b, a)
-            at += SIDE
+        ocean_ref[f, top, :] = jnp.zeros((SIDE, columns), F32)
+        ocean_ref[f, bottom, :] = jnp.zeros((SIDE, columns), F32)
+    for k in range(columns // 128):
+        lanes = slice(k * 128, (k + 1) * 128)
+        for f in range(fields):
+            n = DEEP[f]
+            b, a = from_b[at : at + n, :], from_a[at : at + n, :]
+            ocean_ref[f, SIDE - n : SIDE, lanes] = jnp.where(odd, a, b)
+            ocean_ref[f, SIDE + rows : SIDE + rows + n, lanes] = jnp.where(odd, b, a)
+            at += n
     b, a = from_b[at : at + SIDE, :], from_a[at : at + SIDE, :]
     marks_ref[SIDE : SIDE + rows, :] = marks[...]
     marks_ref[top, :] = jnp.where(odd, a, b)
@@ -284,11 +315,20 @@
 
     eta, u, v_sea = ocean_ref[0], ocean_ref[1], ocean_ref[2]
     depth, wet = ocean_ref[3], ocean_ref[4]
-    owner = marks_ref[:, 0:1] - base.astype(F32)
+    window = min(WINDOW, count)
+    base = jnp.clip(tile - REACH - 1, 0, count - window)
+    owner = jnp.broadcast_to(marks_ref[:, 0:1] - base.astype(F32), (total, 128))
     share = marks_ref[:, 1:2]
-    uplift = jnp.zeros((total, columns), F32)
-    for k in range(patches.shape[0]):
-        uplift = jnp.where(owner == float(k), patches[k : k + 1, :], uplift)
+    pieces = own // 128
+    parts = [(sec, k) for k in range(pieces)] + [(1 - sec, sec * (pieces - 1))]
+    uplift = []
+    for half, piece in parts:
+        level = jnp.zeros((total, 128), F32)
+        for k in range(window):
+            row = (half * count + base + k) * pieces + piece
+            level = jnp.where(owner == float(k), patches[pl.ds(row, 1), :], level)
+        uplift.append(level)
+    uplift = jnp.concatenate(uplift, axis=1)
     lift = ODT * (share * wet * uplift)
     for _ in range(2):
         u = wet * (u - ODT * down(eta))
@@ -300,20 +340,24 @@
     ocean_out[2] = v_sea[part, :own]
 
 
-def call(body, name, outs, scratch, operands, flops):
+VMEM = pl.BlockSpec(memory_space=pltpu.VMEM)
+ANY = pl.BlockSpec(memory_space=pl.ANY)
+
+
+def call(body, name, outs, scratch, operands, weight=1, ins=VMEM, where=VMEM):
     shapes = [jax.ShapeDtypeStruct(o, F32) for o in outs]
-    smem = pl.BlockSpec(memory_space=pltpu.SMEM)
-    vmem = pl.BlockSpec(memory_space=pltpu.VMEM)
     moved = sum(o.size for o in operands) * 4 + sum(o.size for o in shapes) * 4
     return pl.pallas_call(
         body,
         name=name,
         out_shape=shapes,
-        in_specs=[smem] + [vmem] * (len(operands) - 1),
-        out_specs=[vmem] * len(outs),
-        scratch_shapes=[pltpu.VMEM(shape, F32) for shape in scratch],
+        in_specs=[ins] * len(operands),
+        out_specs=[where] * len(outs),
+        scratch_shapes=scratch,
         compiler_params=pltpu.CompilerParams(vmem_limit_bytes=32 * 1024 * 1024),
-        cost_estimate=pl.CostEstimate(flops=flops, bytes_accessed=moved, transcendentals=0),
+        cost_estimate=pl.CostEstimate(
+            flops=moved, bytes_accessed=moved * weight, transcendentals=0
+        ),
     )(*operands)
 
 
@@ -344,25 +388,27 @@
     intersection_share,
 ):
     count = lax.axis_size("tile")
-    tile, sec = lax.axis_index("tile"), lax.axis_index("sec")
-    odd = lax.rem(tile, 2)
+    sec = lax.axis_index("sec")
     _, cx, cy, nz = stresses.shape
     _, rows, columns = ocean_state.shape
-    base = jnp.clip(tile - REACH - 1, 0, max(count - WINDOW, 0))
-    info = jnp.stack([odd, sec, tile, jnp.int32(count), base]).astype(jnp.int32)
-
-    up = jnp.concatenate([stresses[c, x] for c, x in stress_up(cx)])
-    down = jnp.concatenate([stresses[c, x] for c, x in stress_down(cx)])
-    pay_b, pay_a = jnp.where(odd == 1, up, down), jnp.where(odd == 1, down, up)
+    side = (EDGE * cy, nz)
+    strip = (3 * cx * SIDE, nz)
+    halo_rows = pltpu.VMEM((3, cx, cy + 2 * SIDE, nz), F32)
+
+    pay_b, pay_a, pay_s = call(
+        first_sides,
+        "first_sides",
+        [side, side, (3, cx, SIDE, nz)],
+        [pltpu.SemaphoreType.DMA((2 * EDGE + 3,))],
+        [stresses],
+        ins=ANY,
+    )
     from_b, from_a = exchange(pay_b, pay_a, count)
-
-    edge = jnp.stack([stresses[c] for c in STRESS_ROWS])
-    edge = jnp.where(sec == 0, edge[:, :, cy - SIDE :, :], edge[:, :, :SIDE, :])
+    from_s = across(pay_s.reshape(strip))
+
     fields = jnp.concatenate([ocean_state, depth_map[None], wet_mask.astype(F32)[None]])
     near = jnp.where(sec == 0, fields[:, :, columns - 128 :], fields[:, :, :128])
-    got = across(jnp.concatenate([edge.reshape(-1, nz), near.reshape(-1, 128)]))
-    from_s = got[: 3 * cx * SIDE]
-    ocean = jnp.concatenate([fields, got[3 * cx * SIDE :].reshape(-1, rows, 128)], axis=2)
+    ocean = jnp.concatenate([fields, across(near)], axis=2)
     lane = lax.broadcasted_iota(jnp.int32, (rows, 128), 1)
     marks = jnp.where(
         lane == 0,
@@ -370,19 +416,12 @@
         jnp.where(lane == 1, intersection_share[:, None], 0.0),
     )
 
-    cells = cx * cy * nz
-    side = (EDGE * cy, nz)
-    strip = (3 * cx * SIDE, nz)
-    halo_rows = (3, cx, cy + 2 * SIDE, nz)
-    tiles = (ocean.shape[0] * ocean.shape[2] // 128 + 1) * SIDE
-    long_side = (EDGE * cy + tiles, nz)
     velocity, pay_b, pay_a, pay_s = call(
         step_velocity,
         "velocity_step",
         [velocity.shape, side, side, strip],
         [halo_rows],
-        [info, stresses, velocity, buoyancy, from_b, from_a, from_s],
-        60 * cells,
+        [stresses, velocity, buoyancy, from_b, from_a, from_s],
     )
     from_b, from_a = exchange(pay_b, pay_a, count)
     from_s = across(pay_s)
@@ -391,41 +430,40 @@
         "stress_step",
         [stresses.shape, side, side, strip],
         [halo_rows],
-        [info, velocity, stresses, lame_first, shear_mod, from_b, from_a, from_s],
-        70 * cells,
+        [velocity, stresses, lame_first, shear_mod, from_b, from_a, from_s],
     )
     from_b, from_a = exchange(pay_b, pay_a, count)
     from_s = across(pay_s)
+    long_side = (EDGE * cy + ocean.shape[2] // 128 * PACK + SIDE, nz)
+    pieces = cx * cy // 128
     velocity, pay_b, pay_a, pay_s, patch = call(
         last_velocity,
         "velocity_last",
-        [velocity.shape, long_side, long_side, strip, (1, cx * cy)],
+        [velocity.shape, long_side, long_side, strip, (2 * count * pieces, 128)],
         [halo_rows],
-        [info, stresses, velocity, buoyancy, from_b, from_a, from_s, ocean, marks],
-        60 * cells,
+        [stresses, velocity, buoyancy, from_b, from_a, from_s, ocean, marks],
     )
     from_b, from_a = exchange(pay_b, pay_a, count)
     from_s = across(pay_s)
-    spread = jnp.broadcast_to(patch.reshape(1, -1, 128), (2 * count, cx * cy // 128, 128))
-    patches = lax.all_to_all(spread, ("sec", "tile"), 0, 0).reshape(2, count, cx * cy)
-    window = min(WINDOW, count)
-    mine = lax.dynamic_slice(patches, (sec, base, 0), (1, window, cx * cy))[0]
-    theirs = lax.dynamic_slice(
-        patches, (1 - sec, base, sec * (cx * cy - 128)), (1, window, 128)
-    )[0]
-    patches = jnp.concatenate([mine, theirs], axis=1)
-    stresses, ocean_state = call(
+    patches = lax.all_to_all(patch.reshape(2 * count, pieces, 128), ("sec", "tile"), 0, 0)
+    velocity, stresses = call(
         last_stress,
         "stress_last",
-        [stresses.shape, ocean_state.shape],
+        [velocity.shape, stresses.shape],
+        [halo_rows, pltpu.VMEM(stresses.shape, F32), pltpu.SemaphoreType.DMA((cx + 1,))],
+        [velocity, stresses, lame_first, shear_mod, from_b, from_a, from_s],
+        weight=8,
+        where=ANY,
+    )
+    (ocean_state,) = call(
+        functools.partial(ocean_steps, EDGE * cy),
+        "ocean_steps",
+        [ocean_state.shape],
         [
-            halo_rows,
-            (ocean.shape[0], rows + 2 * SIDE, ocean.shape[2]),
-            (rows + 2 * SIDE, 128),
+            pltpu.VMEM((ocean.shape[0], rows + 2 * SIDE, ocean.shape[2]), F32),
+            pltpu.VMEM((rows + 2 * SIDE, 128), F32),
         ],
-        [info, velocity, stresses, lame_first, shear_mod, from_b, from_a, from_s, ocean, marks]
-        + [patches],
-        80 * cells,
+        [from_b, from_a, ocean, marks, patches.reshape(-1, 128)],
     )
     return velocity, stresses, ocean_state
 

time: 67.5 us -> 62.2 us (0.921)
  local copies, waits for them, and re-layouts: 4.85 us -> 1.97 us
  starting transfers between devices: 28.5 us -> 26.5 us
  Pallas kernels: 6.27 us -> 5.1 us
  other arithmetic: 1.07 us -> 1.97 us
    ppermute x8, waiting for transfers between devices: 22 us -> 16.7 us  [swap(): return lax.ppermute(pay, 'tile', pairs)]
    all_to_all x1, waiting for transfers between devices: 1.78 us -> 6.89 us  [shards(): lax.all_to_all(patch.reshape(2 * count, pieces, 128), ('sec', 'tile'), 0, 0)]
    ppermute x8, starting transfers between devices: 21.8 us -> 18.1 us  [swap(): return lax.ppermute(pay, 'tile', pairs)]
    pallas_call x4 -> x6, Pallas kernels: 6.27 us -> 5.1 us  [call(): pl.pallas_call(body, name=name, out_shape=shapes, in_specs=[ins] * len(op...]
    slice x3 -> x0, local copies, waits for them, and re-layouts: 1.12 us -> none  [the longest x1 1.1 us: shards(): edge = jnp.stack([stresses[c] for c in STRESS_ROWS])]
    all_to_all x1, starting transfers between devices: 5.79 us -> 6.9 us  [shards(): lax.all_to_all(patch.reshape(2 * count, pieces, 128), ('sec', 'tile'), 0, 0)]
    concatenate x1, other arithmetic: 0.02 us -> 0.99 us  [shards(): jnp.concatenate([ocean_state, depth_map[None], wet_mask.astype(F32)[None]])]
    unnamed x24 -> x20, local copies, waits for them, and re-layouts: 2.89 us -> 1.97 us
  transfers between devices with their start and end apart: 13 -> 14, of which waited for: 7 -> 6; matrix products, arithmetic and copies ran while one was open for 1% -> 3% of each run, Pallas kernels for 0% -> 3%
where the time goes in v2:
time: 62.2 us; the launch traced here: 61.9 us
  starting transfers between devices  26.5 us (43%)
  waiting for transfers between devices  25.5 us (41%)
  Pallas kernels  5.1 us (8%)
  local copies, waits for them, and re-layouts  1.97 us (3%)
  other arithmetic  1.97 us (3%)
  between operations  0.84 us (1%)
    ppermute x8, starting transfers between devices, swap(): return lax.ppermute(pay, 'tile', pairs)  18.1 us
    ppermute x8, waiting for transfers between devices, swap(): return lax.ppermute(pay, 'tile', pairs)  16.7 us
    all_to_all x1, starting transfers between devices, shards(): lax.all_to_all(patch.reshape(2 * count, pieces, 128), ('sec', 'tile'), 0, 0)  6.9 us
    all_to_all x1, waiting for transfers between devices, shards(): lax.all_to_all(patch.reshape(2 * count, pieces, 128), ('sec', 'tile'), 0, 0)  6.89 us
    pallas_call x6, Pallas kernels, call(): pl.pallas_call(body, name=name, out_shape=shapes, in_specs=[ins] * len(op...  5.1 us
    unnamed x20, local copies, waits for them, and re-layouts  1.97 us
    ppermute x5, waiting for transfers between devices, across(): return lax.ppermute(pay, 'sec', [(0, 1), (1, 0)])  1.95 us
    ppermute x5, starting transfers between devices, across(): return lax.ppermute(pay, 'sec', [(0, 1), (1, 0)])  1.46 us
  transfers between devices with their start and end apart: 14, of which 6 were waited for; matrix products, arithmetic and copies ran while one was open for 3% of the time, Pallas kernels for 3%

profile of v2, /device:TPU:0, one launch (start us, length us, event | category | flops | bytes accessed | tf_op | source)
XLA Modules:
  0.0 61.9 jit_solution(17788661950533923240)
XLA Ops:
  0.6 1.1 %copy-done = f32[6,4,64,128]{3,2,1,0:T(8,128)S(1)} copy-done((f32[6,4,64,128]{3,2,1,0:T(8,128)S(1)}, f32[6,4,64,128]{3,2,1,0:T(8,128)}, u32[]{:S(2)}) %copy-start) | copy-done | bytes 786456
  1.8 0.6 first_sides.1
  2.3 0.5 collective-permute-start.2
  2.8 0.7 %collective-permute-start = (f32[320,128]{1,0:T(8,128)S(1)}, f32[320,128]{1,0:T(8,128)S(1)}, u32[]{:S(2)}, u32[]{:S(2)}) collective-permute-start(f32[320,128]{1,0:T(8,128)S(1)} %get-tuple-element.21), channel_id=1, source_target_pairs={{1,2},{2,1},{3,4},{4,3},{5,6},{6,5},{7,8},{8,7},{9,10},{10,9},{11,... | collective-permute-start | bytes 491528 | tf_op jit(solution)/shard_map/ppermute | solution.py:369
  3.5 5.3 %collective-permute-start.1 = (f32[320,128]{1,0:T(8,128)S(1)}, f32[320,128]{1,0:T(8,128)S(1)}, u32[]{:S(2)}, u32[]{:S(2)}) collective-permute-start(f32[320,128]{1,0:T(8,128)S(1)} %get-tuple-element.22), channel_id=1, source_target_pairs={{0,1},{1,0},{2,3},{3,2},{4,5},{5,4},{6,7},{7,6},{8,9},{9,8},{10,11... | collective-permute-start | bytes 491528 | tf_op jit(solution)/shard_map/ppermute | solution.py:369
  8.8 0.8 %convert_bitcast_fusion = f32[1,64,256]{2,1,0:T(8,128)S(1)} fusion(s32[64,256]{1,0:T(8,128)} %param.17), kind=kLoop, calls=%fused_computation.3 | loop fusion | flops 16384 | bytes 131072 | tf_op jit(solution)/shard_map/broadcast_in_dim | solution.py:409
  9.7 1.0 %pad_maximum_fusion.1 = f32[5,64,256]{2,1,0:T(8,128)S(1)} fusion(f32[1,64,256]{2,1,0:T(8,128)S(1)} %convert_bitcast_fusion, f32[1,64,256]{2,1,0:T(8,128)S(1)} %bitcast.8, f32[3,64,256]{2,1,0:T(8,128)} %param.15), kind=kLoop, calls=%fused_computation.1 | loop fusion | flops 163840 | bytes 655360 | tf_op jit(solution)/shard_map/concatenate | solution.py:409
  10.7 6.1 %collective-permute-done.1.from_a = f32[320,128]{1,0:T(8,128)S(1)} collective-permute-done((f32[320,128]{1,0:T(8,128)S(1)}, f32[320,128]{1,0:T(8,128)S(1)}, u32[]{:S(2)}, u32[]{:S(2)}) %collective-permute-start.1) | collective-permute-done | bytes 163872 | tf_op jit(solution)/shard_map/ppermute | solution.py:369
  16.8 0.4 velocity_step.1
  17.3 0.7 %collective-permute-start.3 = (f32[320,128]{1,0:T(8,128)S(1)}, f32[320,128]{1,0:T(8,128)S(1)}, u32[]{:S(2)}, u32[]{:S(2)}) collective-permute-start(f32[320,128]{1,0:T(8,128)S(1)} %get-tuple-element.25), channel_id=1, source_target_pairs={{1,2},{2,1},{3,4},{4,3},{5,6},{6,5},{7,8},{8,7},{9,10},{10,9},{11,... | collective-permute-start | bytes 491528 | tf_op jit(solution)/shard_map/ppermute | solution.py:369
  18.0 3.2 %collective-permute-start.4 = (f32[320,128]{1,0:T(8,128)S(1)}, f32[320,128]{1,0:T(8,128)S(1)}, u32[]{:S(2)}, u32[]{:S(2)}) collective-permute-start(f32[320,128]{1,0:T(8,128)S(1)} %get-tuple-element.26), channel_id=1, source_target_pairs={{0,1},{1,0},{2,3},{3,2},{4,5},{5,4},{6,7},{7,6},{8,9},{9,8},{10,11... | collective-permute-start | bytes 491528 | tf_op jit(solution)/shard_map/ppermute | solution.py:369
  21.2 0.1 collective-permute-start.9
  21.3 0.5 collective-permute-start.5
  21.7 0.2 copy-done.9
  21.9 0.8 %collective-permute-done.5.from_s = f32[96,128]{1,0:T(8,128)S(1)} collective-permute-done((f32[96,128]{1,0:T(8,128)S(1)}, f32[96,128]{1,0:T(8,128)S(1)}, u32[]{:S(2)}, u32[]{:S(2)}) %collective-permute-start.5) | collective-permute-done | bytes 49184 | tf_op jit(solution)/shard_map/ppermute | solution.py:375
  22.7 5.7 %collective-permute-done.4.from_a = f32[320,128]{1,0:T(8,128)S(1)} collective-permute-done((f32[320,128]{1,0:T(8,128)S(1)}, f32[320,128]{1,0:T(8,128)S(1)}, u32[]{:S(2)}, u32[]{:S(2)}) %collective-permute-start.4) | collective-permute-done | bytes 163872 | tf_op jit(solution)/shard_map/ppermute | solution.py:369
  28.4 0.5 stress_step.1
  29.0 0.7 %collective-permute-start.6 = (f32[320,128]{1,0:T(8,128)S(1)}, f32[320,128]{1,0:T(8,128)S(1)}, u32[]{:S(2)}, u32[]{:S(2)}) collective-permute-start(f32[320,128]{1,0:T(8,128)S(1)} %get-tuple-element.29), channel_id=1, source_target_pairs={{1,2},{2,1},{3,4},{4,3},{5,6},{6,5},{7,8},{8,7},{9,10},{10,9},{11,... | collective-permute-start | bytes 491528 | tf_op jit(solution)/shard_map/ppermute | solution.py:369
  29.6 3.5 %collective-permute-start.7 = (f32[320,128]{1,0:T(8,128)S(1)}, f32[320,128]{1,0:T(8,128)S(1)}, u32[]{:S(2)}, u32[]{:S(2)}) collective-permute-start(f32[320,128]{1,0:T(8,128)S(1)} %get-tuple-element.30), channel_id=1, source_target_pairs={{0,1},{1,0},{2,3},{3,2},{4,5},{5,4},{6,7},{7,6},{8,9},{9,8},{10,11... | collective-permute-start | bytes 491528 | tf_op jit(solution)/shard_map/ppermute | solution.py:369
  33.1 0.7 %copy-done.8 = f32[64]{0:T(128)S(1)} copy-done((f32[64]{0:T(128)S(1)}, f32[64]{0:T(128)}, u32[]{:S(2)}) %copy-start.8) | copy-done | bytes 280
  33.8 0.1 select_select_fusion.marks
  33.9 0.1 collective-permute-start.8
  34.0 1.2 %collective-permute-done.8.from_s = f32[96,128]{1,0:T(8,128)S(1)} collective-permute-done((f32[96,128]{1,0:T(8,128)S(1)}, f32[96,128]{1,0:T(8,128)S(1)}, u32[]{:S(2)}, u32[]{:S(2)}) %collective-permute-start.8) | collective-permute-done | bytes 49184 | tf_op jit(solution)/shard_map/ppermute | solution.py:375
  35.2 4.9 %collective-permute-done.7.from_a = f32[320,128]{1,0:T(8,128)S(1)} collective-permute-done((f32[320,128]{1,0:T(8,128)S(1)}, f32[320,128]{1,0:T(8,128)S(1)}, u32[]{:S(2)}, u32[]{:S(2)}) %collective-permute-start.7) | collective-permute-done | bytes 163872 | tf_op jit(solution)/shard_map/ppermute | solution.py:369
  40.0 1.1 %velocity_last.1 = (f32[3,4,64,128]{3,2,1,0:T(8,128)S(1)}, f32[376,128]{1,0:T(8,128)S(1)}, f32[376,128]{1,0:T(8,128)S(1)}, f32[96,128]{1,0:T(8,128)S(1)}, f32[64,128]{1,0:T(8,128)}) custom-call(f32[6,4,64,128]{3,2,1,0:T(8,128)S(1)} %get-tuple-element.28.s, f32[3,4,64,128]{3,2,1,0:T(8,128)S(1)} %get-tuple-element.24.v, f32[4,64,128]{2,1,0:T(8,128)S(1)} %copy-done.4, ...), custom_call_target="tpu_custom_call" | custom-call | flops 3072000 | bytes 3072000 | tf_op jit(solution)/shard_map/velocity_last/pallas_call | solution.py:350
  41.1 0.7 %collective-permute-start.10 = (f32[376,128]{1,0:T(8,128)S(1)}, f32[376,128]{1,0:T(8,128)S(1)}, u32[]{:S(2)}, u32[]{:S(2)}) collective-permute-start(f32[376,128]{1,0:T(8,128)S(1)} %get-tuple-element.33), channel_id=1, source_target_pairs={{1,2},{2,1},{3,4},{4,3},{5,6},{6,5},{7,8},{8,7},{9,10},{10,9},{11,... | collective-permute-start | bytes 577544 | tf_op jit(solution)/shard_map/ppermute | solution.py:369
  41.8 3.5 %collective-permute-start.11 = (f32[376,128]{1,0:T(8,128)S(1)}, f32[376,128]{1,0:T(8,128)S(1)}, u32[]{:S(2)}, u32[]{:S(2)}) collective-permute-start(f32[376,128]{1,0:T(8,128)S(1)} %get-tuple-element.34), channel_id=1, source_target_pairs={{0,1},{1,0},{2,3},{3,2},{4,5},{5,4},{6,7},{7,6},{8,9},{9,8},{10,11... | collective-permute-start | bytes 577544 | tf_op jit(solution)/shard_map/ppermute | solution.py:369
  45.3 6.9 %all-to-all-start = ((f32[32,2,128]{2,1,0:T(2,128)}), f32[32,2,128]{2,1,0:T(2,128)S(1)}, u32[]{:S(2)}, u32[]{:S(2)}) async-start(f32[32,2,128]{2,1,0:T(2,128)} %bitcast.3), calls=%async_computation | async-start | bytes 65536 | tf_op jit(solution)/shard_map/all_to_all | solution.py:448
  52.2 0.3 collective-permute-start.12
  52.5 6.9 %all-to-all-done = f32[32,2,128]{2,1,0:T(2,128)S(1)} async-done(((f32[32,2,128]{2,1,0:T(2,128)}), f32[32,2,128]{2,1,0:T(2,128)S(1)}, u32[]{:S(2)}, u32[]{:S(2)}) %all-to-all-start) | async-done | bytes 32800 | tf_op jit(solution)/shard_map/all_to_all | solution.py:448
  59.4 1.3 %ocean_steps.1 = f32[3,64,256]{2,1,0:T(8,128)} custom-call(f32[376,128]{1,0:T(8,128)S(1)} %collective-permute-done.10.from_b, f32[376,128]{1,0:T(8,128)S(1)} %collective-permute-done.11.from_a, f32[5,64,384]{2,1,0:T(8,128)S(1)} %pad_maximum_fusion.ocean, f32[64,128]{1,0:T(8,128)S(1)} %select_select_fusion.marks, f32[64,128]{1,0:T(8,128)S(1)} %bitcast.6), custom_call_target="tpu_custom_call" | custom-call | flops 1138688 | bytes 1138688 | tf_op jit(solution)/shard_map/ocean_steps/pallas_call | solution.py:350
  60.6 1.2 %stress_last.1 = (f32[3,4,64,128]{3,2,1,0:T(8,128)}, f32[6,4,64,128]{3,2,1,0:T(8,128)}) custom-call(f32[3,4,64,128]{3,2,1,0:T(8,128)S(1)} %get-tuple-element.32.v, f32[6,4,64,128]{3,2,1,0:T(8,128)S(1)} %get-tuple-element.28.s, f32[4,64,128]{2,1,0:T(8,128)S(1)} %copy-done.2, f32[4,64,128]{2,1,0:T(8,128)S(1)} %copy-done.3, ...), custom_call_target="tpu_custom_call" | custom-call | flops 3055616 | bytes 24444928 | tf_op jit(solution)/shard_map/stress_last/pallas_call | solution.py:350
  (29 shorter events, 0.1 us)
Async XLA Ops:
  0.6 1.1 %copy-start = (f32[6,4,64,128]{3,2,1,0:T(8,128)S(1)}, f32[6,4,64,128]{3,2,1,0:T(8,128)}, u32[]{:S(2)}) copy-start(f32[6,4,64,128]{3,2,1,0:T(8,128)} %s.5) | copy-start | bytes 2359300
  1.8 15.0 %copy-start.1 = (f32[6,4,64,128]{3,2,1,0:T(8,128)S(1)}, f32[6,4,64,128]{3,2,1,0:T(8,128)}, u32[]{:S(2)}) copy-start(f32[6,4,64,128]{3,2,1,0:T(8,128)} %s.5) | copy-start | bytes 2359300
  2.3 8.4 %collective-permute-start.2 = (f32[96,128]{1,0:T(8,128)S(1)}, f32[96,128]{1,0:T(8,128)S(1)}, u32[]{:S(2)}, u32[]{:S(2)}) collective-permute-start(f32[96,128]{1,0:T(8,128)S(1)} %bitcast.7), channel_id=1, source_target_pairs={{0,16},{16,0},{1,17},{17,1},{2,18},{18,2},{3,19},{19,3},{4,20},{20... | collective-permute-start | bytes 147464 | tf_op jit(solution)/shard_map/ppermute | solution.py:375
  2.8 7.9 %collective-permute-start = (f32[320,128]{1,0:T(8,128)S(1)}, f32[320,128]{1,0:T(8,128)S(1)}, u32[]{:S(2)}, u32[]{:S(2)}) collective-permute-start(f32[320,128]{1,0:T(8,128)S(1)} %get-tuple-element.21), channel_id=1, source_target_pairs={{1,2},{2,1},{3,4},{4,3},{5,6},{6,5},{7,8},{8,7},{9,10},{10,9},{11,... | collective-permute-start | bytes 491528 | tf_op jit(solution)/shard_map/ppermute | solution.py:369
  3.5 6.2 %copy-start.7 = (f32[64,256]{1,0:T(8,128)S(1)}, f32[64,256]{1,0:T(8,128)}, u32[]{:S(2)}) copy-start(f32[64,256]{1,0:T(8,128)} %param.16) | copy-start | bytes 196612
  3.5 13.3 %copy-start.5 = (f32[3,4,64,128]{3,2,1,0:T(8,128)S(1)}, f32[3,4,64,128]{3,2,1,0:T(8,128)}, u32[]{:S(2)}) copy-start(f32[3,4,64,128]{3,2,1,0:T(8,128)} %v.1) | copy-start | bytes 1179652
  3.5 13.3 %collective-permute-start.1 = (f32[320,128]{1,0:T(8,128)S(1)}, f32[320,128]{1,0:T(8,128)S(1)}, u32[]{:S(2)}, u32[]{:S(2)}) collective-permute-start(f32[320,128]{1,0:T(8,128)S(1)} %get-tuple-element.22), channel_id=1, source_target_pairs={{0,1},{1,0},{2,3},{3,2},{4,5},{5,4},{6,7},{7,6},{8,9},{9,8},{10,11... | collective-permute-start | bytes 491528 | tf_op jit(solution)/shard_map/ppermute | solution.py:369
  9.7 7.1 %copy-start.4 = (f32[4,64,128]{2,1,0:T(8,128)S(1)}, f32[4,64,128]{2,1,0:T(8,128)}, u32[]{:S(2)}) copy-start(f32[4,64,128]{2,1,0:T(8,128)} %b.3) | copy-start | bytes 393220
  17.3 5.4 %collective-permute-start.3 = (f32[320,128]{1,0:T(8,128)S(1)}, f32[320,128]{1,0:T(8,128)S(1)}, u32[]{:S(2)}, u32[]{:S(2)}) collective-permute-start(f32[320,128]{1,0:T(8,128)S(1)} %get-tuple-element.25), channel_id=1, source_target_pairs={{1,2},{2,1},{3,4},{4,3},{5,6},{6,5},{7,8},{8,7},{9,10},{10,9},{11,... | collective-permute-start | bytes 491528 | tf_op jit(solution)/shard_map/ppermute | solution.py:369
  17.9 10.5 %copy-start.2 = (f32[4,64,128]{2,1,0:T(8,128)S(1)}, f32[4,64,128]{2,1,0:T(8,128)}, u32[]{:S(2)}) copy-start(f32[4,64,128]{2,1,0:T(8,128)} %lam.3) | copy-start | bytes 393220
  18.0 10.5 %copy-start.3 = (f32[4,64,128]{2,1,0:T(8,128)S(1)}, f32[4,64,128]{2,1,0:T(8,128)}, u32[]{:S(2)}) copy-start(f32[4,64,128]{2,1,0:T(8,128)} %mu.3) | copy-start | bytes 393220
  18.0 10.4 %collective-permute-start.4 = (f32[320,128]{1,0:T(8,128)S(1)}, f32[320,128]{1,0:T(8,128)S(1)}, u32[]{:S(2)}, u32[]{:S(2)}) collective-permute-start(f32[320,128]{1,0:T(8,128)S(1)} %get-tuple-element.26), channel_id=1, source_target_pairs={{0,1},{1,0},{2,3},{3,2},{4,5},{5,4},{6,7},{7,6},{8,9},{9,8},{10,11... | collective-permute-start | bytes 491528 | tf_op jit(solution)/shard_map/ppermute | solution.py:369
  21.2 12.8 %collective-permute-start.9 = (f32[5,64,128]{2,1,0:T(8,128)S(1)}, f32[5,64,128]{2,1,0:T(8,128)S(1)}, u32[]{:S(2)}, u32[]{:S(2)}) collective-permute-start(f32[5,64,128]{2,1,0:T(8,128)S(1)} %slice_select_fusion), channel_id=1, source_target_pairs={{0,16},{16,0},{1,17},{17,1},{2,18},{18,2},{3,19},{19,3},{4,20},{20... | collective-permute-start | bytes 491528 | tf_op jit(solution)/shard_map/ppermute | solution.py:375
  21.2 0.7 %copy-start.9 = (s32[64]{0:T(128)S(1)}, s32[64]{0:T(128)}, u32[]{:S(2)}) copy-start(s32[64]{0:T(128)} %param.18) | copy-start | bytes 772
  21.3 1.4 %collective-permute-start.5 = (f32[96,128]{1,0:T(8,128)S(1)}, f32[96,128]{1,0:T(8,128)S(1)}, u32[]{:S(2)}, u32[]{:S(2)}) collective-permute-start(f32[96,128]{1,0:T(8,128)S(1)} %get-tuple-element.27), channel_id=1, source_target_pairs={{0,16},{16,0},{1,17},{17,1},{2,18},{18,2},{3,19},{19,3},{4,20},{20... | collective-permute-start | bytes 147464 | tf_op jit(solution)/shard_map/ppermute | solution.py:375
  28.4 5.5 %copy-start.6 = (f32[3,64,256]{2,1,0:T(8,128)S(1)}, f32[3,64,256]{2,1,0:T(8,128)}, u32[]{:S(2)}) copy-start(f32[3,64,256]{2,1,0:T(8,128)} %param.15) | copy-start | bytes 589828
  29.0 6.2 %collective-permute-start.6 = (f32[320,128]{1,0:T(8,128)S(1)}, f32[320,128]{1,0:T(8,128)S(1)}, u32[]{:S(2)}, u32[]{:S(2)}) collective-permute-start(f32[320,128]{1,0:T(8,128)S(1)} %get-tuple-element.29), channel_id=1, source_target_pairs={{1,2},{2,1},{3,4},{4,3},{5,6},{6,5},{7,8},{8,7},{9,10},{10,9},{11,... | collective-permute-start | bytes 491528 | tf_op jit(solution)/shard_map/ppermute | solution.py:369
  29.6 10.4 %collective-permute-start.7 = (f32[320,128]{1,0:T(8,128)S(1)}, f32[320,128]{1,0:T(8,128)S(1)}, u32[]{:S(2)}, u32[]{:S(2)}) collective-permute-start(f32[320,128]{1,0:T(8,128)S(1)} %get-tuple-element.30), channel_id=1, source_target_pairs={{0,1},{1,0},{2,3},{3,2},{4,5},{5,4},{6,7},{7,6},{8,9},{9,8},{10,11... | collective-permute-start | bytes 491528 | tf_op jit(solution)/shard_map/ppermute | solution.py:369
  33.1 0.7 %copy-start.8 = (f32[64]{0:T(128)S(1)}, f32[64]{0:T(128)}, u32[]{:S(2)}) copy-start(f32[64]{0:T(128)} %param.19) | copy-start | bytes 772
  33.9 1.3 %collective-permute-start.8 = (f32[96,128]{1,0:T(8,128)S(1)}, f32[96,128]{1,0:T(8,128)S(1)}, u32[]{:S(2)}, u32[]{:S(2)}) collective-permute-start(f32[96,128]{1,0:T(8,128)S(1)} %get-tuple-element.31), channel_id=1, source_target_pairs={{0,16},{16,0},{1,17},{17,1},{2,18},{18,2},{3,19},{19,3},{4,20},{20... | collective-permute-start | bytes 147464 | tf_op jit(solution)/shard_map/ppermute | solution.py:375
  41.1 18.3 %collective-permute-start.10 = (f32[376,128]{1,0:T(8,128)S(1)}, f32[376,128]{1,0:T(8,128)S(1)}, u32[]{:S(2)}, u32[]{:S(2)}) collective-permute-start(f32[376,128]{1,0:T(8,128)S(1)} %get-tuple-element.33), channel_id=1, source_target_pairs={{1,2},{2,1},{3,4},{4,3},{5,6},{6,5},{7,8},{8,7},{9,10},{10,9},{11,... | collective-permute-start | bytes 577544 | tf_op jit(solution)/shard_map/ppermute | solution.py:369
  41.8 17.6 %collective-permute-start.11 = (f32[376,128]{1,0:T(8,128)S(1)}, f32[376,128]{1,0:T(8,128)S(1)}, u32[]{:S(2)}, u32[]{:S(2)}) collective-permute-start(f32[376,128]{1,0:T(8,128)S(1)} %get-tuple-element.34), channel_id=1, source_target_pairs={{0,1},{1,0},{2,3},{3,2},{4,5},{5,4},{6,7},{7,6},{8,9},{9,8},{10,11... | collective-permute-start | bytes 577544 | tf_op jit(solution)/shard_map/ppermute | solution.py:369
  45.3 14.1 %all-to-all-start = ((f32[32,2,128]{2,1,0:T(2,128)}), f32[32,2,128]{2,1,0:T(2,128)S(1)}, u32[]{:S(2)}, u32[]{:S(2)}) async-start(f32[32,2,128]{2,1,0:T(2,128)} %bitcast.3), calls=%async_computation | async-start | bytes 65536 | tf_op jit(solution)/shard_map/all_to_all | solution.py:448
  52.2 8.5 %collective-permute-start.12 = (f32[96,128]{1,0:T(8,128)S(1)}, f32[96,128]{1,0:T(8,128)S(1)}, u32[]{:S(2)}, u32[]{:S(2)}) collective-permute-start(f32[96,128]{1,0:T(8,128)S(1)} %get-tuple-element.35), channel_id=1, source_target_pairs={{0,16},{16,0},{1,17},{17,1},{2,18},{18,2},{3,19},{19,3},{4,20},{20... | collective-permute-start | bytes 147464 | tf_op jit(solution)/shard_map/ppermute | solution.py:375

commit v3 on v2

--- a/solution.py
+++ b/solution.py
@@ -67,7 +67,7 @@
     return lax.rem(tile, 2) == 1, sec, tile
 
 
-def sides(odd, from_b, from_a, rows):
+def sides(odd, from_a, from_b, rows):
     def low(k):
         part = slice(k * rows, (k + 1) * rows)
         return jnp.where(odd, from_a[part, :], from_b[part, :])
@@ -105,7 +105,7 @@
     return lambda shift: rows_ref[k, x, SIDE + shift : SIDE + shift + cy, :]
 
 
-def send_sides(odd, up, down, pay_b, pay_a, rows, get):
+def send_sides(odd, up, down, pay_a, pay_b, rows, get):
     for k, (u, d) in enumerate(zip(up, down)):
         part = slice(k * rows, (k + 1) * rows)
         upper, lower = get(*u), get(*d)
@@ -142,13 +142,13 @@
     return [(0, 0), (1, 0), (1, 1), (2, 0), (2, 1)]
 
 
-def first_sides(s, pay_b, pay_a, pay_s, sems):
+def first_sides(s, pay_a, pay_b, pay_s, sems):
     odd, sec, _ = place()
     _, cx, cy, _ = s.shape
     copies = []
     for k, (u, d) in enumerate(zip(stress_up(cx), stress_down(cx))):
         part = pl.ds(k * cy, cy)
-        for pay, (p, q) in ((pay_b, (u, d)), (pay_a, (d, u))):
+        for pay, (p, q) in ((pay_a, (d, u)), (pay_b, (u, d))):
             source = s.at[jnp.where(odd, p[0], q[0]), jnp.where(odd, p[1], q[1])]
             copies.append(pltpu.make_async_copy(source, pay.at[part], sems.at[len(copies)]))
     begin = pl.multiple_of(jnp.where(sec == 0, cy - SIDE, 0), SIDE)
@@ -161,11 +161,11 @@
         copy.wait()
 
 
-def step_velocity(s, v, b, from_b, from_a, from_s, v_out, pay_b, pay_a, pay_s, rows_ref):
+def step_velocity(s, v, b, from_a, from_b, from_s, v_out, pay_a, pay_b, pay_s, rows_ref):
     odd, sec, _ = place()
     _, cx, cy, nz = s.shape
     fw, bw = depth_weights(nz)
-    low, high = sides(odd, from_b, from_a, cy)
+    low, high = sides(odd, from_a, from_b, cy)
     fill_rows(rows_ref, STRESS_ROWS, lambda c, x: s[c, x], from_s, sec, cx, cy)
     xx = along(lambda x: s[0, x], cx, low, {-1: 0}, high, {cx: 0, cx + 1: 1})
     xy = along(lambda x: s[3, x], cx, low, {-2: 1, -1: 2}, high, {cx: 2})
@@ -184,14 +184,14 @@
         v_out[2, x] = v[2, x] + scale * (
             backward(xz, x) + backward(yz, 0) + forward_z(s[2, x], fw)
         )
-    send_sides(odd, velocity_up(cx), velocity_down(cx), pay_b, pay_a, cy, lambda c, x: v_out[c, x])
+    send_sides(odd, velocity_up(cx), velocity_down(cx), pay_a, pay_b, cy, lambda c, x: v_out[c, x])
     send_rows(sec, VELOCITY_ROWS, pay_s, lambda c, x, y: v_out[c, x, y : y + SIDE, :], cx, cy)
 
 
 def last_velocity(
-    s, v, b, from_b, from_a, from_s, ocean, marks, v_out, pay_b, pay_a, pay_s, patch, rows_ref
+    s, v, b, from_a, from_b, from_s, ocean, marks, v_out, pay_a, pay_b, pay_s, patch, rows_ref
 ):
-    step_velocity(s, v, b, from_b, from_a, from_s, v_out, pay_b, pay_a, pay_s, rows_ref)
+    step_velocity(s, v, b, from_a, from_b, from_s, v_out, pay_a, pay_b, pay_s, rows_ref)
     odd, _, _ = place()
     _, cx, cy, nz = s.shape
     first = (lax.broadcasted_iota(jnp.int32, (8, nz), 1) == 0).astype(F32)
@@ -225,11 +225,11 @@
     pay_a[base : base + SIDE, :] = jnp.where(odd, lower, upper)
 
 
-def update_stress(v, s, lam, mu, from_b, from_a, from_s, s_out, rows_ref, each=None):
+def update_stress(v, s, lam, mu, from_a, from_b, from_s, s_out, rows_ref, each=None):
     odd, sec, _ = place()
     _, cx, cy, nz = s.shape
     fw, bw = depth_weights(nz)
-    low, high = sides(odd, from_b, from_a, cy)
+    low, high = sides(odd, from_a, from_b, cy)
     fill_rows(rows_ref, VELOCITY_ROWS, lambda c, x: v[c, x], from_s, sec, cx, cy)
     vx = along(lambda x: v[0, x], cx, low, {-2: 0, -1: 1}, high, {cx: 0})
     vy = along(lambda x: v[1, x], cx, low, {-1: 2}, high, {cx: 1, cx + 1: 2})
@@ -252,15 +252,18 @@
             each(x)
 
 
-def step_stress(v, s, lam, mu, from_b, from_a, from_s, s_out, pay_b, pay_a, pay_s, rows_ref):
+def step_stress(v, s, lam, mu, from_a, from_b, from_s, s_out, pay_a, pay_b, pay_s, rows_ref):
     odd, sec, _ = place()
     _, cx, cy, nz = s.shape
-    update_stress(v, s, lam, mu, from_b, from_a, from_s, s_out, rows_ref)
-    send_sides(odd, stress_up(cx), stress_down(cx), pay_b, pay_a, cy, lambda c, x: s_out[c, x])
+    update_stress(v, s, lam, mu, from_a, from_b, from_s, s_out, rows_ref)
+    send_sides(odd, stress_up(cx), stress_down(cx), pay_a, pay_b, cy, lambda c, x: s_out[c, x])
     send_rows(sec, STRESS_ROWS, pay_s, lambda c, x, y: s_out[c, x, y : y + SIDE, :], cx, cy)
 
 
-def last_stress(v, s, lam, mu, from_b, from_a, from_s, v_out, s_out, rows_ref, made, sems):
+def last_stress(
+    v, s, lam, mu, from_a, from_b, from_s, v_out, s_out, done, rows_ref, made, sems
+):
+    done[...] = jnp.zeros(done.shape, F32)
     cx = s.shape[1]
     copies = [pltpu.make_async_copy(v, v_out, sems.at[cx])]
     copies[0].start()
@@ -270,12 +273,14 @@
         copy.start()
         copies.append(copy)
 
-    update_stress(v, s, lam, mu, from_b, from_a, from_s, made, rows_ref, each)
+    update_stress(v, s, lam, mu, from_a, from_b, from_s, made, rows_ref, each)
     for copy in copies:
         copy.wait()
 
 
-def ocean_steps(start, from_b, from_a, ocean, marks, patches, ocean_out, ocean_ref, marks_ref):
+def ocean_steps(
+    start, from_a, from_b, ocean, marks, patches, _, ocean_out, ocean_ref, marks_ref
+):
     odd, sec, tile = place()
     count = lax.axis_size("tile")
     fields, rows, columns = ocean.shape
@@ -344,31 +349,32 @@
 ANY = pl.BlockSpec(memory_space=pl.ANY)
 
 
-def call(body, name, outs, scratch, operands, weight=1, ins=VMEM, where=VMEM):
+def call(body, name, outs, scratch, operands, weight=1, ins=VMEM, where=VMEM, grant=32):
     shapes = [jax.ShapeDtypeStruct(o, F32) for o in outs]
     moved = sum(o.size for o in operands) * 4 + sum(o.size for o in shapes) * 4
     return pl.pallas_call(
         body,
         name=name,
         out_shape=shapes,
-        in_specs=[ins] * len(operands),
-        out_specs=[where] * len(outs),
+        in_specs=ins if isinstance(ins, list) else [ins] * len(operands),
+        out_specs=where if isinstance(where, list) else [where] * len(outs),
         scratch_shapes=scratch,
-        compiler_params=pltpu.CompilerParams(vmem_limit_bytes=32 * 1024 * 1024),
+        compiler_params=pltpu.CompilerParams(vmem_limit_bytes=grant * 1024 * 1024),
         cost_estimate=pl.CostEstimate(
             flops=moved, bytes_accessed=moved * weight, transcendentals=0
         ),
     )(*operands)
 
 
-def exchange(pay_b, pay_a, count):
+def exchange(pay_a, pay_b, count):
     def swap(pay, first):
         pairs = []
         for i in range(first, count - 1, 2):
             pairs += [(i, i + 1), (i + 1, i)]
         return lax.ppermute(pay, "tile", pairs)
 
-    return swap(pay_b, 1), swap(pay_a, 0)
+    from_a = swap(pay_a, 0)
+    return from_a, swap(pay_b, 1)
 
 
 def across(pay):
@@ -395,15 +401,16 @@
     strip = (3 * cx * SIDE, nz)
     halo_rows = pltpu.VMEM((3, cx, cy + 2 * SIDE, nz), F32)
 
-    pay_b, pay_a, pay_s = call(
+    pay_a, pay_b, pay_s = call(
         first_sides,
         "first_sides",
         [side, side, (3, cx, SIDE, nz)],
         [pltpu.SemaphoreType.DMA((2 * EDGE + 3,))],
         [stresses],
         ins=ANY,
-    )
-    from_b, from_a = exchange(pay_b, pay_a, count)
+        grant=60,
+    )
+    from_a, from_b = exchange(pay_a, pay_b, count)
     from_s = across(pay_s.reshape(strip))
 
     fields = jnp.concatenate([ocean_state, depth_map[None], wet_mask.astype(F32)[None]])
@@ -416,44 +423,44 @@
         jnp.where(lane == 1, intersection_share[:, None], 0.0),
     )
 
-    velocity, pay_b, pay_a, pay_s = call(
+    velocity, pay_a, pay_b, pay_s = call(
         step_velocity,
         "velocity_step",
         [velocity.shape, side, side, strip],
         [halo_rows],
-        [stresses, velocity, buoyancy, from_b, from_a, from_s],
-    )
-    from_b, from_a = exchange(pay_b, pay_a, count)
+        [stresses, velocity, buoyancy, from_a, from_b, from_s],
+    )
+    from_a, from_b = exchange(pay_a, pay_b, count)
     from_s = across(pay_s)
-    stresses, pay_b, pay_a, pay_s = call(
+    stresses, pay_a, pay_b, pay_s = call(
         step_stress,
         "stress_step",
         [stresses.shape, side, side, strip],
         [halo_rows],
-        [velocity, stresses, lame_first, shear_mod, from_b, from_a, from_s],
-    )
-    from_b, from_a = exchange(pay_b, pay_a, count)
+        [velocity, stresses, lame_first, shear_mod, from_a, from_b, from_s],
+    )
+    from_a, from_b = exchange(pay_a, pay_b, count)
     from_s = across(pay_s)
     long_side = (EDGE * cy + ocean.shape[2] // 128 * PACK + SIDE, nz)
     pieces = cx * cy // 128
-    velocity, pay_b, pay_a, pay_s, patch = call(
+    velocity, pay_a, pay_b, pay_s, patch = call(
         last_velocity,
         "velocity_last",
         [velocity.shape, long_side, long_side, strip, (2 * count * pieces, 128)],
         [halo_rows],
-        [stresses, velocity, buoyancy, from_b, from_a, from_s, ocean, marks],
-    )
-    from_b, from_a = exchange(pay_b, pay_a, count)
+        [stresses, velocity, buoyancy, from_a, from_b, from_s, ocean, marks],
+    )
+    from_a, from_b = exchange(pay_a, pay_b, count)
     from_s = across(pay_s)
     patches = lax.all_to_all(patch.reshape(2 * count, pieces, 128), ("sec", "tile"), 0, 0)
-    velocity, stresses = call(
+    velocity, stresses, done = call(
         last_stress,
         "stress_last",
-        [velocity.shape, stresses.shape],
+        [velocity.shape, stresses.shape, (8, 128)],
         [halo_rows, pltpu.VMEM(stresses.shape, F32), pltpu.SemaphoreType.DMA((cx + 1,))],
-        [velocity, stresses, lame_first, shear_mod, from_b, from_a, from_s],
+        [velocity, stresses, lame_first, shear_mod, from_a, from_b, from_s],
         weight=8,
-        where=ANY,
+        where=[ANY, ANY, VMEM],
     )
     (ocean_state,) = call(
         functools.partial(ocean_steps, EDGE * cy),
@@ -463,7 +470,7 @@
             pltpu.VMEM((ocean.shape[0], rows + 2 * SIDE, ocean.shape[2]), F32),
             pltpu.VMEM((rows + 2 * SIDE, 128), F32),
         ],
-        [from_b, from_a, ocean, marks, patches.reshape(-1, 128)],
+        [from_a, from_b, ocean, marks, patches.reshape(-1, 128), done],
     )
     return velocity, stresses, ocean_state
 

time: 62.2 us -> 55.5 us (0.89)
  waiting for transfers between devices: 25.5 us -> 13.6 us
  starting transfers between devices: 26.5 us -> 31.5 us
  Pallas kernels: 5.1 us -> 6.38 us
  local copies, waits for them, and re-layouts: 1.97 us -> 0.84 us
    ppermute x8, waiting for transfers between devices: 16.7 us -> 6.02 us  [swap(): return lax.ppermute(pay, 'tile', pairs)]
    ppermute x8, starting transfers between devices: 18.1 us -> 22.2 us  [swap(): return lax.ppermute(pay, 'tile', pairs)]
    all_to_all x1, waiting for transfers between devices: 6.89 us -> 4.67 us  [shards(): lax.all_to_all(patch.reshape(2 * count, pieces, 128), ('sec', 'tile'), 0, 0)]
    pallas_call x6, Pallas kernels: 5.1 us -> 6.38 us  [call(): pl.pallas_call(body, name=name, out_shape=shapes, in_specs=ins if isinsta...]
    unnamed x20 -> x18, local copies, waits for them, and re-layouts: 1.97 us -> 0.84 us
    ppermute x5, waiting for transfers between devices: 1.95 us -> 2.93 us  [across(): return lax.ppermute(pay, 'sec', [(0, 1), (1, 0)])]
    all_to_all x1, starting transfers between devices: 6.9 us -> 7.88 us  [shards(): lax.all_to_all(patch.reshape(2 * count, pieces, 128), ('sec', 'tile'), 0, 0)]
  transfers between devices with their start and end apart: 14 -> 14, of which waited for: 6 -> 7; matrix products, arithmetic and copies ran while one was open for 3% -> 4% of each run, Pallas kernels for 3% -> 3%
where the time goes in v3:
time: 55.5 us; the launch traced here: 55.1 us
  starting transfers between devices  31.5 us (57%)
  waiting for transfers between devices  13.6 us (25%)
  Pallas kernels  6.38 us (11%)
  other arithmetic  1.98 us (4%)
  local copies, waits for them, and re-layouts  0.84 us (2%)
  between operations  0.84 us (2%)
    ppermute x8, starting transfers between devices, swap(): return lax.ppermute(pay, 'tile', pairs)  22.2 us
    all_to_all x1, starting transfers between devices, shards(): lax.all_to_all(patch.reshape(2 * count, pieces, 128), ('sec', 'tile'), 0, 0)  7.88 us
    pallas_call x6, Pallas kernels, call(): pl.pallas_call(body, name=name, out_shape=shapes, in_specs=ins if isinsta...  6.38 us
    ppermute x8, waiting for transfers between devices, swap(): return lax.ppermute(pay, 'tile', pairs)  6.02 us
    all_to_all x1, waiting for transfers between devices, shards(): lax.all_to_all(patch.reshape(2 * count, pieces, 128), ('sec', 'tile'), 0, 0)  4.67 us
    ppermute x5, waiting for transfers between devices, across(): return lax.ppermute(pay, 'sec', [(0, 1), (1, 0)])  2.93 us
    ppermute x5, starting transfers between devices, across(): return lax.ppermute(pay, 'sec', [(0, 1), (1, 0)])  1.46 us
  transfers between devices with their start and end apart: 14, of which 7 were waited for; matrix products, arithmetic and copies ran while one was open for 4% of the time, Pallas kernels for 3%

profile of v3, /device:TPU:0, one launch (start us, length us, event | category | flops | bytes accessed | tf_op | source)
XLA Modules:
  0.0 55.1 jit_solution(4700591492948747555)
XLA Ops:
  0.6 1.8 %first_sides.1 = (f32[320,128]{1,0:T(8,128)}, f32[320,128]{1,0:T(8,128)}, f32[3,4,8,128]{3,2,1,0:T(8,128)}) custom-call(f32[6,4,64,128]{3,2,1,0:T(8,128)} %s.5), custom_call_target="tpu_custom_call" | custom-call | flops 1163264 | bytes 1163264 | tf_op jit(solution)/shard_map/first_sides/pallas_call | solution.py:355
  2.5 0.5 collective-permute-start.2
  3.0 2.6 %collective-permute-start = (f32[320,128]{1,0:T(8,128)}, f32[320,128]{1,0:T(8,128)S(1)}, u32[]{:S(2)}, u32[]{:S(2)}) collective-permute-start(f32[320,128]{1,0:T(8,128)} %get-tuple-element.22), channel_id=1, source_target_pairs={{0,1},{1,0},{2,3},{3,2},{4,5},{5,4},{6,7},{7,6},{8,9},{9,8},{10,11... | collective-permute-start | bytes 491528 | tf_op jit(solution)/shard_map/ppermute | solution.py:374
  5.6 0.8 %collective-permute-start.1 = (f32[320,128]{1,0:T(8,128)}, f32[320,128]{1,0:T(8,128)S(1)}, u32[]{:S(2)}, u32[]{:S(2)}) collective-permute-start(f32[320,128]{1,0:T(8,128)} %get-tuple-element.23), channel_id=1, source_target_pairs={{1,2},{2,1},{3,4},{4,3},{5,6},{6,5},{7,8},{8,7},{9,10},{10,9},{11,... | collective-permute-start | bytes 491528 | tf_op jit(solution)/shard_map/ppermute | solution.py:374
  6.4 0.8 %convert_bitcast_fusion = f32[1,64,256]{2,1,0:T(8,128)S(1)} fusion(s32[64,256]{1,0:T(8,128)} %param.17), kind=kLoop, calls=%fused_computation.3 | loop fusion | flops 16384 | bytes 131072 | tf_op jit(solution)/shard_map/broadcast_in_dim | solution.py:416
  7.2 1.0 %pad_maximum_fusion.1 = f32[5,64,256]{2,1,0:T(8,128)S(1)} fusion(f32[1,64,256]{2,1,0:T(8,128)S(1)} %convert_bitcast_fusion, f32[1,64,256]{2,1,0:T(8,128)S(1)} %bitcast.7, f32[3,64,256]{2,1,0:T(8,128)} %param.15), kind=kLoop, calls=%fused_computation.1 | loop fusion | flops 163840 | bytes 655360 | tf_op jit(solution)/shard_map/concatenate | solution.py:416
  8.2 2.3 %collective-permute-done.from_a = f32[320,128]{1,0:T(8,128)S(1)} collective-permute-done((f32[320,128]{1,0:T(8,128)}, f32[320,128]{1,0:T(8,128)S(1)}, u32[]{:S(2)}, u32[]{:S(2)}) %collective-permute-start) | collective-permute-done | bytes 163872 | tf_op jit(solution)/shard_map/ppermute | solution.py:374
  10.6 0.4 velocity_step.1
  11.0 6.3 %collective-permute-start.3 = (f32[320,128]{1,0:T(8,128)S(1)}, f32[320,128]{1,0:T(8,128)S(1)}, u32[]{:S(2)}, u32[]{:S(2)}) collective-permute-start(f32[320,128]{1,0:T(8,128)S(1)} %get-tuple-element.26), channel_id=1, source_target_pairs={{0,1},{1,0},{2,3},{3,2},{4,5},{5,4},{6,7},{7,6},{8,9},{9,8},{10,11... | collective-permute-start | bytes 491528 | tf_op jit(solution)/shard_map/ppermute | solution.py:374
  17.3 0.8 %collective-permute-start.4 = (f32[320,128]{1,0:T(8,128)S(1)}, f32[320,128]{1,0:T(8,128)S(1)}, u32[]{:S(2)}, u32[]{:S(2)}) collective-permute-start(f32[320,128]{1,0:T(8,128)S(1)} %get-tuple-element.27), channel_id=1, source_target_pairs={{1,2},{2,1},{3,4},{4,3},{5,6},{6,5},{7,8},{8,7},{9,10},{10,9},{11,... | collective-permute-start | bytes 491528 | tf_op jit(solution)/shard_map/ppermute | solution.py:374
  18.1 0.1 collective-permute-start.9
  18.2 0.5 collective-permute-start.5
  18.7 0.2 copy-done.8
  18.9 0.8 %collective-permute-done.5.from_s = f32[96,128]{1,0:T(8,128)S(1)} collective-permute-done((f32[96,128]{1,0:T(8,128)S(1)}, f32[96,128]{1,0:T(8,128)S(1)}, u32[]{:S(2)}, u32[]{:S(2)}) %collective-permute-start.5) | collective-permute-done | bytes 49184 | tf_op jit(solution)/shard_map/ppermute | solution.py:381
  19.7 1.7 %collective-permute-done.3.from_a = f32[320,128]{1,0:T(8,128)S(1)} collective-permute-done((f32[320,128]{1,0:T(8,128)S(1)}, f32[320,128]{1,0:T(8,128)S(1)}, u32[]{:S(2)}, u32[]{:S(2)}) %collective-permute-start.3) | collective-permute-done | bytes 163872 | tf_op jit(solution)/shard_map/ppermute | solution.py:374
  21.4 0.5 stress_step.1
  21.9 5.5 %collective-permute-start.6 = (f32[320,128]{1,0:T(8,128)S(1)}, f32[320,128]{1,0:T(8,128)S(1)}, u32[]{:S(2)}, u32[]{:S(2)}) collective-permute-start(f32[320,128]{1,0:T(8,128)S(1)} %get-tuple-element.30), channel_id=1, source_target_pairs={{0,1},{1,0},{2,3},{3,2},{4,5},{5,4},{6,7},{7,6},{8,9},{9,8},{10,11... | collective-permute-start | bytes 491528 | tf_op jit(solution)/shard_map/ppermute | solution.py:374
  27.4 0.7 %collective-permute-start.7 = (f32[320,128]{1,0:T(8,128)S(1)}, f32[320,128]{1,0:T(8,128)S(1)}, u32[]{:S(2)}, u32[]{:S(2)}) collective-permute-start(f32[320,128]{1,0:T(8,128)S(1)} %get-tuple-element.31), channel_id=1, source_target_pairs={{1,2},{2,1},{3,4},{4,3},{5,6},{6,5},{7,8},{8,7},{9,10},{10,9},{11,... | collective-permute-start | bytes 491528 | tf_op jit(solution)/shard_map/ppermute | solution.py:374
  28.1 0.6 %copy-done.7 = f32[64]{0:T(128)S(1)} copy-done((f32[64]{0:T(128)S(1)}, f32[64]{0:T(128)}, u32[]{:S(2)}) %copy-start.7) | copy-done | bytes 280
  28.8 0.1 select_select_fusion.marks
  28.8 0.1 collective-permute-start.8
  29.0 1.2 %collective-permute-done.8.from_s = f32[96,128]{1,0:T(8,128)S(1)} collective-permute-done((f32[96,128]{1,0:T(8,128)S(1)}, f32[96,128]{1,0:T(8,128)S(1)}, u32[]{:S(2)}, u32[]{:S(2)}) %collective-permute-start.8) | collective-permute-done | bytes 49184 | tf_op jit(solution)/shard_map/ppermute | solution.py:381
  30.1 2.0 %collective-permute-done.6.from_a = f32[320,128]{1,0:T(8,128)S(1)} collective-permute-done((f32[320,128]{1,0:T(8,128)S(1)}, f32[320,128]{1,0:T(8,128)S(1)}, u32[]{:S(2)}, u32[]{:S(2)}) %collective-permute-start.6) | collective-permute-done | bytes 163872 | tf_op jit(solution)/shard_map/ppermute | solution.py:374
  32.2 1.1 %velocity_last.1 = (f32[3,4,64,128]{3,2,1,0:T(8,128)S(1)}, f32[376,128]{1,0:T(8,128)S(1)}, f32[376,128]{1,0:T(8,128)S(1)}, f32[96,128]{1,0:T(8,128)S(1)}, f32[64,128]{1,0:T(8,128)}) custom-call(f32[6,4,64,128]{3,2,1,0:T(8,128)S(1)} %get-tuple-element.29.s, f32[3,4,64,128]{3,2,1,0:T(8,128)S(1)} %get-tuple-element.25.v, f32[4,64,128]{2,1,0:T(8,128)S(1)} %copy-done.3, ...), custom_call_target="tpu_custom_call" | custom-call | flops 3072000 | bytes 3072000 | tf_op jit(solution)/shard_map/velocity_last/pallas_call | solution.py:355
  33.3 4.9 %collective-permute-start.10 = (f32[376,128]{1,0:T(8,128)S(1)}, f32[376,128]{1,0:T(8,128)S(1)}, u32[]{:S(2)}, u32[]{:S(2)}) collective-permute-start(f32[376,128]{1,0:T(8,128)S(1)} %get-tuple-element.34), channel_id=1, source_target_pairs={{0,1},{1,0},{2,3},{3,2},{4,5},{5,4},{6,7},{7,6},{8,9},{9,8},{10,11... | collective-permute-start | bytes 577544 | tf_op jit(solution)/shard_map/ppermute | solution.py:374
  38.1 0.7 %collective-permute-start.11 = (f32[376,128]{1,0:T(8,128)S(1)}, f32[376,128]{1,0:T(8,128)S(1)}, u32[]{:S(2)}, u32[]{:S(2)}) collective-permute-start(f32[376,128]{1,0:T(8,128)S(1)} %get-tuple-element.35), channel_id=1, source_target_pairs={{1,2},{2,1},{3,4},{4,3},{5,6},{6,5},{7,8},{8,7},{9,10},{10,9},{11,... | collective-permute-start | bytes 577544 | tf_op jit(solution)/shard_map/ppermute | solution.py:374
  38.8 7.9 %all-to-all-start = ((f32[32,2,128]{2,1,0:T(2,128)}), f32[32,2,128]{2,1,0:T(2,128)S(1)}, u32[]{:S(2)}, u32[]{:S(2)}) async-start(f32[32,2,128]{2,1,0:T(2,128)} %bitcast.3), calls=%async_computation | async-start | bytes 65536 | tf_op jit(solution)/shard_map/all_to_all | solution.py:455
  46.7 0.3 collective-permute-start.12
  47.0 1.0 %collective-permute-done.12.from_s = f32[96,128]{1,0:T(8,128)S(1)} collective-permute-done((f32[96,128]{1,0:T(8,128)S(1)}, f32[96,128]{1,0:T(8,128)S(1)}, u32[]{:S(2)}, u32[]{:S(2)}) %collective-permute-start.12) | collective-permute-done | bytes 49184 | tf_op jit(solution)/shard_map/ppermute | solution.py:381
  48.0 1.2 %stress_last.1 = (f32[3,4,64,128]{3,2,1,0:T(8,128)}, f32[6,4,64,128]{3,2,1,0:T(8,128)}, f32[8,128]{1,0:T(8,128)S(1)}) custom-call(f32[3,4,64,128]{3,2,1,0:T(8,128)S(1)} %get-tuple-element.33.v, f32[6,4,64,128]{3,2,1,0:T(8,128)S(1)} %get-tuple-element.29.s, f32[4,64,128]{2,1,0:T(8,128)S(1)} %copy-done.1, f32[4,64,128]{2,1,0:T(8,128)S(1)} %copy-done.2, ...), custom_call_target="tpu_custom_call" | custom-call | flops 3059712 | bytes 24477696 | tf_op jit(solution)/shard_map/stress_last/pallas_call | solution.py:355
  49.2 4.7 %all-to-all-done = f32[32,2,128]{2,1,0:T(2,128)S(1)} async-done(((f32[32,2,128]{2,1,0:T(2,128)}), f32[32,2,128]{2,1,0:T(2,128)S(1)}, u32[]{:S(2)}, u32[]{:S(2)}) %all-to-all-start) | async-done | bytes 32800 | tf_op jit(solution)/shard_map/all_to_all | solution.py:455
  53.9 1.3 %ocean_steps.1 = f32[3,64,256]{2,1,0:T(8,128)} custom-call(f32[376,128]{1,0:T(8,128)S(1)} %collective-permute-done.10.from_a, f32[376,128]{1,0:T(8,128)S(1)} %collective-permute-done.11.from_b, f32[5,64,384]{2,1,0:T(8,128)S(1)} %pad_maximum_fusion.ocean, f32[64,128]{1,0:T(8,128)S(1)} %select_select_fusion.marks, f32[64,128]{1,0:T(8,128)S(1)} %bitcast.6, ...), custom_call_target="tpu_custom_call" | custom-call | flops 1142784 | bytes 1142784 | tf_op jit(solution)/shard_map/ocean_steps/pallas_call | solution.py:355
  (27 shorter events, 0.1 us)
Async XLA Ops:
  0.6 9.9 %copy-start = (f32[6,4,64,128]{3,2,1,0:T(8,128)S(1)}, f32[6,4,64,128]{3,2,1,0:T(8,128)}, u32[]{:S(2)}) copy-start(f32[6,4,64,128]{3,2,1,0:T(8,128)} %s.5) | copy-start | bytes 2359300
  2.5 5.7 %collective-permute-start.2 = (f32[96,128]{1,0:T(8,128)}, f32[96,128]{1,0:T(8,128)S(1)}, u32[]{:S(2)}, u32[]{:S(2)}) collective-permute-start(f32[96,128]{1,0:T(8,128)} %bitcast.9), channel_id=1, source_target_pairs={{0,16},{16,0},{1,17},{17,1},{2,18},{18,2},{3,19},{19,3},{4,20},{20... | collective-permute-start | bytes 147464 | tf_op jit(solution)/shard_map/ppermute | solution.py:381
  3.0 7.6 %collective-permute-start = (f32[320,128]{1,0:T(8,128)}, f32[320,128]{1,0:T(8,128)S(1)}, u32[]{:S(2)}, u32[]{:S(2)}) collective-permute-start(f32[320,128]{1,0:T(8,128)} %get-tuple-element.22), channel_id=1, source_target_pairs={{0,1},{1,0},{2,3},{3,2},{4,5},{5,4},{6,7},{7,6},{8,9},{9,8},{10,11... | collective-permute-start | bytes 491528 | tf_op jit(solution)/shard_map/ppermute | solution.py:374
  5.6 1.7 %copy-start.6 = (f32[64,256]{1,0:T(8,128)S(1)}, f32[64,256]{1,0:T(8,128)}, u32[]{:S(2)}) copy-start(f32[64,256]{1,0:T(8,128)} %param.16) | copy-start | bytes 196612
  5.6 5.0 %copy-start.4 = (f32[3,4,64,128]{3,2,1,0:T(8,128)S(1)}, f32[3,4,64,128]{3,2,1,0:T(8,128)}, u32[]{:S(2)}) copy-start(f32[3,4,64,128]{3,2,1,0:T(8,128)} %v.1) | copy-start | bytes 1179652
  5.6 5.0 %collective-permute-start.1 = (f32[320,128]{1,0:T(8,128)}, f32[320,128]{1,0:T(8,128)S(1)}, u32[]{:S(2)}, u32[]{:S(2)}) collective-permute-start(f32[320,128]{1,0:T(8,128)} %get-tuple-element.23), channel_id=1, source_target_pairs={{1,2},{2,1},{3,4},{4,3},{5,6},{6,5},{7,8},{8,7},{9,10},{10,9},{11,... | collective-permute-start | bytes 491528 | tf_op jit(solution)/shard_map/ppermute | solution.py:374
  7.2 3.4 %copy-start.3 = (f32[4,64,128]{2,1,0:T(8,128)S(1)}, f32[4,64,128]{2,1,0:T(8,128)}, u32[]{:S(2)}) copy-start(f32[4,64,128]{2,1,0:T(8,128)} %b.3) | copy-start | bytes 393220
  11.0 10.3 %collective-permute-start.3 = (f32[320,128]{1,0:T(8,128)S(1)}, f32[320,128]{1,0:T(8,128)S(1)}, u32[]{:S(2)}, u32[]{:S(2)}) collective-permute-start(f32[320,128]{1,0:T(8,128)S(1)} %get-tuple-element.26), channel_id=1, source_target_pairs={{0,1},{1,0},{2,3},{3,2},{4,5},{5,4},{6,7},{7,6},{8,9},{9,8},{10,11... | collective-permute-start | bytes 491528 | tf_op jit(solution)/shard_map/ppermute | solution.py:374
  17.3 4.0 %copy-start.1 = (f32[4,64,128]{2,1,0:T(8,128)S(1)}, f32[4,64,128]{2,1,0:T(8,128)}, u32[]{:S(2)}) copy-start(f32[4,64,128]{2,1,0:T(8,128)} %lam.3) | copy-start | bytes 393220
  17.3 4.0 %copy-start.2 = (f32[4,64,128]{2,1,0:T(8,128)S(1)}, f32[4,64,128]{2,1,0:T(8,128)}, u32[]{:S(2)}) copy-start(f32[4,64,128]{2,1,0:T(8,128)} %mu.3) | copy-start | bytes 393220
  17.3 4.0 %collective-permute-start.4 = (f32[320,128]{1,0:T(8,128)S(1)}, f32[320,128]{1,0:T(8,128)S(1)}, u32[]{:S(2)}, u32[]{:S(2)}) collective-permute-start(f32[320,128]{1,0:T(8,128)S(1)} %get-tuple-element.27), channel_id=1, source_target_pairs={{1,2},{2,1},{3,4},{4,3},{5,6},{6,5},{7,8},{8,7},{9,10},{10,9},{11,... | collective-permute-start | bytes 491528 | tf_op jit(solution)/shard_map/ppermute | solution.py:374
  18.1 10.8 %collective-permute-start.9 = (f32[5,64,128]{2,1,0:T(8,128)S(1)}, f32[5,64,128]{2,1,0:T(8,128)S(1)}, u32[]{:S(2)}, u32[]{:S(2)}) collective-permute-start(f32[5,64,128]{2,1,0:T(8,128)S(1)} %slice_select_fusion), channel_id=1, source_target_pairs={{0,16},{16,0},{1,17},{17,1},{2,18},{18,2},{3,19},{19,3},{4,20},{20... | collective-permute-start | bytes 491528 | tf_op jit(solution)/shard_map/ppermute | solution.py:381
  18.2 0.7 %copy-start.8 = (s32[64]{0:T(128)S(1)}, s32[64]{0:T(128)}, u32[]{:S(2)}) copy-start(s32[64]{0:T(128)} %param.18) | copy-start | bytes 772
  18.2 1.4 %collective-permute-start.5 = (f32[96,128]{1,0:T(8,128)S(1)}, f32[96,128]{1,0:T(8,128)S(1)}, u32[]{:S(2)}, u32[]{:S(2)}) collective-permute-start(f32[96,128]{1,0:T(8,128)S(1)} %get-tuple-element.28), channel_id=1, source_target_pairs={{0,16},{16,0},{1,17},{17,1},{2,18},{18,2},{3,19},{19,3},{4,20},{20... | collective-permute-start | bytes 147464 | tf_op jit(solution)/shard_map/ppermute | solution.py:381
  21.3 7.6 %copy-start.5 = (f32[3,64,256]{2,1,0:T(8,128)S(1)}, f32[3,64,256]{2,1,0:T(8,128)}, u32[]{:S(2)}) copy-start(f32[3,64,256]{2,1,0:T(8,128)} %param.15) | copy-start | bytes 589828
  21.9 10.3 %collective-permute-start.6 = (f32[320,128]{1,0:T(8,128)S(1)}, f32[320,128]{1,0:T(8,128)S(1)}, u32[]{:S(2)}, u32[]{:S(2)}) collective-permute-start(f32[320,128]{1,0:T(8,128)S(1)} %get-tuple-element.30), channel_id=1, source_target_pairs={{0,1},{1,0},{2,3},{3,2},{4,5},{5,4},{6,7},{7,6},{8,9},{9,8},{10,11... | collective-permute-start | bytes 491528 | tf_op jit(solution)/shard_map/ppermute | solution.py:374
  27.4 4.7 %collective-permute-start.7 = (f32[320,128]{1,0:T(8,128)S(1)}, f32[320,128]{1,0:T(8,128)S(1)}, u32[]{:S(2)}, u32[]{:S(2)}) collective-permute-start(f32[320,128]{1,0:T(8,128)S(1)} %get-tuple-element.31), channel_id=1, source_target_pairs={{1,2},{2,1},{3,4},{4,3},{5,6},{6,5},{7,8},{8,7},{9,10},{10,9},{11,... | collective-permute-start | bytes 491528 | tf_op jit(solution)/shard_map/ppermute | solution.py:374
  28.1 0.7 %copy-start.7 = (f32[64]{0:T(128)S(1)}, f32[64]{0:T(128)}, u32[]{:S(2)}) copy-start(f32[64]{0:T(128)} %param.19) | copy-start | bytes 772
  28.8 1.3 %collective-permute-start.8 = (f32[96,128]{1,0:T(8,128)S(1)}, f32[96,128]{1,0:T(8,128)S(1)}, u32[]{:S(2)}, u32[]{:S(2)}) collective-permute-start(f32[96,128]{1,0:T(8,128)S(1)} %get-tuple-element.32), channel_id=1, source_target_pairs={{0,16},{16,0},{1,17},{17,1},{2,18},{18,2},{3,19},{19,3},{4,20},{20... | collective-permute-start | bytes 147464 | tf_op jit(solution)/shard_map/ppermute | solution.py:381
  33.3 14.7 %collective-permute-start.10 = (f32[376,128]{1,0:T(8,128)S(1)}, f32[376,128]{1,0:T(8,128)S(1)}, u32[]{:S(2)}, u32[]{:S(2)}) collective-permute-start(f32[376,128]{1,0:T(8,128)S(1)} %get-tuple-element.34), channel_id=1, source_target_pairs={{0,1},{1,0},{2,3},{3,2},{4,5},{5,4},{6,7},{7,6},{8,9},{9,8},{10,11... | collective-permute-start | bytes 577544 | tf_op jit(solution)/shard_map/ppermute | solution.py:374
  38.1 9.9 %collective-permute-start.11 = (f32[376,128]{1,0:T(8,128)S(1)}, f32[376,128]{1,0:T(8,128)S(1)}, u32[]{:S(2)}, u32[]{:S(2)}) collective-permute-start(f32[376,128]{1,0:T(8,128)S(1)} %get-tuple-element.35), channel_id=1, source_target_pairs={{1,2},{2,1},{3,4},{4,3},{5,6},{6,5},{7,8},{8,7},{9,10},{10,9},{11,... | collective-permute-start | bytes 577544 | tf_op jit(solution)/shard_map/ppermute | solution.py:374
  38.8 15.1 %all-to-all-start = ((f32[32,2,128]{2,1,0:T(2,128)}), f32[32,2,128]{2,1,0:T(2,128)S(1)}, u32[]{:S(2)}, u32[]{:S(2)}) async-start(f32[32,2,128]{2,1,0:T(2,128)} %bitcast.3), calls=%async_computation | async-start | bytes 65536 | tf_op jit(solution)/shard_map/all_to_all | solution.py:455
  46.7 1.3 %collective-permute-start.12 = (f32[96,128]{1,0:T(8,128)S(1)}, f32[96,128]{1,0:T(8,128)S(1)}, u32[]{:S(2)}, u32[]{:S(2)}) collective-permute-start(f32[96,128]{1,0:T(8,128)S(1)} %get-tuple-element.36), channel_id=1, source_target_pairs={{0,16},{16,0},{1,17},{17,1},{2,18},{18,2},{3,19},{19,3},{4,20},{20... | collective-permute-start | bytes 147464 | tf_op jit(solution)/shard_map/ppermute | solution.py:381

commit v4 on v3

--- a/solution.py
+++ b/solution.py
@@ -189,40 +189,26 @@
 
 
 def last_velocity(
-    s, v, b, from_a, from_b, from_s, ocean, marks, v_out, pay_a, pay_b, pay_s, patch, rows_ref
+    s, v, b, from_a, from_b, from_s, v_out, pay_a, pay_b, pay_s, patch, rows_ref
 ):
     step_velocity(s, v, b, from_a, from_b, from_s, v_out, pay_a, pay_b, pay_s, rows_ref)
-    odd, _, _ = place()
-    _, cx, cy, nz = s.shape
-    first = (lax.broadcasted_iota(jnp.int32, (8, nz), 1) == 0).astype(F32)
-    floor = jnp.concatenate([v_out[2, x] for x in range(cx)], axis=0)
-    line = lax.dot_general(
-        first,
-        floor,
-        (((1,), (1,)), ((), ())),
-        precision=lax.Precision.HIGHEST,
-        preferred_element_type=F32,
-    )
+    _, cx, cy, _ = s.shape
     pieces = cx * cy // 128
+    row = lax.broadcasted_iota(jnp.int32, (cy, 128), 0)
+    lane = lax.broadcasted_iota(jnp.int32, (cy, 128), 1)
+    lines = []
+    for x in range(cx):
+        here = lane == row + x * cy % 128
+        column = jnp.broadcast_to(v_out[2, x, :, 0:1], (cy, 128))
+        lines.append(jnp.sum(jnp.where(here, column, 0.0), axis=0, keepdims=True))
+    per = cx // pieces
+    lines = [sum(lines[k * per + 1 : (k + 1) * per], lines[k * per]) for k in range(pieces)]
     turn = lax.rem(lax.broadcasted_iota(jnp.int32, (8, 128), 0), pieces)
-    tiled = line[:, 0:128]
+    tiled = jnp.broadcast_to(lines[0], (8, 128))
     for k in range(1, pieces):
-        tiled = jnp.where(turn == k, line[:, k * 128 : (k + 1) * 128], tiled)
+        tiled = jnp.where(turn == k, lines[k], tiled)
     for k in range(0, patch.shape[0], 8):
         patch[k : k + 8, :] = tiled
-    fields, rows, columns = ocean.shape
-    base = EDGE * cy
-    for k in range(columns // 128):
-        lanes = slice(k * 128, (k + 1) * 128)
-        for f in range(fields):
-            n = DEEP[f]
-            upper, lower = ocean[f, rows - n : rows, lanes], ocean[f, 0:n, lanes]
-            pay_b[base : base + n, :] = jnp.where(odd, upper, lower)
-            pay_a[base : base + n, :] = jnp.where(odd, lower, upper)
-            base += n
-    upper, lower = marks[rows - SIDE : rows, :], marks[0:SIDE, :]
-    pay_b[base : base + SIDE, :] = jnp.where(odd, upper, lower)
-    pay_a[base : base + SIDE, :] = jnp.where(odd, lower, upper)
 
 
 def update_stress(v, s, lam, mu, from_a, from_b, from_s, s_out, rows_ref, each=None):
@@ -252,18 +238,32 @@
             each(x)
 
 
-def step_stress(v, s, lam, mu, from_a, from_b, from_s, s_out, pay_a, pay_b, pay_s, rows_ref):
+def step_stress(
+    v, s, lam, mu, from_a, from_b, from_s, ocean, marks, s_out, pay_a, pay_b, pay_s, rows_ref
+):
     odd, sec, _ = place()
     _, cx, cy, nz = s.shape
     update_stress(v, s, lam, mu, from_a, from_b, from_s, s_out, rows_ref)
     send_sides(odd, stress_up(cx), stress_down(cx), pay_a, pay_b, cy, lambda c, x: s_out[c, x])
     send_rows(sec, STRESS_ROWS, pay_s, lambda c, x, y: s_out[c, x, y : y + SIDE, :], cx, cy)
+    fields, rows, columns = ocean.shape
+    base = EDGE * cy
+    for k in range(columns // 128):
+        lanes = slice(k * 128, (k + 1) * 128)
+        for f in range(fields):
+            n = DEEP[f]
+            upper, lower = ocean[f, rows - n : rows, lanes], ocean[f, 0:n, lanes]
+            pay_b[base : base + n, :] = jnp.where(odd, upper, lower)
+            pay_a[base : base + n, :] = jnp.where(odd, lower, upper)
+            base += n
+    upper, lower = marks[rows - SIDE : rows, :], marks[0:SIDE, :]
+    pay_b[base : base + SIDE, :] = jnp.where(odd, upper, lower)
+    pay_a[base : base + SIDE, :] = jnp.where(odd, lower, upper)
 
 
 def last_stress(
-    v, s, lam, mu, from_a, from_b, from_s, v_out, s_out, done, rows_ref, made, sems
+    v, s, lam, mu, from_a, from_b, from_s, _, v_out, s_out, rows_ref, made, sems
 ):
-    done[...] = jnp.zeros(done.shape, F32)
     cx = s.shape[1]
     copies = [pltpu.make_async_copy(v, v_out, sems.at[cx])]
     copies[0].start()
@@ -279,8 +279,9 @@
 
 
 def ocean_steps(
-    start, from_a, from_b, ocean, marks, patches, _, ocean_out, ocean_ref, marks_ref
+    start, from_a, from_b, ocean, marks, patches, ocean_out, done, ocean_ref, marks_ref
 ):
+    done[...] = jnp.zeros(done.shape, F32)
     odd, sec, tile = place()
     count = lax.axis_size("tile")
     fields, rows, columns = ocean.shape
@@ -361,7 +362,7 @@
         scratch_shapes=scratch,
         compiler_params=pltpu.CompilerParams(vmem_limit_bytes=grant * 1024 * 1024),
         cost_estimate=pl.CostEstimate(
-            flops=moved, bytes_accessed=moved * weight, transcendentals=0
+            flops=moved * weight, bytes_accessed=moved * weight, transcendentals=0
         ),
     )(*operands)
 
@@ -432,45 +433,46 @@
     )
     from_a, from_b = exchange(pay_a, pay_b, count)
     from_s = across(pay_s)
+    long_side = (EDGE * cy + ocean.shape[2] // 128 * PACK + SIDE, nz)
     stresses, pay_a, pay_b, pay_s = call(
         step_stress,
         "stress_step",
-        [stresses.shape, side, side, strip],
+        [stresses.shape, long_side, long_side, strip],
         [halo_rows],
-        [velocity, stresses, lame_first, shear_mod, from_a, from_b, from_s],
+        [velocity, stresses, lame_first, shear_mod, from_a, from_b, from_s, ocean, marks],
     )
     from_a, from_b = exchange(pay_a, pay_b, count)
+    sea_a, sea_b = from_a, from_b
     from_s = across(pay_s)
-    long_side = (EDGE * cy + ocean.shape[2] // 128 * PACK + SIDE, nz)
     pieces = cx * cy // 128
     velocity, pay_a, pay_b, pay_s, patch = call(
         last_velocity,
         "velocity_last",
-        [velocity.shape, long_side, long_side, strip, (2 * count * pieces, 128)],
+        [velocity.shape, side, side, strip, (2 * count * pieces, 128)],
         [halo_rows],
-        [stresses, velocity, buoyancy, from_a, from_b, from_s, ocean, marks],
-    )
+        [stresses, velocity, buoyancy, from_a, from_b, from_s],
+    )
+    patches = lax.all_to_all(patch.reshape(2 * count, pieces, 128), ("sec", "tile"), 0, 0)
     from_a, from_b = exchange(pay_a, pay_b, count)
     from_s = across(pay_s)
-    patches = lax.all_to_all(patch.reshape(2 * count, pieces, 128), ("sec", "tile"), 0, 0)
-    velocity, stresses, done = call(
-        last_stress,
-        "stress_last",
-        [velocity.shape, stresses.shape, (8, 128)],
-        [halo_rows, pltpu.VMEM(stresses.shape, F32), pltpu.SemaphoreType.DMA((cx + 1,))],
-        [velocity, stresses, lame_first, shear_mod, from_a, from_b, from_s],
-        weight=8,
-        where=[ANY, ANY, VMEM],
-    )
-    (ocean_state,) = call(
+    ocean_state, done = call(
         functools.partial(ocean_steps, EDGE * cy),
         "ocean_steps",
-        [ocean_state.shape],
+        [ocean_state.shape, (8, 128)],
         [
             pltpu.VMEM((ocean.shape[0], rows + 2 * SIDE, ocean.shape[2]), F32),
             pltpu.VMEM((rows + 2 * SIDE, 128), F32),
         ],
-        [from_a, from_b, ocean, marks, patches.reshape(-1, 128), done],
+        [sea_a, sea_b, ocean, marks, patches.reshape(-1, 128)],
+        weight=2000,
+    )
+    velocity, stresses = call(
+        last_stress,
+        "stress_last",
+        [velocity.shape, stresses.shape],
+        [halo_rows, pltpu.VMEM(stresses.shape, F32), pltpu.SemaphoreType.DMA((cx + 1,))],
+        [velocity, stresses, lame_first, shear_mod, from_a, from_b, from_s, done],
+        where=ANY,
     )
     return velocity, stresses, ocean_state
 

time: 55.5 us -> 53 us (0.955)
  the two profiles are of different devices: /device:TPU:0 before, /device:TPU:8 now
where the time goes in v4:
time: 53 us; the launch traced here: 52.7 us
  starting transfers between devices  21.9 us (41%)
  waiting for transfers between devices  21.4 us (40%)
  Pallas kernels  6.37 us (12%)
  local copies, waits for them, and re-layouts  2.01 us (4%)
  between operations  0.9 us (2%)
    ppermute x8, waiting for transfers between devices, swap(): return lax.ppermute(pay, 'tile', pairs)  17.3 us
    ppermute x8, starting transfers between devices, swap(): return lax.ppermute(pay, 'tile', pairs)  17 us
    pallas_call x6, Pallas kernels, call(): pl.pallas_call(body, name=name, out_shape=shapes, in_specs=ins if isinsta...  6.37 us
    all_to_all x1, starting transfers between devices, shards(): lax.all_to_all(patch.reshape(2 * count, pieces, 128), ('sec', 'tile'), 0, 0)  4.47 us
    ppermute x5, waiting for transfers between devices, across(): return lax.ppermute(pay, 'sec', [(0, 1), (1, 0)])  2.96 us
    unnamed x22, local copies, waits for them, and re-layouts  2.01 us
    all_to_all x1, waiting for transfers between devices, shards(): lax.all_to_all(patch.reshape(2 * count, pieces, 128), ('sec', 'tile'), 0, 0)  1.09 us
  transfers between devices with their start and end apart: 14, of which 10 were waited for; matrix products, arithmetic and copies ran while one was open for 0% of the time, Pallas kernels for 3%

profile of v4, /device:TPU:8, one launch (start us, length us, event | category | flops | bytes accessed | tf_op | source)
XLA Modules:
  0.0 52.7 jit_solution(13730595529428414905)
XLA Ops:
  0.7 1.8 %first_sides.1 = (f32[320,128]{1,0:T(8,128)}, f32[320,128]{1,0:T(8,128)}, f32[3,4,8,128]{3,2,1,0:T(8,128)}) custom-call(f32[6,4,64,128]{3,2,1,0:T(8,128)} %s.5), custom_call_target="tpu_custom_call" | custom-call | flops 1163264 | bytes 1163264 | tf_op jit(solution)/shard_map/first_sides/pallas_call | solution.py:356
  2.5 1.6 %collective-permute-start = (f32[320,128]{1,0:T(8,128)}, f32[320,128]{1,0:T(8,128)S(1)}, u32[]{:S(2)}, u32[]{:S(2)}) collective-permute-start(f32[320,128]{1,0:T(8,128)} %get-tuple-element.23), channel_id=1, source_target_pairs={{0,1},{1,0},{2,3},{3,2},{4,5},{5,4},{6,7},{7,6},{8,9},{9,8},{10,11... | collective-permute-start | bytes 491528 | tf_op jit(solution)/shard_map/ppermute | solution.py:375
  4.1 3.3 %collective-permute-start.1 = (f32[320,128]{1,0:T(8,128)}, f32[320,128]{1,0:T(8,128)S(1)}, u32[]{:S(2)}, u32[]{:S(2)}) collective-permute-start(f32[320,128]{1,0:T(8,128)} %get-tuple-element.24), channel_id=1, source_target_pairs={{1,2},{2,1},{3,4},{4,3},{5,6},{6,5},{7,8},{8,7},{9,10},{10,9},{11,... | collective-permute-start | bytes 491528 | tf_op jit(solution)/shard_map/ppermute | solution.py:375
  7.5 0.1 collective-permute-start.6
  7.6 0.7 %copy-done.9 = f32[3,4,8,128]{3,2,1,0:T(8,128)S(1)} copy-done((f32[3,4,8,128]{3,2,1,0:T(8,128)S(1)}, f32[3,4,8,128]{3,2,1,0:T(8,128)}, u32[]{:S(2)}) %copy-start.9) | copy-done | bytes 49176
  8.3 0.6 %copy-done.10 = s32[64]{0:T(128)S(1)} copy-done((s32[64]{0:T(128)S(1)}, s32[64]{0:T(128)}, u32[]{:S(2)}) %copy-start.10) | copy-done | bytes 280
  8.9 0.6 %collective-permute-done.2.from_s = f32[96,128]{1,0:T(8,128)S(1)} collective-permute-done((f32[96,128]{1,0:T(8,128)S(1)}, f32[96,128]{1,0:T(8,128)S(1)}, u32[]{:S(2)}, u32[]{:S(2)}) %collective-permute-start.2) | collective-permute-done | bytes 49184 | tf_op jit(solution)/shard_map/ppermute | solution.py:382
  9.5 4.1 %collective-permute-done.1.from_b = f32[320,128]{1,0:T(8,128)S(1)} collective-permute-done((f32[320,128]{1,0:T(8,128)}, f32[320,128]{1,0:T(8,128)S(1)}, u32[]{:S(2)}, u32[]{:S(2)}) %collective-permute-start.1) | collective-permute-done | bytes 163872 | tf_op jit(solution)/shard_map/ppermute | solution.py:375
  13.6 0.4 velocity_step.1
  14.1 1.1 %collective-permute-start.3 = (f32[320,128]{1,0:T(8,128)S(1)}, f32[320,128]{1,0:T(8,128)S(1)}, u32[]{:S(2)}, u32[]{:S(2)}) collective-permute-start(f32[320,128]{1,0:T(8,128)S(1)} %get-tuple-element.27), channel_id=1, source_target_pairs={{0,1},{1,0},{2,3},{3,2},{4,5},{5,4},{6,7},{7,6},{8,9},{9,8},{10,11... | collective-permute-start | bytes 491528 | tf_op jit(solution)/shard_map/ppermute | solution.py:375
  15.2 2.8 %collective-permute-start.4 = (f32[320,128]{1,0:T(8,128)S(1)}, f32[320,128]{1,0:T(8,128)S(1)}, u32[]{:S(2)}, u32[]{:S(2)}) collective-permute-start(f32[320,128]{1,0:T(8,128)S(1)} %get-tuple-element.28), channel_id=1, source_target_pairs={{1,2},{2,1},{3,4},{4,3},{5,6},{6,5},{7,8},{8,7},{9,10},{10,9},{11,... | collective-permute-start | bytes 491528 | tf_op jit(solution)/shard_map/ppermute | solution.py:375
  18.0 0.6 %copy-done.8 = f32[64]{0:T(128)S(1)} copy-done((f32[64]{0:T(128)S(1)}, f32[64]{0:T(128)}, u32[]{:S(2)}) %copy-start.8) | copy-done | bytes 280
  18.7 0.1 select_select_fusion.marks
  18.8 0.1 collective-permute-start.5
  18.9 1.2 %collective-permute-done.5.from_s = f32[96,128]{1,0:T(8,128)S(1)} collective-permute-done((f32[96,128]{1,0:T(8,128)S(1)}, f32[96,128]{1,0:T(8,128)S(1)}, u32[]{:S(2)}, u32[]{:S(2)}) %collective-permute-start.5) | collective-permute-done | bytes 49184 | tf_op jit(solution)/shard_map/ppermute | solution.py:382
  20.1 0.4 collective-permute-done.3.from_a
  20.5 3.7 %collective-permute-done.4.from_b = f32[320,128]{1,0:T(8,128)S(1)} collective-permute-done((f32[320,128]{1,0:T(8,128)S(1)}, f32[320,128]{1,0:T(8,128)S(1)}, u32[]{:S(2)}, u32[]{:S(2)}) %collective-permute-start.4) | collective-permute-done | bytes 163872 | tf_op jit(solution)/shard_map/ppermute | solution.py:375
  24.2 0.5 stress_step.1
  24.8 0.3 collective-permute-start.7
  25.1 3.1 %collective-permute-start.8 = (f32[376,128]{1,0:T(8,128)S(1)}, f32[376,128]{1,0:T(8,128)S(1)}, u32[]{:S(2)}, u32[]{:S(2)}) collective-permute-start(f32[376,128]{1,0:T(8,128)S(1)} %get-tuple-element.32), channel_id=1, source_target_pairs={{1,2},{2,1},{3,4},{4,3},{5,6},{6,5},{7,8},{8,7},{9,10},{10,9},{11,... | collective-permute-start | bytes 577544 | tf_op jit(solution)/shard_map/ppermute | solution.py:375
  28.2 1.2 %collective-permute-done.9.from_s = f32[96,128]{1,0:T(8,128)S(1)} collective-permute-done((f32[96,128]{1,0:T(8,128)S(1)}, f32[96,128]{1,0:T(8,128)S(1)}, u32[]{:S(2)}, u32[]{:S(2)}) %collective-permute-start.9) | collective-permute-done | bytes 49184 | tf_op jit(solution)/shard_map/ppermute | solution.py:382
  29.5 2.8 %collective-permute-done.7.from_a = f32[376,128]{1,0:T(8,128)S(1)} collective-permute-done((f32[376,128]{1,0:T(8,128)S(1)}, f32[376,128]{1,0:T(8,128)S(1)}, u32[]{:S(2)}, u32[]{:S(2)}) %collective-permute-start.7) | collective-permute-done | bytes 192544 | tf_op jit(solution)/shard_map/ppermute | solution.py:375
  32.2 2.2 %collective-permute-done.8.from_b = f32[376,128]{1,0:T(8,128)S(1)} collective-permute-done((f32[376,128]{1,0:T(8,128)S(1)}, f32[376,128]{1,0:T(8,128)S(1)}, u32[]{:S(2)}, u32[]{:S(2)}) %collective-permute-start.8) | collective-permute-done | bytes 192544 | tf_op jit(solution)/shard_map/ppermute | solution.py:375
  34.4 1.2 %velocity_last.1 = (f32[3,4,64,128]{3,2,1,0:T(8,128)S(1)}, f32[320,128]{1,0:T(8,128)S(1)}, f32[320,128]{1,0:T(8,128)S(1)}, f32[96,128]{1,0:T(8,128)S(1)}, f32[64,128]{1,0:T(8,128)}) custom-call(f32[6,4,64,128]{3,2,1,0:T(8,128)S(1)} %get-tuple-element.30.s, f32[3,4,64,128]{3,2,1,0:T(8,128)S(1)} %get-tuple-element.26.v, f32[4,64,128]{2,1,0:T(8,128)S(1)} %copy-done.3, ...), custom_call_target="tpu_custom_call" | custom-call | flops 2547712 | bytes 2547712 | tf_op jit(solution)/shard_map/velocity_last/pallas_call | solution.py:356
  35.5 4.5 %all-to-all-start = ((f32[32,2,128]{2,1,0:T(2,128)}), f32[32,2,128]{2,1,0:T(2,128)S(1)}, u32[]{:S(2)}, u32[]{:S(2)}) async-start(f32[32,2,128]{2,1,0:T(2,128)} %bitcast.3), calls=%async_computation | async-start | bytes 65536 | tf_op jit(solution)/shard_map/all_to_all | solution.py:455
  40.0 0.2 collective-permute-start.12
  40.2 1.5 %collective-permute-start.10 = (f32[320,128]{1,0:T(8,128)S(1)}, f32[320,128]{1,0:T(8,128)S(1)}, u32[]{:S(2)}, u32[]{:S(2)}) collective-permute-start(f32[320,128]{1,0:T(8,128)S(1)} %get-tuple-element.35), channel_id=1, source_target_pairs={{0,1},{1,0},{2,3},{3,2},{4,5},{5,4},{6,7},{7,6},{8,9},{9,8},{10,11... | collective-permute-start | bytes 491528 | tf_op jit(solution)/shard_map/ppermute | solution.py:375
  41.7 3.4 %collective-permute-start.11 = (f32[320,128]{1,0:T(8,128)S(1)}, f32[320,128]{1,0:T(8,128)S(1)}, u32[]{:S(2)}, u32[]{:S(2)}) collective-permute-start(f32[320,128]{1,0:T(8,128)S(1)} %get-tuple-element.36), channel_id=1, source_target_pairs={{1,2},{2,1},{3,4},{4,3},{5,6},{6,5},{7,8},{8,7},{9,10},{10,9},{11,... | collective-permute-start | bytes 491528 | tf_op jit(solution)/shard_map/ppermute | solution.py:375
  45.1 1.1 %all-to-all-done = f32[32,2,128]{2,1,0:T(2,128)S(1)} async-done(((f32[32,2,128]{2,1,0:T(2,128)}), f32[32,2,128]{2,1,0:T(2,128)S(1)}, u32[]{:S(2)}, u32[]{:S(2)}) %all-to-all-start) | async-done | bytes 32800 | tf_op jit(solution)/shard_map/all_to_all | solution.py:455
  46.2 1.2 %ocean_steps.1 = (f32[3,64,256]{2,1,0:T(8,128)}, f32[8,128]{1,0:T(8,128)S(1)}) custom-call(f32[376,128]{1,0:T(8,128)S(1)} %collective-permute-done.7.from_a, f32[376,128]{1,0:T(8,128)S(1)} %collective-permute-done.8.from_b, f32[5,64,384]{2,1,0:T(8,128)S(1)} %pad_maximum_fusion.ocean, f32[64,128]{1,0:T(8,128)S(1)} %select_select_fusion.marks, ...), custom_call_target="tpu_custom_call" | custom-call | flops 2285568000 | bytes 2285568000 | tf_op jit(solution)/shard_map/ocean_steps/pallas_call | solution.py:356
  47.4 4.1 %collective-permute-done.11.from_b = f32[320,128]{1,0:T(8,128)S(1)} collective-permute-done((f32[320,128]{1,0:T(8,128)S(1)}, f32[320,128]{1,0:T(8,128)S(1)}, u32[]{:S(2)}, u32[]{:S(2)}) %collective-permute-start.11) | collective-permute-done | bytes 163872 | tf_op jit(solution)/shard_map/ppermute | solution.py:375
  51.6 1.2 %stress_last.1 = (f32[3,4,64,128]{3,2,1,0:T(8,128)}, f32[6,4,64,128]{3,2,1,0:T(8,128)}) custom-call(f32[3,4,64,128]{3,2,1,0:T(8,128)S(1)} %get-tuple-element.34.v, f32[6,4,64,128]{3,2,1,0:T(8,128)S(1)} %get-tuple-element.30.s, f32[4,64,128]{2,1,0:T(8,128)S(1)} %copy-done.1, f32[4,64,128]{2,1,0:T(8,128)S(1)} %copy-done.2, ...), custom_call_target="tpu_custom_call" | custom-call | flops 3002368 | bytes 3002368 | tf_op jit(solution)/shard_map/stress_last/pallas_call | solution.py:356
  (31 shorter events, 0.2 us)
Async XLA Ops:
  0.6 6.7 %copy-start.7 = (s32[64,256]{1,0:T(8,128)S(1)}, s32[64,256]{1,0:T(8,128)}, u32[]{:S(2)}) copy-start(s32[64,256]{1,0:T(8,128)} %param.17) | copy-start | bytes 196612
  0.6 6.8 %copy-start.5 = (f32[3,64,256]{2,1,0:T(8,128)S(1)}, f32[3,64,256]{2,1,0:T(8,128)}, u32[]{:S(2)}) copy-start(f32[3,64,256]{2,1,0:T(8,128)} %param.15) | copy-start | bytes 589828
  0.7 6.8 %copy-start.6 = (f32[64,256]{1,0:T(8,128)S(1)}, f32[64,256]{1,0:T(8,128)}, u32[]{:S(2)}) copy-start(f32[64,256]{1,0:T(8,128)} %param.16) | copy-start | bytes 196612
  0.7 13.0 %copy-start.4 = (f32[3,4,64,128]{3,2,1,0:T(8,128)S(1)}, f32[3,4,64,128]{3,2,1,0:T(8,128)}, u32[]{:S(2)}) copy-start(f32[3,4,64,128]{3,2,1,0:T(8,128)} %v.1) | copy-start | bytes 1179652
  2.5 11.1 %copy-start = (f32[6,4,64,128]{3,2,1,0:T(8,128)S(1)}, f32[6,4,64,128]{3,2,1,0:T(8,128)}, u32[]{:S(2)}) copy-start(f32[6,4,64,128]{3,2,1,0:T(8,128)} %s.5) | copy-start | bytes 2359300
  2.5 7.0 %collective-permute-start = (f32[320,128]{1,0:T(8,128)}, f32[320,128]{1,0:T(8,128)S(1)}, u32[]{:S(2)}, u32[]{:S(2)}) collective-permute-start(f32[320,128]{1,0:T(8,128)} %get-tuple-element.23), channel_id=1, source_target_pairs={{0,1},{1,0},{2,3},{3,2},{4,5},{5,4},{6,7},{7,6},{8,9},{9,8},{10,11... | collective-permute-start | bytes 491528 | tf_op jit(solution)/shard_map/ppermute | solution.py:375
  4.1 9.5 %collective-permute-start.1 = (f32[320,128]{1,0:T(8,128)}, f32[320,128]{1,0:T(8,128)S(1)}, u32[]{:S(2)}, u32[]{:S(2)}) collective-permute-start(f32[320,128]{1,0:T(8,128)} %get-tuple-element.24), channel_id=1, source_target_pairs={{1,2},{2,1},{3,4},{4,3},{5,6},{6,5},{7,8},{8,7},{9,10},{10,9},{11,... | collective-permute-start | bytes 491528 | tf_op jit(solution)/shard_map/ppermute | solution.py:375
  7.5 0.8 %copy-start.9 = (f32[3,4,8,128]{3,2,1,0:T(8,128)S(1)}, f32[3,4,8,128]{3,2,1,0:T(8,128)}, u32[]{:S(2)}) copy-start(f32[3,4,8,128]{3,2,1,0:T(8,128)} %get-tuple-element.25) | copy-start | bytes 147460
  7.5 6.2 %copy-start.3 = (f32[4,64,128]{2,1,0:T(8,128)S(1)}, f32[4,64,128]{2,1,0:T(8,128)}, u32[]{:S(2)}) copy-start(f32[4,64,128]{2,1,0:T(8,128)} %b.3) | copy-start | bytes 393220
  7.5 11.4 %collective-permute-start.6 = (f32[5,64,128]{2,1,0:T(8,128)S(1)}, f32[5,64,128]{2,1,0:T(8,128)S(1)}, u32[]{:S(2)}, u32[]{:S(2)}) collective-permute-start(f32[5,64,128]{2,1,0:T(8,128)S(1)} %slice_select_fusion), channel_id=1, source_target_pairs={{0,16},{16,0},{1,17},{17,1},{2,18},{18,2},{3,19},{19,3},{4,20},{20... | collective-permute-start | bytes 491528 | tf_op jit(solution)/shard_map/ppermute | solution.py:382
  8.3 0.7 %copy-start.10 = (s32[64]{0:T(128)S(1)}, s32[64]{0:T(128)}, u32[]{:S(2)}) copy-start(s32[64]{0:T(128)} %param.18) | copy-start | bytes 772
  8.3 1.2 %collective-permute-start.2 = (f32[96,128]{1,0:T(8,128)S(1)}, f32[96,128]{1,0:T(8,128)S(1)}, u32[]{:S(2)}, u32[]{:S(2)}) collective-permute-start(f32[96,128]{1,0:T(8,128)S(1)} %bitcast.9), channel_id=1, source_target_pairs={{0,16},{16,0},{1,17},{17,1},{2,18},{18,2},{3,19},{19,3},{4,20},{20... | collective-permute-start | bytes 147464 | tf_op jit(solution)/shard_map/ppermute | solution.py:382
  14.1 6.4 %collective-permute-start.3 = (f32[320,128]{1,0:T(8,128)S(1)}, f32[320,128]{1,0:T(8,128)S(1)}, u32[]{:S(2)}, u32[]{:S(2)}) collective-permute-start(f32[320,128]{1,0:T(8,128)S(1)} %get-tuple-element.27), channel_id=1, source_target_pairs={{0,1},{1,0},{2,3},{3,2},{4,5},{5,4},{6,7},{7,6},{8,9},{9,8},{10,11... | collective-permute-start | bytes 491528 | tf_op jit(solution)/shard_map/ppermute | solution.py:375
  15.2 9.0 %collective-permute-start.4 = (f32[320,128]{1,0:T(8,128)S(1)}, f32[320,128]{1,0:T(8,128)S(1)}, u32[]{:S(2)}, u32[]{:S(2)}) collective-permute-start(f32[320,128]{1,0:T(8,128)S(1)} %get-tuple-element.28), channel_id=1, source_target_pairs={{1,2},{2,1},{3,4},{4,3},{5,6},{6,5},{7,8},{8,7},{9,10},{10,9},{11,... | collective-permute-start | bytes 491528 | tf_op jit(solution)/shard_map/ppermute | solution.py:375
  18.0 0.7 %copy-start.8 = (f32[64]{0:T(128)S(1)}, f32[64]{0:T(128)}, u32[]{:S(2)}) copy-start(f32[64]{0:T(128)} %param.19) | copy-start | bytes 772
  18.8 5.5 %copy-start.1 = (f32[4,64,128]{2,1,0:T(8,128)S(1)}, f32[4,64,128]{2,1,0:T(8,128)}, u32[]{:S(2)}) copy-start(f32[4,64,128]{2,1,0:T(8,128)} %lam.3) | copy-start | bytes 393220
  18.8 5.4 %copy-start.2 = (f32[4,64,128]{2,1,0:T(8,128)S(1)}, f32[4,64,128]{2,1,0:T(8,128)}, u32[]{:S(2)}) copy-start(f32[4,64,128]{2,1,0:T(8,128)} %mu.3) | copy-start | bytes 393220
  18.8 1.3 %collective-permute-start.5 = (f32[96,128]{1,0:T(8,128)S(1)}, f32[96,128]{1,0:T(8,128)S(1)}, u32[]{:S(2)}, u32[]{:S(2)}) collective-permute-start(f32[96,128]{1,0:T(8,128)S(1)} %get-tuple-element.29), channel_id=1, source_target_pairs={{0,16},{16,0},{1,17},{17,1},{2,18},{18,2},{3,19},{19,3},{4,20},{20... | collective-permute-start | bytes 147464 | tf_op jit(solution)/shard_map/ppermute | solution.py:382
  24.8 7.5 %collective-permute-start.7 = (f32[376,128]{1,0:T(8,128)S(1)}, f32[376,128]{1,0:T(8,128)S(1)}, u32[]{:S(2)}, u32[]{:S(2)}) collective-permute-start(f32[376,128]{1,0:T(8,128)S(1)} %get-tuple-element.31), channel_id=1, source_target_pairs={{0,1},{1,0},{2,3},{3,2},{4,5},{5,4},{6,7},{7,6},{8,9},{9,8},{10,11... | collective-permute-start | bytes 577544 | tf_op jit(solution)/shard_map/ppermute | solution.py:375
  25.1 9.3 %collective-permute-start.8 = (f32[376,128]{1,0:T(8,128)S(1)}, f32[376,128]{1,0:T(8,128)S(1)}, u32[]{:S(2)}, u32[]{:S(2)}) collective-permute-start(f32[376,128]{1,0:T(8,128)S(1)} %get-tuple-element.32), channel_id=1, source_target_pairs={{1,2},{2,1},{3,4},{4,3},{5,6},{6,5},{7,8},{8,7},{9,10},{10,9},{11,... | collective-permute-start | bytes 577544 | tf_op jit(solution)/shard_map/ppermute | solution.py:375
  28.2 1.3 %collective-permute-start.9 = (f32[96,128]{1,0:T(8,128)S(1)}, f32[96,128]{1,0:T(8,128)S(1)}, u32[]{:S(2)}, u32[]{:S(2)}) collective-permute-start(f32[96,128]{1,0:T(8,128)S(1)} %get-tuple-element.33), channel_id=1, source_target_pairs={{0,16},{16,0},{1,17},{17,1},{2,18},{18,2},{3,19},{19,3},{4,20},{20... | collective-permute-start | bytes 147464 | tf_op jit(solution)/shard_map/ppermute | solution.py:382
  35.5 10.6 %all-to-all-start = ((f32[32,2,128]{2,1,0:T(2,128)}), f32[32,2,128]{2,1,0:T(2,128)S(1)}, u32[]{:S(2)}, u32[]{:S(2)}) async-start(f32[32,2,128]{2,1,0:T(2,128)} %bitcast.3), calls=%async_computation | async-start | bytes 65536 | tf_op jit(solution)/shard_map/all_to_all | solution.py:455
  40.0 7.4 %collective-permute-start.12 = (f32[96,128]{1,0:T(8,128)S(1)}, f32[96,128]{1,0:T(8,128)S(1)}, u32[]{:S(2)}, u32[]{:S(2)}) collective-permute-start(f32[96,128]{1,0:T(8,128)S(1)} %get-tuple-element.37), channel_id=1, source_target_pairs={{0,16},{16,0},{1,17},{17,1},{2,18},{18,2},{3,19},{19,3},{4,20},{20... | collective-permute-start | bytes 147464 | tf_op jit(solution)/shard_map/ppermute | solution.py:382
  40.2 7.2 %collective-permute-start.10 = (f32[320,128]{1,0:T(8,128)S(1)}, f32[320,128]{1,0:T(8,128)S(1)}, u32[]{:S(2)}, u32[]{:S(2)}) collective-permute-start(f32[320,128]{1,0:T(8,128)S(1)} %get-tuple-element.35), channel_id=1, source_target_pairs={{0,1},{1,0},{2,3},{3,2},{4,5},{5,4},{6,7},{7,6},{8,9},{9,8},{10,11... | collective-permute-start | bytes 491528 | tf_op jit(solution)/shard_map/ppermute | solution.py:375
  41.7 9.9 %collective-permute-start.11 = (f32[320,128]{1,0:T(8,128)S(1)}, f32[320,128]{1,0:T(8,128)S(1)}, u32[]{:S(2)}, u32[]{:S(2)}) collective-permute-start(f32[320,128]{1,0:T(8,128)S(1)} %get-tuple-element.36), channel_id=1, source_target_pairs={{1,2},{2,1},{3,4},{4,3},{5,6},{6,5},{7,8},{8,7},{9,10},{10,9},{11,... | collective-permute-start | bytes 491528 | tf_op jit(solution)/shard_map/ppermute | solution.py:375

commit v5 on v0

v5 whole, which is shorter than its diff:
```python
import functools

import jax
import jax.numpy as jnp
from jax import lax
from jax.experimental import pallas as pl
from jax.experimental.pallas import tpu as pltpu
from jax.sharding import PartitionSpec as P

REACH = 2
NEAR = 9.0 / 8.0
FAR = 1.0 / 24.0
DT = 0.15
ODT = 0.3
F32 = jnp.float32
SIDE = 8
WINDOW = 8
DEEP = (4, 3, 3, 3, 3)
PACK = sum(DEEP)
NEEDED = {"s": 5, "v": 3, "b": 3}
LAST_NEEDED = 2
LAYERS = 9
STRESS_X = ((0, True), (3, False), (4, False))


def depth_weights(width):
    lane = lax.broadcasted_iota(jnp.int32, (1, width), 1)

    def weight(value, first, last):
        return jnp.where((lane >= first) & (lane < last), value, 0.0).astype(F32)

    forward = (weight(NEAR, 0, width - 1), weight(-FAR, 0, width - 2), weight(FAR, 1, width))
    backward = (weight(-NEAR, 1, width), weight(-FAR, 0, width - 1), weight(FAR, 2, width))
    return forward, backward


def forward_z(f, weights):
    near, far, behind = weights
    n = f.shape[-1]
    return (
        pltpu.roll(f, n - 1, 1) * near
        - NEAR * f
        + pltpu.roll(f, n - 2, 1) * far
        + pltpu.roll(f, 1, 1) * behind
    )


def backward_z(f, weights):
    near, far, behind = weights
    n = f.shape[-1]
    return (
        NEAR * f
        + pltpu.roll(f, 1, 1) * near
        + pltpu.roll(f, n - 1, 1) * far
        + pltpu.roll(f, 2, 1) * behind
    )


def forward(at, i):
    return NEAR * (at(i + 1) - at(i)) - FAR * (at(i + 2) - at(i - 1))


def backward(at, i):
    return NEAR * (at(i) - at(i - 1)) - FAR * (at(i + 1) - at(i - 2))


def place():
    tile, sec = lax.axis_index("tile"), lax.axis_index("sec")
    return lax.rem(tile, 2) == 1, sec, tile


def along_x(ahead, i, get):
    if ahead:
        taps = ((i + 1, NEAR), (i, -NEAR), (i + 2, -FAR), (i - 1, FAR))
    else:
        taps = ((i, NEAR), (i - 1, -NEAR), (i + 1, -FAR), (i - 2, FAR))
    total = None
    for j, weight in taps:
        layer = get(j)
        if layer is not None:
            total = weight * layer if total is None else total + weight * layer
    return total


def up_layers(cx):
    stress = [(0, cx - 1), (3, cx - 2), (3, cx - 1), (4, cx - 2), (4, cx - 1)]
    return stress, [(0, cx - 2), (0, cx - 1), (1, cx - 1), (2, cx - 1)]


def down_layers(cx):
    return [(0, 0), (0, 1), (3, 0), (4, 0)], [(0, 0), (1, 0), (1, 1), (2, 0), (2, 1)]


def halo_stress(cx):
    low = [(c, x - cx) for c, x in up_layers(cx)[0]]
    return {key: k for k, key in enumerate(low + [(c, x + cx) for c, x in down_layers(cx)[0]])}


def halo_velocity(cx):
    low = [(c, x - cx) for c, x in up_layers(cx)[1]]
    return {key: k for k, key in enumerate(low + [(c, x + cx) for c, x in down_layers(cx)[1]])}


def strip(ref, k, x, cx):
    return ref[(k * cx + x) * SIDE : (k * cx + x + 1) * SIDE, :]


def with_strip(own, edge, sec):
    return jnp.concatenate(
        [jnp.where(sec == 1, edge, 0.0), own, jnp.where(sec == 0, edge, 0.0)], axis=0
    )


def far_strip(rows, sec):
    return jnp.where(sec == 0, rows[-SIDE:], rows[:SIDE])


def yz_terms(s, comp, x, base, rows, weights):
    fw, bw = weights
    here = slice(base, base + rows)

    def beside(c):
        return lambda shift: s[c, x, base + shift : base + shift + rows, :]

    if comp == 0:
        return backward(beside(3), 0) + backward_z(s[4, x, here, :], bw)
    if comp == 1:
        return forward(beside(1), 0) + backward_z(s[5, x, here, :], bw)
    return backward(beside(5), 0) + forward_z(s[2, x, here, :], fw)


def force(s, comp, x, base, rows, weights, halo=None):
    source, ahead = STRESS_X[comp]
    cx = s.shape[1]

    def get(j):
        if 0 <= j < cx:
            return s[source, j, base : base + rows, :]
        return None if halo is None else halo(source, j)

    return along_x(ahead, x, get) + yz_terms(s, comp, x, base, rows, weights)


def own_share(s, comp, i, base, rows):
    source, ahead = STRESS_X[comp]
    cx = s.shape[1]
    return along_x(
        ahead, i, lambda j: s[source, j, base : base + rows, :] if 0 <= j < cx else None
    )


def load_stress(s, strips, s_pad, sec):
    comps, cx, cy, nz = s.shape
    nothing = jnp.zeros((SIDE, nz), F32)
    for c in range(comps):
        for x in range(cx):
            s_pad[c, x, 0:SIDE, :] = nothing
            s_pad[c, x, SIDE : 3 * SIDE + cy, :] = with_strip(s[c, x], strip(strips, c, x, cx), sec)
            s_pad[c, x, 3 * SIDE + cy :, :] = nothing


def send(odd, upper, lower, pay_a, pay_b, at):
    part = slice(at, at + upper.shape[0])
    pay_a[part, :] = jnp.where(odd, lower, upper)
    pay_b[part, :] = jnp.where(odd, upper, lower)


def send_layers(odd, up, down, layer, pay_a, pay_b, at):
    for k, (upper, lower) in enumerate(zip(up, down)):
        rows = layer(*upper)
        send(odd, rows, layer(*lower), pay_a, pay_b, at)
        at += rows.shape[0]


def first_lists(cx):
    (up_s, up_v), (down_s, down_v) = up_layers(cx), down_layers(cx)
    up_s, down_s = [("s", *key) for key in up_s], [("s", *key) for key in down_s]
    up_v, down_v = [("v", *key) for key in up_v], [("v", *key) for key in down_v]
    early = up_s + [("b", 0, cx - 1)], down_s + [("b", 0, 0), ("b", 0, 1)]
    late = up_v + [("b", 0, cx - 2)], down_v
    return early, late


def second_lists(cx):
    (up_s, up_v), (down_s, down_v) = up_layers(cx), down_layers(cx)
    up_s, down_s = [("s", *key) for key in up_s], [("s", *key) for key in down_s]
    up = up_s + [("v", *key) for key in up_v]
    return (up, down_s + [("v", *key) for key in down_v]), (up_s, down_s + down_s[-1:])


def thin_counts(lists):
    return [max(NEEDED[upper[0]], NEEDED[lower[0]]) for upper, lower in zip(*lists)]


def send_thin(odd, sec, lists, counts, edge, pay_a, pay_b, at):
    for upper, lower, n in zip(*lists, counts):

        def rows(key):
            whole = edge(*key)
            return jnp.where(sec == 0, whole[:n], whole[SIDE - n :])

        send(odd, rows(upper), rows(lower), pay_a, pay_b, at)
        at += n


def received(odd, lists, counts, pay_a, pay_b, cx, at):
    found = {}
    for upper, lower, n in zip(*lists, counts):
        part = slice(at, at + n)
        at += n
        for kind, c, x, below in ((*upper, True), (*lower, False)):

            def get(part=part, below=below):
                a, b = pay_a[part, :], pay_b[part, :]
                return jnp.where(odd, a, b) if below else jnp.where(odd, b, a)

            found[kind, c, x - cx if below else x + cx] = get
    return found


def put_layer(ref, k, own, thin, sec):
    cy, nz = own.shape
    n = thin.shape[0]
    ref[k, 0:SIDE, :] = jnp.zeros((SIDE, nz), F32)
    ref[k, SIDE : SIDE + cy, :] = own
    ref[k, SIDE + cy :, :] = jnp.zeros((SIDE, nz), F32)
    ref[k, SIDE - n : SIDE, :] = jnp.where(sec == 1, thin, 0.0)
    ref[k, SIDE + cy : SIDE + cy + n, :] = jnp.where(sec == 0, thin, 0.0)


def strains(velocity, halo, x, base, rows, weights):
    fw, bw = weights
    cx = velocity.shape[1]

    def layers(c):
        def get(j):
            if 0 <= j < cx:
                return velocity[c, j, base : base + rows, :]
            return halo(c, j)

        return get

    def beside(c):
        return lambda shift: velocity[c, x, base + shift : base + shift + rows, :]

    vx, vy, vz = (velocity[c, x, base : base + rows, :] for c in range(3))
    return (
        along_x(False, x, layers(0)),
        backward(beside(1), 0),
        backward_z(vz, bw),
        forward(beside(0), 0) + along_x(True, x, layers(1)),
        forward_z(vx, fw) + along_x(True, x, layers(2)),
        forward_z(vy, fw) + forward(beside(2), 0),
    )


def stress_change(lam, mu, parts):
    exx, eyy, ezz, xy, xz, yz = parts
    shear = DT * mu
    volume = (DT * lam) * (exx + eyy + ezz)
    double = 2.0 * shear
    return (
        volume + double * exx,
        volume + double * eyy,
        volume + double * ezz,
        shear * xy,
        shear * xz,
        shear * yz,
    )


def edge_rows(*refs):
    *fields, out = refs
    _, sec, _ = place()
    at = 0
    for field in fields:
        flat = field if len(field.shape) == 4 else None
        for c in range(field.shape[0] if flat is not None else 1):
            layers = field.shape[-3]
            for x in range(layers):
                rows = field[c, x] if flat is not None else field[x]
                out[at : at + SIDE, :] = jnp.where(sec == 0, rows[-SIDE:], rows[:SIDE])
                at += SIDE


def opening(s, v, b, pay_a, pay_b, edges, sems):
    odd, sec, _ = place()
    cx, cy, _ = b.shape
    up, down = first_lists(cx)[0]
    begin = pl.multiple_of(jnp.where(sec == 0, cy - SIDE, 0), SIDE)
    rows = [s.at[c, :, pl.ds(begin, SIDE), :] for c in range(6)]
    rows += [v.at[c, :, pl.ds(begin, SIDE), :] for c in range(3)]
    rows.append(b.at[:, pl.ds(begin, SIDE), :])
    rows = [pltpu.make_async_copy(r, edges.at[k], sems.at[k]) for k, r in enumerate(rows)]

    def run(above, below):
        copies = []
        for pay, layers in ((above, up), (below, down)):
            for k, (kind, c, x) in enumerate(layers):
                source = s.at[c, x] if kind == "s" else b.at[x]
                sem = sems.at[len(rows) + len(copies)]
                copies.append(pltpu.make_async_copy(source, pay.at[pl.ds(k * cy, cy)], sem))
        for copy in copies + rows:
            copy.start()
        for copy in copies:
            copy.wait()

    @pl.when(odd)
    def _():
        run(pay_b, pay_a)

    @pl.when(jnp.logical_not(odd))
    def _():
        run(pay_a, pay_b)

    for copy in rows:
        copy.wait()


def near_columns(state, depth, wet, out):
    _, sec, _ = place()
    rows, own = depth.shape
    for k, field in enumerate((state.at[0], state.at[1], state.at[2], depth, wet)):
        near = jnp.where(sec == 0, field[:, own - 128 :], field[:, :128])
        out[k * rows : (k + 1) * rows, :] = near.astype(F32)


def ocean_field(state, depth, wet, near, f, k):
    rows, own = depth.shape
    if k == own // 128:
        return near[f * rows : (f + 1) * rows, :]
    field = state.at[f] if f < 3 else depth if f == 3 else wet
    return field[:, k * 128 : (k + 1) * 128].astype(F32)


def ocean_edges(state, depth, wet, near, edges):
    rows, own = depth.shape
    at = 0
    for k in range(own // 128 + 1):
        for f, n in enumerate(DEEP):
            field = ocean_field(state, depth, wet, near, f, k)
            edges[0, at : at + n, :] = field[rows - n :]
            edges[1, at : at + n, :] = field[:n]
            at += n


def first_round(s, v, b, strips, pay_a, pay_b, s_pad):
    odd, sec, _ = place()
    _, cx, cy, nz = s.shape
    weights = depth_weights(nz)
    rows = cy + 2 * SIDE
    load_stress(s, strips, s_pad, sec)
    made = {}

    def velocity(c, x):
        if (c, x) not in made:
            old = with_strip(v[c, x], strip(strips, 6 + c, x, cx), sec)
            scale = DT * with_strip(b[x], strip(strips, 9, x, cx), sec)
            made[c, x] = old + scale * force(s_pad, c, x, SIDE, rows, weights)
        return made[c, x]

    def layer(kind, c, x):
        return velocity(c, x)[SIDE : SIDE + cy] if kind == "v" else b[x]

    def edge(kind, c, x):
        if kind == "v":
            return far_strip(velocity(c, x), sec)
        return strip(strips, c if kind == "s" else 9, x, cx)

    early, late = first_lists(cx)
    send_layers(odd, *late, layer, pay_a, pay_b, 0)
    at = len(late[0]) * cy
    for lists in (early, late):
        counts = thin_counts(lists)
        send_thin(odd, sec, lists, counts, edge, pay_a, pay_b, at)
        at += sum(counts)


def first_received(odd, cx, cy, early_a, early_b, late_a, late_b):
    early, late = first_lists(cx)
    own = received(odd, early, [cy] * len(early[0]), early_a, early_b, cx, 0)
    own.update(received(odd, late, [cy] * len(late[0]), late_a, late_b, cx, 0))
    at = len(late[0]) * cy
    rest = received(odd, early, thin_counts(early), late_a, late_b, cx, at)
    at += sum(thin_counts(early))
    rest.update(received(odd, late, thin_counts(late), late_a, late_b, cx, at))
    return own, rest


def whole_step(
    s,
    v,
    b,
    lam,
    mu,
    strips,
    more_strips,
    early_a,
    early_b,
    late_a,
    late_b,
    sea,
    v_out,
    s_out,
    pay_a,
    pay_b,
    b_near,
    s_pad,
    v_pad,
    halo_s,
    halo_v,
    halo_b,
):
    odd, sec, _ = place()
    _, cx, cy, nz = s.shape
    weights = depth_weights(nz)
    rows = cy + 2 * SIDE
    load_stress(s, strips, s_pad, sec)
    index_s, index_v = halo_stress(cx), halo_velocity(cx)
    own, rest = first_received(odd, cx, cy, early_a, early_b, late_a, late_b)
    for key, k in index_s.items():
        put_layer(halo_s, k, own["s", *key](), rest["s", *key](), sec)
    for key, k in index_v.items():
        put_layer(halo_v, k, own["v", *key](), rest["v", *key](), sec)
    index_b = {i: k for k, i in enumerate((-2, -1, cx, cx + 1))}
    for i, k in index_b.items():
        put_layer(halo_b, k, own["b", 0, i](), rest["b", 0, i](), sec)
        b_near[k * cy : (k + 1) * cy, :] = own["b", 0, i]()
    for x in range(cx):
        part = slice(4 * cy + x * SIDE, 4 * cy + (x + 1) * SIDE)
        b_near[part, :] = strip(strips, 9, x, cx)
    nothing = jnp.zeros((SIDE, nz), F32)
    for x in range(cx):
        scale = DT * with_strip(b[x], strip(strips, 9, x, cx), sec)
        for c in range(3):
            old = with_strip(v[c, x], strip(strips, 6 + c, x, cx), sec)
            terms = force(s_pad, c, x, SIDE, rows, weights, lambda k, j: halo_s[index_s[k, j]])
            new = old + scale * terms
            v_out[c, x] = new
            v_pad[c, x, 0:SIDE, :] = nothing
            v_pad[c, x, SIDE : SIDE + rows, :] = new
            v_pad[c, x, SIDE + rows :, :] = nothing
    for (c, i), k in index_v.items():
        halo_v[k] = halo_v[k] + DT * halo_b[index_b[i]] * own_share(s_pad, c, i, SIDE, rows)
    for x in range(cx):
        parts = strains(v_pad, lambda c, j: halo_v[index_v[c, j]], x, SIDE, rows, weights)
        lam_rows = with_strip(lam[x], strip(more_strips, 0, x, cx), sec)
        mu_rows = with_strip(mu[x], strip(more_strips, 1, x, cx), sec)
        for c, change in enumerate(stress_change(lam_rows, mu_rows, parts)):
            s_out[c, x] = s_pad[c, x, SIDE : SIDE + rows, :] + change

    def layer(kind, c, x):
        if kind == "s":
            return s_out[c, x, SIDE : SIDE + cy, :]
        old = v_out[c, x, SIDE : SIDE + cy, :]
        return old + DT * b[x] * force(s_out, c, x, SIDE, cy, weights)

    def edge(_, c, x):
        return jnp.where(sec == 0, s_out[c, x, SIDE + cy :, :], s_out[c, x, 0:SIDE, :])

    layers, edges = second_lists(cx)
    send_layers(odd, *layers, layer, pay_a, pay_b, 0)
    counts = [LAST_NEEDED] * len(edges[0])
    at = LAYERS * cy
    send(odd, sea[0], sea[1], pay_a, pay_b, at)
    send_thin(odd, sec, edges, counts, edge, pay_a, pay_b, at + sea.shape[1])


def last_step(
    sea_rows,
    s,
    v,
    b,
    lam,
    mu,
    b_near,
    from_a,
    from_b,
    v_out,
    s_out,
    done,
    v_rows,
    b_rows,
    halo_s,
    halo_v,
    made,
    sems,
):
    done[...] = jnp.zeros(done.shape, F32)
    odd, sec, _ = place()
    cx, cy, nz = b.shape
    weights = depth_weights(nz)
    half = SIDE // 2
    rows = cy + SIDE
    index_s, index_v = halo_stress(cx), halo_velocity(cx)
    layers, edges = second_lists(cx)
    own = received(odd, layers, [cy] * LAYERS, from_a, from_b, cx, 0)
    counts = [LAST_NEEDED] * len(edges[0])
    rest = received(odd, edges, counts, from_a, from_b, cx, LAYERS * cy + sea_rows)
    for key, k in index_s.items():
        put_layer(halo_s, k, own["s", *key](), rest["s", *key](), sec)
    for x in range(cx):
        part = slice(4 * cy + x * SIDE, 4 * cy + (x + 1) * SIDE)
        b_rows[...] = with_strip(b[x], b_near[part, :], sec)
        scale = DT * b_rows[half : half + rows, :]
        for c in range(3):
            terms = force(
                s, c, x, half, rows, weights, lambda k, j: halo_s[index_s[k, j], half : half + rows, :]
            )
            v_rows[c, x, half : half + rows, :] = v[c, x, half : half + rows, :] + scale * terms
    copies = [pltpu.make_async_copy(v_rows.at[:, :, pl.ds(SIDE, cy), :], v_out, sems.at[cx])]
    copies[0].start()
    for (c, i), k in index_v.items():
        at = (i + 2 if i < 0 else i - cx + 2) * cy
        scale = DT * b_near[at : at + cy, :]
        halo_v[k] = own["v", c, i]() + scale * own_share(s, c, i, SIDE, cy)
    for x in range(cx):
        parts = strains(v_rows, lambda c, j: halo_v[index_v[c, j]], x, SIDE, cy, weights)
        for c, change in enumerate(stress_change(lam[x], mu[x], parts)):
            made[c, x] = s[c, x, SIDE : SIDE + cy, :] + change
        copies.append(pltpu.make_async_copy(made.at[:, x], s_out.at[:, x], sems.at[x]))
        copies[-1].start()
    for copy in copies:
        copy.wait()


def floor_line(left, right):
    rows = left.shape[0]
    row = lax.broadcasted_iota(jnp.int32, (rows, 2 * rows), 0)
    lane = lax.broadcasted_iota(jnp.int32, (rows, 2 * rows), 1)
    picked = jnp.where(lane == row, left[:, 0:1], 0.0)
    picked = jnp.where(lane == row + rows, right[:, 0:1], picked)
    return jnp.sum(picked, axis=0, keepdims=True)


def floor_parts(s, v, b, info, parts):
    cx, cy, nz = b.shape
    weights = depth_weights(nz)
    own = slice(SIDE, SIDE + cy)
    layers = [
        v[2, x, own, :] + DT * b[x] * force(s, 2, x, SIDE, cy, weights) for x in range(cx)
    ]
    lines = [floor_line(layers[x], layers[x + 1]) for x in range(0, cx, 2)]
    last = s[4, cx - 1, own, :]
    lines.append(floor_line(last, last))
    lines.append(floor_line(s[4, cx - 2, own, :], s[4, 0, own, :]))
    lines.append(floor_line(DT * b[0], DT * b[1]))
    lines.append(floor_line(jnp.zeros((cy, nz), F32), (-FAR * DT) * b[cx - 1]))
    lines.append(info[...])
    row = lax.broadcasted_iota(jnp.int32, (SIDE, 2 * cy), 0)
    tiled = jnp.zeros((SIDE, 2 * cy), F32)
    for k, line in enumerate(lines):
        tiled = jnp.where(row == k, line, tiled)
    for k in range(parts.shape[0]):
        parts[k] = tiled


def column(line, first, count):
    wide = jnp.broadcast_to(line, (count, line.shape[1]))
    row = lax.broadcasted_iota(jnp.int32, wide.shape, 0)
    lane = lax.broadcasted_iota(jnp.int32, wide.shape, 1)
    return jnp.sum(jnp.where(lane == row + first, wide, 0.0), axis=1, keepdims=True)


def ocean_steps(
    start, from_a, from_b, near, state, depth, wet_ref, info, patches, _, ocean_out, ocean_ref
):
    odd, sec, tile = place()
    count = lax.axis_size("tile")
    rows, own = depth.shape
    columns = own + 128
    at = start
    for k in range(columns // 128):
        lanes = slice(k * 128, (k + 1) * 128)
        for f, n in enumerate(DEEP):
            here = ocean_field(state, depth, wet_ref, near, f, k)
            a, b = from_a[at : at + n, :], from_b[at : at + n, :]
            low, high = jnp.where(odd, a, b), jnp.where(odd, b, a)
            ocean_ref[f, 0:SIDE, lanes] = jnp.zeros((SIDE, 128), F32)
            ocean_ref[f, SIDE + rows :, lanes] = jnp.zeros((SIDE, 128), F32)
            ocean_ref[f, SIDE - n : SIDE, lanes] = low
            ocean_ref[f, SIDE : SIDE + rows, lanes] = here
            ocean_ref[f, SIDE + rows : SIDE + rows + n, lanes] = high
            at += n

    total = rows + 2 * SIDE
    lane = lax.broadcasted_iota(jnp.int32, (1, columns), 1)
    ahead = jnp.where((lane == own - 1) & (sec == 1), 0.0, 0.5).astype(F32)
    behind = jnp.where((lane == 0) & (sec == 0), 0.0, 0.5).astype(F32)
    line = lax.broadcasted_iota(jnp.int32, (total, 1), 0)
    inside = ((line >= SIDE) | (tile > 0)) & ((line < SIDE + rows) | (tile < count - 1))
    inside = inside.astype(F32)

    def across(f):
        return pltpu.roll(f, columns - 1, 1) * ahead - pltpu.roll(f, 1, 1) * behind

    def down(f):
        return 0.5 * (pltpu.roll(f, total - 1, 0) - pltpu.roll(f, 1, 0))

    eta, u, v_sea = ocean_ref[0], ocean_ref[1], ocean_ref[2]
    depth, wet = ocean_ref[3], ocean_ref[4]
    window = min(WINDOW, count)
    base = jnp.clip(tile - REACH - 1, 0, count - window)
    below = patches[sec * count + jnp.maximum(tile - 1, 0)][6:7]
    above = patches[sec * count + jnp.minimum(tile + 1, count - 1)][6:7]
    line = info[...]
    marks = [
        jnp.concatenate(
            [
                column(below, k * rows + rows - SIDE, SIDE),
                column(line, k * rows, rows),
                column(above, k * rows, SIDE),
            ],
            axis=0,
        )
        for k in range(2)
    ]
    owner = jnp.broadcast_to(marks[0] - base.astype(F32), (total, 128))
    share = marks[1]
    width = own // 4
    left = lax.broadcasted_iota(jnp.int32, (1, 128), 1) < width
    near = jnp.where(left, -NEAR, FAR).astype(F32)
    far = jnp.where(left, FAR, 0.0).astype(F32)
    uplift = []
    for half in (sec, 1 - sec):
        tiles = []
        for k in range(-1, window + 1):
            here = jnp.clip(base + k, 0, count - 1)
            there = (here == base + k).astype(F32)
            tiles.append(patches[half * count + here] * there)
        levels = [jnp.zeros((total, 128), F32) for _ in range(2)]
        for k in range(window):
            below, this, above = tiles[k], tiles[k + 1], tiles[k + 2]
            first = this[0:1] + this[4:5] * (near * below[2:3] + far * below[3:4])
            second = this[1:2] + this[5:6] * above[3:4]
            mine = owner == float(k)
            levels = [jnp.where(mine, q, level) for q, level in zip((first, second), levels)]
        uplift.append(levels)
    uplift = uplift[0] + [jnp.where(sec == 0, uplift[1][0], uplift[1][1])]
    uplift = jnp.concatenate(uplift, axis=1)
    lift = ODT * (share * wet * uplift)
    for _ in range(2):
        u = wet * (u - ODT * down(eta))
        v_sea = wet * (v_sea - ODT * across(eta))
        eta = inside * (eta - ODT * (down(depth * u) + across(depth * v_sea)) + lift)
    part = slice(SIDE, SIDE + rows)
    ocean_out[0] = eta[part, :own]
    ocean_out[1] = u[part, :own]
    ocean_out[2] = v_sea[part, :own]


VMEM = pl.BlockSpec(memory_space=pltpu.VMEM)
ANY = pl.BlockSpec(memory_space=pl.ANY)


def call(body, name, outs, scratch, operands, weight=1, ins=VMEM, where=VMEM, grant=8):
    shapes = [jax.ShapeDtypeStruct(o, F32) for o in outs]
    moved = sum(o.size for o in operands) * 4 + sum(o.size for o in shapes) * 4
    return pl.pallas_call(
        body,
        name=name,
        out_shape=shapes,
        in_specs=ins if isinstance(ins, list) else [ins] * len(operands),
        out_specs=where if isinstance(where, list) else [where] * len(outs),
        scratch_shapes=scratch,
        compiler_params=pltpu.CompilerParams(vmem_limit_bytes=grant * 1024 * 1024),
        cost_estimate=pl.CostEstimate(
            flops=moved * weight, bytes_accessed=moved * weight, transcendentals=0
        ),
    )(*operands)


def exchange(pay_a, pay_b, count):
    def swap(pay, first):
        pairs = []
        for i in range(first, count - 1, 2):
            pairs += [(i, i + 1), (i + 1, i)]
        return lax.ppermute(pay, "tile", pairs)

    from_a = swap(pay_a, 0)
    return from_a, swap(pay_b, 1)


def across(pay):
    return lax.ppermute(pay, "sec", [(0, 1), (1, 0)])


def shards(
    velocity,
    stresses,
    buoyancy,
    lame_first,
    shear_mod,
    ocean_state,
    depth_map,
    wet_mask,
    intersection_src,
    intersection_share,
):
    count = lax.axis_size("tile")
    sec = lax.axis_index("sec")
    _, cx, cy, nz = stresses.shape
    _, rows, columns = ocean_state.shape
    tall = cy + 2 * SIDE
    halo = pltpu.VMEM((LAYERS, tall, nz), F32)

    first = ((LAYERS + 2) // 2 + 1) * cy
    pay_a, pay_b, edges = call(
        opening,
        "opening",
        [(first, nz), (first, nz), (10, cx, SIDE, nz)],
        [pltpu.SemaphoreType.DMA((10 + 2 * (first // cy),))],
        [stresses, velocity, buoyancy],
        ins=ANY,
        grant=60,
    )
    early_a, early_b = exchange(pay_a, pay_b, count)
    strips = across(edges.reshape(10 * cx * SIDE, nz))
    early_list, late_list = first_lists(cx)
    per = (columns // 128 + 1) * PACK
    late = len(late_list[0]) * cy + sum(thin_counts(early_list) + thin_counts(late_list))
    pay_a, pay_b = call(
        first_round,
        "first_round",
        [(late, nz), (late, nz)],
        [pltpu.VMEM((6, cx, tall + 2 * SIDE, nz), F32)],
        [stresses, velocity, buoyancy, strips],
    )
    late_a, late_b = exchange(pay_a, pay_b, count)

    source, share, lame, shear, ocean_state, depth_map, wet_mask, _, _ = lax.optimization_barrier(
        (intersection_src, intersection_share, lame_first, shear_mod)
        + (ocean_state, depth_map, wet_mask, early_a, early_b)
    )
    (edges,) = call(edge_rows, "edge_rows", [(2 * cx * SIDE, nz)], [], [lame, shear])
    more_strips = across(edges)
    sea = [ocean_state, depth_map, wet_mask]
    (near,) = call(near_columns, "near_columns", [(len(DEEP) * rows, 128)], [], sea)
    near = across(near)
    (edges,) = call(ocean_edges, "ocean_edges", [(2, per, 128)], [], sea + [near])
    info = jnp.concatenate([source.astype(F32), share])[None]

    second = (LAYERS * cy + per + 5 * LAST_NEEDED, nz)
    velocity, stresses, pay_a, pay_b, b_near = call(
        whole_step,
        "whole_step",
        [(3, cx, tall, nz), (6, cx, tall, nz), second, second]
        + [(4 * cy + cx * SIDE, nz)],
        [
            pltpu.VMEM((6, cx, tall + 2 * SIDE, nz), F32),
            pltpu.VMEM((3, cx, tall + 2 * SIDE, nz), F32),
            halo,
            halo,
            pltpu.VMEM((4, tall, nz), F32),
        ],
        [stresses, velocity, buoyancy, lame_first, shear_mod, strips, more_strips]
        + [early_a, early_b, late_a, late_b, edges],
    )
    from_a, from_b = exchange(pay_a, pay_b, count)
    (parts,) = call(
        floor_parts,
        "floor_parts",
        [(2 * count, SIDE, 2 * cy)],
        [],
        [stresses, velocity, buoyancy, info],
    )
    patches = lax.all_to_all(parts, ("sec", "tile"), 0, 0)
    velocity, stresses, done = call(
        functools.partial(last_step, per),
        "last_step",
        [(3, cx, cy, nz), (6, cx, cy, nz), (8, 128)],
        [
            pltpu.VMEM((3, cx, tall, nz), F32),
            pltpu.VMEM((tall, nz), F32),
            halo,
            pltpu.VMEM((LAYERS, cy, nz), F32),
            pltpu.VMEM((6, cx, cy, nz), F32),
            pltpu.SemaphoreType.DMA((cx + 1,)),
        ],
        [stresses, velocity, buoyancy, lame_first, shear_mod, b_near]
        + [from_a, from_b],
        where=[ANY, ANY, VMEM],
    )
    (ocean_state,) = call(
        functools.partial(ocean_steps, LAYERS * cy),
        "ocean_steps",
        [ocean_state.shape],
        [pltpu.VMEM((len(DEEP), rows + 2 * SIDE, columns + 128), F32)],
        [from_a, from_b, near] + sea + [info, patches, done],
    )
    return velocity, stresses, ocean_state


def solution(mesh):
    cube = P("tile", "sec", None)
    return jax.shard_map(
        shards,
        mesh=mesh,
        in_specs=(
            P(None, "tile", "sec", None),
            P(None, "tile", "sec", None),
            cube,
            cube,
            cube,
            P(None, "tile", "sec"),
            P("tile", "sec"),
            P("tile", "sec"),
            P("tile"),
            P("tile"),
        ),
        out_specs=(
            P(None, "tile", "sec", None),
            P(None, "tile", "sec", None),
            P(None, "tile", "sec"),
        ),
        check_vma=False,
    )
```

time: 161 us -> 46.9 us (0.29)
  the two profiles are of different devices: /device:TPU:21 before, /device:TPU:0 now
where the time goes in v5:
time: 46.9 us; the launch traced here: 46.7 us
  starting transfers between devices  21 us (45%)
  waiting for transfers between devices  15.9 us (34%)
  Pallas kernels  8.76 us (19%)
  between operations  0.85 us (2%)
    ppermute x6, starting transfers between devices, swap(): return lax.ppermute(pay, 'tile', pairs)  12.8 us
    ppermute x6, waiting for transfers between devices, swap(): return lax.ppermute(pay, 'tile', pairs)  12.5 us
    pallas_call x9, Pallas kernels, call(): pl.pallas_call(body, name=name, out_shape=shapes, in_specs=ins if isinsta...  8.76 us
    all_to_all x1, starting transfers between devices, shards(): patches = lax.all_to_all(parts, ('sec', 'tile'), 0, 0)  7.55 us
    ppermute x3, waiting for transfers between devices, across(): return lax.ppermute(pay, 'sec', [(0, 1), (1, 0)])  2.43 us
  transfers between devices with their start and end apart: 10, of which 6 were waited for; matrix products, arithmetic and copies ran while one was open for 0% of the time, Pallas kernels for 7%

profile of v5, /device:TPU:0, one launch (start us, length us, event | category | flops | bytes accessed | tf_op | source)
XLA Modules:
  0.0 46.7 jit_solution(2578411407877842932)
XLA Ops:
  0.6 0.0 copy-start
  0.7 2.1 %opening.1 = (f32[384,128]{1,0:T(8,128)}, f32[384,128]{1,0:T(8,128)}, f32[10,4,8,128]{3,2,1,0:T(8,128)}) custom-call(f32[6,4,64,128]{3,2,1,0:T(8,128)} %s.5, f32[3,4,64,128]{3,2,1,0:T(8,128)} %v.5, f32[4,64,128]{2,1,0:T(8,128)} %b.9), custom_call_target="tpu_custom_call" | custom-call | flops 1867776 | bytes 1867776 | tf_op jit(solution)/shard_map/opening/pallas_call | solution.py:659
  2.8 3.0 %collective-permute-start.1 = (f32[384,128]{1,0:T(8,128)}, f32[384,128]{1,0:T(8,128)S(1)}, u32[]{:S(2)}, u32[]{:S(2)}) collective-permute-start(f32[384,128]{1,0:T(8,128)} %get-tuple-element.24), channel_id=1, source_target_pairs={{0,1},{1,0},{2,3},{3,2},{4,5},{5,4},{6,7},{7,6},{8,9},{9,8},{10,11... | collective-permute-start | bytes 589832 | tf_op jit(solution)/shard_map/ppermute | solution.py:678
  5.7 0.7 %collective-permute-start.2 = (f32[384,128]{1,0:T(8,128)}, f32[384,128]{1,0:T(8,128)S(1)}, u32[]{:S(2)}, u32[]{:S(2)}) collective-permute-start(f32[384,128]{1,0:T(8,128)} %get-tuple-element.25), channel_id=1, source_target_pairs={{1,2},{2,1},{3,4},{4,3},{5,6},{6,5},{7,8},{8,7},{9,10},{10,9},{11,... | collective-permute-start | bytes 589832 | tf_op jit(solution)/shard_map/ppermute | solution.py:678
  6.4 0.0 copy-start.3
  6.4 0.0 copy-start.6
  6.4 0.0 copy-start.7
  6.4 0.1 collective-permute-start
  6.5 1.6 %collective-permute-done.strips = f32[320,128]{1,0:T(8,128)S(1)} collective-permute-done((f32[320,128]{1,0:T(8,128)}, f32[320,128]{1,0:T(8,128)S(1)}, u32[]{:S(2)}, u32[]{:S(2)}) %collective-permute-start) | collective-permute-done | bytes 163872 | tf_op jit(solution)/shard_map/ppermute | solution.py:685
  8.1 0.4 first_round.1
  8.5 4.3 %collective-permute-start.4 = (f32[363,128]{1,0:T(8,128)S(1)}, f32[363,128]{1,0:T(8,128)S(1)}, u32[]{:S(2)}, u32[]{:S(2)}) collective-permute-start(f32[363,128]{1,0:T(8,128)S(1)} %get-tuple-element.28), channel_id=1, source_target_pairs={{0,1},{1,0},{2,3},{3,2},{4,5},{5,4},{6,7},{7,6},{8,9},{9,8},{10,11... | collective-permute-start | bytes 557576 | tf_op jit(solution)/shard_map/ppermute | solution.py:678
  12.8 0.8 %collective-permute-start.5 = (f32[363,128]{1,0:T(8,128)S(1)}, f32[363,128]{1,0:T(8,128)S(1)}, u32[]{:S(2)}, u32[]{:S(2)}) collective-permute-start(f32[363,128]{1,0:T(8,128)S(1)} %get-tuple-element.29), channel_id=1, source_target_pairs={{1,2},{2,1},{3,4},{4,3},{5,6},{6,5},{7,8},{8,7},{9,10},{10,9},{11,... | collective-permute-start | bytes 557576 | tf_op jit(solution)/shard_map/ppermute | solution.py:678
  13.6 0.0 collective-permute-done.1.early_a
  13.6 0.0 collective-permute-done.2.early_b
  13.7 0.0 copy-start.8
  13.7 0.1 collective-permute-start.6
  13.8 0.5 %collective-permute-start.3 = (f32[64,128]{1,0:T(8,128)S(1)}, f32[64,128]{1,0:T(8,128)S(1)}, u32[]{:S(2)}, u32[]{:S(2)}) collective-permute-start(f32[64,128]{1,0:T(8,128)S(1)} %edge_rows.1), channel_id=1, source_target_pairs={{0,16},{16,0},{1,17},{17,1},{2,18},{18,2},{3,19},{19,3},{4,20},{20... | collective-permute-start | bytes 98312 | tf_op jit(solution)/shard_map/ppermute | solution.py:685
  14.4 0.8 %collective-permute-done.6.near = f32[320,128]{1,0:T(8,128)S(1)} collective-permute-done((f32[320,128]{1,0:T(8,128)S(1)}, f32[320,128]{1,0:T(8,128)S(1)}, u32[]{:S(2)}, u32[]{:S(2)}) %collective-permute-start.6) | collective-permute-done | bytes 163872 | tf_op jit(solution)/shard_map/ppermute | solution.py:685
  15.2 0.1 collective-permute-done.3.more_strips
  15.2 7.2 %collective-permute-done.4.late_a = f32[363,128]{1,0:T(8,128)S(1)} collective-permute-done((f32[363,128]{1,0:T(8,128)S(1)}, f32[363,128]{1,0:T(8,128)S(1)}, u32[]{:S(2)}, u32[]{:S(2)}) %collective-permute-start.4) | collective-permute-done | bytes 185888 | tf_op jit(solution)/shard_map/ppermute | solution.py:678
  22.4 0.0 collective-permute-done.5.late_b
  22.4 2.3 %whole_step.1 = (f32[3,4,80,128]{3,2,1,0:T(8,128)S(1)}, f32[6,4,80,128]{3,2,1,0:T(8,128)S(1)}, f32[634,128]{1,0:T(8,128)}, f32[634,128]{1,0:T(8,128)}, f32[288,128]{1,0:T(8,128)S(1)}) custom-call(f32[6,4,64,128]{3,2,1,0:T(8,128)S(1)} %copy-done, f32[3,4,64,128]{3,2,1,0:T(8,128)S(1)} %copy-done.1, f32[4,64,128]{2,1,0:T(8,128)S(1)} %copy-done.2, ...), custom_call_target="tpu_custom_call" | custom-call | flops 4854784 | bytes 4854784 | tf_op jit(solution)/shard_map/whole_step/pallas_call | solution.py:659
  24.7 3.4 %collective-permute-start.7 = (f32[634,128]{1,0:T(8,128)}, f32[634,128]{1,0:T(8,128)S(1)}, u32[]{:S(2)}, u32[]{:S(2)}) collective-permute-start(f32[634,128]{1,0:T(8,128)} %get-tuple-element.36), channel_id=1, source_target_pairs={{0,1},{1,0},{2,3},{3,2},{4,5},{5,4},{6,7},{7,6},{8,9},{9,8},{10,11... | collective-permute-start | bytes 973832 | tf_op jit(solution)/shard_map/ppermute | solution.py:678
  28.1 0.7 %collective-permute-start.8 = (f32[634,128]{1,0:T(8,128)}, f32[634,128]{1,0:T(8,128)S(1)}, u32[]{:S(2)}, u32[]{:S(2)}) collective-permute-start(f32[634,128]{1,0:T(8,128)} %get-tuple-element.37), channel_id=1, source_target_pairs={{1,2},{2,1},{3,4},{4,3},{5,6},{6,5},{7,8},{8,7},{9,10},{10,9},{11,... | collective-permute-start | bytes 973832 | tf_op jit(solution)/shard_map/ppermute | solution.py:678
  28.8 0.1 maximum_bitcast_fusion.info
  28.9 1.0 %floor_parts.1 = f32[32,8,128]{2,1,0:T(8,128)} custom-call(f32[6,4,80,128]{3,2,1,0:T(8,128)S(1)} %get-tuple-element.33.s, f32[3,4,80,128]{3,2,1,0:T(8,128)S(1)} %get-tuple-element.34.v, f32[4,64,128]{2,1,0:T(8,128)S(1)} %copy-done.2, f32[1,128]{1,0:T(1,128)S(1)} %maximum_bitcast_fusion.info), custom_call_target="tpu_custom_call" | custom-call | flops 1737216 | bytes 1737216 | tf_op jit(solution)/shard_map/floor_parts/pallas_call | solution.py:659
  29.9 7.6 %all-to-all-start = ((f32[32,8,128]{2,1,0:T(8,128)}), f32[32,8,128]{2,1,0:T(8,128)S(1)}, u32[]{:S(2)}, u32[]{:S(2)}) async-start(f32[32,8,128]{2,1,0:T(8,128)} %floor_parts.1), calls=%async_computation | async-start | bytes 262144 | tf_op jit(solution)/shard_map/all_to_all | solution.py:767
  37.4 5.4 %collective-permute-done.7.from_a = f32[634,128]{1,0:T(8,128)S(1)} collective-permute-done((f32[634,128]{1,0:T(8,128)}, f32[634,128]{1,0:T(8,128)S(1)}, u32[]{:S(2)}, u32[]{:S(2)}) %collective-permute-start.7) | collective-permute-done | bytes 324640 | tf_op jit(solution)/shard_map/ppermute | solution.py:678
  42.8 0.0 collective-permute-done.8.from_b
  42.8 1.6 %last_step.1 = (f32[3,4,64,128]{3,2,1,0:T(8,128)}, f32[6,4,64,128]{3,2,1,0:T(8,128)}, f32[8,128]{1,0:T(8,128)S(1)}) custom-call(f32[6,4,80,128]{3,2,1,0:T(8,128)S(1)} %get-tuple-element.33.s, f32[3,4,80,128]{3,2,1,0:T(8,128)S(1)} %get-tuple-element.34.v, f32[4,64,128]{2,1,0:T(8,128)S(1)} %copy-done.2, f32[4,64,128]{2,1,0:T(8,128)S(1)} %copy-done.4, ...), custom_call_target="tpu_custom_call" | custom-call | flops 3848192 | bytes 3848192 | tf_op jit(solution)/shard_map/last_step/pallas_call | solution.py:659
  44.4 0.9 %all-to-all-done.patches = f32[32,8,128]{2,1,0:T(8,128)S(1)} async-done(((f32[32,8,128]{2,1,0:T(8,128)}), f32[32,8,128]{2,1,0:T(8,128)S(1)}, u32[]{:S(2)}, u32[]{:S(2)}) %all-to-all-start) | async-done | bytes 131104 | tf_op jit(solution)/shard_map/all_to_all | solution.py:767
  45.3 1.3 %ocean_steps.1 = f32[3,64,256]{2,1,0:T(8,128)} custom-call(f32[634,128]{1,0:T(8,128)S(1)} %collective-permute-done.7.from_a, f32[634,128]{1,0:T(8,128)S(1)} %collective-permute-done.8.from_b, f32[320,128]{1,0:T(8,128)S(1)} %collective-permute-done.6.near, f32[3,64,256]{2,1,0:T(8,128)S(1)} %copy-done.3, f32[64,256]{1,0:T(8,128)S(1)} %copy-done.6, ...), custom_call_target="tpu_custom_call" | custom-call | flops 1473024 | bytes 1473024 | tf_op jit(solution)/shard_map/ocean_steps/pallas_call | solution.py:659
  (19 shorter events, 0.1 us)
Async XLA Ops:
  0.6 7.5 %copy-start = (f32[6,4,64,128]{3,2,1,0:T(8,128)S(1)}, f32[6,4,64,128]{3,2,1,0:T(8,128)}, u32[]{:S(2)}) copy-start(f32[6,4,64,128]{3,2,1,0:T(8,128)} %s.5) | copy-start | bytes 2359300
  0.6 7.5 %copy-start.1 = (f32[3,4,64,128]{3,2,1,0:T(8,128)S(1)}, f32[3,4,64,128]{3,2,1,0:T(8,128)}, u32[]{:S(2)}) copy-start(f32[3,4,64,128]{3,2,1,0:T(8,128)} %v.5) | copy-start | bytes 1179652
  0.7 7.5 %copy-start.2 = (f32[4,64,128]{2,1,0:T(8,128)S(1)}, f32[4,64,128]{2,1,0:T(8,128)}, u32[]{:S(2)}) copy-start(f32[4,64,128]{2,1,0:T(8,128)} %b.9) | copy-start | bytes 393220
  2.8 10.9 %collective-permute-start.1 = (f32[384,128]{1,0:T(8,128)}, f32[384,128]{1,0:T(8,128)S(1)}, u32[]{:S(2)}, u32[]{:S(2)}) collective-permute-start(f32[384,128]{1,0:T(8,128)} %get-tuple-element.24), channel_id=1, source_target_pairs={{0,1},{1,0},{2,3},{3,2},{4,5},{5,4},{6,7},{7,6},{8,9},{9,8},{10,11... | collective-permute-start | bytes 589832 | tf_op jit(solution)/shard_map/ppermute | solution.py:678
  5.7 7.9 %collective-permute-start.2 = (f32[384,128]{1,0:T(8,128)}, f32[384,128]{1,0:T(8,128)S(1)}, u32[]{:S(2)}, u32[]{:S(2)}) collective-permute-start(f32[384,128]{1,0:T(8,128)} %get-tuple-element.25), channel_id=1, source_target_pairs={{1,2},{2,1},{3,4},{4,3},{5,6},{6,5},{7,8},{8,7},{9,10},{10,9},{11,... | collective-permute-start | bytes 589832 | tf_op jit(solution)/shard_map/ppermute | solution.py:678
  6.4 7.2 %copy-start.3 = (f32[3,64,256]{2,1,0:T(8,128)S(1)}, f32[3,64,256]{2,1,0:T(8,128)}, u32[]{:S(2)}) copy-start(f32[3,64,256]{2,1,0:T(8,128)} %state.2) | copy-start | bytes 589828
  6.4 7.2 %copy-start.6 = (f32[64,256]{1,0:T(8,128)S(1)}, f32[64,256]{1,0:T(8,128)}, u32[]{:S(2)}) copy-start(f32[64,256]{1,0:T(8,128)} %depth.2) | copy-start | bytes 196612
  6.4 7.2 %copy-start.7 = (s32[64,256]{1,0:T(8,128)S(1)}, s32[64,256]{1,0:T(8,128)}, u32[]{:S(2)}) copy-start(s32[64,256]{1,0:T(8,128)} %wet_ref) | copy-start | bytes 196612
  6.4 1.7 %collective-permute-start = (f32[320,128]{1,0:T(8,128)}, f32[320,128]{1,0:T(8,128)S(1)}, u32[]{:S(2)}, u32[]{:S(2)}) collective-permute-start(f32[320,128]{1,0:T(8,128)} %bitcast.3), channel_id=1, source_target_pairs={{0,16},{16,0},{1,17},{17,1},{2,18},{18,2},{3,19},{19,3},{4,20},{20... | collective-permute-start | bytes 491528 | tf_op jit(solution)/shard_map/ppermute | solution.py:685
  8.5 13.9 %collective-permute-start.4 = (f32[363,128]{1,0:T(8,128)S(1)}, f32[363,128]{1,0:T(8,128)S(1)}, u32[]{:S(2)}, u32[]{:S(2)}) collective-permute-start(f32[363,128]{1,0:T(8,128)S(1)} %get-tuple-element.28), channel_id=1, source_target_pairs={{0,1},{1,0},{2,3},{3,2},{4,5},{5,4},{6,7},{7,6},{8,9},{9,8},{10,11... | collective-permute-start | bytes 557576 | tf_op jit(solution)/shard_map/ppermute | solution.py:678
  12.8 1.0 %copy-start.4 = (f32[4,64,128]{2,1,0:T(8,128)S(1)}, f32[4,64,128]{2,1,0:T(8,128)}, u32[]{:S(2)}) copy-start(f32[4,64,128]{2,1,0:T(8,128)} %lam.3) | copy-start | bytes 393220
  12.8 1.0 %copy-start.5 = (f32[4,64,128]{2,1,0:T(8,128)S(1)}, f32[4,64,128]{2,1,0:T(8,128)}, u32[]{:S(2)}) copy-start(f32[4,64,128]{2,1,0:T(8,128)} %mu.3) | copy-start | bytes 393220
  12.8 9.6 %collective-permute-start.5 = (f32[363,128]{1,0:T(8,128)S(1)}, f32[363,128]{1,0:T(8,128)S(1)}, u32[]{:S(2)}, u32[]{:S(2)}) collective-permute-start(f32[363,128]{1,0:T(8,128)S(1)} %get-tuple-element.29), channel_id=1, source_target_pairs={{1,2},{2,1},{3,4},{4,3},{5,6},{6,5},{7,8},{8,7},{9,10},{10,9},{11,... | collective-permute-start | bytes 557576 | tf_op jit(solution)/shard_map/ppermute | solution.py:678
  13.7 0.7 %copy-start.8 = (s32[64]{0:T(128)S(1)}, s32[64]{0:T(128)}, u32[]{:S(2)}) copy-start(s32[64]{0:T(128)} %param.18) | copy-start | bytes 772
  13.7 1.5 %collective-permute-start.6 = (f32[320,128]{1,0:T(8,128)S(1)}, f32[320,128]{1,0:T(8,128)S(1)}, u32[]{:S(2)}, u32[]{:S(2)}) collective-permute-start(f32[320,128]{1,0:T(8,128)S(1)} %near_columns.1), channel_id=1, source_target_pairs={{0,16},{16,0},{1,17},{17,1},{2,18},{18,2},{3,19},{19,3},{4,20},{20... | collective-permute-start | bytes 491528 | tf_op jit(solution)/shard_map/ppermute | solution.py:685
  13.8 1.4 %collective-permute-start.3 = (f32[64,128]{1,0:T(8,128)S(1)}, f32[64,128]{1,0:T(8,128)S(1)}, u32[]{:S(2)}, u32[]{:S(2)}) collective-permute-start(f32[64,128]{1,0:T(8,128)S(1)} %edge_rows.1), channel_id=1, source_target_pairs={{0,16},{16,0},{1,17},{17,1},{2,18},{18,2},{3,19},{19,3},{4,20},{20... | collective-permute-start | bytes 98312 | tf_op jit(solution)/shard_map/ppermute | solution.py:685
  24.7 4.1 %copy-start.9 = (f32[64]{0:T(128)S(1)}, f32[64]{0:T(128)}, u32[]{:S(2)}) copy-start(f32[64]{0:T(128)} %param.19) | copy-start | bytes 772
  24.7 18.1 %collective-permute-start.7 = (f32[634,128]{1,0:T(8,128)}, f32[634,128]{1,0:T(8,128)S(1)}, u32[]{:S(2)}, u32[]{:S(2)}) collective-permute-start(f32[634,128]{1,0:T(8,128)} %get-tuple-element.36), channel_id=1, source_target_pairs={{0,1},{1,0},{2,3},{3,2},{4,5},{5,4},{6,7},{7,6},{8,9},{9,8},{10,11... | collective-permute-start | bytes 973832 | tf_op jit(solution)/shard_map/ppermute | solution.py:678
  28.1 14.7 %collective-permute-start.8 = (f32[634,128]{1,0:T(8,128)}, f32[634,128]{1,0:T(8,128)S(1)}, u32[]{:S(2)}, u32[]{:S(2)}) collective-permute-start(f32[634,128]{1,0:T(8,128)} %get-tuple-element.37), channel_id=1, source_target_pairs={{1,2},{2,1},{3,4},{4,3},{5,6},{6,5},{7,8},{8,7},{9,10},{10,9},{11,... | collective-permute-start | bytes 973832 | tf_op jit(solution)/shard_map/ppermute | solution.py:678
  29.9 15.5 %all-to-all-start = ((f32[32,8,128]{2,1,0:T(8,128)}), f32[32,8,128]{2,1,0:T(8,128)S(1)}, u32[]{:S(2)}, u32[]{:S(2)}) async-start(f32[32,8,128]{2,1,0:T(8,128)} %floor_parts.1), calls=%async_computation | async-start | bytes 262144 | tf_op jit(solution)/shard_map/all_to_all | solution.py:767

commit v6 on v5

--- a/solution.py
+++ b/solution.py
@@ -15,8 +15,9 @@
 F32 = jnp.float32
 SIDE = 8
 WINDOW = 8
-DEEP = (4, 3, 3, 3, 3)
-PACK = sum(DEEP)
+DEEP = (4, 3, 2, 3, 3)
+CORNER = (2, 1, 2, 2, 2)
+LINES = 6
 NEEDED = {"s": 5, "v": 3, "b": 3}
 LAST_NEEDED = 2
 LAYERS = 9
@@ -111,10 +112,6 @@
     )
 
 
-def far_strip(rows, sec):
-    return jnp.where(sec == 0, rows[-SIDE:], rows[:SIDE])
-
-
 def yz_terms(s, comp, x, base, rows, weights):
     fw, bw = weights
     here = slice(base, base + rows)
@@ -139,6 +136,11 @@
         return None if halo is None else halo(source, j)
 
     return along_x(ahead, x, get) + yz_terms(s, comp, x, base, rows, weights)
+
+
+def halo_share(comp, x, cx, halo):
+    source, ahead = STRESS_X[comp]
+    return along_x(ahead, x, lambda j: None if 0 <= j < cx else halo(source, j))
 
 
 def own_share(s, comp, i, base, rows):
@@ -337,34 +339,31 @@
     rows, own = depth.shape
     at = 0
     for k in range(own // 128 + 1):
-        for f, n in enumerate(DEEP):
+        for f, n in enumerate(DEEP if k < own // 128 else CORNER):
             field = ocean_field(state, depth, wet, near, f, k)
             edges[0, at : at + n, :] = field[rows - n :]
             edges[1, at : at + n, :] = field[:n]
             at += n
 
 
-def first_round(s, v, b, strips, pay_a, pay_b, s_pad):
+def first_round(s, v, b, strips, pay_a, pay_b, s_pad, v_part):
     odd, sec, _ = place()
     _, cx, cy, nz = s.shape
     weights = depth_weights(nz)
     rows = cy + 2 * SIDE
     load_stress(s, strips, s_pad, sec)
-    made = {}
-
-    def velocity(c, x):
-        if (c, x) not in made:
+    for x in range(cx):
+        scale = DT * with_strip(b[x], strip(strips, 9, x, cx), sec)
+        for c in range(3):
             old = with_strip(v[c, x], strip(strips, 6 + c, x, cx), sec)
-            scale = DT * with_strip(b[x], strip(strips, 9, x, cx), sec)
-            made[c, x] = old + scale * force(s_pad, c, x, SIDE, rows, weights)
-        return made[c, x]
+            v_part[c, x] = old + scale * force(s_pad, c, x, SIDE, rows, weights)
 
     def layer(kind, c, x):
-        return velocity(c, x)[SIDE : SIDE + cy] if kind == "v" else b[x]
+        return v_part[c, x, SIDE : SIDE + cy, :] if kind == "v" else b[x]
 
     def edge(kind, c, x):
         if kind == "v":
-            return far_strip(velocity(c, x), sec)
+            return jnp.where(sec == 0, v_part[c, x, SIDE + cy :, :], v_part[c, x, 0:SIDE, :])
         return strip(strips, c if kind == "s" else 9, x, cx)
 
     early, late = first_lists(cx)
@@ -388,8 +387,8 @@
 
 
 def whole_step(
-    s,
-    v,
+    s_pad,
+    v_part,
     b,
     lam,
     mu,
@@ -405,17 +404,15 @@
     pay_a,
     pay_b,
     b_near,
-    s_pad,
     v_pad,
     halo_s,
     halo_v,
     halo_b,
 ):
     odd, sec, _ = place()
-    _, cx, cy, nz = s.shape
+    cx, cy, nz = b.shape
     weights = depth_weights(nz)
     rows = cy + 2 * SIDE
-    load_stress(s, strips, s_pad, sec)
     index_s, index_v = halo_stress(cx), halo_velocity(cx)
     own, rest = first_received(odd, cx, cy, early_a, early_b, late_a, late_b)
     for key, k in index_s.items():
@@ -433,9 +430,10 @@
     for x in range(cx):
         scale = DT * with_strip(b[x], strip(strips, 9, x, cx), sec)
         for c in range(3):
-            old = with_strip(v[c, x], strip(strips, 6 + c, x, cx), sec)
-            terms = force(s_pad, c, x, SIDE, rows, weights, lambda k, j: halo_s[index_s[k, j]])
-            new = old + scale * terms
+            new = v_part[c, x]
+            terms = halo_share(c, x, cx, lambda k, j: halo_s[index_s[k, j]])
+            if terms is not None:
+                new = new + scale * terms
             v_out[c, x] = new
             v_pad[c, x, 0:SIDE, :] = nothing
             v_pad[c, x, SIDE : SIDE + rows, :] = new
@@ -541,18 +539,18 @@
         v[2, x, own, :] + DT * b[x] * force(s, 2, x, SIDE, cy, weights) for x in range(cx)
     ]
     lines = [floor_line(layers[x], layers[x + 1]) for x in range(0, cx, 2)]
-    last = s[4, cx - 1, own, :]
-    lines.append(floor_line(last, last))
-    lines.append(floor_line(s[4, cx - 2, own, :], s[4, 0, own, :]))
+    lines.append(floor_line(s[4, cx - 1, own, :], s[4, cx - 2, own, :]))
+    lines.append(floor_line(s[4, 0, own, :], (-FAR * DT) * b[cx - 1]))
     lines.append(floor_line(DT * b[0], DT * b[1]))
-    lines.append(floor_line(jnp.zeros((cy, nz), F32), (-FAR * DT) * b[cx - 1]))
     lines.append(info[...])
     row = lax.broadcasted_iota(jnp.int32, (SIDE, 2 * cy), 0)
-    tiled = jnp.zeros((SIDE, 2 * cy), F32)
-    for k, line in enumerate(lines):
-        tiled = jnp.where(row == k, line, tiled)
-    for k in range(parts.shape[0]):
-        parts[k] = tiled
+    period = 3 * SIDE
+    for k in range(0, period, SIDE):
+        tiled = jnp.zeros((SIDE, 2 * cy), F32)
+        for j in range(SIDE):
+            tiled = jnp.where(row == j, lines[(k + j) % LINES], tiled)
+        for at in range(k, parts.shape[0], period):
+            parts[at : at + SIDE, :] = tiled
 
 
 def column(line, first, count):
@@ -572,7 +570,7 @@
     at = start
     for k in range(columns // 128):
         lanes = slice(k * 128, (k + 1) * 128)
-        for f, n in enumerate(DEEP):
+        for f, n in enumerate(DEEP if k < own // 128 else CORNER):
             here = ocean_field(state, depth, wet_ref, near, f, k)
             a, b = from_a[at : at + n, :], from_b[at : at + n, :]
             low, high = jnp.where(odd, a, b), jnp.where(odd, b, a)
@@ -601,8 +599,12 @@
     depth, wet = ocean_ref[3], ocean_ref[4]
     window = min(WINDOW, count)
     base = jnp.clip(tile - REACH - 1, 0, count - window)
-    below = patches[sec * count + jnp.maximum(tile - 1, 0)][6:7]
-    above = patches[sec * count + jnp.minimum(tile + 1, count - 1)][6:7]
+
+    def told(half, k):
+        return patches[pl.ds((half * count + k) * LINES, LINES), :]
+
+    below = told(sec, jnp.maximum(tile - 1, 0))[5:6]
+    above = told(sec, jnp.minimum(tile + 1, count - 1))[5:6]
     line = info[...]
     marks = [
         jnp.concatenate(
@@ -627,12 +629,14 @@
         for k in range(-1, window + 1):
             here = jnp.clip(base + k, 0, count - 1)
             there = (here == base + k).astype(F32)
-            tiles.append(patches[half * count + here] * there)
+            tiles.append(told(half, here) * there)
         levels = [jnp.zeros((total, 128), F32) for _ in range(2)]
         for k in range(window):
             below, this, above = tiles[k], tiles[k + 1], tiles[k + 2]
-            first = this[0:1] + this[4:5] * (near * below[2:3] + far * below[3:4])
-            second = this[1:2] + this[5:6] * above[3:4]
+            last = pltpu.roll(below[2:3], width, 1)
+            last = near * jnp.where(left, below[2:3], last) + far * last
+            first = this[0:1] + this[4:5] * last
+            second = this[1:2] + jnp.where(left, 0.0, this[3:4]) * pltpu.roll(above[3:4], width, 1)
             mine = owner == float(k)
             levels = [jnp.where(mine, q, level) for q, level in zip((first, second), levels)]
         uplift.append(levels)
@@ -663,7 +667,7 @@
         in_specs=ins if isinstance(ins, list) else [ins] * len(operands),
         out_specs=where if isinstance(where, list) else [where] * len(outs),
         scratch_shapes=scratch,
-        compiler_params=pltpu.CompilerParams(vmem_limit_bytes=grant * 1024 * 1024),
+        compiler_params=pltpu.CompilerParams(vmem_limit_bytes=int(grant * 1024 * 1024)),
         cost_estimate=pl.CostEstimate(
             flops=moved * weight, bytes_accessed=moved * weight, transcendentals=0
         ),
@@ -714,23 +718,25 @@
         ins=ANY,
         grant=60,
     )
+    strips = across(edges.reshape(10 * cx * SIDE, nz))
     early_a, early_b = exchange(pay_a, pay_b, count)
-    strips = across(edges.reshape(10 * cx * SIDE, nz))
     early_list, late_list = first_lists(cx)
-    per = (columns // 128 + 1) * PACK
+    per = columns // 128 * sum(DEEP) + sum(CORNER)
     late = len(late_list[0]) * cy + sum(thin_counts(early_list) + thin_counts(late_list))
-    pay_a, pay_b = call(
+    pay_a, pay_b, stresses, velocity = call(
         first_round,
         "first_round",
-        [(late, nz), (late, nz)],
-        [pltpu.VMEM((6, cx, tall + 2 * SIDE, nz), F32)],
+        [(late, nz), (late, nz), (6, cx, tall + 2 * SIDE, nz), (3, cx, tall, nz)],
+        [],
         [stresses, velocity, buoyancy, strips],
     )
     late_a, late_b = exchange(pay_a, pay_b, count)
 
-    source, share, lame, shear, ocean_state, depth_map, wet_mask, _, _ = lax.optimization_barrier(
-        (intersection_src, intersection_share, lame_first, shear_mod)
-        + (ocean_state, depth_map, wet_mask, early_a, early_b)
+    source, share, lame, shear, _ = lax.optimization_barrier(
+        (intersection_src, intersection_share, lame_first, shear_mod, early_b)
+    )
+    ocean_state, depth_map, wet_mask, _ = lax.optimization_barrier(
+        (ocean_state, depth_map, wet_mask, early_a)
     )
     (edges,) = call(edge_rows, "edge_rows", [(2 * cx * SIDE, nz)], [], [lame, shear])
     more_strips = across(edges)
@@ -747,7 +753,6 @@
         [(3, cx, tall, nz), (6, cx, tall, nz), second, second]
         + [(4 * cy + cx * SIDE, nz)],
         [
-            pltpu.VMEM((6, cx, tall + 2 * SIDE, nz), F32),
             pltpu.VMEM((3, cx, tall + 2 * SIDE, nz), F32),
             halo,
             halo,
@@ -760,11 +765,12 @@
     (parts,) = call(
         floor_parts,
         "floor_parts",
-        [(2 * count, SIDE, 2 * cy)],
+        [(2 * count * LINES, 2 * cy)],
         [],
         [stresses, velocity, buoyancy, info],
     )
-    patches = lax.all_to_all(parts, ("sec", "tile"), 0, 0)
+    parts = parts.reshape(2 * count * LINES // 2, 2, 2 * cy)
+    patches = lax.all_to_all(parts, ("sec", "tile"), 0, 0, tiled=True).reshape(-1, 2 * cy)
     velocity, stresses, done = call(
         functools.partial(last_step, per),
         "last_step",

time: 46.9 us -> 46.3 us (0.987)
  starting transfers between devices: 21 us -> 19.2 us
  waiting for transfers between devices: 15.9 us -> 17.4 us
    ppermute x6, waiting for transfers between devices: 12.5 us -> 15.4 us  [swap(): return lax.ppermute(pay, 'tile', pairs)]
    ppermute x6, starting transfers between devices: 12.8 us -> 11 us  [swap(): return lax.ppermute(pay, 'tile', pairs)]
    all_to_all x1, waiting for transfers between devices: 0.91 us -> 0.18 us  [shards(): lax.all_to_all(parts, ('sec', 'tile'), 0, 0, tiled=True).reshape(-1, 2 * cy)]
    ppermute x3, waiting for transfers between devices: 2.43 us -> 1.78 us  [across(): return lax.ppermute(pay, 'sec', [(0, 1), (1, 0)])]
where the time goes in v6:
time: 46.3 us; the launch traced here: 46 us
  starting transfers between devices  19.2 us (41%)
  waiting for transfers between devices  17.4 us (38%)
  Pallas kernels  8.5 us (18%)
  between operations  0.87 us (2%)
    ppermute x6, waiting for transfers between devices, swap(): return lax.ppermute(pay, 'tile', pairs)  15.4 us
    ppermute x6, starting transfers between devices, swap(): return lax.ppermute(pay, 'tile', pairs)  11 us
    pallas_call x9, Pallas kernels, call(): pl.pallas_call(body, name=name, out_shape=shapes, in_specs=ins if isinsta...  8.5 us
    all_to_all x1, starting transfers between devices, shards(): lax.all_to_all(parts, ('sec', 'tile'), 0, 0, tiled=True).reshape(-1, 2 * cy)  7.55 us
    ppermute x3, waiting for transfers between devices, across(): return lax.ppermute(pay, 'sec', [(0, 1), (1, 0)])  1.78 us
  transfers between devices with their start and end apart: 10, of which 6 were waited for; matrix products, arithmetic and copies ran while one was open for 0% of the time, Pallas kernels for 7%

profile of v6, /device:TPU:0, one launch (start us, length us, event | category | flops | bytes accessed | tf_op | source)
XLA Modules:
  0.0 46.0 jit_solution(11778299283747854)
XLA Ops:
  0.7 2.1 %opening.1 = (f32[384,128]{1,0:T(8,128)}, f32[384,128]{1,0:T(8,128)}, f32[10,4,8,128]{3,2,1,0:T(8,128)}) custom-call(f32[6,4,64,128]{3,2,1,0:T(8,128)} %s.3, f32[3,4,64,128]{3,2,1,0:T(8,128)} %v.3, f32[4,64,128]{2,1,0:T(8,128)} %b.9), custom_call_target="tpu_custom_call" | custom-call | flops 1867776 | bytes 1867776 | tf_op jit(solution)/shard_map/opening/pallas_call | solution.py:663
  2.8 0.0 copy-start.4
  2.8 0.0 copy-start.5
  2.8 3.0 %collective-permute-start.3 = (f32[384,128]{1,0:T(8,128)}, f32[384,128]{1,0:T(8,128)S(1)}, u32[]{:S(2)}, u32[]{:S(2)}) collective-permute-start(f32[384,128]{1,0:T(8,128)} %get-tuple-element.31), channel_id=1, source_target_pairs={{0,1},{1,0},{2,3},{3,2},{4,5},{5,4},{6,7},{7,6},{8,9},{9,8},{10,11... | collective-permute-start | bytes 589832 | tf_op jit(solution)/shard_map/ppermute | solution.py:682
  5.8 0.0 collective-permute-start
  5.8 0.7 %collective-permute-start.1 = (f32[384,128]{1,0:T(8,128)}, f32[384,128]{1,0:T(8,128)S(1)}, u32[]{:S(2)}, u32[]{:S(2)}) collective-permute-start(f32[384,128]{1,0:T(8,128)} %get-tuple-element.28), channel_id=1, source_target_pairs={{1,2},{2,1},{3,4},{4,3},{5,6},{6,5},{7,8},{8,7},{9,10},{10,9},{11,... | collective-permute-start | bytes 589832 | tf_op jit(solution)/shard_map/ppermute | solution.py:682
  6.5 0.9 %collective-permute-done.strips = f32[320,128]{1,0:T(8,128)S(1)} collective-permute-done((f32[320,128]{1,0:T(8,128)}, f32[320,128]{1,0:T(8,128)S(1)}, u32[]{:S(2)}, u32[]{:S(2)}) %collective-permute-start) | collective-permute-done | bytes 163872 | tf_op jit(solution)/shard_map/ppermute | solution.py:689
  7.4 0.0 copy-done.3
  7.4 0.5 %first_round.1 = (f32[363,128]{1,0:T(8,128)S(1)}, f32[363,128]{1,0:T(8,128)S(1)}, f32[6,4,96,128]{3,2,1,0:T(8,128)S(1)}, f32[3,4,80,128]{3,2,1,0:T(8,128)S(1)}) custom-call(f32[6,4,64,128]{3,2,1,0:T(8,128)S(1)} %copy-done.1, f32[3,4,64,128]{3,2,1,0:T(8,128)S(1)} %copy-done.3, f32[4,64,128]{2,1,0:T(8,128)S(1)} %copy-done, ...), custom_call_target="tpu_custom_call" | custom-call | flops 3517440 | bytes 3517440 | tf_op jit(solution)/shard_map/first_round/pallas_call | solution.py:663
  7.9 3.4 %collective-permute-start.4 = (f32[363,128]{1,0:T(8,128)S(1)}, f32[363,128]{1,0:T(8,128)S(1)}, u32[]{:S(2)}, u32[]{:S(2)}) collective-permute-start(f32[363,128]{1,0:T(8,128)S(1)} %get-tuple-element.32), channel_id=1, source_target_pairs={{0,1},{1,0},{2,3},{3,2},{4,5},{5,4},{6,7},{7,6},{8,9},{9,8},{10,11... | collective-permute-start | bytes 557576 | tf_op jit(solution)/shard_map/ppermute | solution.py:682
  11.3 0.7 %collective-permute-start.5 = (f32[363,128]{1,0:T(8,128)S(1)}, f32[363,128]{1,0:T(8,128)S(1)}, u32[]{:S(2)}, u32[]{:S(2)}) collective-permute-start(f32[363,128]{1,0:T(8,128)S(1)} %get-tuple-element.33), channel_id=1, source_target_pairs={{1,2},{2,1},{3,4},{4,3},{5,6},{6,5},{7,8},{8,7},{9,10},{10,9},{11,... | collective-permute-start | bytes 557576 | tf_op jit(solution)/shard_map/ppermute | solution.py:682
  12.0 0.0 collective-permute-done.3.early_a
  12.1 0.1 collective-permute-start.6
  12.1 0.0 collective-permute-done.1.early_b
  12.2 0.0 copy-done.4
  12.2 0.0 copy-done.5
  12.2 0.5 %collective-permute-start.2 = (f32[64,128]{1,0:T(8,128)S(1)}, f32[64,128]{1,0:T(8,128)S(1)}, u32[]{:S(2)}, u32[]{:S(2)}) collective-permute-start(f32[64,128]{1,0:T(8,128)S(1)} %edge_rows.1), channel_id=1, source_target_pairs={{0,16},{16,0},{1,17},{17,1},{2,18},{18,2},{3,19},{19,3},{4,20},{20... | collective-permute-start | bytes 98312 | tf_op jit(solution)/shard_map/ppermute | solution.py:689
  12.7 0.8 %collective-permute-done.6.near = f32[320,128]{1,0:T(8,128)S(1)} collective-permute-done((f32[320,128]{1,0:T(8,128)S(1)}, f32[320,128]{1,0:T(8,128)S(1)}, u32[]{:S(2)}, u32[]{:S(2)}) %collective-permute-start.6) | collective-permute-done | bytes 163872 | tf_op jit(solution)/shard_map/ppermute | solution.py:689
  13.5 0.1 collective-permute-done.2.more_strips
  13.6 9.6 %collective-permute-done.4.late_a = f32[363,128]{1,0:T(8,128)S(1)} collective-permute-done((f32[363,128]{1,0:T(8,128)S(1)}, f32[363,128]{1,0:T(8,128)S(1)}, u32[]{:S(2)}, u32[]{:S(2)}) %collective-permute-start.4) | collective-permute-done | bytes 185888 | tf_op jit(solution)/shard_map/ppermute | solution.py:682
  23.2 0.0 collective-permute-done.5.late_b
  23.2 1.8 %whole_step.1 = (f32[3,4,80,128]{3,2,1,0:T(8,128)S(1)}, f32[6,4,80,128]{3,2,1,0:T(8,128)S(1)}, f32[625,128]{1,0:T(8,128)}, f32[625,128]{1,0:T(8,128)}, f32[288,128]{1,0:T(8,128)S(1)}) custom-call(f32[6,4,96,128]{3,2,1,0:T(8,128)S(1)} %get-tuple-element.26.s_pad, f32[3,4,80,128]{3,2,1,0:T(8,128)S(1)} %get-tuple-element.27.v_part, f32[4,64,128]{2,1,0:T(8,128)S(1)} %copy-done, ...), custom_call_target="tpu_custom_call" | custom-call | flops 5327872 | bytes 5327872 | tf_op jit(solution)/shard_map/whole_step/pallas_call | solution.py:663
  25.1 2.7 %collective-permute-start.7 = (f32[625,128]{1,0:T(8,128)}, f32[625,128]{1,0:T(8,128)S(1)}, u32[]{:S(2)}, u32[]{:S(2)}) collective-permute-start(f32[625,128]{1,0:T(8,128)} %get-tuple-element.40), channel_id=1, source_target_pairs={{0,1},{1,0},{2,3},{3,2},{4,5},{5,4},{6,7},{7,6},{8,9},{9,8},{10,11... | collective-permute-start | bytes 960008 | tf_op jit(solution)/shard_map/ppermute | solution.py:682
  27.7 0.7 %collective-permute-start.8 = (f32[625,128]{1,0:T(8,128)}, f32[625,128]{1,0:T(8,128)S(1)}, u32[]{:S(2)}, u32[]{:S(2)}) collective-permute-start(f32[625,128]{1,0:T(8,128)} %get-tuple-element.41), channel_id=1, source_target_pairs={{1,2},{2,1},{3,4},{4,3},{5,6},{6,5},{7,8},{8,7},{9,10},{10,9},{11,... | collective-permute-start | bytes 960008 | tf_op jit(solution)/shard_map/ppermute | solution.py:682
  28.4 0.1 maximum_bitcast_fusion.info
  28.5 1.0 %floor_parts.1 = f32[192,128]{1,0:T(8,128)} custom-call(f32[6,4,80,128]{3,2,1,0:T(8,128)S(1)} %get-tuple-element.37.s, f32[3,4,80,128]{3,2,1,0:T(8,128)S(1)} %get-tuple-element.38.v, f32[4,64,128]{2,1,0:T(8,128)S(1)} %copy-done, f32[1,128]{1,0:T(1,128)S(1)} %maximum_bitcast_fusion.info), custom_call_target="tpu_custom_call" | custom-call | flops 1704448 | bytes 1704448 | tf_op jit(solution)/shard_map/floor_parts/pallas_call | solution.py:663
  29.5 7.6 %all-to-all-start = ((f32[96,2,128]{2,1,0:T(2,128)}), f32[96,2,128]{2,1,0:T(2,128)S(1)}, u32[]{:S(2)}, u32[]{:S(2)}) async-start(f32[96,2,128]{2,1,0:T(2,128)} %bitcast.2), calls=%async_computation | async-start | bytes 196608 | tf_op jit(solution)/shard_map/all_to_all | solution.py:773
  37.0 5.8 %collective-permute-done.7.from_a = f32[625,128]{1,0:T(8,128)S(1)} collective-permute-done((f32[625,128]{1,0:T(8,128)}, f32[625,128]{1,0:T(8,128)S(1)}, u32[]{:S(2)}, u32[]{:S(2)}) %collective-permute-start.7) | collective-permute-done | bytes 320032 | tf_op jit(solution)/shard_map/ppermute | solution.py:682
  42.8 0.0 collective-permute-done.8.from_b
  42.8 1.7 %last_step.1 = (f32[3,4,64,128]{3,2,1,0:T(8,128)}, f32[6,4,64,128]{3,2,1,0:T(8,128)}, f32[8,128]{1,0:T(8,128)S(1)}) custom-call(f32[6,4,80,128]{3,2,1,0:T(8,128)S(1)} %get-tuple-element.37.s, f32[3,4,80,128]{3,2,1,0:T(8,128)S(1)} %get-tuple-element.38.v, f32[4,64,128]{2,1,0:T(8,128)S(1)} %copy-done, f32[4,64,128]{2,1,0:T(8,128)S(1)} %copy-done.4, ...), custom_call_target="tpu_custom_call" | custom-call | flops 3838976 | bytes 3838976 | tf_op jit(solution)/shard_map/last_step/pallas_call | solution.py:663
  44.5 0.2 all-to-all-done
  44.7 1.3 %ocean_steps.1 = f32[3,64,256]{2,1,0:T(8,128)} custom-call(f32[625,128]{1,0:T(8,128)S(1)} %collective-permute-done.7.from_a, f32[625,128]{1,0:T(8,128)S(1)} %collective-permute-done.8.from_b, f32[320,128]{1,0:T(8,128)S(1)} %collective-permute-done.6.near, f32[3,64,256]{2,1,0:T(8,128)S(1)} %copy-done.2, f32[64,256]{1,0:T(8,128)S(1)} %copy-done.6, ...), custom_call_target="tpu_custom_call" | custom-call | flops 1431040 | bytes 1431040 | tf_op jit(solution)/shard_map/ocean_steps/pallas_call | solution.py:663
  (19 shorter events, 0.1 us)
Async XLA Ops:
  0.6 6.8 %copy-start.3 = (f32[3,4,64,128]{3,2,1,0:T(8,128)S(1)}, f32[3,4,64,128]{3,2,1,0:T(8,128)}, u32[]{:S(2)}) copy-start(f32[3,4,64,128]{3,2,1,0:T(8,128)} %v.3) | copy-start | bytes 1179652
  0.6 6.8 %copy-start.1 = (f32[6,4,64,128]{3,2,1,0:T(8,128)S(1)}, f32[6,4,64,128]{3,2,1,0:T(8,128)}, u32[]{:S(2)}) copy-start(f32[6,4,64,128]{3,2,1,0:T(8,128)} %s.3) | copy-start | bytes 2359300
  0.7 6.8 %copy-start = (f32[4,64,128]{2,1,0:T(8,128)S(1)}, f32[4,64,128]{2,1,0:T(8,128)}, u32[]{:S(2)}) copy-start(f32[4,64,128]{2,1,0:T(8,128)} %b.9) | copy-start | bytes 393220
  0.7 11.3 %copy-start.2 = (f32[3,64,256]{2,1,0:T(8,128)S(1)}, f32[3,64,256]{2,1,0:T(8,128)}, u32[]{:S(2)}) copy-start(f32[3,64,256]{2,1,0:T(8,128)} %state.2) | copy-start | bytes 589828
  0.7 11.3 %copy-start.6 = (f32[64,256]{1,0:T(8,128)S(1)}, f32[64,256]{1,0:T(8,128)}, u32[]{:S(2)}) copy-start(f32[64,256]{1,0:T(8,128)} %depth.2) | copy-start | bytes 196612
  0.7 11.3 %copy-start.7 = (s32[64,256]{1,0:T(8,128)S(1)}, s32[64,256]{1,0:T(8,128)}, u32[]{:S(2)}) copy-start(s32[64,256]{1,0:T(8,128)} %wet_ref) | copy-start | bytes 196612
  2.8 9.4 %copy-start.4 = (f32[4,64,128]{2,1,0:T(8,128)S(1)}, f32[4,64,128]{2,1,0:T(8,128)}, u32[]{:S(2)}) copy-start(f32[4,64,128]{2,1,0:T(8,128)} %lam.3) | copy-start | bytes 393220
  2.8 9.4 %copy-start.5 = (f32[4,64,128]{2,1,0:T(8,128)S(1)}, f32[4,64,128]{2,1,0:T(8,128)}, u32[]{:S(2)}) copy-start(f32[4,64,128]{2,1,0:T(8,128)} %mu.3) | copy-start | bytes 393220
  2.8 9.2 %collective-permute-start.3 = (f32[384,128]{1,0:T(8,128)}, f32[384,128]{1,0:T(8,128)S(1)}, u32[]{:S(2)}, u32[]{:S(2)}) collective-permute-start(f32[384,128]{1,0:T(8,128)} %get-tuple-element.31), channel_id=1, source_target_pairs={{0,1},{1,0},{2,3},{3,2},{4,5},{5,4},{6,7},{7,6},{8,9},{9,8},{10,11... | collective-permute-start | bytes 589832 | tf_op jit(solution)/shard_map/ppermute | solution.py:682
  5.8 1.6 %collective-permute-start = (f32[320,128]{1,0:T(8,128)}, f32[320,128]{1,0:T(8,128)S(1)}, u32[]{:S(2)}, u32[]{:S(2)}) collective-permute-start(f32[320,128]{1,0:T(8,128)} %bitcast.6), channel_id=1, source_target_pairs={{0,16},{16,0},{1,17},{17,1},{2,18},{18,2},{3,19},{19,3},{4,20},{20... | collective-permute-start | bytes 491528 | tf_op jit(solution)/shard_map/ppermute | solution.py:689
  5.8 6.4 %collective-permute-start.1 = (f32[384,128]{1,0:T(8,128)}, f32[384,128]{1,0:T(8,128)S(1)}, u32[]{:S(2)}, u32[]{:S(2)}) collective-permute-start(f32[384,128]{1,0:T(8,128)} %get-tuple-element.28), channel_id=1, source_target_pairs={{1,2},{2,1},{3,4},{4,3},{5,6},{6,5},{7,8},{8,7},{9,10},{10,9},{11,... | collective-permute-start | bytes 589832 | tf_op jit(solution)/shard_map/ppermute | solution.py:682
  7.9 15.3 %collective-permute-start.4 = (f32[363,128]{1,0:T(8,128)S(1)}, f32[363,128]{1,0:T(8,128)S(1)}, u32[]{:S(2)}, u32[]{:S(2)}) collective-permute-start(f32[363,128]{1,0:T(8,128)S(1)} %get-tuple-element.32), channel_id=1, source_target_pairs={{0,1},{1,0},{2,3},{3,2},{4,5},{5,4},{6,7},{7,6},{8,9},{9,8},{10,11... | collective-permute-start | bytes 557576 | tf_op jit(solution)/shard_map/ppermute | solution.py:682
  11.3 11.9 %collective-permute-start.5 = (f32[363,128]{1,0:T(8,128)S(1)}, f32[363,128]{1,0:T(8,128)S(1)}, u32[]{:S(2)}, u32[]{:S(2)}) collective-permute-start(f32[363,128]{1,0:T(8,128)S(1)} %get-tuple-element.33), channel_id=1, source_target_pairs={{1,2},{2,1},{3,4},{4,3},{5,6},{6,5},{7,8},{8,7},{9,10},{10,9},{11,... | collective-permute-start | bytes 557576 | tf_op jit(solution)/shard_map/ppermute | solution.py:682
  12.1 1.5 %collective-permute-start.6 = (f32[320,128]{1,0:T(8,128)S(1)}, f32[320,128]{1,0:T(8,128)S(1)}, u32[]{:S(2)}, u32[]{:S(2)}) collective-permute-start(f32[320,128]{1,0:T(8,128)S(1)} %near_columns.1), channel_id=1, source_target_pairs={{0,16},{16,0},{1,17},{17,1},{2,18},{18,2},{3,19},{19,3},{4,20},{20... | collective-permute-start | bytes 491528 | tf_op jit(solution)/shard_map/ppermute | solution.py:689
  12.2 1.4 %collective-permute-start.2 = (f32[64,128]{1,0:T(8,128)S(1)}, f32[64,128]{1,0:T(8,128)S(1)}, u32[]{:S(2)}, u32[]{:S(2)}) collective-permute-start(f32[64,128]{1,0:T(8,128)S(1)} %edge_rows.1), channel_id=1, source_target_pairs={{0,16},{16,0},{1,17},{17,1},{2,18},{18,2},{3,19},{19,3},{4,20},{20... | collective-permute-start | bytes 98312 | tf_op jit(solution)/shard_map/ppermute | solution.py:689
  23.2 5.2 %copy-start.8 = (s32[64]{0:T(128)S(1)}, s32[64]{0:T(128)}, u32[]{:S(2)}) copy-start(s32[64]{0:T(128)} %param.18) | copy-start | bytes 772
  23.2 5.2 %copy-start.9 = (f32[64]{0:T(128)S(1)}, f32[64]{0:T(128)}, u32[]{:S(2)}) copy-start(f32[64]{0:T(128)} %param.19) | copy-start | bytes 772
  25.1 17.7 %collective-permute-start.7 = (f32[625,128]{1,0:T(8,128)}, f32[625,128]{1,0:T(8,128)S(1)}, u32[]{:S(2)}, u32[]{:S(2)}) collective-permute-start(f32[625,128]{1,0:T(8,128)} %get-tuple-element.40), channel_id=1, source_target_pairs={{0,1},{1,0},{2,3},{3,2},{4,5},{5,4},{6,7},{7,6},{8,9},{9,8},{10,11... | collective-permute-start | bytes 960008 | tf_op jit(solution)/shard_map/ppermute | solution.py:682
  27.7 15.1 %collective-permute-start.8 = (f32[625,128]{1,0:T(8,128)}, f32[625,128]{1,0:T(8,128)S(1)}, u32[]{:S(2)}, u32[]{:S(2)}) collective-permute-start(f32[625,128]{1,0:T(8,128)} %get-tuple-element.41), channel_id=1, source_target_pairs={{1,2},{2,1},{3,4},{4,3},{5,6},{6,5},{7,8},{8,7},{9,10},{10,9},{11,... | collective-permute-start | bytes 960008 | tf_op jit(solution)/shard_map/ppermute | solution.py:682
  29.5 15.2 %all-to-all-start = ((f32[96,2,128]{2,1,0:T(2,128)}), f32[96,2,128]{2,1,0:T(2,128)S(1)}, u32[]{:S(2)}, u32[]{:S(2)}) async-start(f32[96,2,128]{2,1,0:T(2,128)} %bitcast.2), calls=%async_computation | async-start | bytes 196608 | tf_op jit(solution)/shard_map/all_to_all | solution.py:773

commit v7 on v6

--- a/solution.py
+++ b/solution.py
@@ -13,6 +13,7 @@
 DT = 0.15
 ODT = 0.3
 F32 = jnp.float32
+EDGE = 4
 SIDE = 8
 WINDOW = 8
 DEEP = (4, 3, 2, 3, 3)
@@ -194,14 +195,10 @@
     return [max(NEEDED[upper[0]], NEEDED[lower[0]]) for upper, lower in zip(*lists)]
 
 
-def send_thin(odd, sec, lists, counts, edge, pay_a, pay_b, at):
+def send_thin(odd, lists, counts, edge, pay_a, pay_b, at):
     for upper, lower, n in zip(*lists, counts):
 
-        def rows(key):
-            whole = edge(*key)
-            return jnp.where(sec == 0, whole[:n], whole[SIDE - n :])
-
-        send(odd, rows(upper), rows(lower), pay_a, pay_b, at)
+        send(odd, edge(*upper, n), edge(*lower, n), pay_a, pay_b, at)
         at += n
 
 
@@ -361,17 +358,19 @@
     def layer(kind, c, x):
         return v_part[c, x, SIDE : SIDE + cy, :] if kind == "v" else b[x]
 
-    def edge(kind, c, x):
+    def edge(kind, c, x, n):
         if kind == "v":
-            return jnp.where(sec == 0, v_part[c, x, SIDE + cy :, :], v_part[c, x, 0:SIDE, :])
-        return strip(strips, c if kind == "s" else 9, x, cx)
+            past = slice(SIDE + cy, SIDE + cy + n)
+            return jnp.where(sec == 0, v_part[c, x, past, :], v_part[c, x, SIDE - n : SIDE, :])
+        whole = strip(strips, c if kind == "s" else 9, x, cx)
+        return jnp.where(sec == 0, whole[:n], whole[SIDE - n :])
 
     early, late = first_lists(cx)
     send_layers(odd, *late, layer, pay_a, pay_b, 0)
     at = len(late[0]) * cy
     for lists in (early, late):
         counts = thin_counts(lists)
-        send_thin(odd, sec, lists, counts, edge, pay_a, pay_b, at)
+        send_thin(odd, lists, counts, edge, pay_a, pay_b, at)
         at += sum(counts)
 
 
@@ -408,6 +407,7 @@
     halo_s,
     halo_v,
     halo_b,
+    materials,
 ):
     odd, sec, _ = place()
     cx, cy, nz = b.shape
@@ -434,34 +434,39 @@
             terms = halo_share(c, x, cx, lambda k, j: halo_s[index_s[k, j]])
             if terms is not None:
                 new = new + scale * terms
-            v_out[c, x] = new
             v_pad[c, x, 0:SIDE, :] = nothing
             v_pad[c, x, SIDE : SIDE + rows, :] = new
             v_pad[c, x, SIDE + rows :, :] = nothing
+            v_out[c, x] = v_pad[c, x, SIDE + EDGE : SIDE + rows - EDGE, :]
     for (c, i), k in index_v.items():
         halo_v[k] = halo_v[k] + DT * halo_b[index_b[i]] * own_share(s_pad, c, i, SIDE, rows)
+    kept = slice(EDGE, rows - EDGE)
+    base, fewer = SIDE + EDGE, rows - 2 * EDGE
+    halo = lambda c, j: halo_v[index_v[c, j], kept, :]
     for x in range(cx):
-        parts = strains(v_pad, lambda c, j: halo_v[index_v[c, j]], x, SIDE, rows, weights)
-        lam_rows = with_strip(lam[x], strip(more_strips, 0, x, cx), sec)
-        mu_rows = with_strip(mu[x], strip(more_strips, 1, x, cx), sec)
-        for c, change in enumerate(stress_change(lam_rows, mu_rows, parts)):
-            s_out[c, x] = s_pad[c, x, SIDE : SIDE + rows, :] + change
+        parts = strains(v_pad, halo, x, base, fewer, weights)
+        materials[0] = with_strip(lam[x], strip(more_strips, 0, x, cx), sec)
+        materials[1] = with_strip(mu[x], strip(more_strips, 1, x, cx), sec)
+        changes = stress_change(materials[0, kept, :], materials[1, kept, :], parts)
+        for c, change in enumerate(changes):
+            s_out[c, x] = s_pad[c, x, base : base + fewer, :] + change
 
     def layer(kind, c, x):
         if kind == "s":
-            return s_out[c, x, SIDE : SIDE + cy, :]
-        old = v_out[c, x, SIDE : SIDE + cy, :]
-        return old + DT * b[x] * force(s_out, c, x, SIDE, cy, weights)
-
-    def edge(_, c, x):
-        return jnp.where(sec == 0, s_out[c, x, SIDE + cy :, :], s_out[c, x, 0:SIDE, :])
+            return s_out[c, x, EDGE : EDGE + cy, :]
+        old = v_out[c, x, EDGE : EDGE + cy, :]
+        return old + DT * b[x] * force(s_out, c, x, EDGE, cy, weights)
+
+    def edge(_, c, x, n):
+        past = slice(EDGE + cy, EDGE + cy + n)
+        return jnp.where(sec == 0, s_out[c, x, past, :], s_out[c, x, EDGE - n : EDGE, :])
 
     layers, edges = second_lists(cx)
     send_layers(odd, *layers, layer, pay_a, pay_b, 0)
     counts = [LAST_NEEDED] * len(edges[0])
     at = LAYERS * cy
     send(odd, sea[0], sea[1], pay_a, pay_b, at)
-    send_thin(odd, sec, edges, counts, edge, pay_a, pay_b, at + sea.shape[1])
+    send_thin(odd, edges, counts, edge, pay_a, pay_b, at + sea.shape[1])
 
 
 def last_step(
@@ -476,7 +481,6 @@
     from_b,
     v_out,
     s_out,
-    done,
     v_rows,
     b_rows,
     halo_s,
@@ -484,12 +488,11 @@
     made,
     sems,
 ):
-    done[...] = jnp.zeros(done.shape, F32)
     odd, sec, _ = place()
     cx, cy, nz = b.shape
     weights = depth_weights(nz)
-    half = SIDE // 2
-    rows = cy + SIDE
+    first, rows = EDGE - LAST_NEEDED, cy + 2 * LAST_NEEDED
+    here = slice(SIDE - LAST_NEEDED, SIDE - LAST_NEEDED + rows)
     index_s, index_v = halo_stress(cx), halo_velocity(cx)
     layers, edges = second_lists(cx)
     own = received(odd, layers, [cy] * LAYERS, from_a, from_b, cx, 0)
@@ -500,26 +503,24 @@
     for x in range(cx):
         part = slice(4 * cy + x * SIDE, 4 * cy + (x + 1) * SIDE)
         b_rows[...] = with_strip(b[x], b_near[part, :], sec)
-        scale = DT * b_rows[half : half + rows, :]
+        scale = DT * b_rows[here, :]
         for c in range(3):
-            terms = force(
-                s, c, x, half, rows, weights, lambda k, j: halo_s[index_s[k, j], half : half + rows, :]
-            )
-            v_rows[c, x, half : half + rows, :] = v[c, x, half : half + rows, :] + scale * terms
+            halo = lambda k, j: halo_s[index_s[k, j], here, :]
+            terms = force(s, c, x, first, rows, weights, halo)
+            v_rows[c, x, here, :] = v[c, x, first : first + rows, :] + scale * terms
     copies = [pltpu.make_async_copy(v_rows.at[:, :, pl.ds(SIDE, cy), :], v_out, sems.at[cx])]
     copies[0].start()
     for (c, i), k in index_v.items():
         at = (i + 2 if i < 0 else i - cx + 2) * cy
         scale = DT * b_near[at : at + cy, :]
-        halo_v[k] = own["v", c, i]() + scale * own_share(s, c, i, SIDE, cy)
+        halo_v[k] = own["v", c, i]() + scale * own_share(s, c, i, EDGE, cy)
     for x in range(cx):
         parts = strains(v_rows, lambda c, j: halo_v[index_v[c, j]], x, SIDE, cy, weights)
         for c, change in enumerate(stress_change(lam[x], mu[x], parts)):
-            made[c, x] = s[c, x, SIDE : SIDE + cy, :] + change
+            made[c, x] = s[c, x, EDGE : EDGE + cy, :] + change
         copies.append(pltpu.make_async_copy(made.at[:, x], s_out.at[:, x], sems.at[x]))
         copies[-1].start()
-    for copy in copies:
-        copy.wait()
+    return copies
 
 
 def floor_line(left, right):
@@ -534,9 +535,9 @@
 def floor_parts(s, v, b, info, parts):
     cx, cy, nz = b.shape
     weights = depth_weights(nz)
-    own = slice(SIDE, SIDE + cy)
+    own = slice(EDGE, EDGE + cy)
     layers = [
-        v[2, x, own, :] + DT * b[x] * force(s, 2, x, SIDE, cy, weights) for x in range(cx)
+        v[2, x, own, :] + DT * b[x] * force(s, 2, x, EDGE, cy, weights) for x in range(cx)
     ]
     lines = [floor_line(layers[x], layers[x + 1]) for x in range(0, cx, 2)]
     lines.append(floor_line(s[4, cx - 1, own, :], s[4, cx - 2, own, :]))
@@ -561,7 +562,7 @@
 
 
 def ocean_steps(
-    start, from_a, from_b, near, state, depth, wet_ref, info, patches, _, ocean_out, ocean_ref
+    start, from_a, from_b, near, state, depth, wet_ref, info, patches, ocean_out, ocean_ref, send_out
 ):
     odd, sec, tile = place()
     count = lax.axis_size("tile")
@@ -643,14 +644,95 @@
     uplift = uplift[0] + [jnp.where(sec == 0, uplift[1][0], uplift[1][1])]
     uplift = jnp.concatenate(uplift, axis=1)
     lift = ODT * (share * wet * uplift)
-    for _ in range(2):
+    part = slice(SIDE, SIDE + rows)
+    for step in range(2):
         u = wet * (u - ODT * down(eta))
         v_sea = wet * (v_sea - ODT * across(eta))
+        if step == 1:
+            ocean_out[1] = u[part, :own]
+            ocean_out[2] = v_sea[part, :own]
+            send_out(slice(1, 3))
         eta = inside * (eta - ODT * (down(depth * u) + across(depth * v_sea)) + lift)
-    part = slice(SIDE, SIDE + rows)
     ocean_out[0] = eta[part, :own]
-    ocean_out[1] = u[part, :own]
-    ocean_out[2] = v_sea[part, :own]
+    send_out(slice(0, 1))
+
+
+def finish(
+    sea_rows,
+    s,
+    v,
+    b,
+    lam,
+    mu,
+    b_near,
+    from_a,
+    from_b,
+    near,
+    state,
+    depth,
+    wet,
+    info,
+    patches,
+    v_out,
+    s_out,
+    ocean_out,
+    v_rows,
+    b_rows,
+    halo_s,
+    halo_v,
+    made,
+    ocean_ref,
+    ocean_made,
+    sems,
+    ocean_sems,
+):
+    cx, cy, _ = b.shape
+    copies = last_step(
+        sea_rows,
+        s,
+        v,
+        b,
+        lam,
+        mu,
+        b_near,
+        from_a,
+        from_b,
+        v_out,
+        s_out,
+        v_rows,
+        b_rows,
+        halo_s,
+        halo_v,
+        made,
+        sems,
+    )
+
+    def send_out(part):
+        size = part.stop - part.start
+        here = (pl.ds(part.start, size),)
+        copies.append(
+            pltpu.make_async_copy(
+                ocean_made.at[here], ocean_out.at[here], ocean_sems.at[part.start]
+            )
+        )
+        copies[-1].start()
+
+    ocean_steps(
+        LAYERS * cy,
+        from_a,
+        from_b,
+        near,
+        state,
+        depth,
+        wet,
+        info,
+        patches,
+        ocean_made,
+        ocean_ref,
+        send_out,
+    )
+    for copy in copies:
+        copy.wait()
 
 
 VMEM = pl.BlockSpec(memory_space=pltpu.VMEM)
@@ -750,13 +832,14 @@
     velocity, stresses, pay_a, pay_b, b_near = call(
         whole_step,
         "whole_step",
-        [(3, cx, tall, nz), (6, cx, tall, nz), second, second]
+        [(3, cx, cy + 2 * EDGE, nz), (6, cx, cy + 2 * EDGE, nz), second, second]
         + [(4 * cy + cx * SIDE, nz)],
         [
             pltpu.VMEM((3, cx, tall + 2 * SIDE, nz), F32),
             halo,
             halo,
             pltpu.VMEM((4, tall, nz), F32),
+            pltpu.VMEM((2, tall, nz), F32),
         ],
         [stresses, velocity, buoyancy, lame_first, shear_mod, strips, more_strips]
         + [early_a, early_b, late_a, late_b, edges],
@@ -771,28 +854,24 @@
     )
     parts = parts.reshape(2 * count * LINES // 2, 2, 2 * cy)
     patches = lax.all_to_all(parts, ("sec", "tile"), 0, 0, tiled=True).reshape(-1, 2 * cy)
-    velocity, stresses, done = call(
-        functools.partial(last_step, per),
-        "last_step",
-        [(3, cx, cy, nz), (6, cx, cy, nz), (8, 128)],
+    velocity, stresses, ocean_state = call(
+        functools.partial(finish, per),
+        "finish",
+        [(3, cx, cy, nz), (6, cx, cy, nz), ocean_state.shape],
         [
             pltpu.VMEM((3, cx, tall, nz), F32),
             pltpu.VMEM((tall, nz), F32),
             halo,
             pltpu.VMEM((LAYERS, cy, nz), F32),
             pltpu.VMEM((6, cx, cy, nz), F32),
+            pltpu.VMEM((len(DEEP), rows + 2 * SIDE, columns + 128), F32),
+            pltpu.VMEM(ocean_state.shape, F32),
             pltpu.SemaphoreType.DMA((cx + 1,)),
+            pltpu.SemaphoreType.DMA((2,)),
         ],
         [stresses, velocity, buoyancy, lame_first, shear_mod, b_near]
-        + [from_a, from_b],
-        where=[ANY, ANY, VMEM],
-    )
-    (ocean_state,) = call(
-        functools.partial(ocean_steps, LAYERS * cy),
-        "ocean_steps",
-        [ocean_state.shape],
-        [pltpu.VMEM((len(DEEP), rows + 2 * SIDE, columns + 128), F32)],
-        [from_a, from_b, near] + sea + [info, patches, done],
+        + [from_a, from_b, near] + sea + [info, patches],
+        where=ANY,
     )
     return velocity, stresses, ocean_state
 

time: 46.3 us -> 46 us (level)
  blocking collectives: 0 us -> 15 us
  starting transfers between devices: 19.2 us -> 11.7 us
  waiting for transfers between devices: 17.4 us -> 11.4 us
  Pallas kernels: 8.5 us -> 6.68 us
    all_to_all x0 -> x1, blocking collectives: none -> 15 us  [shards(): lax.all_to_all(parts, ('sec', 'tile'), 0, 0, tiled=True).reshape(-1, 2 * cy)]
    all_to_all x1 -> x0, starting transfers between devices: 7.55 us -> none  [shards(): lax.all_to_all(parts, ('sec', 'tile'), 0, 0, tiled=True).reshape(-1, 2 * cy)]
    ppermute x6, waiting for transfers between devices: 15.4 us -> 9.61 us  [swap(): return lax.ppermute(pay, 'tile', pairs)]
    pallas_call x9 -> x8, Pallas kernels: 8.5 us -> 6.68 us  [call(): pl.pallas_call(body, name=name, out_shape=shapes, in_specs=ins if isinsta...]
  transfers between devices with their start and end apart: 10 -> 9, of which waited for: 6 -> 4; matrix products, arithmetic and copies ran while one was open for 0% -> 0% of each run, Pallas kernels for 7% -> 2%
where the time goes in v7:
time: 46 us; the launch traced here: 45.8 us
  blocking collectives  15 us (33%)
  starting transfers between devices  11.7 us (25%)
  waiting for transfers between devices  11.4 us (25%)
  Pallas kernels  6.68 us (15%)
  between operations  0.87 us (2%)
    all_to_all x1, blocking collectives, shards(): lax.all_to_all(parts, ('sec', 'tile'), 0, 0, tiled=True).reshape(-1, 2 * cy)  15 us
    ppermute x6, starting transfers between devices, swap(): return lax.ppermute(pay, 'tile', pairs)  11.1 us
    ppermute x6, waiting for transfers between devices, swap(): return lax.ppermute(pay, 'tile', pairs)  9.61 us
    pallas_call x8, Pallas kernels, call(): pl.pallas_call(body, name=name, out_shape=shapes, in_specs=ins if isinsta...  6.68 us
    ppermute x3, waiting for transfers between devices, across(): return lax.ppermute(pay, 'sec', [(0, 1), (1, 0)])  1.78 us
  transfers between devices with their start and end apart: 9, of which 4 were waited for; matrix products, arithmetic and copies ran while one was open for 0% of the time, Pallas kernels for 2%

profile of v7, /device:TPU:0, one launch (start us, length us, event | category | flops | bytes accessed | tf_op | source)
XLA Modules:
  0.0 45.8 jit_solution(17876050090831068989)
XLA Ops:
  0.6 0.0 copy-start.3
  0.6 0.0 copy-start.1
  0.7 0.0 copy-start
  0.7 0.0 copy-start.2
  0.7 0.0 copy-start.6
  0.7 2.1 %opening.1 = (f32[384,128]{1,0:T(8,128)}, f32[384,128]{1,0:T(8,128)}, f32[10,4,8,128]{3,2,1,0:T(8,128)}) custom-call(f32[6,4,64,128]{3,2,1,0:T(8,128)} %s.3, f32[3,4,64,128]{3,2,1,0:T(8,128)} %v.3, f32[4,64,128]{2,1,0:T(8,128)} %b.9), custom_call_target="tpu_custom_call" | custom-call | flops 1867776 | bytes 1867776 | tf_op jit(solution)/shard_map/opening/pallas_call | solution.py:745
  2.8 0.0 copy-start.4
  2.8 0.0 copy-start.5
  2.8 3.0 %collective-permute-start.3 = (f32[384,128]{1,0:T(8,128)}, f32[384,128]{1,0:T(8,128)S(1)}, u32[]{:S(2)}, u32[]{:S(2)}) collective-permute-start(f32[384,128]{1,0:T(8,128)} %get-tuple-element.28), channel_id=1, source_target_pairs={{0,1},{1,0},{2,3},{3,2},{4,5},{5,4},{6,7},{7,6},{8,9},{9,8},{10,11... | collective-permute-start | bytes 589832 | tf_op jit(solution)/shard_map/ppermute | solution.py:764
  5.8 0.0 collective-permute-start
  5.8 0.7 %collective-permute-start.1 = (f32[384,128]{1,0:T(8,128)}, f32[384,128]{1,0:T(8,128)S(1)}, u32[]{:S(2)}, u32[]{:S(2)}) collective-permute-start(f32[384,128]{1,0:T(8,128)} %get-tuple-element.25), channel_id=1, source_target_pairs={{1,2},{2,1},{3,4},{4,3},{5,6},{6,5},{7,8},{8,7},{9,10},{10,9},{11,... | collective-permute-start | bytes 589832 | tf_op jit(solution)/shard_map/ppermute | solution.py:764
  6.5 0.9 %collective-permute-done.strips = f32[320,128]{1,0:T(8,128)S(1)} collective-permute-done((f32[320,128]{1,0:T(8,128)}, f32[320,128]{1,0:T(8,128)S(1)}, u32[]{:S(2)}, u32[]{:S(2)}) %collective-permute-start) | collective-permute-done | bytes 163872 | tf_op jit(solution)/shard_map/ppermute | solution.py:771
  7.4 0.5 %first_round.1 = (f32[363,128]{1,0:T(8,128)S(1)}, f32[363,128]{1,0:T(8,128)S(1)}, f32[6,4,96,128]{3,2,1,0:T(8,128)S(1)}, f32[3,4,80,128]{3,2,1,0:T(8,128)S(1)}) custom-call(f32[6,4,64,128]{3,2,1,0:T(8,128)S(1)} %copy-done.1, f32[3,4,64,128]{3,2,1,0:T(8,128)S(1)} %copy-done.3, f32[4,64,128]{2,1,0:T(8,128)S(1)} %copy-done, ...), custom_call_target="tpu_custom_call" | custom-call | flops 3517440 | bytes 3517440 | tf_op jit(solution)/shard_map/first_round/pallas_call | solution.py:745
  8.0 3.4 %collective-permute-start.4 = (f32[363,128]{1,0:T(8,128)S(1)}, f32[363,128]{1,0:T(8,128)S(1)}, u32[]{:S(2)}, u32[]{:S(2)}) collective-permute-start(f32[363,128]{1,0:T(8,128)S(1)} %get-tuple-element.29), channel_id=1, source_target_pairs={{0,1},{1,0},{2,3},{3,2},{4,5},{5,4},{6,7},{7,6},{8,9},{9,8},{10,11... | collective-permute-start | bytes 557576 | tf_op jit(solution)/shard_map/ppermute | solution.py:764
  11.3 0.7 %collective-permute-start.5 = (f32[363,128]{1,0:T(8,128)S(1)}, f32[363,128]{1,0:T(8,128)S(1)}, u32[]{:S(2)}, u32[]{:S(2)}) collective-permute-start(f32[363,128]{1,0:T(8,128)S(1)} %get-tuple-element.30), channel_id=1, source_target_pairs={{1,2},{2,1},{3,4},{4,3},{5,6},{6,5},{7,8},{8,7},{9,10},{10,9},{11,... | collective-permute-start | bytes 557576 | tf_op jit(solution)/shard_map/ppermute | solution.py:764
  12.0 0.0 collective-permute-done.3.early_a
  12.1 0.1 collective-permute-start.6
  12.2 0.0 collective-permute-done.1.early_b
  12.2 0.5 %collective-permute-start.2 = (f32[64,128]{1,0:T(8,128)S(1)}, f32[64,128]{1,0:T(8,128)S(1)}, u32[]{:S(2)}, u32[]{:S(2)}) collective-permute-start(f32[64,128]{1,0:T(8,128)S(1)} %edge_rows.1), channel_id=1, source_target_pairs={{0,16},{16,0},{1,17},{17,1},{2,18},{18,2},{3,19},{19,3},{4,20},{20... | collective-permute-start | bytes 98312 | tf_op jit(solution)/shard_map/ppermute | solution.py:771
  12.8 0.8 %collective-permute-done.6.near = f32[320,128]{1,0:T(8,128)S(1)} collective-permute-done((f32[320,128]{1,0:T(8,128)S(1)}, f32[320,128]{1,0:T(8,128)S(1)}, u32[]{:S(2)}, u32[]{:S(2)}) %collective-permute-start.6) | collective-permute-done | bytes 163872 | tf_op jit(solution)/shard_map/ppermute | solution.py:771
  13.6 0.1 collective-permute-done.2.more_strips
  13.6 9.6 %collective-permute-done.4.late_a = f32[363,128]{1,0:T(8,128)S(1)} collective-permute-done((f32[363,128]{1,0:T(8,128)S(1)}, f32[363,128]{1,0:T(8,128)S(1)}, u32[]{:S(2)}, u32[]{:S(2)}) %collective-permute-start.4) | collective-permute-done | bytes 185888 | tf_op jit(solution)/shard_map/ppermute | solution.py:764
  23.2 0.0 collective-permute-done.5.late_b
  23.2 1.2 %whole_step.1 = (f32[3,4,72,128]{3,2,1,0:T(8,128)S(1)}, f32[6,4,72,128]{3,2,1,0:T(8,128)S(1)}, f32[625,128]{1,0:T(8,128)S(1)}, f32[625,128]{1,0:T(8,128)S(1)}, f32[288,128]{1,0:T(8,128)S(1)}) custom-call(f32[6,4,96,128]{3,2,1,0:T(8,128)S(1)} %get-tuple-element.23.s_pad, f32[3,4,80,128]{3,2,1,0:T(8,128)S(1)} %get-tuple-element.24.v_part, ...), custom_call_target="tpu_custom_call" | custom-call | flops 5180416 | bytes 5180416 | tf_op jit(solution)/shard_map/whole_step/pallas_call | solution.py:745
  24.4 2.7 %collective-permute-start.7 = (f32[625,128]{1,0:T(8,128)S(1)}, f32[625,128]{1,0:T(8,128)S(1)}, u32[]{:S(2)}, u32[]{:S(2)}) collective-permute-start(f32[625,128]{1,0:T(8,128)S(1)} %get-tuple-element.37), channel_id=1, source_target_pairs={{0,1},{1,0},{2,3},{3,2},{4,5},{5,4},{6,7},{7,6},{8,9},{9,8},{10,11... | collective-permute-start | bytes 960008 | tf_op jit(solution)/shard_map/ppermute | solution.py:764
  27.2 0.7 %collective-permute-start.8 = (f32[625,128]{1,0:T(8,128)S(1)}, f32[625,128]{1,0:T(8,128)S(1)}, u32[]{:S(2)}, u32[]{:S(2)}) collective-permute-start(f32[625,128]{1,0:T(8,128)S(1)} %get-tuple-element.38), channel_id=1, source_target_pairs={{1,2},{2,1},{3,4},{4,3},{5,6},{6,5},{7,8},{8,7},{9,10},{10,9},{11,... | collective-permute-start | bytes 960008 | tf_op jit(solution)/shard_map/ppermute | solution.py:764
  27.9 0.1 maximum_bitcast_fusion.info
  28.0 0.3 floor_parts.1
  28.3 15.0 %all_to_all.5 = f32[96,2,128]{2,1,0:T(2,128)S(1)} all-to-all(f32[96,2,128]{2,1,0:T(2,128)S(1)} %bitcast.6), channel_id=1, replica_groups=mesh['sec'=2,'tile'=16] {'sec','tile'}, dimensions={0} | all-to-all | bytes 196608 | tf_op jit(solution)/shard_map/all_to_all | solution.py:856
  43.3 0.0 collective-permute-done.7.from_a
  43.3 0.0 collective-permute-done.8.from_b
  43.3 2.5 %finish.1 = (f32[3,4,64,128]{3,2,1,0:T(8,128)}, f32[6,4,64,128]{3,2,1,0:T(8,128)}, f32[3,64,256]{2,1,0:T(8,128)}) custom-call(f32[6,4,72,128]{3,2,1,0:T(8,128)S(1)} %get-tuple-element.34.s, f32[3,4,72,128]{3,2,1,0:T(8,128)S(1)} %get-tuple-element.35.v, f32[4,64,128]{2,1,0:T(8,128)S(1)} %copy-done, f32[4,64,128]{2,1,0:T(8,128)S(1)} %copy-done.4, ...), custom_call_target="tpu_custom_call" | custom-call | flops 4474368 | bytes 4474368 | tf_op jit(solution)/shard_map/finish/pallas_call | solution.py:745
  (17 shorter events, 0.1 us)
Async XLA Ops:
  0.6 6.8 %copy-start.3 = (f32[3,4,64,128]{3,2,1,0:T(8,128)S(1)}, f32[3,4,64,128]{3,2,1,0:T(8,128)}, u32[]{:S(2)}) copy-start(f32[3,4,64,128]{3,2,1,0:T(8,128)} %v.3) | copy-start | bytes 1179652
  0.6 6.8 %copy-start.1 = (f32[6,4,64,128]{3,2,1,0:T(8,128)S(1)}, f32[6,4,64,128]{3,2,1,0:T(8,128)}, u32[]{:S(2)}) copy-start(f32[6,4,64,128]{3,2,1,0:T(8,128)} %s.3) | copy-start | bytes 2359300
  0.7 6.8 %copy-start = (f32[4,64,128]{2,1,0:T(8,128)S(1)}, f32[4,64,128]{2,1,0:T(8,128)}, u32[]{:S(2)}) copy-start(f32[4,64,128]{2,1,0:T(8,128)} %b.9) | copy-start | bytes 393220
  0.7 11.4 %copy-start.2 = (f32[3,64,256]{2,1,0:T(8,128)S(1)}, f32[3,64,256]{2,1,0:T(8,128)}, u32[]{:S(2)}) copy-start(f32[3,64,256]{2,1,0:T(8,128)} %state.2) | copy-start | bytes 589828
  0.7 11.4 %copy-start.6 = (f32[64,256]{1,0:T(8,128)S(1)}, f32[64,256]{1,0:T(8,128)}, u32[]{:S(2)}) copy-start(f32[64,256]{1,0:T(8,128)} %depth.2) | copy-start | bytes 196612
  0.7 11.4 %copy-start.7 = (s32[64,256]{1,0:T(8,128)S(1)}, s32[64,256]{1,0:T(8,128)}, u32[]{:S(2)}) copy-start(s32[64,256]{1,0:T(8,128)} %wet.2) | copy-start | bytes 196612
  2.8 9.4 %copy-start.4 = (f32[4,64,128]{2,1,0:T(8,128)S(1)}, f32[4,64,128]{2,1,0:T(8,128)}, u32[]{:S(2)}) copy-start(f32[4,64,128]{2,1,0:T(8,128)} %lam.3) | copy-start | bytes 393220
  2.8 9.4 %copy-start.5 = (f32[4,64,128]{2,1,0:T(8,128)S(1)}, f32[4,64,128]{2,1,0:T(8,128)}, u32[]{:S(2)}) copy-start(f32[4,64,128]{2,1,0:T(8,128)} %mu.3) | copy-start | bytes 393220
  2.8 9.2 %collective-permute-start.3 = (f32[384,128]{1,0:T(8,128)}, f32[384,128]{1,0:T(8,128)S(1)}, u32[]{:S(2)}, u32[]{:S(2)}) collective-permute-start(f32[384,128]{1,0:T(8,128)} %get-tuple-element.28), channel_id=1, source_target_pairs={{0,1},{1,0},{2,3},{3,2},{4,5},{5,4},{6,7},{7,6},{8,9},{9,8},{10,11... | collective-permute-start | bytes 589832 | tf_op jit(solution)/shard_map/ppermute | solution.py:764
  5.8 1.6 %collective-permute-start = (f32[320,128]{1,0:T(8,128)}, f32[320,128]{1,0:T(8,128)S(1)}, u32[]{:S(2)}, u32[]{:S(2)}) collective-permute-start(f32[320,128]{1,0:T(8,128)} %bitcast.7), channel_id=1, source_target_pairs={{0,16},{16,0},{1,17},{17,1},{2,18},{18,2},{3,19},{19,3},{4,20},{20... | collective-permute-start | bytes 491528 | tf_op jit(solution)/shard_map/ppermute | solution.py:771
  5.8 6.4 %collective-permute-start.1 = (f32[384,128]{1,0:T(8,128)}, f32[384,128]{1,0:T(8,128)S(1)}, u32[]{:S(2)}, u32[]{:S(2)}) collective-permute-start(f32[384,128]{1,0:T(8,128)} %get-tuple-element.25), channel_id=1, source_target_pairs={{1,2},{2,1},{3,4},{4,3},{5,6},{6,5},{7,8},{8,7},{9,10},{10,9},{11,... | collective-permute-start | bytes 589832 | tf_op jit(solution)/shard_map/ppermute | solution.py:764
  8.0 15.3 %collective-permute-start.4 = (f32[363,128]{1,0:T(8,128)S(1)}, f32[363,128]{1,0:T(8,128)S(1)}, u32[]{:S(2)}, u32[]{:S(2)}) collective-permute-start(f32[363,128]{1,0:T(8,128)S(1)} %get-tuple-element.29), channel_id=1, source_target_pairs={{0,1},{1,0},{2,3},{3,2},{4,5},{5,4},{6,7},{7,6},{8,9},{9,8},{10,11... | collective-permute-start | bytes 557576 | tf_op jit(solution)/shard_map/ppermute | solution.py:764
  11.3 11.9 %collective-permute-start.5 = (f32[363,128]{1,0:T(8,128)S(1)}, f32[363,128]{1,0:T(8,128)S(1)}, u32[]{:S(2)}, u32[]{:S(2)}) collective-permute-start(f32[363,128]{1,0:T(8,128)S(1)} %get-tuple-element.30), channel_id=1, source_target_pairs={{1,2},{2,1},{3,4},{4,3},{5,6},{6,5},{7,8},{8,7},{9,10},{10,9},{11,... | collective-permute-start | bytes 557576 | tf_op jit(solution)/shard_map/ppermute | solution.py:764
  12.1 1.5 %collective-permute-start.6 = (f32[320,128]{1,0:T(8,128)S(1)}, f32[320,128]{1,0:T(8,128)S(1)}, u32[]{:S(2)}, u32[]{:S(2)}) collective-permute-start(f32[320,128]{1,0:T(8,128)S(1)} %near_columns.1), channel_id=1, source_target_pairs={{0,16},{16,0},{1,17},{17,1},{2,18},{18,2},{3,19},{19,3},{4,20},{20... | collective-permute-start | bytes 491528 | tf_op jit(solution)/shard_map/ppermute | solution.py:771
  12.2 1.4 %collective-permute-start.2 = (f32[64,128]{1,0:T(8,128)S(1)}, f32[64,128]{1,0:T(8,128)S(1)}, u32[]{:S(2)}, u32[]{:S(2)}) collective-permute-start(f32[64,128]{1,0:T(8,128)S(1)} %edge_rows.1), channel_id=1, source_target_pairs={{0,16},{16,0},{1,17},{17,1},{2,18},{18,2},{3,19},{19,3},{4,20},{20... | collective-permute-start | bytes 98312 | tf_op jit(solution)/shard_map/ppermute | solution.py:771
  23.2 4.6 %copy-start.8 = (s32[64]{0:T(128)S(1)}, s32[64]{0:T(128)}, u32[]{:S(2)}) copy-start(s32[64]{0:T(128)} %param.18) | copy-start | bytes 772
  23.2 4.6 %copy-start.9 = (f32[64]{0:T(128)S(1)}, f32[64]{0:T(128)}, u32[]{:S(2)}) copy-start(f32[64]{0:T(128)} %param.19) | copy-start | bytes 772
  24.4 18.9 %collective-permute-start.7 = (f32[625,128]{1,0:T(8,128)S(1)}, f32[625,128]{1,0:T(8,128)S(1)}, u32[]{:S(2)}, u32[]{:S(2)}) collective-permute-start(f32[625,128]{1,0:T(8,128)S(1)} %get-tuple-element.37), channel_id=1, source_target_pairs={{0,1},{1,0},{2,3},{3,2},{4,5},{5,4},{6,7},{7,6},{8,9},{9,8},{10,11... | collective-permute-start | bytes 960008 | tf_op jit(solution)/shard_map/ppermute | solution.py:764
  27.2 16.2 %collective-permute-start.8 = (f32[625,128]{1,0:T(8,128)S(1)}, f32[625,128]{1,0:T(8,128)S(1)}, u32[]{:S(2)}, u32[]{:S(2)}) collective-permute-start(f32[625,128]{1,0:T(8,128)S(1)} %get-tuple-element.38), channel_id=1, source_target_pairs={{1,2},{2,1},{3,4},{4,3},{5,6},{6,5},{7,8},{8,7},{9,10},{10,9},{11,... | collective-permute-start | bytes 960008 | tf_op jit(solution)/shard_map/ppermute | solution.py:764

commit v8 on v7

--- a/solution.py
+++ b/solution.py
@@ -491,7 +491,7 @@
     odd, sec, _ = place()
     cx, cy, nz = b.shape
     weights = depth_weights(nz)
-    first, rows = EDGE - LAST_NEEDED, cy + 2 * LAST_NEEDED
+    rows = cy + 2 * LAST_NEEDED
     here = slice(SIDE - LAST_NEEDED, SIDE - LAST_NEEDED + rows)
     index_s, index_v = halo_stress(cx), halo_velocity(cx)
     layers, edges = second_lists(cx)
@@ -505,9 +505,9 @@
         b_rows[...] = with_strip(b[x], b_near[part, :], sec)
         scale = DT * b_rows[here, :]
         for c in range(3):
-            halo = lambda k, j: halo_s[index_s[k, j], here, :]
-            terms = force(s, c, x, first, rows, weights, halo)
-            v_rows[c, x, here, :] = v[c, x, first : first + rows, :] + scale * terms
+            terms = halo_share(c, x, cx, lambda k, j: halo_s[index_s[k, j], here, :])
+            new = v[c, x, here, :]
+            v_rows[c, x, here, :] = new if terms is None else new + scale * terms
     copies = [pltpu.make_async_copy(v_rows.at[:, :, pl.ds(SIDE, cy), :], v_out, sems.at[cx])]
     copies[0].start()
     for (c, i), k in index_v.items():
@@ -532,13 +532,21 @@
     return jnp.sum(picked, axis=0, keepdims=True)
 
 
-def floor_parts(s, v, b, info, parts):
+def floor_parts(s, v, b, b_near, info, parts, v_part, b_rows):
     cx, cy, nz = b.shape
     weights = depth_weights(nz)
+    _, sec, _ = place()
     own = slice(EDGE, EDGE + cy)
-    layers = [
-        v[2, x, own, :] + DT * b[x] * force(s, 2, x, EDGE, cy, weights) for x in range(cx)
-    ]
+    first, rows = EDGE - LAST_NEEDED, cy + 2 * LAST_NEEDED
+    here = slice(SIDE - LAST_NEEDED, SIDE - LAST_NEEDED + rows)
+    for x in range(cx):
+        part = slice(4 * cy + x * SIDE, 4 * cy + (x + 1) * SIDE)
+        b_rows[...] = with_strip(b[x], b_near[part, :], sec)
+        scale = DT * b_rows[here, :]
+        for c in range(3):
+            terms = force(s, c, x, first, rows, weights)
+            v_part[c, x, here, :] = v[c, x, first : first + rows, :] + scale * terms
+    layers = [v_part[2, x, SIDE : SIDE + cy, :] for x in range(cx)]
     lines = [floor_line(layers[x], layers[x + 1]) for x in range(0, cx, 2)]
     lines.append(floor_line(s[4, cx - 1, own, :], s[4, cx - 2, own, :]))
     lines.append(floor_line(s[4, 0, own, :], (-FAR * DT) * b[cx - 1]))
@@ -845,12 +853,12 @@
         + [early_a, early_b, late_a, late_b, edges],
     )
     from_a, from_b = exchange(pay_a, pay_b, count)
-    (parts,) = call(
+    parts, velocity = call(
         floor_parts,
         "floor_parts",
-        [(2 * count * LINES, 2 * cy)],
-        [],
-        [stresses, velocity, buoyancy, info],
+        [(2 * count * LINES, 2 * cy), (3, cx, tall, nz)],
+        [pltpu.VMEM((tall, nz), F32)],
+        [stresses, velocity, buoyancy, b_near, info],
     )
     parts = parts.reshape(2 * count * LINES // 2, 2, 2 * cy)
     patches = lax.all_to_all(parts, ("sec", "tile"), 0, 0, tiled=True).reshape(-1, 2 * cy)

time: 46 us -> 45.9 us (level)
  transfers between devices with their start and end apart: 9 -> 9, of which waited for: 4 -> 4; matrix products, arithmetic and copies ran while one was open for 0% -> 0% of each run, Pallas kernels for 2% -> 3%
where the time goes in v8:
time: 45.9 us; the launch traced here: 45.7 us
  blocking collectives  15 us (33%)
  starting transfers between devices  11.7 us (25%)
  waiting for transfers between devices  11.4 us (25%)
  Pallas kernels  6.56 us (14%)
  between operations  0.87 us (2%)
    all_to_all x1, blocking collectives, shards(): lax.all_to_all(parts, ('sec', 'tile'), 0, 0, tiled=True).reshape(-1, 2 * cy)  15 us
    ppermute x6, starting transfers between devices, swap(): return lax.ppermute(pay, 'tile', pairs)  11.1 us
    ppermute x6, waiting for transfers between devices, swap(): return lax.ppermute(pay, 'tile', pairs)  9.61 us
    pallas_call x8, Pallas kernels, call(): pl.pallas_call(body, name=name, out_shape=shapes, in_specs=ins if isinsta...  6.56 us
    ppermute x3, waiting for transfers between devices, across(): return lax.ppermute(pay, 'sec', [(0, 1), (1, 0)])  1.78 us
  transfers between devices with their start and end apart: 9, of which 4 were waited for; matrix products, arithmetic and copies ran while one was open for 0% of the time, Pallas kernels for 3%

profile of v8, /device:TPU:0, one launch (start us, length us, event | category | flops | bytes accessed | tf_op | source)
XLA Modules:
  0.0 45.7 jit_solution(4168206323742576264)
XLA Ops:
  0.6 0.0 copy-start.3
  0.6 0.0 copy-start.1
  0.7 0.0 copy-start
  0.7 0.0 copy-start.2
  0.7 0.0 copy-start.6
  0.7 2.1 %opening.1 = (f32[384,128]{1,0:T(8,128)}, f32[384,128]{1,0:T(8,128)}, f32[10,4,8,128]{3,2,1,0:T(8,128)}) custom-call(f32[6,4,64,128]{3,2,1,0:T(8,128)} %s.3, f32[3,4,64,128]{3,2,1,0:T(8,128)} %v.3, f32[4,64,128]{2,1,0:T(8,128)} %b.9), custom_call_target="tpu_custom_call" | custom-call | flops 1867776 | bytes 1867776 | tf_op jit(solution)/shard_map/opening/pallas_call | solution.py:753
  2.8 0.0 copy-start.4
  2.8 0.0 copy-start.5
  2.8 3.0 %collective-permute-start.3 = (f32[384,128]{1,0:T(8,128)}, f32[384,128]{1,0:T(8,128)S(1)}, u32[]{:S(2)}, u32[]{:S(2)}) collective-permute-start(f32[384,128]{1,0:T(8,128)} %get-tuple-element.30), channel_id=1, source_target_pairs={{0,1},{1,0},{2,3},{3,2},{4,5},{5,4},{6,7},{7,6},{8,9},{9,8},{10,11... | collective-permute-start | bytes 589832 | tf_op jit(solution)/shard_map/ppermute | solution.py:772
  5.8 0.0 collective-permute-start
  5.8 0.7 %collective-permute-start.1 = (f32[384,128]{1,0:T(8,128)}, f32[384,128]{1,0:T(8,128)S(1)}, u32[]{:S(2)}, u32[]{:S(2)}) collective-permute-start(f32[384,128]{1,0:T(8,128)} %get-tuple-element.27), channel_id=1, source_target_pairs={{1,2},{2,1},{3,4},{4,3},{5,6},{6,5},{7,8},{8,7},{9,10},{10,9},{11,... | collective-permute-start | bytes 589832 | tf_op jit(solution)/shard_map/ppermute | solution.py:772
  6.5 0.9 %collective-permute-done.strips = f32[320,128]{1,0:T(8,128)S(1)} collective-permute-done((f32[320,128]{1,0:T(8,128)}, f32[320,128]{1,0:T(8,128)S(1)}, u32[]{:S(2)}, u32[]{:S(2)}) %collective-permute-start) | collective-permute-done | bytes 163872 | tf_op jit(solution)/shard_map/ppermute | solution.py:779
  7.4 0.5 %first_round.1 = (f32[363,128]{1,0:T(8,128)S(1)}, f32[363,128]{1,0:T(8,128)S(1)}, f32[6,4,96,128]{3,2,1,0:T(8,128)S(1)}, f32[3,4,80,128]{3,2,1,0:T(8,128)S(1)}) custom-call(f32[6,4,64,128]{3,2,1,0:T(8,128)S(1)} %copy-done.1, f32[3,4,64,128]{3,2,1,0:T(8,128)S(1)} %copy-done.3, f32[4,64,128]{2,1,0:T(8,128)S(1)} %copy-done, ...), custom_call_target="tpu_custom_call" | custom-call | flops 3517440 | bytes 3517440 | tf_op jit(solution)/shard_map/first_round/pallas_call | solution.py:753
  8.0 3.4 %collective-permute-start.4 = (f32[363,128]{1,0:T(8,128)S(1)}, f32[363,128]{1,0:T(8,128)S(1)}, u32[]{:S(2)}, u32[]{:S(2)}) collective-permute-start(f32[363,128]{1,0:T(8,128)S(1)} %get-tuple-element.31), channel_id=1, source_target_pairs={{0,1},{1,0},{2,3},{3,2},{4,5},{5,4},{6,7},{7,6},{8,9},{9,8},{10,11... | collective-permute-start | bytes 557576 | tf_op jit(solution)/shard_map/ppermute | solution.py:772
  11.3 0.7 %collective-permute-start.5 = (f32[363,128]{1,0:T(8,128)S(1)}, f32[363,128]{1,0:T(8,128)S(1)}, u32[]{:S(2)}, u32[]{:S(2)}) collective-permute-start(f32[363,128]{1,0:T(8,128)S(1)} %get-tuple-element.32), channel_id=1, source_target_pairs={{1,2},{2,1},{3,4},{4,3},{5,6},{6,5},{7,8},{8,7},{9,10},{10,9},{11,... | collective-permute-start | bytes 557576 | tf_op jit(solution)/shard_map/ppermute | solution.py:772
  12.0 0.0 collective-permute-done.3.early_a
  12.1 0.1 collective-permute-start.6
  12.2 0.0 collective-permute-done.1.early_b
  12.2 0.5 %collective-permute-start.2 = (f32[64,128]{1,0:T(8,128)S(1)}, f32[64,128]{1,0:T(8,128)S(1)}, u32[]{:S(2)}, u32[]{:S(2)}) collective-permute-start(f32[64,128]{1,0:T(8,128)S(1)} %edge_rows.1), channel_id=1, source_target_pairs={{0,16},{16,0},{1,17},{17,1},{2,18},{18,2},{3,19},{19,3},{4,20},{20... | collective-permute-start | bytes 98312 | tf_op jit(solution)/shard_map/ppermute | solution.py:779
  12.8 0.8 %collective-permute-done.6.near = f32[320,128]{1,0:T(8,128)S(1)} collective-permute-done((f32[320,128]{1,0:T(8,128)S(1)}, f32[320,128]{1,0:T(8,128)S(1)}, u32[]{:S(2)}, u32[]{:S(2)}) %collective-permute-start.6) | collective-permute-done | bytes 163872 | tf_op jit(solution)/shard_map/ppermute | solution.py:779
  13.6 0.1 collective-permute-done.2.more_strips
  13.6 9.6 %collective-permute-done.4.late_a = f32[363,128]{1,0:T(8,128)S(1)} collective-permute-done((f32[363,128]{1,0:T(8,128)S(1)}, f32[363,128]{1,0:T(8,128)S(1)}, u32[]{:S(2)}, u32[]{:S(2)}) %collective-permute-start.4) | collective-permute-done | bytes 185888 | tf_op jit(solution)/shard_map/ppermute | solution.py:772
  23.2 0.0 collective-permute-done.5.late_b
  23.2 1.2 %whole_step.1 = (f32[3,4,72,128]{3,2,1,0:T(8,128)S(1)}, f32[6,4,72,128]{3,2,1,0:T(8,128)S(1)}, f32[625,128]{1,0:T(8,128)S(1)}, f32[625,128]{1,0:T(8,128)S(1)}, f32[288,128]{1,0:T(8,128)S(1)}) custom-call(f32[6,4,96,128]{3,2,1,0:T(8,128)S(1)} %get-tuple-element.25.s_pad, f32[3,4,80,128]{3,2,1,0:T(8,128)S(1)} %get-tuple-element.26.v_part, ...), custom_call_target="tpu_custom_call" | custom-call | flops 5180416 | bytes 5180416 | tf_op jit(solution)/shard_map/whole_step/pallas_call | solution.py:753
  24.4 2.7 %collective-permute-start.7 = (f32[625,128]{1,0:T(8,128)S(1)}, f32[625,128]{1,0:T(8,128)S(1)}, u32[]{:S(2)}, u32[]{:S(2)}) collective-permute-start(f32[625,128]{1,0:T(8,128)S(1)} %get-tuple-element.42), channel_id=1, source_target_pairs={{0,1},{1,0},{2,3},{3,2},{4,5},{5,4},{6,7},{7,6},{8,9},{9,8},{10,11... | collective-permute-start | bytes 960008 | tf_op jit(solution)/shard_map/ppermute | solution.py:772
  27.1 0.7 %collective-permute-start.8 = (f32[625,128]{1,0:T(8,128)S(1)}, f32[625,128]{1,0:T(8,128)S(1)}, u32[]{:S(2)}, u32[]{:S(2)}) collective-permute-start(f32[625,128]{1,0:T(8,128)S(1)} %get-tuple-element.43), channel_id=1, source_target_pairs={{1,2},{2,1},{3,4},{4,3},{5,6},{6,5},{7,8},{8,7},{9,10},{10,9},{11,... | collective-permute-start | bytes 960008 | tf_op jit(solution)/shard_map/ppermute | solution.py:772
  27.8 0.1 maximum_bitcast_fusion.info
  27.9 0.7 %floor_parts.1 = (f32[192,128]{1,0:T(8,128)S(1)}, f32[3,4,80,128]{3,2,1,0:T(8,128)S(1)}) custom-call(f32[6,4,72,128]{3,2,1,0:T(8,128)S(1)} %get-tuple-element.36.s, f32[3,4,72,128]{3,2,1,0:T(8,128)S(1)} %get-tuple-element.37.v, f32[4,64,128]{2,1,0:T(8,128)S(1)} %copy-done, f32[288,128]{1,0:T(8,128)S(1)} %get-tuple-element.38.b_near, ...), custom_call_target="tpu_custom_call" | custom-call | flops 2195968 | bytes 2195968 | tf_op jit(solution)/shard_map/floor_parts/pallas_call | solution.py:753
  28.6 15.0 %all_to_all.5 = f32[96,2,128]{2,1,0:T(2,128)S(1)} all-to-all(f32[96,2,128]{2,1,0:T(2,128)S(1)} %bitcast.6), channel_id=1, replica_groups=mesh['sec'=2,'tile'=16] {'sec','tile'}, dimensions={0} | all-to-all | bytes 196608 | tf_op jit(solution)/shard_map/all_to_all | solution.py:864
  43.6 0.0 collective-permute-done.7.from_a
  43.6 0.0 collective-permute-done.8.from_b
  43.6 2.1 %finish.1 = (f32[3,4,64,128]{3,2,1,0:T(8,128)}, f32[6,4,64,128]{3,2,1,0:T(8,128)}, f32[3,64,256]{2,1,0:T(8,128)}) custom-call(f32[6,4,72,128]{3,2,1,0:T(8,128)S(1)} %get-tuple-element.36.s, f32[3,4,80,128]{3,2,1,0:T(8,128)S(1)} %get-tuple-element.41.v, f32[4,64,128]{2,1,0:T(8,128)S(1)} %copy-done, f32[4,64,128]{2,1,0:T(8,128)S(1)} %copy-done.4, ...), custom_call_target="tpu_custom_call" | custom-call | flops 4523520 | bytes 4523520 | tf_op jit(solution)/shard_map/finish/pallas_call | solution.py:753
  (17 shorter events, 0.1 us)
Async XLA Ops:
  0.6 6.8 %copy-start.3 = (f32[3,4,64,128]{3,2,1,0:T(8,128)S(1)}, f32[3,4,64,128]{3,2,1,0:T(8,128)}, u32[]{:S(2)}) copy-start(f32[3,4,64,128]{3,2,1,0:T(8,128)} %v.3) | copy-start | bytes 1179652
  0.6 6.8 %copy-start.1 = (f32[6,4,64,128]{3,2,1,0:T(8,128)S(1)}, f32[6,4,64,128]{3,2,1,0:T(8,128)}, u32[]{:S(2)}) copy-start(f32[6,4,64,128]{3,2,1,0:T(8,128)} %s.3) | copy-start | bytes 2359300
  0.7 6.8 %copy-start = (f32[4,64,128]{2,1,0:T(8,128)S(1)}, f32[4,64,128]{2,1,0:T(8,128)}, u32[]{:S(2)}) copy-start(f32[4,64,128]{2,1,0:T(8,128)} %b.9) | copy-start | bytes 393220
  0.7 11.4 %copy-start.2 = (f32[3,64,256]{2,1,0:T(8,128)S(1)}, f32[3,64,256]{2,1,0:T(8,128)}, u32[]{:S(2)}) copy-start(f32[3,64,256]{2,1,0:T(8,128)} %state.2) | copy-start | bytes 589828
  0.7 11.4 %copy-start.6 = (f32[64,256]{1,0:T(8,128)S(1)}, f32[64,256]{1,0:T(8,128)}, u32[]{:S(2)}) copy-start(f32[64,256]{1,0:T(8,128)} %depth.2) | copy-start | bytes 196612
  0.7 11.4 %copy-start.7 = (s32[64,256]{1,0:T(8,128)S(1)}, s32[64,256]{1,0:T(8,128)}, u32[]{:S(2)}) copy-start(s32[64,256]{1,0:T(8,128)} %wet.2) | copy-start | bytes 196612
  2.8 9.4 %copy-start.4 = (f32[4,64,128]{2,1,0:T(8,128)S(1)}, f32[4,64,128]{2,1,0:T(8,128)}, u32[]{:S(2)}) copy-start(f32[4,64,128]{2,1,0:T(8,128)} %lam.3) | copy-start | bytes 393220
  2.8 9.4 %copy-start.5 = (f32[4,64,128]{2,1,0:T(8,128)S(1)}, f32[4,64,128]{2,1,0:T(8,128)}, u32[]{:S(2)}) copy-start(f32[4,64,128]{2,1,0:T(8,128)} %mu.3) | copy-start | bytes 393220
  2.8 9.2 %collective-permute-start.3 = (f32[384,128]{1,0:T(8,128)}, f32[384,128]{1,0:T(8,128)S(1)}, u32[]{:S(2)}, u32[]{:S(2)}) collective-permute-start(f32[384,128]{1,0:T(8,128)} %get-tuple-element.30), channel_id=1, source_target_pairs={{0,1},{1,0},{2,3},{3,2},{4,5},{5,4},{6,7},{7,6},{8,9},{9,8},{10,11... | collective-permute-start | bytes 589832 | tf_op jit(solution)/shard_map/ppermute | solution.py:772
  5.8 1.6 %collective-permute-start = (f32[320,128]{1,0:T(8,128)}, f32[320,128]{1,0:T(8,128)S(1)}, u32[]{:S(2)}, u32[]{:S(2)}) collective-permute-start(f32[320,128]{1,0:T(8,128)} %bitcast.7), channel_id=1, source_target_pairs={{0,16},{16,0},{1,17},{17,1},{2,18},{18,2},{3,19},{19,3},{4,20},{20... | collective-permute-start | bytes 491528 | tf_op jit(solution)/shard_map/ppermute | solution.py:779
  5.8 6.4 %collective-permute-start.1 = (f32[384,128]{1,0:T(8,128)}, f32[384,128]{1,0:T(8,128)S(1)}, u32[]{:S(2)}, u32[]{:S(2)}) collective-permute-start(f32[384,128]{1,0:T(8,128)} %get-tuple-element.27), channel_id=1, source_target_pairs={{1,2},{2,1},{3,4},{4,3},{5,6},{6,5},{7,8},{8,7},{9,10},{10,9},{11,... | collective-permute-start | bytes 589832 | tf_op jit(solution)/shard_map/ppermute | solution.py:772
  8.0 15.3 %collective-permute-start.4 = (f32[363,128]{1,0:T(8,128)S(1)}, f32[363,128]{1,0:T(8,128)S(1)}, u32[]{:S(2)}, u32[]{:S(2)}) collective-permute-start(f32[363,128]{1,0:T(8,128)S(1)} %get-tuple-element.31), channel_id=1, source_target_pairs={{0,1},{1,0},{2,3},{3,2},{4,5},{5,4},{6,7},{7,6},{8,9},{9,8},{10,11... | collective-permute-start | bytes 557576 | tf_op jit(solution)/shard_map/ppermute | solution.py:772
  11.3 11.9 %collective-permute-start.5 = (f32[363,128]{1,0:T(8,128)S(1)}, f32[363,128]{1,0:T(8,128)S(1)}, u32[]{:S(2)}, u32[]{:S(2)}) collective-permute-start(f32[363,128]{1,0:T(8,128)S(1)} %get-tuple-element.32), channel_id=1, source_target_pairs={{1,2},{2,1},{3,4},{4,3},{5,6},{6,5},{7,8},{8,7},{9,10},{10,9},{11,... | collective-permute-start | bytes 557576 | tf_op jit(solution)/shard_map/ppermute | solution.py:772
  12.1 1.5 %collective-permute-start.6 = (f32[320,128]{1,0:T(8,128)S(1)}, f32[320,128]{1,0:T(8,128)S(1)}, u32[]{:S(2)}, u32[]{:S(2)}) collective-permute-start(f32[320,128]{1,0:T(8,128)S(1)} %near_columns.1), channel_id=1, source_target_pairs={{0,16},{16,0},{1,17},{17,1},{2,18},{18,2},{3,19},{19,3},{4,20},{20... | collective-permute-start | bytes 491528 | tf_op jit(solution)/shard_map/ppermute | solution.py:779
  12.2 1.4 %collective-permute-start.2 = (f32[64,128]{1,0:T(8,128)S(1)}, f32[64,128]{1,0:T(8,128)S(1)}, u32[]{:S(2)}, u32[]{:S(2)}) collective-permute-start(f32[64,128]{1,0:T(8,128)S(1)} %edge_rows.1), channel_id=1, source_target_pairs={{0,16},{16,0},{1,17},{17,1},{2,18},{18,2},{3,19},{19,3},{4,20},{20... | collective-permute-start | bytes 98312 | tf_op jit(solution)/shard_map/ppermute | solution.py:779
  23.2 4.6 %copy-start.8 = (s32[64]{0:T(128)S(1)}, s32[64]{0:T(128)}, u32[]{:S(2)}) copy-start(s32[64]{0:T(128)} %param.18) | copy-start | bytes 772
  23.2 4.6 %copy-start.9 = (f32[64]{0:T(128)S(1)}, f32[64]{0:T(128)}, u32[]{:S(2)}) copy-start(f32[64]{0:T(128)} %param.19) | copy-start | bytes 772
  24.4 19.2 %collective-permute-start.7 = (f32[625,128]{1,0:T(8,128)S(1)}, f32[625,128]{1,0:T(8,128)S(1)}, u32[]{:S(2)}, u32[]{:S(2)}) collective-permute-start(f32[625,128]{1,0:T(8,128)S(1)} %get-tuple-element.42), channel_id=1, source_target_pairs={{0,1},{1,0},{2,3},{3,2},{4,5},{5,4},{6,7},{7,6},{8,9},{9,8},{10,11... | collective-permute-start | bytes 960008 | tf_op jit(solution)/shard_map/ppermute | solution.py:772
  27.1 16.5 %collective-permute-start.8 = (f32[625,128]{1,0:T(8,128)S(1)}, f32[625,128]{1,0:T(8,128)S(1)}, u32[]{:S(2)}, u32[]{:S(2)}) collective-permute-start(f32[625,128]{1,0:T(8,128)S(1)} %get-tuple-element.43), channel_id=1, source_target_pairs={{1,2},{2,1},{3,4},{4,3},{5,6},{6,5},{7,8},{8,7},{9,10},{10,9},{11,... | collective-permute-start | bytes 960008 | tf_op jit(solution)/shard_map/ppermute | solution.py:772

commit v9 on v8

--- a/solution.py
+++ b/solution.py
@@ -66,6 +66,10 @@
     return NEAR * (at(i) - at(i - 1)) - FAR * (at(i + 1) - at(i - 2))
 
 
+def rounded(rows):
+    return -(-rows // 8) * 8
+
+
 def place():
     tile, sec = lax.axis_index("tile"), lax.axis_index("sec")
     return lax.rem(tile, 2) == 1, sec, tile
@@ -366,6 +370,7 @@
         return jnp.where(sec == 0, whole[:n], whole[SIDE - n :])
 
     early, late = first_lists(cx)
+    pay_a[-8:, :] = pay_b[-8:, :] = jnp.zeros((8, nz), F32)
     send_layers(odd, *late, layer, pay_a, pay_b, 0)
     at = len(late[0]) * cy
     for lists in (early, late):
@@ -386,6 +391,7 @@
 
 
 def whole_step(
+    sea_rows,
     s_pad,
     v_part,
     b,
@@ -437,7 +443,8 @@
             v_pad[c, x, 0:SIDE, :] = nothing
             v_pad[c, x, SIDE : SIDE + rows, :] = new
             v_pad[c, x, SIDE + rows :, :] = nothing
-            v_out[c, x] = v_pad[c, x, SIDE + EDGE : SIDE + rows - EDGE, :]
+            v_out[c, x, 0 : rows - 2 * EDGE, :] = v_pad[c, x, SIDE + EDGE : SIDE + rows - EDGE, :]
+            v_out[c, x, rows - 2 * EDGE :, :] = nothing
     for (c, i), k in index_v.items():
         halo_v[k] = halo_v[k] + DT * halo_b[index_b[i]] * own_share(s_pad, c, i, SIDE, rows)
     kept = slice(EDGE, rows - EDGE)
@@ -449,7 +456,8 @@
         materials[1] = with_strip(mu[x], strip(more_strips, 1, x, cx), sec)
         changes = stress_change(materials[0, kept, :], materials[1, kept, :], parts)
         for c, change in enumerate(changes):
-            s_out[c, x] = s_pad[c, x, base : base + fewer, :] + change
+            s_out[c, x, 0:fewer, :] = s_pad[c, x, base : base + fewer, :] + change
+            s_out[c, x, fewer:, :] = nothing
 
     def layer(kind, c, x):
         if kind == "s":
@@ -462,11 +470,12 @@
         return jnp.where(sec == 0, s_out[c, x, past, :], s_out[c, x, EDGE - n : EDGE, :])
 
     layers, edges = second_lists(cx)
+    pay_a[-8:, :] = pay_b[-8:, :] = jnp.zeros((8, nz), F32)
     send_layers(odd, *layers, layer, pay_a, pay_b, 0)
     counts = [LAST_NEEDED] * len(edges[0])
     at = LAYERS * cy
-    send(odd, sea[0], sea[1], pay_a, pay_b, at)
-    send_thin(odd, edges, counts, edge, pay_a, pay_b, at + sea.shape[1])
+    send(odd, sea[0, :sea_rows], sea[1, :sea_rows], pay_a, pay_b, at)
+    send_thin(odd, edges, counts, edge, pay_a, pay_b, at + sea_rows)
 
 
 def last_step(
@@ -570,7 +579,7 @@
 
 
 def ocean_steps(
-    start, from_a, from_b, near, state, depth, wet_ref, info, patches, ocean_out, ocean_ref, send_out
+    start, from_a, from_b, near, state, depth, wet_ref, info, patches, ocean_out, ocean_ref, send_out, told_ref
 ):
     odd, sec, tile = place()
     count = lax.axis_size("tile")
@@ -609,8 +618,11 @@
     window = min(WINDOW, count)
     base = jnp.clip(tile - REACH - 1, 0, count - window)
 
+    told_ref[0 : patches.shape[0], :] = patches[...]
+    told_ref[patches.shape[0] :, :] = jnp.zeros((8, 128), F32)
+
     def told(half, k):
-        return patches[pl.ds((half * count + k) * LINES, LINES), :]
+        return told_ref[pl.ds((half * count + k) * LINES, LINES), :]
 
     below = told(sec, jnp.maximum(tile - 1, 0))[5:6]
     above = told(sec, jnp.minimum(tile + 1, count - 1))[5:6]
@@ -691,6 +703,7 @@
     made,
     ocean_ref,
     ocean_made,
+    told_ref,
     sems,
     ocean_sems,
 ):
@@ -738,6 +751,7 @@
         ocean_made,
         ocean_ref,
         send_out,
+        told_ref,
     )
     for copy in copies:
         copy.wait()
@@ -812,7 +826,7 @@
     early_a, early_b = exchange(pay_a, pay_b, count)
     early_list, late_list = first_lists(cx)
     per = columns // 128 * sum(DEEP) + sum(CORNER)
-    late = len(late_list[0]) * cy + sum(thin_counts(early_list) + thin_counts(late_list))
+    late = len(late_list[0]) * cy + rounded(sum(thin_counts(early_list) + thin_counts(late_list)))
     pay_a, pay_b, stresses, velocity = call(
         first_round,
         "first_round",
@@ -833,14 +847,15 @@
     sea = [ocean_state, depth_map, wet_mask]
     (near,) = call(near_columns, "near_columns", [(len(DEEP) * rows, 128)], [], sea)
     near = across(near)
-    (edges,) = call(ocean_edges, "ocean_edges", [(2, per, 128)], [], sea + [near])
+    (edges,) = call(ocean_edges, "ocean_edges", [(2, rounded(per) + 8, 128)], [], sea + [near])
     info = jnp.concatenate([source.astype(F32), share])[None]
 
-    second = (LAYERS * cy + per + 5 * LAST_NEEDED, nz)
+    kept = cy + 2 * EDGE + 8
+    second = (LAYERS * cy + rounded(per + 5 * LAST_NEEDED), nz)
     velocity, stresses, pay_a, pay_b, b_near = call(
-        whole_step,
+        functools.partial(whole_step, per),
         "whole_step",
-        [(3, cx, cy + 2 * EDGE, nz), (6, cx, cy + 2 * EDGE, nz), second, second]
+        [(3, cx, kept, nz), (6, cx, kept, nz), second, second]
         + [(4 * cy + cx * SIDE, nz)],
         [
             pltpu.VMEM((3, cx, tall + 2 * SIDE, nz), F32),
@@ -874,12 +889,14 @@
             pltpu.VMEM((6, cx, cy, nz), F32),
             pltpu.VMEM((len(DEEP), rows + 2 * SIDE, columns + 128), F32),
             pltpu.VMEM(ocean_state.shape, F32),
+            pltpu.VMEM((2 * count * LINES + 8, 128), F32),
             pltpu.SemaphoreType.DMA((cx + 1,)),
             pltpu.SemaphoreType.DMA((2,)),
         ],
         [stresses, velocity, buoyancy, lame_first, shear_mod, b_near]
         + [from_a, from_b, near] + sea + [info, patches],
         where=ANY,
+        grant=16,
     )
     return velocity, stresses, ocean_state
 

time: 45.9 us -> 45.9 us (level)
  no operation moved by 1% of the time
where the time goes in v9:
time: 45.9 us; the launch traced here: 45.7 us
  blocking collectives  15 us (33%)
  starting transfers between devices  11.7 us (25%)
  waiting for transfers between devices  11.3 us (25%)
  Pallas kernels  6.62 us (14%)
  between operations  0.87 us (2%)
    all_to_all x1, blocking collectives, shards(): lax.all_to_all(parts, ('sec', 'tile'), 0, 0, tiled=True).reshape(-1, 2 * cy)  15 us
    ppermute x6, starting transfers between devices, swap(): return lax.ppermute(pay, 'tile', pairs)  11.1 us
    ppermute x6, waiting for transfers between devices, swap(): return lax.ppermute(pay, 'tile', pairs)  9.54 us
    pallas_call x8, Pallas kernels, call(): pl.pallas_call(body, name=name, out_shape=shapes, in_specs=ins if isinsta...  6.62 us
    ppermute x3, waiting for transfers between devices, across(): return lax.ppermute(pay, 'sec', [(0, 1), (1, 0)])  1.78 us
  transfers between devices with their start and end apart: 9, of which 4 were waited for; matrix products, arithmetic and copies ran while one was open for 0% of the time, Pallas kernels for 3%

profile of v9, /device:TPU:0, one launch (start us, length us, event | category | flops | bytes accessed | tf_op | source)
XLA Modules:
  0.0 45.7 jit_solution(1173179085842363796)
XLA Ops:
  0.6 0.0 copy-start.3
  0.6 0.0 copy-start.1
  0.7 0.0 copy-start
  0.7 0.0 copy-start.2
  0.7 2.1 %opening.1 = (f32[384,128]{1,0:T(8,128)}, f32[384,128]{1,0:T(8,128)}, f32[10,4,8,128]{3,2,1,0:T(8,128)}) custom-call(f32[6,4,64,128]{3,2,1,0:T(8,128)} %s.3, f32[3,4,64,128]{3,2,1,0:T(8,128)} %v.3, f32[4,64,128]{2,1,0:T(8,128)} %b.9), custom_call_target="tpu_custom_call" | custom-call | flops 1867776 | bytes 1867776 | tf_op jit(solution)/shard_map/opening/pallas_call | solution.py:767
  2.8 0.0 copy-start.4
  2.8 0.0 copy-start.5
  2.8 3.0 %collective-permute-start.3 = (f32[384,128]{1,0:T(8,128)}, f32[384,128]{1,0:T(8,128)S(1)}, u32[]{:S(2)}, u32[]{:S(2)}) collective-permute-start(f32[384,128]{1,0:T(8,128)} %get-tuple-element.30), channel_id=1, source_target_pairs={{0,1},{1,0},{2,3},{3,2},{4,5},{5,4},{6,7},{7,6},{8,9},{9,8},{10,11... | collective-permute-start | bytes 589832 | tf_op jit(solution)/shard_map/ppermute | solution.py:786
  5.8 0.0 collective-permute-start
  5.8 0.7 %collective-permute-start.1 = (f32[384,128]{1,0:T(8,128)}, f32[384,128]{1,0:T(8,128)S(1)}, u32[]{:S(2)}, u32[]{:S(2)}) collective-permute-start(f32[384,128]{1,0:T(8,128)} %get-tuple-element.27), channel_id=1, source_target_pairs={{1,2},{2,1},{3,4},{4,3},{5,6},{6,5},{7,8},{8,7},{9,10},{10,9},{11,... | collective-permute-start | bytes 589832 | tf_op jit(solution)/shard_map/ppermute | solution.py:786
  6.5 0.9 %collective-permute-done.strips = f32[320,128]{1,0:T(8,128)S(1)} collective-permute-done((f32[320,128]{1,0:T(8,128)}, f32[320,128]{1,0:T(8,128)S(1)}, u32[]{:S(2)}, u32[]{:S(2)}) %collective-permute-start) | collective-permute-done | bytes 163872 | tf_op jit(solution)/shard_map/ppermute | solution.py:793
  7.4 0.6 %first_round.1 = (f32[368,128]{1,0:T(8,128)S(1)}, f32[368,128]{1,0:T(8,128)S(1)}, f32[6,4,96,128]{3,2,1,0:T(8,128)S(1)}, f32[3,4,80,128]{3,2,1,0:T(8,128)S(1)}) custom-call(f32[6,4,64,128]{3,2,1,0:T(8,128)S(1)} %copy-done.1, f32[3,4,64,128]{3,2,1,0:T(8,128)S(1)} %copy-done.3, f32[4,64,128]{2,1,0:T(8,128)S(1)} %copy-done, ...), custom_call_target="tpu_custom_call" | custom-call | flops 3522560 | bytes 3522560 | tf_op jit(solution)/shard_map/first_round/pallas_call | solution.py:767
  8.0 3.4 %collective-permute-start.4 = (f32[368,128]{1,0:T(8,128)S(1)}, f32[368,128]{1,0:T(8,128)S(1)}, u32[]{:S(2)}, u32[]{:S(2)}) collective-permute-start(f32[368,128]{1,0:T(8,128)S(1)} %get-tuple-element.31), channel_id=1, source_target_pairs={{0,1},{1,0},{2,3},{3,2},{4,5},{5,4},{6,7},{7,6},{8,9},{9,8},{10,11... | collective-permute-start | bytes 565256 | tf_op jit(solution)/shard_map/ppermute | solution.py:786
  11.4 0.7 %collective-permute-start.5 = (f32[368,128]{1,0:T(8,128)S(1)}, f32[368,128]{1,0:T(8,128)S(1)}, u32[]{:S(2)}, u32[]{:S(2)}) collective-permute-start(f32[368,128]{1,0:T(8,128)S(1)} %get-tuple-element.32), channel_id=1, source_target_pairs={{1,2},{2,1},{3,4},{4,3},{5,6},{6,5},{7,8},{8,7},{9,10},{10,9},{11,... | collective-permute-start | bytes 565256 | tf_op jit(solution)/shard_map/ppermute | solution.py:786
  12.1 0.0 collective-permute-done.3.early_a
  12.2 0.1 collective-permute-start.6
  12.2 0.0 collective-permute-done.1.early_b
  12.3 0.5 %collective-permute-start.2 = (f32[64,128]{1,0:T(8,128)S(1)}, f32[64,128]{1,0:T(8,128)S(1)}, u32[]{:S(2)}, u32[]{:S(2)}) collective-permute-start(f32[64,128]{1,0:T(8,128)S(1)} %edge_rows.1), channel_id=1, source_target_pairs={{0,16},{16,0},{1,17},{17,1},{2,18},{18,2},{3,19},{19,3},{4,20},{20... | collective-permute-start | bytes 98312 | tf_op jit(solution)/shard_map/ppermute | solution.py:793
  12.8 0.8 %collective-permute-done.6.near = f32[320,128]{1,0:T(8,128)S(1)} collective-permute-done((f32[320,128]{1,0:T(8,128)S(1)}, f32[320,128]{1,0:T(8,128)S(1)}, u32[]{:S(2)}, u32[]{:S(2)}) %collective-permute-start.6) | collective-permute-done | bytes 163872 | tf_op jit(solution)/shard_map/ppermute | solution.py:793
  13.6 0.1 collective-permute-done.2.more_strips
  13.7 9.5 %collective-permute-done.4.late_a = f32[368,128]{1,0:T(8,128)S(1)} collective-permute-done((f32[368,128]{1,0:T(8,128)S(1)}, f32[368,128]{1,0:T(8,128)S(1)}, u32[]{:S(2)}, u32[]{:S(2)}) %collective-permute-start.4) | collective-permute-done | bytes 188448 | tf_op jit(solution)/shard_map/ppermute | solution.py:786
  23.2 0.0 collective-permute-done.5.late_b
  23.2 1.2 %whole_step.1 = (f32[3,4,80,128]{3,2,1,0:T(8,128)S(1)}, f32[6,4,80,128]{3,2,1,0:T(8,128)S(1)}, f32[632,128]{1,0:T(8,128)S(1)}, f32[632,128]{1,0:T(8,128)S(1)}, f32[288,128]{1,0:T(8,128)S(1)}) custom-call(f32[6,4,96,128]{3,2,1,0:T(8,128)S(1)} %get-tuple-element.25.s_pad, f32[3,4,80,128]{3,2,1,0:T(8,128)S(1)} %get-tuple-element.26.v_part, ...), custom_call_target="tpu_custom_call" | custom-call | flops 5349376 | bytes 5349376 | tf_op jit(solution)/shard_map/whole_step/pallas_call | solution.py:767
  24.4 2.7 %collective-permute-start.7 = (f32[632,128]{1,0:T(8,128)S(1)}, f32[632,128]{1,0:T(8,128)S(1)}, u32[]{:S(2)}, u32[]{:S(2)}) collective-permute-start(f32[632,128]{1,0:T(8,128)S(1)} %get-tuple-element.42), channel_id=1, source_target_pairs={{0,1},{1,0},{2,3},{3,2},{4,5},{5,4},{6,7},{7,6},{8,9},{9,8},{10,11... | collective-permute-start | bytes 970760 | tf_op jit(solution)/shard_map/ppermute | solution.py:786
  27.1 0.7 %collective-permute-start.8 = (f32[632,128]{1,0:T(8,128)S(1)}, f32[632,128]{1,0:T(8,128)S(1)}, u32[]{:S(2)}, u32[]{:S(2)}) collective-permute-start(f32[632,128]{1,0:T(8,128)S(1)} %get-tuple-element.43), channel_id=1, source_target_pairs={{1,2},{2,1},{3,4},{4,3},{5,6},{6,5},{7,8},{8,7},{9,10},{10,9},{11,... | collective-permute-start | bytes 970760 | tf_op jit(solution)/shard_map/ppermute | solution.py:786
  27.8 0.0 copy-done.9
  27.9 0.1 maximum_bitcast_fusion.info
  27.9 0.6 %floor_parts.1 = (f32[192,128]{1,0:T(8,128)S(1)}, f32[3,4,80,128]{3,2,1,0:T(8,128)S(1)}) custom-call(f32[6,4,80,128]{3,2,1,0:T(8,128)S(1)} %get-tuple-element.36.s, f32[3,4,80,128]{3,2,1,0:T(8,128)S(1)} %get-tuple-element.37.v, f32[4,64,128]{2,1,0:T(8,128)S(1)} %copy-done, f32[288,128]{1,0:T(8,128)S(1)} %get-tuple-element.38.b_near, ...), custom_call_target="tpu_custom_call" | custom-call | flops 2343424 | bytes 2343424 | tf_op jit(solution)/shard_map/floor_parts/pallas_call | solution.py:767
  28.6 15.0 %all_to_all.5 = f32[96,2,128]{2,1,0:T(2,128)S(1)} all-to-all(f32[96,2,128]{2,1,0:T(2,128)S(1)} %bitcast.6), channel_id=1, replica_groups=mesh['sec'=2,'tile'=16] {'sec','tile'}, dimensions={0} | all-to-all | bytes 196608 | tf_op jit(solution)/shard_map/all_to_all | solution.py:879
  43.6 0.0 collective-permute-done.7.from_a
  43.6 0.0 collective-permute-done.8.from_b
  43.6 2.0 %finish.1 = (f32[3,4,64,128]{3,2,1,0:T(8,128)}, f32[6,4,64,128]{3,2,1,0:T(8,128)}, f32[3,64,256]{2,1,0:T(8,128)}) custom-call(f32[6,4,80,128]{3,2,1,0:T(8,128)S(1)} %get-tuple-element.36.s, f32[3,4,80,128]{3,2,1,0:T(8,128)S(1)} %get-tuple-element.41.v, f32[4,64,128]{2,1,0:T(8,128)S(1)} %copy-done, f32[4,64,128]{2,1,0:T(8,128)S(1)} %copy-done.4, ...), custom_call_target="tpu_custom_call" | custom-call | flops 4628992 | bytes 4628992 | tf_op jit(solution)/shard_map/finish/pallas_call | solution.py:767
  (17 shorter events, 0.1 us)
Async XLA Ops:
  0.6 6.8 %copy-start.3 = (f32[3,4,64,128]{3,2,1,0:T(8,128)S(1)}, f32[3,4,64,128]{3,2,1,0:T(8,128)}, u32[]{:S(2)}) copy-start(f32[3,4,64,128]{3,2,1,0:T(8,128)} %v.3) | copy-start | bytes 1179652
  0.6 6.8 %copy-start.1 = (f32[6,4,64,128]{3,2,1,0:T(8,128)S(1)}, f32[6,4,64,128]{3,2,1,0:T(8,128)}, u32[]{:S(2)}) copy-start(f32[6,4,64,128]{3,2,1,0:T(8,128)} %s.3) | copy-start | bytes 2359300
  0.7 6.8 %copy-start = (f32[4,64,128]{2,1,0:T(8,128)S(1)}, f32[4,64,128]{2,1,0:T(8,128)}, u32[]{:S(2)}) copy-start(f32[4,64,128]{2,1,0:T(8,128)} %b.9) | copy-start | bytes 393220
  0.7 11.4 %copy-start.2 = (f32[3,64,256]{2,1,0:T(8,128)S(1)}, f32[3,64,256]{2,1,0:T(8,128)}, u32[]{:S(2)}) copy-start(f32[3,64,256]{2,1,0:T(8,128)} %state.2) | copy-start | bytes 589828
  0.7 11.4 %copy-start.6 = (f32[64,256]{1,0:T(8,128)S(1)}, f32[64,256]{1,0:T(8,128)}, u32[]{:S(2)}) copy-start(f32[64,256]{1,0:T(8,128)} %depth.2) | copy-start | bytes 196612
  0.7 11.4 %copy-start.7 = (s32[64,256]{1,0:T(8,128)S(1)}, s32[64,256]{1,0:T(8,128)}, u32[]{:S(2)}) copy-start(s32[64,256]{1,0:T(8,128)} %wet.2) | copy-start | bytes 196612
  2.8 9.4 %copy-start.4 = (f32[4,64,128]{2,1,0:T(8,128)S(1)}, f32[4,64,128]{2,1,0:T(8,128)}, u32[]{:S(2)}) copy-start(f32[4,64,128]{2,1,0:T(8,128)} %lam.3) | copy-start | bytes 393220
  2.8 9.4 %copy-start.5 = (f32[4,64,128]{2,1,0:T(8,128)S(1)}, f32[4,64,128]{2,1,0:T(8,128)}, u32[]{:S(2)}) copy-start(f32[4,64,128]{2,1,0:T(8,128)} %mu.3) | copy-start | bytes 393220
  2.8 9.3 %collective-permute-start.3 = (f32[384,128]{1,0:T(8,128)}, f32[384,128]{1,0:T(8,128)S(1)}, u32[]{:S(2)}, u32[]{:S(2)}) collective-permute-start(f32[384,128]{1,0:T(8,128)} %get-tuple-element.30), channel_id=1, source_target_pairs={{0,1},{1,0},{2,3},{3,2},{4,5},{5,4},{6,7},{7,6},{8,9},{9,8},{10,11... | collective-permute-start | bytes 589832 | tf_op jit(solution)/shard_map/ppermute | solution.py:786
  5.8 1.6 %collective-permute-start = (f32[320,128]{1,0:T(8,128)}, f32[320,128]{1,0:T(8,128)S(1)}, u32[]{:S(2)}, u32[]{:S(2)}) collective-permute-start(f32[320,128]{1,0:T(8,128)} %bitcast.7), channel_id=1, source_target_pairs={{0,16},{16,0},{1,17},{17,1},{2,18},{18,2},{3,19},{19,3},{4,20},{20... | collective-permute-start | bytes 491528 | tf_op jit(solution)/shard_map/ppermute | solution.py:793
  5.8 6.4 %collective-permute-start.1 = (f32[384,128]{1,0:T(8,128)}, f32[384,128]{1,0:T(8,128)S(1)}, u32[]{:S(2)}, u32[]{:S(2)}) collective-permute-start(f32[384,128]{1,0:T(8,128)} %get-tuple-element.27), channel_id=1, source_target_pairs={{1,2},{2,1},{3,4},{4,3},{5,6},{6,5},{7,8},{8,7},{9,10},{10,9},{11,... | collective-permute-start | bytes 589832 | tf_op jit(solution)/shard_map/ppermute | solution.py:786
  8.0 15.2 %collective-permute-start.4 = (f32[368,128]{1,0:T(8,128)S(1)}, f32[368,128]{1,0:T(8,128)S(1)}, u32[]{:S(2)}, u32[]{:S(2)}) collective-permute-start(f32[368,128]{1,0:T(8,128)S(1)} %get-tuple-element.31), channel_id=1, source_target_pairs={{0,1},{1,0},{2,3},{3,2},{4,5},{5,4},{6,7},{7,6},{8,9},{9,8},{10,11... | collective-permute-start | bytes 565256 | tf_op jit(solution)/shard_map/ppermute | solution.py:786
  11.4 11.8 %collective-permute-start.5 = (f32[368,128]{1,0:T(8,128)S(1)}, f32[368,128]{1,0:T(8,128)S(1)}, u32[]{:S(2)}, u32[]{:S(2)}) collective-permute-start(f32[368,128]{1,0:T(8,128)S(1)} %get-tuple-element.32), channel_id=1, source_target_pairs={{1,2},{2,1},{3,4},{4,3},{5,6},{6,5},{7,8},{8,7},{9,10},{10,9},{11,... | collective-permute-start | bytes 565256 | tf_op jit(solution)/shard_map/ppermute | solution.py:786
  12.2 1.5 %collective-permute-start.6 = (f32[320,128]{1,0:T(8,128)S(1)}, f32[320,128]{1,0:T(8,128)S(1)}, u32[]{:S(2)}, u32[]{:S(2)}) collective-permute-start(f32[320,128]{1,0:T(8,128)S(1)} %near_columns.1), channel_id=1, source_target_pairs={{0,16},{16,0},{1,17},{17,1},{2,18},{18,2},{3,19},{19,3},{4,20},{20... | collective-permute-start | bytes 491528 | tf_op jit(solution)/shard_map/ppermute | solution.py:793
  12.3 1.4 %collective-permute-start.2 = (f32[64,128]{1,0:T(8,128)S(1)}, f32[64,128]{1,0:T(8,128)S(1)}, u32[]{:S(2)}, u32[]{:S(2)}) collective-permute-start(f32[64,128]{1,0:T(8,128)S(1)} %edge_rows.1), channel_id=1, source_target_pairs={{0,16},{16,0},{1,17},{17,1},{2,18},{18,2},{3,19},{19,3},{4,20},{20... | collective-permute-start | bytes 98312 | tf_op jit(solution)/shard_map/ppermute | solution.py:793
  23.2 4.6 %copy-start.8 = (s32[64]{0:T(128)S(1)}, s32[64]{0:T(128)}, u32[]{:S(2)}) copy-start(s32[64]{0:T(128)} %param.18) | copy-start | bytes 772
  23.2 4.6 %copy-start.9 = (f32[64]{0:T(128)S(1)}, f32[64]{0:T(128)}, u32[]{:S(2)}) copy-start(f32[64]{0:T(128)} %param.19) | copy-start | bytes 772
  24.4 19.2 %collective-permute-start.7 = (f32[632,128]{1,0:T(8,128)S(1)}, f32[632,128]{1,0:T(8,128)S(1)}, u32[]{:S(2)}, u32[]{:S(2)}) collective-permute-start(f32[632,128]{1,0:T(8,128)S(1)} %get-tuple-element.42), channel_id=1, source_target_pairs={{0,1},{1,0},{2,3},{3,2},{4,5},{5,4},{6,7},{7,6},{8,9},{9,8},{10,11... | collective-permute-start | bytes 970760 | tf_op jit(solution)/shard_map/ppermute | solution.py:786
  27.1 16.5 %collective-permute-start.8 = (f32[632,128]{1,0:T(8,128)S(1)}, f32[632,128]{1,0:T(8,128)S(1)}, u32[]{:S(2)}, u32[]{:S(2)}) collective-permute-start(f32[632,128]{1,0:T(8,128)S(1)} %get-tuple-element.43), channel_id=1, source_target_pairs={{1,2},{2,1},{3,4},{4,3},{5,6},{6,5},{7,8},{8,7},{9,10},{10,9},{11,... | collective-permute-start | bytes 970760 | tf_op jit(solution)/shard_map/ppermute | solution.py:786

commit v10 on v9

--- a/solution.py
+++ b/solution.py
@@ -18,7 +18,7 @@
 WINDOW = 8
 DEEP = (4, 3, 2, 3, 3)
 CORNER = (2, 1, 2, 2, 2)
-LINES = 6
+LINES = 4
 NEEDED = {"s": 5, "v": 3, "b": 3}
 LAST_NEEDED = 2
 LAYERS = 9
@@ -404,6 +404,7 @@
     late_a,
     late_b,
     sea,
+    info,
     v_out,
     s_out,
     pay_a,
@@ -475,7 +476,8 @@
     counts = [LAST_NEEDED] * len(edges[0])
     at = LAYERS * cy
     send(odd, sea[0, :sea_rows], sea[1, :sea_rows], pay_a, pay_b, at)
-    send_thin(odd, edges, counts, edge, pay_a, pay_b, at + sea_rows)
+    send(odd, info[...], info[...], pay_a, pay_b, at + sea_rows)
+    send_thin(odd, edges, counts, edge, pay_a, pay_b, at + sea_rows + 1)
 
 
 def last_step(
@@ -506,7 +508,7 @@
     layers, edges = second_lists(cx)
     own = received(odd, layers, [cy] * LAYERS, from_a, from_b, cx, 0)
     counts = [LAST_NEEDED] * len(edges[0])
-    rest = received(odd, edges, counts, from_a, from_b, cx, LAYERS * cy + sea_rows)
+    rest = received(odd, edges, counts, from_a, from_b, cx, LAYERS * cy + sea_rows + 1)
     for key, k in index_s.items():
         put_layer(halo_s, k, own["s", *key](), rest["s", *key](), sec)
     for x in range(cx):
@@ -541,7 +543,7 @@
     return jnp.sum(picked, axis=0, keepdims=True)
 
 
-def floor_parts(s, v, b, b_near, info, parts, v_part, b_rows):
+def floor_parts(s, v, b, b_near, parts, v_part, b_rows):
     cx, cy, nz = b.shape
     weights = depth_weights(nz)
     _, sec, _ = place()
@@ -557,18 +559,19 @@
             v_part[c, x, here, :] = v[c, x, first : first + rows, :] + scale * terms
     layers = [v_part[2, x, SIDE : SIDE + cy, :] for x in range(cx)]
     lines = [floor_line(layers[x], layers[x + 1]) for x in range(0, cx, 2)]
-    lines.append(floor_line(s[4, cx - 1, own, :], s[4, cx - 2, own, :]))
-    lines.append(floor_line(s[4, 0, own, :], (-FAR * DT) * b[cx - 1]))
-    lines.append(floor_line(DT * b[0], DT * b[1]))
-    lines.append(info[...])
+    below, first_above, second_above = (
+        DT * b_near[k * cy : (k + 1) * cy, :] for k in (1, 2, 3)
+    )
+    last, before, start = s[4, cx - 1, own, :], s[4, cx - 2, own, :], s[4, 0, own, :]
+    reached = first_above * (FAR * before - NEAR * last)
+    lines.append(floor_line(reached, second_above * (FAR * last)))
+    lines.append(floor_line(jnp.zeros((cy, nz), F32), below * (-FAR * start)))
     row = lax.broadcasted_iota(jnp.int32, (SIDE, 2 * cy), 0)
-    period = 3 * SIDE
-    for k in range(0, period, SIDE):
-        tiled = jnp.zeros((SIDE, 2 * cy), F32)
-        for j in range(SIDE):
-            tiled = jnp.where(row == j, lines[(k + j) % LINES], tiled)
-        for at in range(k, parts.shape[0], period):
-            parts[at : at + SIDE, :] = tiled
+    tiled = jnp.zeros((SIDE, 2 * cy), F32)
+    for j in range(SIDE):
+        tiled = jnp.where(row == j, lines[j % LINES], tiled)
+    for at in range(0, parts.shape[0], SIDE):
+        parts[at : at + SIDE, :] = tiled
 
 
 def column(line, first, count):
@@ -624,8 +627,8 @@
     def told(half, k):
         return told_ref[pl.ds((half * count + k) * LINES, LINES), :]
 
-    below = told(sec, jnp.maximum(tile - 1, 0))[5:6]
-    above = told(sec, jnp.minimum(tile + 1, count - 1))[5:6]
+    a, b = from_a[at : at + 1, :], from_b[at : at + 1, :]
+    below, above = jnp.where(odd, a, b), jnp.where(odd, b, a)
     line = info[...]
     marks = [
         jnp.concatenate(
@@ -640,10 +643,6 @@
     ]
     owner = jnp.broadcast_to(marks[0] - base.astype(F32), (total, 128))
     share = marks[1]
-    width = own // 4
-    left = lax.broadcasted_iota(jnp.int32, (1, 128), 1) < width
-    near = jnp.where(left, -NEAR, FAR).astype(F32)
-    far = jnp.where(left, FAR, 0.0).astype(F32)
     uplift = []
     for half in (sec, 1 - sec):
         tiles = []
@@ -654,10 +653,7 @@
         levels = [jnp.zeros((total, 128), F32) for _ in range(2)]
         for k in range(window):
             below, this, above = tiles[k], tiles[k + 1], tiles[k + 2]
-            last = pltpu.roll(below[2:3], width, 1)
-            last = near * jnp.where(left, below[2:3], last) + far * last
-            first = this[0:1] + this[4:5] * last
-            second = this[1:2] + jnp.where(left, 0.0, this[3:4]) * pltpu.roll(above[3:4], width, 1)
+            first, second = this[0:1] + below[2:3], this[1:2] + above[3:4]
             mine = owner == float(k)
             levels = [jnp.where(mine, q, level) for q, level in zip((first, second), levels)]
         uplift.append(levels)
@@ -851,7 +847,7 @@
     info = jnp.concatenate([source.astype(F32), share])[None]
 
     kept = cy + 2 * EDGE + 8
-    second = (LAYERS * cy + rounded(per + 5 * LAST_NEEDED), nz)
+    second = (LAYERS * cy + rounded(per + 1 + 5 * LAST_NEEDED), nz)
     velocity, stresses, pay_a, pay_b, b_near = call(
         functools.partial(whole_step, per),
         "whole_step",
@@ -865,7 +861,7 @@
             pltpu.VMEM((2, tall, nz), F32),
         ],
         [stresses, velocity, buoyancy, lame_first, shear_mod, strips, more_strips]
-        + [early_a, early_b, late_a, late_b, edges],
+        + [early_a, early_b, late_a, late_b, edges, info],
     )
     from_a, from_b = exchange(pay_a, pay_b, count)
     parts, velocity = call(
@@ -873,7 +869,7 @@
         "floor_parts",
         [(2 * count * LINES, 2 * cy), (3, cx, tall, nz)],
         [pltpu.VMEM((tall, nz), F32)],
-        [stresses, velocity, buoyancy, b_near, info],
+        [stresses, velocity, buoyancy, b_near],
     )
     parts = parts.reshape(2 * count * LINES // 2, 2, 2 * cy)
     patches = lax.all_to_all(parts, ("sec", "tile"), 0, 0, tiled=True).reshape(-1, 2 * cy)

time: 45.9 us -> 45.3 us (0.987)
  no operation moved by 1% of the time
where the time goes in v10:
time: 45.3 us; the launch traced here: 45.1 us
  blocking collectives  14.7 us (32%)
  starting transfers between devices  11.7 us (26%)
  waiting for transfers between devices  11.2 us (25%)
  Pallas kernels  6.52 us (14%)
  between operations  0.87 us (2%)
    all_to_all x1, blocking collectives, shards(): lax.all_to_all(parts, ('sec', 'tile'), 0, 0, tiled=True).reshape(-1, 2 * cy)  14.7 us
    ppermute x6, starting transfers between devices, swap(): return lax.ppermute(pay, 'tile', pairs)  11.1 us
    ppermute x6, waiting for transfers between devices, swap(): return lax.ppermute(pay, 'tile', pairs)  9.53 us
    pallas_call x8, Pallas kernels, call(): pl.pallas_call(body, name=name, out_shape=shapes, in_specs=ins if isinsta...  6.52 us
    ppermute x3, waiting for transfers between devices, across(): return lax.ppermute(pay, 'sec', [(0, 1), (1, 0)])  1.7 us
  transfers between devices with their start and end apart: 9, of which 4 were waited for; matrix products, arithmetic and copies ran while one was open for 0% of the time, Pallas kernels for 3%

profile of v10, /device:TPU:0, one launch (start us, length us, event | category | flops | bytes accessed | tf_op | source)
XLA Modules:
  0.0 45.1 jit_solution(15899395923917308026)
XLA Ops:
  0.7 2.1 %opening.1 = (f32[384,128]{1,0:T(8,128)}, f32[384,128]{1,0:T(8,128)}, f32[10,4,8,128]{3,2,1,0:T(8,128)}) custom-call(f32[6,4,64,128]{3,2,1,0:T(8,128)} %s.3, f32[3,4,64,128]{3,2,1,0:T(8,128)} %v.3, f32[4,64,128]{2,1,0:T(8,128)} %b.9), custom_call_target="tpu_custom_call" | custom-call | flops 1867776 | bytes 1867776 | tf_op jit(solution)/shard_map/opening/pallas_call | solution.py:763
  2.8 0.0 copy-start.4
  2.8 0.0 copy-start.5
  2.8 0.0 copy-start.8
  2.8 0.0 copy-start.9
  2.9 3.0 %collective-permute-start.3 = (f32[384,128]{1,0:T(8,128)}, f32[384,128]{1,0:T(8,128)S(1)}, u32[]{:S(2)}, u32[]{:S(2)}) collective-permute-start(f32[384,128]{1,0:T(8,128)} %get-tuple-element.30), channel_id=1, source_target_pairs={{0,1},{1,0},{2,3},{3,2},{4,5},{5,4},{6,7},{7,6},{8,9},{9,8},{10,11... | collective-permute-start | bytes 589832 | tf_op jit(solution)/shard_map/ppermute | solution.py:782
  5.8 0.0 collective-permute-start
  5.8 0.7 %collective-permute-start.1 = (f32[384,128]{1,0:T(8,128)}, f32[384,128]{1,0:T(8,128)S(1)}, u32[]{:S(2)}, u32[]{:S(2)}) collective-permute-start(f32[384,128]{1,0:T(8,128)} %get-tuple-element.27), channel_id=1, source_target_pairs={{1,2},{2,1},{3,4},{4,3},{5,6},{6,5},{7,8},{8,7},{9,10},{10,9},{11,... | collective-permute-start | bytes 589832 | tf_op jit(solution)/shard_map/ppermute | solution.py:782
  6.5 0.9 %collective-permute-done.strips = f32[320,128]{1,0:T(8,128)S(1)} collective-permute-done((f32[320,128]{1,0:T(8,128)}, f32[320,128]{1,0:T(8,128)S(1)}, u32[]{:S(2)}, u32[]{:S(2)}) %collective-permute-start) | collective-permute-done | bytes 163872 | tf_op jit(solution)/shard_map/ppermute | solution.py:789
  7.4 0.0 copy-done
  7.4 0.0 copy-done.3
  7.4 0.6 %first_round.1 = (f32[368,128]{1,0:T(8,128)S(1)}, f32[368,128]{1,0:T(8,128)S(1)}, f32[6,4,96,128]{3,2,1,0:T(8,128)S(1)}, f32[3,4,80,128]{3,2,1,0:T(8,128)S(1)}) custom-call(f32[6,4,64,128]{3,2,1,0:T(8,128)S(1)} %copy-done.1, f32[3,4,64,128]{3,2,1,0:T(8,128)S(1)} %copy-done.3, f32[4,64,128]{2,1,0:T(8,128)S(1)} %copy-done, ...), custom_call_target="tpu_custom_call" | custom-call | flops 3522560 | bytes 3522560 | tf_op jit(solution)/shard_map/first_round/pallas_call | solution.py:763
  8.1 3.4 %collective-permute-start.4 = (f32[368,128]{1,0:T(8,128)S(1)}, f32[368,128]{1,0:T(8,128)S(1)}, u32[]{:S(2)}, u32[]{:S(2)}) collective-permute-start(f32[368,128]{1,0:T(8,128)S(1)} %get-tuple-element.31), channel_id=1, source_target_pairs={{0,1},{1,0},{2,3},{3,2},{4,5},{5,4},{6,7},{7,6},{8,9},{9,8},{10,11... | collective-permute-start | bytes 565256 | tf_op jit(solution)/shard_map/ppermute | solution.py:782
  11.4 0.7 %collective-permute-start.5 = (f32[368,128]{1,0:T(8,128)S(1)}, f32[368,128]{1,0:T(8,128)S(1)}, u32[]{:S(2)}, u32[]{:S(2)}) collective-permute-start(f32[368,128]{1,0:T(8,128)S(1)} %get-tuple-element.32), channel_id=1, source_target_pairs={{1,2},{2,1},{3,4},{4,3},{5,6},{6,5},{7,8},{8,7},{9,10},{10,9},{11,... | collective-permute-start | bytes 565256 | tf_op jit(solution)/shard_map/ppermute | solution.py:782
  12.1 0.0 collective-permute-done.3.early_a
  12.1 0.0 copy-done.7
  12.2 0.1 collective-permute-start.6
  12.3 0.0 collective-permute-done.1.early_b
  12.3 0.5 %collective-permute-start.2 = (f32[64,128]{1,0:T(8,128)S(1)}, f32[64,128]{1,0:T(8,128)S(1)}, u32[]{:S(2)}, u32[]{:S(2)}) collective-permute-start(f32[64,128]{1,0:T(8,128)S(1)} %edge_rows.1), channel_id=1, source_target_pairs={{0,16},{16,0},{1,17},{17,1},{2,18},{18,2},{3,19},{19,3},{4,20},{20... | collective-permute-start | bytes 98312 | tf_op jit(solution)/shard_map/ppermute | solution.py:789
  12.9 0.1 maximum_bitcast_fusion.info
  13.0 0.7 %collective-permute-done.6.near = f32[320,128]{1,0:T(8,128)S(1)} collective-permute-done((f32[320,128]{1,0:T(8,128)S(1)}, f32[320,128]{1,0:T(8,128)S(1)}, u32[]{:S(2)}, u32[]{:S(2)}) %collective-permute-start.6) | collective-permute-done | bytes 163872 | tf_op jit(solution)/shard_map/ppermute | solution.py:789
  13.7 0.1 collective-permute-done.2.more_strips
  13.7 9.5 %collective-permute-done.4.late_a = f32[368,128]{1,0:T(8,128)S(1)} collective-permute-done((f32[368,128]{1,0:T(8,128)S(1)}, f32[368,128]{1,0:T(8,128)S(1)}, u32[]{:S(2)}, u32[]{:S(2)}) %collective-permute-start.4) | collective-permute-done | bytes 188448 | tf_op jit(solution)/shard_map/ppermute | solution.py:782
  23.2 0.0 collective-permute-done.5.late_b
  23.3 1.2 %whole_step.1 = (f32[3,4,80,128]{3,2,1,0:T(8,128)S(1)}, f32[6,4,80,128]{3,2,1,0:T(8,128)S(1)}, f32[632,128]{1,0:T(8,128)S(1)}, f32[632,128]{1,0:T(8,128)S(1)}, f32[288,128]{1,0:T(8,128)S(1)}) custom-call(f32[6,4,96,128]{3,2,1,0:T(8,128)S(1)} %get-tuple-element.25.s_pad, f32[3,4,80,128]{3,2,1,0:T(8,128)S(1)} %get-tuple-element.26.v_part, ...), custom_call_target="tpu_custom_call" | custom-call | flops 5349888 | bytes 5349888 | tf_op jit(solution)/shard_map/whole_step/pallas_call | solution.py:763
  24.5 2.7 %collective-permute-start.7 = (f32[632,128]{1,0:T(8,128)S(1)}, f32[632,128]{1,0:T(8,128)S(1)}, u32[]{:S(2)}, u32[]{:S(2)}) collective-permute-start(f32[632,128]{1,0:T(8,128)S(1)} %get-tuple-element.42), channel_id=1, source_target_pairs={{0,1},{1,0},{2,3},{3,2},{4,5},{5,4},{6,7},{7,6},{8,9},{9,8},{10,11... | collective-permute-start | bytes 970760 | tf_op jit(solution)/shard_map/ppermute | solution.py:782
  27.2 0.7 %collective-permute-start.8 = (f32[632,128]{1,0:T(8,128)S(1)}, f32[632,128]{1,0:T(8,128)S(1)}, u32[]{:S(2)}, u32[]{:S(2)}) collective-permute-start(f32[632,128]{1,0:T(8,128)S(1)} %get-tuple-element.43), channel_id=1, source_target_pairs={{1,2},{2,1},{3,4},{4,3},{5,6},{6,5},{7,8},{8,7},{9,10},{10,9},{11,... | collective-permute-start | bytes 970760 | tf_op jit(solution)/shard_map/ppermute | solution.py:782
  27.9 0.6 %floor_parts.1 = (f32[128,128]{1,0:T(8,128)S(1)}, f32[3,4,80,128]{3,2,1,0:T(8,128)S(1)}) custom-call(f32[6,4,80,128]{3,2,1,0:T(8,128)S(1)} %get-tuple-element.38.s, f32[3,4,80,128]{3,2,1,0:T(8,128)S(1)} %get-tuple-element.39.v, f32[4,64,128]{2,1,0:T(8,128)S(1)} %copy-done, f32[288,128]{1,0:T(8,128)S(1)} %get-tuple-element.40.b_near), custom_call_target="tpu_custom_call" | custom-call | flops 2310144 | bytes 2310144 | tf_op jit(solution)/shard_map/floor_parts/pallas_call | solution.py:763
  28.5 14.7 %all_to_all.5 = f32[64,2,128]{2,1,0:T(2,128)S(1)} all-to-all(f32[64,2,128]{2,1,0:T(2,128)S(1)} %bitcast.6), channel_id=1, replica_groups=mesh['sec'=2,'tile'=16] {'sec','tile'}, dimensions={0} | all-to-all | bytes 131072 | tf_op jit(solution)/shard_map/all_to_all | solution.py:875
  43.2 0.0 collective-permute-done.7.from_a
  43.2 0.0 collective-permute-done.8.from_b
  43.2 1.9 %finish.1 = (f32[3,4,64,128]{3,2,1,0:T(8,128)}, f32[6,4,64,128]{3,2,1,0:T(8,128)}, f32[3,64,256]{2,1,0:T(8,128)}) custom-call(f32[6,4,80,128]{3,2,1,0:T(8,128)S(1)} %get-tuple-element.38.s, f32[3,4,80,128]{3,2,1,0:T(8,128)S(1)} %get-tuple-element.41.v, f32[4,64,128]{2,1,0:T(8,128)S(1)} %copy-done, f32[4,64,128]{2,1,0:T(8,128)S(1)} %copy-done.4, ...), custom_call_target="tpu_custom_call" | custom-call | flops 4596224 | bytes 4596224 | tf_op jit(solution)/shard_map/finish/pallas_call | solution.py:763
  (17 shorter events, 0.1 us)
Async XLA Ops:
  0.6 6.8 %copy-start = (f32[4,64,128]{2,1,0:T(8,128)S(1)}, f32[4,64,128]{2,1,0:T(8,128)}, u32[]{:S(2)}) copy-start(f32[4,64,128]{2,1,0:T(8,128)} %b.9) | copy-start | bytes 393220
  0.6 6.8 %copy-start.1 = (f32[6,4,64,128]{3,2,1,0:T(8,128)S(1)}, f32[6,4,64,128]{3,2,1,0:T(8,128)}, u32[]{:S(2)}) copy-start(f32[6,4,64,128]{3,2,1,0:T(8,128)} %s.3) | copy-start | bytes 2359300
  0.7 6.8 %copy-start.3 = (f32[3,4,64,128]{3,2,1,0:T(8,128)S(1)}, f32[3,4,64,128]{3,2,1,0:T(8,128)}, u32[]{:S(2)}) copy-start(f32[3,4,64,128]{3,2,1,0:T(8,128)} %v.3) | copy-start | bytes 1179652
  0.7 11.5 %copy-start.7 = (s32[64,256]{1,0:T(8,128)S(1)}, s32[64,256]{1,0:T(8,128)}, u32[]{:S(2)}) copy-start(s32[64,256]{1,0:T(8,128)} %wet.2) | copy-start | bytes 196612
  0.7 11.5 %copy-start.6 = (f32[64,256]{1,0:T(8,128)S(1)}, f32[64,256]{1,0:T(8,128)}, u32[]{:S(2)}) copy-start(f32[64,256]{1,0:T(8,128)} %depth.2) | copy-start | bytes 196612
  0.7 11.5 %copy-start.2 = (f32[3,64,256]{2,1,0:T(8,128)S(1)}, f32[3,64,256]{2,1,0:T(8,128)}, u32[]{:S(2)}) copy-start(f32[3,64,256]{2,1,0:T(8,128)} %state.2) | copy-start | bytes 589828
  2.8 9.5 %copy-start.4 = (f32[4,64,128]{2,1,0:T(8,128)S(1)}, f32[4,64,128]{2,1,0:T(8,128)}, u32[]{:S(2)}) copy-start(f32[4,64,128]{2,1,0:T(8,128)} %lam.3) | copy-start | bytes 393220
  2.8 9.5 %copy-start.5 = (f32[4,64,128]{2,1,0:T(8,128)S(1)}, f32[4,64,128]{2,1,0:T(8,128)}, u32[]{:S(2)}) copy-start(f32[4,64,128]{2,1,0:T(8,128)} %mu.3) | copy-start | bytes 393220
  2.8 9.5 %copy-start.8 = (s32[64]{0:T(128)S(1)}, s32[64]{0:T(128)}, u32[]{:S(2)}) copy-start(s32[64]{0:T(128)} %param.18) | copy-start | bytes 772
  2.8 10.0 %copy-start.9 = (f32[64]{0:T(128)S(1)}, f32[64]{0:T(128)}, u32[]{:S(2)}) copy-start(f32[64]{0:T(128)} %param.19) | copy-start | bytes 772
  2.9 9.3 %collective-permute-start.3 = (f32[384,128]{1,0:T(8,128)}, f32[384,128]{1,0:T(8,128)S(1)}, u32[]{:S(2)}, u32[]{:S(2)}) collective-permute-start(f32[384,128]{1,0:T(8,128)} %get-tuple-element.30), channel_id=1, source_target_pairs={{0,1},{1,0},{2,3},{3,2},{4,5},{5,4},{6,7},{7,6},{8,9},{9,8},{10,11... | collective-permute-start | bytes 589832 | tf_op jit(solution)/shard_map/ppermute | solution.py:782
  5.8 1.6 %collective-permute-start = (f32[320,128]{1,0:T(8,128)}, f32[320,128]{1,0:T(8,128)S(1)}, u32[]{:S(2)}, u32[]{:S(2)}) collective-permute-start(f32[320,128]{1,0:T(8,128)} %bitcast.7), channel_id=1, source_target_pairs={{0,16},{16,0},{1,17},{17,1},{2,18},{18,2},{3,19},{19,3},{4,20},{20... | collective-permute-start | bytes 491528 | tf_op jit(solution)/shard_map/ppermute | solution.py:789
  5.8 6.4 %collective-permute-start.1 = (f32[384,128]{1,0:T(8,128)}, f32[384,128]{1,0:T(8,128)S(1)}, u32[]{:S(2)}, u32[]{:S(2)}) collective-permute-start(f32[384,128]{1,0:T(8,128)} %get-tuple-element.27), channel_id=1, source_target_pairs={{1,2},{2,1},{3,4},{4,3},{5,6},{6,5},{7,8},{8,7},{9,10},{10,9},{11,... | collective-permute-start | bytes 589832 | tf_op jit(solution)/shard_map/ppermute | solution.py:782
  8.1 15.2 %collective-permute-start.4 = (f32[368,128]{1,0:T(8,128)S(1)}, f32[368,128]{1,0:T(8,128)S(1)}, u32[]{:S(2)}, u32[]{:S(2)}) collective-permute-start(f32[368,128]{1,0:T(8,128)S(1)} %get-tuple-element.31), channel_id=1, source_target_pairs={{0,1},{1,0},{2,3},{3,2},{4,5},{5,4},{6,7},{7,6},{8,9},{9,8},{10,11... | collective-permute-start | bytes 565256 | tf_op jit(solution)/shard_map/ppermute | solution.py:782
  11.4 11.8 %collective-permute-start.5 = (f32[368,128]{1,0:T(8,128)S(1)}, f32[368,128]{1,0:T(8,128)S(1)}, u32[]{:S(2)}, u32[]{:S(2)}) collective-permute-start(f32[368,128]{1,0:T(8,128)S(1)} %get-tuple-element.32), channel_id=1, source_target_pairs={{1,2},{2,1},{3,4},{4,3},{5,6},{6,5},{7,8},{8,7},{9,10},{10,9},{11,... | collective-permute-start | bytes 565256 | tf_op jit(solution)/shard_map/ppermute | solution.py:782
  12.2 1.5 %collective-permute-start.6 = (f32[320,128]{1,0:T(8,128)S(1)}, f32[320,128]{1,0:T(8,128)S(1)}, u32[]{:S(2)}, u32[]{:S(2)}) collective-permute-start(f32[320,128]{1,0:T(8,128)S(1)} %near_columns.1), channel_id=1, source_target_pairs={{0,16},{16,0},{1,17},{17,1},{2,18},{18,2},{3,19},{19,3},{4,20},{20... | collective-permute-start | bytes 491528 | tf_op jit(solution)/shard_map/ppermute | solution.py:789
  12.3 1.4 %collective-permute-start.2 = (f32[64,128]{1,0:T(8,128)S(1)}, f32[64,128]{1,0:T(8,128)S(1)}, u32[]{:S(2)}, u32[]{:S(2)}) collective-permute-start(f32[64,128]{1,0:T(8,128)S(1)} %edge_rows.1), channel_id=1, source_target_pairs={{0,16},{16,0},{1,17},{17,1},{2,18},{18,2},{3,19},{19,3},{4,20},{20... | collective-permute-start | bytes 98312 | tf_op jit(solution)/shard_map/ppermute | solution.py:789
  24.5 18.7 %collective-permute-start.7 = (f32[632,128]{1,0:T(8,128)S(1)}, f32[632,128]{1,0:T(8,128)S(1)}, u32[]{:S(2)}, u32[]{:S(2)}) collective-permute-start(f32[632,128]{1,0:T(8,128)S(1)} %get-tuple-element.42), channel_id=1, source_target_pairs={{0,1},{1,0},{2,3},{3,2},{4,5},{5,4},{6,7},{7,6},{8,9},{9,8},{10,11... | collective-permute-start | bytes 970760 | tf_op jit(solution)/shard_map/ppermute | solution.py:782
  27.2 16.0 %collective-permute-start.8 = (f32[632,128]{1,0:T(8,128)S(1)}, f32[632,128]{1,0:T(8,128)S(1)}, u32[]{:S(2)}, u32[]{:S(2)}) collective-permute-start(f32[632,128]{1,0:T(8,128)S(1)} %get-tuple-element.43), channel_id=1, source_target_pairs={{1,2},{2,1},{3,4},{4,3},{5,6},{6,5},{7,8},{8,7},{9,10},{10,9},{11,... | collective-permute-start | bytes 970760 | tf_op jit(solution)/shard_map/ppermute | solution.py:782

commit v11 on v10

--- a/solution.py
+++ b/solution.py
@@ -16,8 +16,8 @@
 EDGE = 4
 SIDE = 8
 WINDOW = 8
-DEEP = (4, 3, 2, 3, 3)
-CORNER = (2, 1, 2, 2, 2)
+DEEP = (4, 3, 2, 3)
+CORNER = (2, 1, 2, 2)
 LINES = 4
 NEEDED = {"s": 5, "v": 3, "b": 3}
 LAST_NEEDED = 2
@@ -323,17 +323,21 @@
 def near_columns(state, depth, wet, out):
     _, sec, _ = place()
     rows, own = depth.shape
-    for k, field in enumerate((state.at[0], state.at[1], state.at[2], depth, wet)):
-        near = jnp.where(sec == 0, field[:, own - 128 :], field[:, :128])
-        out[k * rows : (k + 1) * rows, :] = near.astype(F32)
+
+    def beside(field):
+        return jnp.where(sec == 0, field[:, own - 128 :], field[:, :128]).astype(F32)
+
+    for k in range(3):
+        out[k * rows : (k + 1) * rows, :] = beside(state.at[k])
+    out[3 * rows :, :] = beside(depth) * beside(wet)
 
 
 def ocean_field(state, depth, wet, near, f, k):
     rows, own = depth.shape
     if k == own // 128:
         return near[f * rows : (f + 1) * rows, :]
-    field = state.at[f] if f < 3 else depth if f == 3 else wet
-    return field[:, k * 128 : (k + 1) * 128].astype(F32)
+    lanes = slice(k * 128, (k + 1) * 128)
+    return state[f, :, lanes] if f < 3 else depth[:, lanes] * wet[:, lanes].astype(F32)
 
 
 def ocean_edges(state, depth, wet, near, edges):
@@ -617,7 +621,8 @@
         return 0.5 * (pltpu.roll(f, total - 1, 0) - pltpu.roll(f, 1, 0))
 
     eta, u, v_sea = ocean_ref[0], ocean_ref[1], ocean_ref[2]
-    depth, wet = ocean_ref[3], ocean_ref[4]
+    depth = ocean_ref[3]
+    wet = (depth > 0.0).astype(F32)
     window = min(WINDOW, count)
     base = jnp.clip(tile - REACH - 1, 0, count - window)
 

time: 45.3 us -> 46 us (1.015)
  starting transfers between devices: 11.7 us -> 13.4 us
  waiting for transfers between devices: 11.2 us -> 10.2 us
    ppermute x6, starting transfers between devices: 11.1 us -> 12.3 us  [swap(): return lax.ppermute(pay, 'tile', pairs)]
    ppermute x3, waiting for transfers between devices: 1.7 us -> 0.77 us  [across(): return lax.ppermute(pay, 'sec', [(0, 1), (1, 0)])]
    ppermute x3, starting transfers between devices: 0.62 us -> 1.13 us  [across(): return lax.ppermute(pay, 'sec', [(0, 1), (1, 0)])]
  transfers between devices with their start and end apart: 9 -> 9, of which waited for: 4 -> 3; matrix products, arithmetic and copies ran while one was open for 0% -> 0% of each run, Pallas kernels for 3% -> 3%
where the time goes in v11:
time: 46 us; the launch traced here: 45.8 us
  blocking collectives  14.7 us (32%)
  starting transfers between devices  13.4 us (29%)
  waiting for transfers between devices  10.2 us (22%)
  Pallas kernels  6.51 us (14%)
  between operations  0.9 us (2%)
    all_to_all x1, blocking collectives, shards(): lax.all_to_all(parts, ('sec', 'tile'), 0, 0, tiled=True).reshape(-1, 2 * cy)  14.7 us
    ppermute x6, starting transfers between devices, swap(): return lax.ppermute(pay, 'tile', pairs)  12.3 us
    ppermute x6, waiting for transfers between devices, swap(): return lax.ppermute(pay, 'tile', pairs)  9.41 us
    pallas_call x8, Pallas kernels, call(): pl.pallas_call(body, name=name, out_shape=shapes, in_specs=ins if isinsta...  6.51 us
    ppermute x3, starting transfers between devices, across(): return lax.ppermute(pay, 'sec', [(0, 1), (1, 0)])  1.13 us
  transfers between devices with their start and end apart: 9, of which 3 were waited for; matrix products, arithmetic and copies ran while one was open for 0% of the time, Pallas kernels for 3%

profile of v11, /device:TPU:0, one launch (start us, length us, event | category | flops | bytes accessed | tf_op | source)
XLA Modules:
  0.0 45.8 jit_solution(14256255400326417870)
XLA Ops:
  0.6 0.0 copy-start
  0.6 0.0 copy-start.1
  0.7 0.0 copy-start.3
  0.7 2.1 %opening.1 = (f32[384,128]{1,0:T(8,128)}, f32[384,128]{1,0:T(8,128)}, f32[10,4,8,128]{3,2,1,0:T(8,128)}) custom-call(f32[6,4,64,128]{3,2,1,0:T(8,128)} %s.3, f32[3,4,64,128]{3,2,1,0:T(8,128)} %v.3, f32[4,64,128]{2,1,0:T(8,128)} %b.9), custom_call_target="tpu_custom_call" | custom-call | flops 1867776 | bytes 1867776 | tf_op jit(solution)/shard_map/opening/pallas_call | solution.py:768
  2.8 0.0 copy-start.4
  2.8 0.0 copy-start.5
  2.8 0.0 copy-start.8
  2.8 0.0 copy-start.9
  2.9 0.5 %collective-permute-start = (f32[320,128]{1,0:T(8,128)}, f32[320,128]{1,0:T(8,128)S(1)}, u32[]{:S(2)}, u32[]{:S(2)}) collective-permute-start(f32[320,128]{1,0:T(8,128)} %bitcast.7), channel_id=1, source_target_pairs={{0,16},{16,0},{1,17},{17,1},{2,18},{18,2},{3,19},{19,3},{4,20},{20... | collective-permute-start | bytes 491528 | tf_op jit(solution)/shard_map/ppermute | solution.py:794
  3.4 2.5 %collective-permute-start.3 = (f32[384,128]{1,0:T(8,128)}, f32[384,128]{1,0:T(8,128)S(1)}, u32[]{:S(2)}, u32[]{:S(2)}) collective-permute-start(f32[384,128]{1,0:T(8,128)} %get-tuple-element.30), channel_id=1, source_target_pairs={{0,1},{1,0},{2,3},{3,2},{4,5},{5,4},{6,7},{7,6},{8,9},{9,8},{10,11... | collective-permute-start | bytes 589832 | tf_op jit(solution)/shard_map/ppermute | solution.py:787
  5.9 0.7 %collective-permute-start.1 = (f32[384,128]{1,0:T(8,128)}, f32[384,128]{1,0:T(8,128)S(1)}, u32[]{:S(2)}, u32[]{:S(2)}) collective-permute-start(f32[384,128]{1,0:T(8,128)} %get-tuple-element.27), channel_id=1, source_target_pairs={{1,2},{2,1},{3,4},{4,3},{5,6},{6,5},{7,8},{8,7},{9,10},{10,9},{11,... | collective-permute-start | bytes 589832 | tf_op jit(solution)/shard_map/ppermute | solution.py:787
  6.6 0.0 collective-permute-done.strips
  6.6 0.6 %first_round.1 = (f32[368,128]{1,0:T(8,128)S(1)}, f32[368,128]{1,0:T(8,128)S(1)}, f32[6,4,96,128]{3,2,1,0:T(8,128)S(1)}, f32[3,4,80,128]{3,2,1,0:T(8,128)S(1)}) custom-call(f32[6,4,64,128]{3,2,1,0:T(8,128)S(1)} %copy-done.1, f32[3,4,64,128]{3,2,1,0:T(8,128)S(1)} %copy-done.3, f32[4,64,128]{2,1,0:T(8,128)S(1)} %copy-done, ...), custom_call_target="tpu_custom_call" | custom-call | flops 3522560 | bytes 3522560 | tf_op jit(solution)/shard_map/first_round/pallas_call | solution.py:768
  7.2 4.3 %collective-permute-start.4 = (f32[368,128]{1,0:T(8,128)S(1)}, f32[368,128]{1,0:T(8,128)S(1)}, u32[]{:S(2)}, u32[]{:S(2)}) collective-permute-start(f32[368,128]{1,0:T(8,128)S(1)} %get-tuple-element.31), channel_id=1, source_target_pairs={{0,1},{1,0},{2,3},{3,2},{4,5},{5,4},{6,7},{7,6},{8,9},{9,8},{10,11... | collective-permute-start | bytes 565256 | tf_op jit(solution)/shard_map/ppermute | solution.py:787
  11.5 0.7 %collective-permute-start.5 = (f32[368,128]{1,0:T(8,128)S(1)}, f32[368,128]{1,0:T(8,128)S(1)}, u32[]{:S(2)}, u32[]{:S(2)}) collective-permute-start(f32[368,128]{1,0:T(8,128)S(1)} %get-tuple-element.32), channel_id=1, source_target_pairs={{1,2},{2,1},{3,4},{4,3},{5,6},{6,5},{7,8},{8,7},{9,10},{10,9},{11,... | collective-permute-start | bytes 565256 | tf_op jit(solution)/shard_map/ppermute | solution.py:787
  12.2 0.0 collective-permute-done.3.early_a
  12.2 0.1 collective-permute-start.6
  12.3 0.0 collective-permute-done.1.early_b
  12.4 0.5 %collective-permute-start.2 = (f32[64,128]{1,0:T(8,128)S(1)}, f32[64,128]{1,0:T(8,128)S(1)}, u32[]{:S(2)}, u32[]{:S(2)}) collective-permute-start(f32[64,128]{1,0:T(8,128)S(1)} %edge_rows.1), channel_id=1, source_target_pairs={{0,16},{16,0},{1,17},{17,1},{2,18},{18,2},{3,19},{19,3},{4,20},{20... | collective-permute-start | bytes 98312 | tf_op jit(solution)/shard_map/ppermute | solution.py:794
  12.9 0.1 maximum_bitcast_fusion.info
  13.0 0.6 %collective-permute-done.6.near = f32[256,128]{1,0:T(8,128)S(1)} collective-permute-done((f32[256,128]{1,0:T(8,128)S(1)}, f32[256,128]{1,0:T(8,128)S(1)}, u32[]{:S(2)}, u32[]{:S(2)}) %collective-permute-start.6) | collective-permute-done | bytes 131104 | tf_op jit(solution)/shard_map/ppermute | solution.py:794
  13.7 0.1 collective-permute-done.2.more_strips
  13.8 9.4 %collective-permute-done.4.late_a = f32[368,128]{1,0:T(8,128)S(1)} collective-permute-done((f32[368,128]{1,0:T(8,128)S(1)}, f32[368,128]{1,0:T(8,128)S(1)}, u32[]{:S(2)}, u32[]{:S(2)}) %collective-permute-start.4) | collective-permute-done | bytes 188448 | tf_op jit(solution)/shard_map/ppermute | solution.py:787
  23.2 0.0 collective-permute-done.5.late_b
  23.2 1.2 %whole_step.1 = (f32[3,4,80,128]{3,2,1,0:T(8,128)S(1)}, f32[6,4,80,128]{3,2,1,0:T(8,128)S(1)}, f32[624,128]{1,0:T(8,128)S(1)}, f32[624,128]{1,0:T(8,128)S(1)}, f32[288,128]{1,0:T(8,128)S(1)}) custom-call(f32[6,4,96,128]{3,2,1,0:T(8,128)S(1)} %get-tuple-element.25.s_pad, f32[3,4,80,128]{3,2,1,0:T(8,128)S(1)} %get-tuple-element.26.v_part, ...), custom_call_target="tpu_custom_call" | custom-call | flops 5333504 | bytes 5333504 | tf_op jit(solution)/shard_map/whole_step/pallas_call | solution.py:768
  24.4 3.5 %collective-permute-start.7 = (f32[624,128]{1,0:T(8,128)S(1)}, f32[624,128]{1,0:T(8,128)S(1)}, u32[]{:S(2)}, u32[]{:S(2)}) collective-permute-start(f32[624,128]{1,0:T(8,128)S(1)} %get-tuple-element.42), channel_id=1, source_target_pairs={{0,1},{1,0},{2,3},{3,2},{4,5},{5,4},{6,7},{7,6},{8,9},{9,8},{10,11... | collective-permute-start | bytes 958472 | tf_op jit(solution)/shard_map/ppermute | solution.py:787
  27.9 0.7 %collective-permute-start.8 = (f32[624,128]{1,0:T(8,128)S(1)}, f32[624,128]{1,0:T(8,128)S(1)}, u32[]{:S(2)}, u32[]{:S(2)}) collective-permute-start(f32[624,128]{1,0:T(8,128)S(1)} %get-tuple-element.43), channel_id=1, source_target_pairs={{1,2},{2,1},{3,4},{4,3},{5,6},{6,5},{7,8},{8,7},{9,10},{10,9},{11,... | collective-permute-start | bytes 958472 | tf_op jit(solution)/shard_map/ppermute | solution.py:787
  28.6 0.6 %floor_parts.1 = (f32[128,128]{1,0:T(8,128)S(1)}, f32[3,4,80,128]{3,2,1,0:T(8,128)S(1)}) custom-call(f32[6,4,80,128]{3,2,1,0:T(8,128)S(1)} %get-tuple-element.38.s, f32[3,4,80,128]{3,2,1,0:T(8,128)S(1)} %get-tuple-element.39.v, f32[4,64,128]{2,1,0:T(8,128)S(1)} %copy-done, f32[288,128]{1,0:T(8,128)S(1)} %get-tuple-element.40.b_near), custom_call_target="tpu_custom_call" | custom-call | flops 2310144 | bytes 2310144 | tf_op jit(solution)/shard_map/floor_parts/pallas_call | solution.py:768
  29.2 14.7 %all_to_all.5 = f32[64,2,128]{2,1,0:T(2,128)S(1)} all-to-all(f32[64,2,128]{2,1,0:T(2,128)S(1)} %bitcast.6), channel_id=1, replica_groups=mesh['sec'=2,'tile'=16] {'sec','tile'}, dimensions={0} | all-to-all | bytes 131072 | tf_op jit(solution)/shard_map/all_to_all | solution.py:880
  43.9 0.0 collective-permute-done.7.from_a
  43.9 0.0 collective-permute-done.8.from_b
  43.9 1.9 %finish.1 = (f32[3,4,64,128]{3,2,1,0:T(8,128)}, f32[6,4,64,128]{3,2,1,0:T(8,128)}, f32[3,64,256]{2,1,0:T(8,128)}) custom-call(f32[6,4,80,128]{3,2,1,0:T(8,128)S(1)} %get-tuple-element.38.s, f32[3,4,80,128]{3,2,1,0:T(8,128)S(1)} %get-tuple-element.41.v, f32[4,64,128]{2,1,0:T(8,128)S(1)} %copy-done, f32[4,64,128]{2,1,0:T(8,128)S(1)} %copy-done.4, ...), custom_call_target="tpu_custom_call" | custom-call | flops 4555264 | bytes 4555264 | tf_op jit(solution)/shard_map/finish/pallas_call | solution.py:768
  (17 shorter events, 0.1 us)
Async XLA Ops:
  0.6 5.9 %copy-start = (f32[4,64,128]{2,1,0:T(8,128)S(1)}, f32[4,64,128]{2,1,0:T(8,128)}, u32[]{:S(2)}) copy-start(f32[4,64,128]{2,1,0:T(8,128)} %b.9) | copy-start | bytes 393220
  0.6 5.9 %copy-start.1 = (f32[6,4,64,128]{3,2,1,0:T(8,128)S(1)}, f32[6,4,64,128]{3,2,1,0:T(8,128)}, u32[]{:S(2)}) copy-start(f32[6,4,64,128]{3,2,1,0:T(8,128)} %s.3) | copy-start | bytes 2359300
  0.7 5.9 %copy-start.3 = (f32[3,4,64,128]{3,2,1,0:T(8,128)S(1)}, f32[3,4,64,128]{3,2,1,0:T(8,128)}, u32[]{:S(2)}) copy-start(f32[3,4,64,128]{3,2,1,0:T(8,128)} %v.3) | copy-start | bytes 1179652
  0.7 11.5 %copy-start.7 = (s32[64,256]{1,0:T(8,128)S(1)}, s32[64,256]{1,0:T(8,128)}, u32[]{:S(2)}) copy-start(s32[64,256]{1,0:T(8,128)} %wet.2) | copy-start | bytes 196612
  0.7 11.5 %copy-start.6 = (f32[64,256]{1,0:T(8,128)S(1)}, f32[64,256]{1,0:T(8,128)}, u32[]{:S(2)}) copy-start(f32[64,256]{1,0:T(8,128)} %depth.2) | copy-start | bytes 196612
  0.7 11.5 %copy-start.2 = (f32[3,64,256]{2,1,0:T(8,128)S(1)}, f32[3,64,256]{2,1,0:T(8,128)}, u32[]{:S(2)}) copy-start(f32[3,64,256]{2,1,0:T(8,128)} %state.2) | copy-start | bytes 589828
  2.8 9.5 %copy-start.4 = (f32[4,64,128]{2,1,0:T(8,128)S(1)}, f32[4,64,128]{2,1,0:T(8,128)}, u32[]{:S(2)}) copy-start(f32[4,64,128]{2,1,0:T(8,128)} %lam.3) | copy-start | bytes 393220
  2.8 9.5 %copy-start.5 = (f32[4,64,128]{2,1,0:T(8,128)S(1)}, f32[4,64,128]{2,1,0:T(8,128)}, u32[]{:S(2)}) copy-start(f32[4,64,128]{2,1,0:T(8,128)} %mu.3) | copy-start | bytes 393220
  2.8 9.5 %copy-start.8 = (s32[64]{0:T(128)S(1)}, s32[64]{0:T(128)}, u32[]{:S(2)}) copy-start(s32[64]{0:T(128)} %param.18) | copy-start | bytes 772
  2.8 10.1 %copy-start.9 = (f32[64]{0:T(128)S(1)}, f32[64]{0:T(128)}, u32[]{:S(2)}) copy-start(f32[64]{0:T(128)} %param.19) | copy-start | bytes 772
  2.9 3.7 %collective-permute-start = (f32[320,128]{1,0:T(8,128)}, f32[320,128]{1,0:T(8,128)S(1)}, u32[]{:S(2)}, u32[]{:S(2)}) collective-permute-start(f32[320,128]{1,0:T(8,128)} %bitcast.7), channel_id=1, source_target_pairs={{0,16},{16,0},{1,17},{17,1},{2,18},{18,2},{3,19},{19,3},{4,20},{20... | collective-permute-start | bytes 491528 | tf_op jit(solution)/shard_map/ppermute | solution.py:794
  3.4 8.8 %collective-permute-start.3 = (f32[384,128]{1,0:T(8,128)}, f32[384,128]{1,0:T(8,128)S(1)}, u32[]{:S(2)}, u32[]{:S(2)}) collective-permute-start(f32[384,128]{1,0:T(8,128)} %get-tuple-element.30), channel_id=1, source_target_pairs={{0,1},{1,0},{2,3},{3,2},{4,5},{5,4},{6,7},{7,6},{8,9},{9,8},{10,11... | collective-permute-start | bytes 589832 | tf_op jit(solution)/shard_map/ppermute | solution.py:787
  5.9 6.4 %collective-permute-start.1 = (f32[384,128]{1,0:T(8,128)}, f32[384,128]{1,0:T(8,128)S(1)}, u32[]{:S(2)}, u32[]{:S(2)}) collective-permute-start(f32[384,128]{1,0:T(8,128)} %get-tuple-element.27), channel_id=1, source_target_pairs={{1,2},{2,1},{3,4},{4,3},{5,6},{6,5},{7,8},{8,7},{9,10},{10,9},{11,... | collective-permute-start | bytes 589832 | tf_op jit(solution)/shard_map/ppermute | solution.py:787
  7.2 16.0 %collective-permute-start.4 = (f32[368,128]{1,0:T(8,128)S(1)}, f32[368,128]{1,0:T(8,128)S(1)}, u32[]{:S(2)}, u32[]{:S(2)}) collective-permute-start(f32[368,128]{1,0:T(8,128)S(1)} %get-tuple-element.31), channel_id=1, source_target_pairs={{0,1},{1,0},{2,3},{3,2},{4,5},{5,4},{6,7},{7,6},{8,9},{9,8},{10,11... | collective-permute-start | bytes 565256 | tf_op jit(solution)/shard_map/ppermute | solution.py:787
  11.5 11.7 %collective-permute-start.5 = (f32[368,128]{1,0:T(8,128)S(1)}, f32[368,128]{1,0:T(8,128)S(1)}, u32[]{:S(2)}, u32[]{:S(2)}) collective-permute-start(f32[368,128]{1,0:T(8,128)S(1)} %get-tuple-element.32), channel_id=1, source_target_pairs={{1,2},{2,1},{3,4},{4,3},{5,6},{6,5},{7,8},{8,7},{9,10},{10,9},{11,... | collective-permute-start | bytes 565256 | tf_op jit(solution)/shard_map/ppermute | solution.py:787
  12.2 1.4 %collective-permute-start.6 = (f32[256,128]{1,0:T(8,128)S(1)}, f32[256,128]{1,0:T(8,128)S(1)}, u32[]{:S(2)}, u32[]{:S(2)}) collective-permute-start(f32[256,128]{1,0:T(8,128)S(1)} %near_columns.1), channel_id=1, source_target_pairs={{0,16},{16,0},{1,17},{17,1},{2,18},{18,2},{3,19},{19,3},{4,20},{20... | collective-permute-start | bytes 393224 | tf_op jit(solution)/shard_map/ppermute | solution.py:794
  12.4 1.4 %collective-permute-start.2 = (f32[64,128]{1,0:T(8,128)S(1)}, f32[64,128]{1,0:T(8,128)S(1)}, u32[]{:S(2)}, u32[]{:S(2)}) collective-permute-start(f32[64,128]{1,0:T(8,128)S(1)} %edge_rows.1), channel_id=1, source_target_pairs={{0,16},{16,0},{1,17},{17,1},{2,18},{18,2},{3,19},{19,3},{4,20},{20... | collective-permute-start | bytes 98312 | tf_op jit(solution)/shard_map/ppermute | solution.py:794
  24.4 19.5 %collective-permute-start.7 = (f32[624,128]{1,0:T(8,128)S(1)}, f32[624,128]{1,0:T(8,128)S(1)}, u32[]{:S(2)}, u32[]{:S(2)}) collective-permute-start(f32[624,128]{1,0:T(8,128)S(1)} %get-tuple-element.42), channel_id=1, source_target_pairs={{0,1},{1,0},{2,3},{3,2},{4,5},{5,4},{6,7},{7,6},{8,9},{9,8},{10,11... | collective-permute-start | bytes 958472 | tf_op jit(solution)/shard_map/ppermute | solution.py:787
  27.9 16.0 %collective-permute-start.8 = (f32[624,128]{1,0:T(8,128)S(1)}, f32[624,128]{1,0:T(8,128)S(1)}, u32[]{:S(2)}, u32[]{:S(2)}) collective-permute-start(f32[624,128]{1,0:T(8,128)S(1)} %get-tuple-element.43), channel_id=1, source_target_pairs={{1,2},{2,1},{3,4},{4,3},{5,6},{6,5},{7,8},{8,7},{9,10},{10,9},{11,... | collective-permute-start | bytes 958472 | tf_op jit(solution)/shard_map/ppermute | solution.py:787
